TPU v7x, 32 devices: a whole 2x2x4 slice. The times are simulated.
32 devices in a mesh: gx: 8 (over z, y), gy: 4 (over x, core).
Axes of the slice: x: 2, y: 2, z: 4, core: 2. Of those that a mesh axis runs over, the one named last changes fastest.
Arguments:
- amplitudes: bfloat16 [64, 1048576], P(None, ('gy', 'gx')), may hold values from -6 to 6
- virt_irreps: int32 [8], replicated, may hold values from 0 to 7, as said below
- w_tiles: bfloat16 [8192, 128, 128], P(('gx', 'gy')), may hold values from -0.1875 to 0.1875
- tile_rows: int32 [8192], P(('gx', 'gy')), may hold values from 0 to 2047, as said below
- tile_cols: int32 [8192], P(('gx', 'gy')), may hold values from 0 to 31
Outputs:
- ladder: float32 [64, 32768], P(None, ('gx', 'gy'))
Inputs may be any that keep to these rules, and one draw needn't show every extreme that they name: virt_irreps names each of the 8 irreps once. `tile_rows`: slot s of a device (s = t % 256) names a row tile in [q * 2048 // 8, (q + 1) * 2048 // 8) with q = s // (256 // 8); every stored tile has irrep(row(t)) == irrep(col(t)) for the drawn virt_irreps.
All inputs are finite; a program needn't handle non-finite values.
Results may differ from a plain program's by a relative error of at most 0.0003.
Values may be sent and summed in bfloat16 or wider, within the bound.
No kernel may reach another device: no remote copies, remote signals or barrier semaphores. Data moves between devices by JAX's collectives and lax.ppermute only.
A program may use at most 128 MiB of HBM per device.

v0:
```python
import jax
import jax.numpy as jnp
from jax import lax
from jax.sharding import PartitionSpec as P

V = 1024
BLK = 128
ABT_X = 32


def pair_irrep(tile, virt_irreps):
    first = tile * BLK // V // BLK
    second = tile * BLK % V // BLK
    return jnp.bitwise_xor(virt_irreps[first], virt_irreps[second])


def per_device(amplitudes, virt_irreps, w_tiles, tile_rows, tile_cols):
    occupied = amplitudes.shape[0]
    block = w_tiles.shape[1]
    peers = lax.axis_size("gx")
    local_tiles = amplitudes.shape[1] // block
    row_count = local_tiles * peers
    groups = lax.axis_size("gy")
    gathered = lax.all_gather(amplitudes, "gx", axis=1, tiled=True)
    amp_tiles = gathered.reshape(occupied, row_count, block)
    pieces = jnp.take(amp_tiles, tile_rows, axis=1)
    row_tile = lax.axis_index("gy") * row_count + tile_rows
    col_tile = lax.axis_index("gx") * ABT_X + tile_cols
    live = (pair_irrep(row_tile, virt_irreps) == pair_irrep(col_tile, virt_irreps)).astype(
        jnp.float32
    )
    product = jnp.einsum("psk,skn->spn", pieces, w_tiles, preferred_element_type=jnp.float32)
    product = product * live[:, None, None]
    summed_cols = jax.ops.segment_sum(product, tile_cols, num_segments=ABT_X)
    partial_value = jnp.transpose(summed_cols, (1, 0, 2)).reshape(occupied, ABT_X * block)
    summed = lax.psum(partial_value, "gy")
    share = partial_value.shape[1] // groups
    result = lax.dynamic_slice_in_dim(summed, lax.axis_index("gy") * share, share, 1)
    return result


def solution(mesh):
    in_specs = (
        P(None, ("gy", "gx")),
        P(),
        P(("gx", "gy"), None, None),
        P(("gx", "gy")),
        P(("gx", "gy")),
    )
    out_specs = P(None, ("gx", "gy"))
    return jax.shard_map(
        per_device, mesh=mesh, in_specs=in_specs, out_specs=out_specs, check_vma=False
    )
```

profile of v0, /device:TPU:8, one launch (start us, length us, event | category | flops | bytes accessed | tf_op | source)
XLA Modules:
  0.0 758.3 jit_solution(261004288208391760)
XLA Ops:
  6.5 0.0 all-gather.2.cloned.1.call-start
  6.5 0.7 all-gather.2.cloned.1.call-update
  7.3 0.0 all-reduce.2.cloned.1.call-start
  7.3 0.7 compare_select_fusion.4
  8.0 1.6 fusion.10
  9.6 5.4 compare_and_fusion
  15.0 632.8 %all-gather.2.cloned.1.call-done = bf16[64,262144]{1,0:T(8,128)(2,1)} async-done(((bf16[64,32768]{1,0:T(8,128)(2,1)}), bf16[64,262144]{1,0:T(8,128)(2,1)}) %all-gather.2.cloned.1.call-update) | async-done | bytes 33554448 | tf_op jit(solution)/shard_map/all_gather | solution.py:24
  647.8 23.1 %copy_bitcast_fusion = bf16[64,2048,128]{2,0,1:T(8,128)(2,1)} fusion(bf16[64,262144]{1,0:T(8,128)(2,1)} %all-gather.2.cloned.1.call-done), kind=kLoop, calls=%fused_computation.2 | loop fusion | bytes 67108864 | tf_op jit(solution)/shard_map/reshape | solution.py:25
  670.9 4.9 gather_fusion
  675.8 0.0 copy-start
  675.8 10.4 %broadcast_multiply_fusion = f32[256,64,128]{2,1,0:T(8,128)} fusion(f32[256]{0:T(256)S(1)} %get-tuple-element.6, bf16[256,128,128]{2,1,0:T(8,128)(2,1)} %param.7, bf16[256,64,128]{2,1,0:T(8,128)(2,1)} %gather_fusion, pred[256]{0:T(512)(128)(4,1)S(1)} %get-tuple-element.5), kind=kOutput, calls=%fused_computation.6 | convolution fusion | flops 541065216 | bytes 20972800 | tf_op jit(solution)/shard_map/psk,skn->spn/dot_general | solution.py:32
  686.2 0.1 broadcast_in_dim.31
  686.3 0.0 copy-done
  686.3 26.2 %scatter_fusion = f32[32,64,128]{2,1,0:T(8,128)S(1)} fusion(f32[32,64,128]{2,1,0:T(8,128)S(1)} %broadcast_in_dim.31, s32[256]{0:T(256)S(1)} %copy-done, f32[256,64,128]{2,1,0:T(8,128)} %broadcast_multiply_fusion), kind=kCustom, calls=%fused_computation.1 | custom fusion | flops 2097152 | bytes 25166848 | tf_op jit(solution)/shard_map/scatter-add | solution.py:34
  712.4 1.1 copy_bitcast_fusion.1
  713.5 0.0 all-reduce.2.cloned.1.call-update
  713.6 36.2 %all-reduce.2.cloned.1.call-done = f32[64,4096]{1,0:T(8,128)} async-done(((f32[64,4096]{1,0:T(8,128)}), f32[64,4096]{1,0:T(8,128)}) %all-reduce.2.cloned.1.call-update) | async-done | bytes 1048592 | tf_op jit(solution)/shard_map/psum | solution.py:36
  749.8 1.7 constant_dynamic-slice_fusion
  (1 shorter events, 0.0 us)
Async XLA Ops:
  6.5 641.3 %all-gather.2.cloned.1.call-start = ((), (), s32[]{:S(2)}) async-start(), calls=%async_computation | async-start | bytes 37748736 | tf_op jit(solution)/shard_map/all_gather | solution.py:24
  7.3 742.5 %all-reduce.2.cloned.1.call-start = ((), (), s32[]{:S(2)}) async-start(), calls=%async_computation.1 | async-start | bytes 2097152 | tf_op jit(solution)/shard_map/psum | solution.py:36
  675.8 10.5 %copy-start = (s32[256]{0:T(256)S(1)}, s32[256]{0:T(256)}, u32[]{:S(2)}) copy-start(s32[256]{0:T(256)} %param.9) | copy-start | bytes 3076
Sparse Core Ops, SparseCore 0:
  8.9 638.8 all-gather.1
  713.7 36.0 all-reduce.1
where the time goes:
time: 761 us; the launch traced here: 758 us
  waiting for transfers between devices  670 us (88%)
  local copies, waits for them, and re-layouts  32.4 us (4%)
  other arithmetic  32.3 us (4%)
  between operations  13.4 us (2%)
  matrix products  10.4 us (1%)
    all_gather x1, waiting for transfers between devices, per_device(): gathered = lax.all_gather(amplitudes, 'gx', axis=1, tiled=True)  633 us
    psum x1, waiting for transfers between devices, per_device(): summed = lax.psum(partial_value, 'gy')  36.2 us
    scatter-add x1, other arithmetic, per_device(): summed_cols = jax.ops.segment_sum(product, tile_cols, num_segments=ABT_X)  26.2 us
    reshape x1, local copies, waits for them, and re-layouts, per_device(): amp_tiles = gathered.reshape(occupied, row_count, block)  23.1 us
  transfers between devices with their start and end apart: 2, of which 2 were waited for; matrix products, arithmetic and copies ran while one was open for 1% of the time, Pallas kernels for 0%

commit v1 on v0

v1 whole, which is shorter than its diff:
```python
import functools

import jax
import jax.numpy as jnp
from jax import lax
from jax.experimental import pallas as pl
from jax.experimental.pallas import tpu as pltpu
from jax.sharding import PartitionSpec as P

V = 1024
BLK = 128
ABT_X = 32
CORES = 2
UNROLL = 4


def pair_irrep(tile, virt_irreps):
    first = tile * BLK // V // BLK
    second = tile * BLK % V // BLK
    return jnp.bitwise_xor(virt_irreps[first], virt_irreps[second])


def pick_kernel(peers, per, wanted, amp, *outs):
    for peer in range(peers):
        out = outs[peer]

        def step(i, carry):
            lane = pl.multiple_of(wanted[peer * per + i] * BLK, BLK)
            out[i] = amp[:, pl.ds(lane, BLK)]
            return carry

        lax.fori_loop(0, per, step, 0, unroll=8)


def pick(amplitudes, wanted, peers, per):
    occupied = amplitudes.shape[0]
    shape = jax.ShapeDtypeStruct((per, occupied, BLK), amplitudes.dtype)
    size = amplitudes.size * 2
    return pl.pallas_call(
        functools.partial(pick_kernel, peers, per),
        out_shape=[shape] * peers,
        in_specs=[
            pl.BlockSpec(memory_space=pltpu.SMEM),
            pl.BlockSpec(memory_space=pltpu.VMEM),
        ],
        out_specs=[pl.BlockSpec(memory_space=pltpu.VMEM)] * peers,
        compiler_params=pltpu.CompilerParams(vmem_limit_bytes=40 * 1024 * 1024),
        cost_estimate=pl.CostEstimate(flops=0, bytes_accessed=2 * size, transcendentals=0),
        name="pick_tiles",
    )(wanted, amplitudes)


def ladder_kernel(count, per, first, last, blocks, cols, live, w, *refs):
    pieces = refs[:count]
    refs = refs[count:]
    if not first:
        start, refs = refs[0], refs[1:]
    if last:
        keep, give, total, wbuf, pbuf, sems = refs
    else:
        total, wbuf, pbuf, sems = refs
    copies = []
    for j in range(count):
        a = pltpu.make_async_copy(w.at[blocks[j]], wbuf.at[j], sems.at[0, j])
        b = pltpu.make_async_copy(pieces[j], pbuf.at[j], sems.at[1, j])
        a.start()
        b.start()
        copies.append((a, b))
    total[...] = jnp.zeros_like(total) if first else start[...]
    for j in range(count):
        for copy in copies[j]:
            copy.wait()
        base = blocks[j] * per

        def step(i, carry):
            slots = [i * UNROLL + u for u in range(UNROLL)]
            products = [
                jnp.dot(pbuf[j, s], wbuf[j, s], preferred_element_type=jnp.float32)
                for s in slots
            ]
            for s, product in zip(slots, products):
                col = cols[base + s]
                total[col] += product * live[base + s]
            return carry

        lax.fori_loop(0, per // UNROLL, step, 0)
    if last:
        half = total.shape[0] // 2
        keep[...] = total[:half]
        give[...] = total[half:]


def ladder(blocks, cols, live, w, pieces, start, last):
    count = len(pieces)
    per, occupied, _ = pieces[0].shape
    first = start is None
    vmem = pl.BlockSpec(memory_space=pltpu.VMEM)
    smem = pl.BlockSpec(memory_space=pltpu.SMEM)
    anyspace = pl.BlockSpec(memory_space=pl.ANY)
    whole = (ABT_X, occupied, BLK)
    half = jax.ShapeDtypeStruct((ABT_X // 2, occupied, BLK), jnp.float32)
    scratch = [
        pltpu.VMEM((count, per, BLK, BLK), w.dtype),
        pltpu.VMEM((count, per, occupied, BLK), w.dtype),
        pltpu.SemaphoreType.DMA((2, count)),
    ]
    if last:
        out_shape = [half, half]
        scratch = [pltpu.VMEM(whole, jnp.float32)] + scratch
    else:
        out_shape = [jax.ShapeDtypeStruct(whole, jnp.float32)]
    args = [blocks, cols, live, w, *pieces] + ([] if first else [start])
    out = pl.pallas_call(
        functools.partial(ladder_kernel, count, per, first, last),
        out_shape=out_shape,
        in_specs=[smem] * 3 + [anyspace] * (1 + count) + [vmem] * (not first),
        out_specs=[vmem] * len(out_shape),
        scratch_shapes=scratch,
        compiler_params=pltpu.CompilerParams(vmem_limit_bytes=40 * 1024 * 1024),
        cost_estimate=pl.CostEstimate(
            flops=2 * count * per * occupied * BLK * BLK,
            bytes_accessed=count * per * 2 * BLK * (BLK + occupied),
            transcendentals=0,
        ),
        name="ladder_tiles",
    )(*args)
    return out if last else out[0]


def per_device(amplitudes, virt_irreps, w_tiles, tile_rows, tile_cols):
    occupied = amplitudes.shape[0]
    peers = lax.axis_size("gx")
    groups = lax.axis_size("gy")
    me = lax.axis_index("gx")
    mine = lax.axis_index("gy")
    local_tiles = amplitudes.shape[1] // BLK
    row_count = local_tiles * peers
    slots = tile_rows.shape[0]
    per = slots // peers

    by_peer = tile_rows.reshape(peers, per) - jnp.arange(peers, dtype=jnp.int32)[:, None] * local_tiles
    wanted = lax.all_to_all(by_peer, "gx", 0, 0)
    order = jnp.arange(peers, dtype=jnp.int32) ^ me
    wanted = jnp.take(wanted, order, axis=0).reshape(slots)

    row_tile = mine * row_count + tile_rows
    col_tile = me * ABT_X + tile_cols
    live = (pair_irrep(row_tile, virt_irreps) == pair_irrep(col_tile, virt_irreps)).astype(
        jnp.float32
    )
    share = ABT_X // groups
    xs = groups // CORES
    owner = tile_cols // share
    other_core = (owner % CORES) ^ (mine % CORES)
    other_x = (owner // CORES) ^ (mine // CORES)
    cols = other_core * (ABT_X // CORES) + other_x * share + tile_cols % share

    outgoing = pick(amplitudes, wanted, peers, per)
    w = w_tiles.reshape(peers, per, BLK, BLK)
    arrived = [outgoing[0]]
    for k in range(1, peers):
        arrived.append(lax.ppermute(outgoing[k], "gx", [(i, i ^ k) for i in range(peers)]))
    near = peers // 2
    total = ladder(order[:near], cols, live, w, arrived[:near], None, False)
    keep, give = ladder(order[near:], cols, live, w, arrived[near:], total, True)

    got = lax.ppermute(give, "gy", [(i, i ^ 1) for i in range(groups)])
    keep = keep.reshape(xs, share, occupied, BLK)
    got = got.reshape(xs, share, occupied, BLK)
    result = keep[0] + got[0]
    for k in range(1, xs):
        result = result + lax.ppermute(
            keep[k] + got[k], "gy", [(i, i ^ (k * CORES)) for i in range(groups)]
        )
    return jnp.transpose(result, (1, 0, 2)).reshape(occupied, share * BLK)


def solution(mesh):
    in_specs = (
        P(None, ("gy", "gx")),
        P(),
        P(("gx", "gy"), None, None),
        P(("gx", "gy")),
        P(("gx", "gy")),
    )
    out_specs = P(None, ("gx", "gy"))
    return jax.shard_map(
        per_device, mesh=mesh, in_specs=in_specs, out_specs=out_specs, check_vma=False
    )
```

time: 761 us -> 131 us (0.17)
  waiting for transfers between devices: 670 us -> 77.4 us
  other arithmetic: 32.3 us -> 8.11 us
  local copies, waits for them, and re-layouts: 32.4 us -> 10.5 us
  starting transfers between devices: 0.04 us -> 17.8 us
  Pallas kernels: 0 us -> 16.5 us
  between operations: 13.4 us -> 0.08 us
  matrix products: 10.4 us -> 0 us
    all_gather x1 -> x0, waiting for transfers between devices: 633 us -> none  [per_device(): gathered = lax.all_gather(amplitudes, 'gx', axis=1, tiled=True)]
    ppermute x0 -> x9, waiting for transfers between devices: none -> 72.5 us  [the longest x7 63.8 us: per_device(): lax.ppermute(outgoing[k], 'gx', [(i, i ^ k) for i in range(peers)])]
    psum x1 -> x0, waiting for transfers between devices: 36.2 us -> none  [per_device(): summed = lax.psum(partial_value, 'gy')]
    scatter-add x1 -> x0, other arithmetic: 26.2 us -> none  [per_device(): summed_cols = jax.ops.segment_sum(product, tile_cols, num_segments=ABT_X)]
    reshape x2 -> x1, local copies, waits for them, and re-layouts: 24.1 us -> 0.76 us  [per_device(): tile_rows.reshape(peers, per)]
    pallas_call x0 -> x3, Pallas kernels: none -> 16.5 us  [the longest x2 13.2 us: ladder(): pl.pallas_call(functools.partial(ladder_kernel, count, per, first, last),...]
    ppermute x0 -> x9, starting transfers between devices: none -> 11.5 us  [the longest x7 9.87 us: per_device(): lax.ppermute(outgoing[k], 'gx', [(i, i ^ k) for i in range(peers)])]
    dot_general x1 -> x0, matrix products: 10.4 us -> none  [per_device(): jnp.einsum('psk,skn->spn', pieces, w_tiles, preferred_element_type=jnp.fl...]
  transfers between devices with their start and end apart: 2 -> 10, of which waited for: 2 -> 8; matrix products, arithmetic and copies ran while one was open for 1% -> 6% of each run, Pallas kernels for 0% -> 5%
where the time goes in v1:
time: 131 us; the launch traced here: 130 us
  waiting for transfers between devices  77.4 us (59%)
  starting transfers between devices  17.8 us (14%)
  Pallas kernels  16.5 us (13%)
  local copies, waits for them, and re-layouts  10.5 us (8%)
  other arithmetic  8.11 us (6%)
    ppermute x7, waiting for transfers between devices, per_device(): lax.ppermute(outgoing[k], 'gx', [(i, i ^ k) for i in range(peers)])  63.8 us
    pallas_call x2, Pallas kernels, ladder(): pl.pallas_call(functools.partial(ladder_kernel, count, per, first, last),...  13.2 us
    ppermute x7, starting transfers between devices, per_device(): lax.ppermute(outgoing[k], 'gx', [(i, i ^ k) for i in range(peers)])  9.87 us
    unnamed x10, local copies, waits for them, and re-layouts  7.41 us
    ppermute x1, waiting for transfers between devices, per_device(): lax.ppermute(keep[k] + got[k], 'gy', [(i, i ^ k * CORES) for i in range(g...  6.86 us
    all_to_all x1, starting transfers between devices, per_device(): wanted = lax.all_to_all(by_peer, 'gx', 0, 0)  6.28 us
    convert_element_type x1, other arithmetic, per_device(): (pair_irrep(row_tile, virt_irreps) == pair_irrep(col_tile, virt_irreps))....  5.86 us
    all_to_all x1, waiting for transfers between devices, per_device(): wanted = lax.all_to_all(by_peer, 'gx', 0, 0)  4.88 us
  transfers between devices with their start and end apart: 10, of which 8 were waited for; matrix products, arithmetic and copies ran while one was open for 6% of the time, Pallas kernels for 5%

profile of v1, /device:TPU:8, one launch (start us, length us, event | category | flops | bytes accessed | tf_op | source)
XLA Modules:
  0.0 130.4 jit_solution(15594934295038140379)
XLA Ops:
  0.0 0.8 reshape.81
  0.8 0.7 broadcast_subtract_fusion
  1.4 6.3 %all-to-all-start = ((s32[8,1,32]{2,1,0:T(1,128)}), s32[8,1,32]{2,1,0:T(1,128)S(1)}, u32[]{:S(2)}, u32[]{:S(2)}) async-start(s32[8,1,32]{2,1,0:T(1,128)} %broadcast_subtract_fusion), calls=%async_computation | async-start | bytes 8192 | tf_op jit(solution)/shard_map/all_to_all | solution.py:142
  7.7 4.9 %all-to-all-done = s32[8,1,32]{2,1,0:T(1,128)S(1)} async-done(((s32[8,1,32]{2,1,0:T(1,128)}), s32[8,1,32]{2,1,0:T(1,128)S(1)}, u32[]{:S(2)}, u32[]{:S(2)}) %all-to-all-start) | async-done | bytes 1056 | tf_op jit(solution)/shard_map/all_to_all | solution.py:142
  12.6 0.6 gather_fusion
  13.2 0.1 broadcast_select_fusion
  13.3 0.1 select_n.112.wanted
  13.3 0.0 copy-start.2
  13.3 2.2 %copy-done.2 = bf16[64,32768]{1,0:T(8,128)(2,1)S(1)} copy-done((bf16[64,32768]{1,0:T(8,128)(2,1)S(1)}, bf16[64,32768]{1,0:T(8,128)(2,1)}, u32[]{:S(2)}) %copy-start.2) | copy-done | bytes 4194328
  15.5 3.3 %pick_tiles.1 = (bf16[32,64,128]{2,1,0:T(8,128)(2,1)S(1)}, bf16[32,64,128]{2,1,0:T(8,128)(2,1)S(1)}, bf16[32,64,128]{2,1,0:T(8,128)(2,1)S(1)}, bf16[32,64,128]{2...) custom-call(s32[256]{0:T(256)S(1)} %select_n.112.wanted, ...), custom_call_target="tpu_custom_call" | custom-call | bytes 8388608 | tf_op jit(solution)/shard_map/pick_tiles/pallas_call | solution.py:39
  18.8 0.6 collective-permute-start.4
  19.4 1.4 %collective-permute-start.5 = (bf16[32,64,128]{2,1,0:T(8,128)(2,1)S(1)}, bf16[32,64,128]{2,1,0:T(8,128)(2,1)S(1)}, u32[]{:S(2)}, u32[]{:S(2)}) collective-permute-start(bf16[32,64,128]{2,1,0:T(8,128)(2,1)S(1)} %get-tuple-element.21), channel_id=1, source_target_pairs={{0,8},{4,12},{8,0},{12,4},{16,24},{20,28},{24,16},{28,20},{1,9},{5... | collective-permute-start | bytes 1572872 | tf_op jit(solution)/shard_map/ppermute | solution.py:162
  20.9 0.1 fusion.7
  20.9 0.6 collective-permute-start
  21.5 3.3 %collective-permute-start.1 = (bf16[32,64,128]{2,1,0:T(8,128)(2,1)}, bf16[32,64,128]{2,1,0:T(8,128)(2,1)S(1)}, u32[]{:S(2)}, u32[]{:S(2)}) collective-permute-start(bf16[32,64,128]{2,1,0:T(8,128)(2,1)} %get-tuple-element.16), channel_id=1, source_target_pairs={{0,20},{4,16},{8,28},{12,24},{16,4},{20,0},{24,12},{28,8},{1,21},{... | collective-permute-start | bytes 1572872 | tf_op jit(solution)/shard_map/ppermute | solution.py:162
  24.8 0.0 collective-permute-start.2
  24.8 6.3 %collective-permute-done.4.refs_1_ = bf16[32,64,128]{2,1,0:T(8,128)(2,1)S(1)} collective-permute-done((bf16[32,64,128]{2,1,0:T(8,128)(2,1)S(1)}, bf16[32,64,128]{2,1,0:T(8,128)(2,1)S(1)}, u32[]{:S(2)}, u32[]{:S(2)}) %collective-permute-start.4) | collective-permute-done | bytes 524320 | tf_op jit(solution)/shard_map/ppermute | solution.py:162
  31.1 0.6 collective-permute-start.3
  31.6 8.5 %collective-permute-done.5.refs_2_ = bf16[32,64,128]{2,1,0:T(8,128)(2,1)S(1)} collective-permute-done((bf16[32,64,128]{2,1,0:T(8,128)(2,1)S(1)}, bf16[32,64,128]{2,1,0:T(8,128)(2,1)S(1)}, u32[]{:S(2)}, u32[]{:S(2)}) %collective-permute-start.5) | collective-permute-done | bytes 524320 | tf_op jit(solution)/shard_map/ppermute | solution.py:162
  40.1 0.0 copy-start.3
  40.1 0.8 copy-done.3
  40.9 3.4 %collective-permute-start.6 = (bf16[32,64,128]{2,1,0:T(8,128)(2,1)}, bf16[32,64,128]{2,1,0:T(8,128)(2,1)}, u32[]{:S(2)}, u32[]{:S(2)}) collective-permute-start(bf16[32,64,128]{2,1,0:T(8,128)(2,1)} %get-tuple-element.22), channel_id=1, source_target_pairs={{0,12},{4,8},{8,4},{12,0},{16,28},{20,24},{24,20},{28,16},{1,13},{... | collective-permute-start | bytes 1572872 | tf_op jit(solution)/shard_map/ppermute | solution.py:162
  44.4 1.6 %fusion.8 = (s32[1]{0:T(128)}, s32[1]{0:T(128)}, s32[1]{0:T(128)}, s32[1]{0:T(128)}, s32[1]{0:T(128)}, /*index=5*/s32[1]{0:T(128)}, s32[1]{0:T(128)}, s32[1]{0:T(128)}) fusion(s32[8]{0:T(128)} %param.6), kind=kLoop, calls=%fused_computation.89 | loop fusion | bytes 64 | tf_op jit(solution)/shard_map/gather | solution.py:20
  46.0 0.7 fusion.5.cols
  46.7 5.9 %compare_convert_fusion.live = f32[256]{0:T(256)S(1)} fusion(s32[256]{0:T(256)} %param.9, s32[256]{0:T(256)} %param.8, s32[]{:T(128)} %bitcast, s32[]{:T(128)} %bitcast.1, s32[]{:T(128)} %bitcast.2, s32[]{:T(128)} %bitcast.3, s32[]{:T(128)} %bitcast.4, s32[]{:T(128)} %bitcast.5, s32[]{:T(128)} %bitcast.6, s32[]{:T(128)} %bitcast.7, s32[]{:T(128)S(6)} %mul.36, ...), kind=kLoop, calls=%fused_computation.44 | loop fusion | flops 44544 | bytes 3112 | tf_op jit(solution)/shard_map/convert_element_type | solution.py:148
  52.6 36.0 %collective-permute-done.6.refs_3_ = bf16[32,64,128]{2,1,0:T(8,128)(2,1)} collective-permute-done((bf16[32,64,128]{2,1,0:T(8,128)(2,1)}, bf16[32,64,128]{2,1,0:T(8,128)(2,1)}, u32[]{:S(2)}, u32[]{:S(2)}) %collective-permute-start.6) | collective-permute-done | bytes 524320 | tf_op jit(solution)/shard_map/ppermute | solution.py:162
  88.6 0.0 copy-start
  88.6 3.4 %copy-done = bf16[256,128,128]{2,1,0:T(8,128)(2,1)S(1)} copy-done((bf16[256,128,128]{2,1,0:T(8,128)(2,1)S(1)}, bf16[256,128,128]{2,1,0:T(8,128)(2,1)}, u32[]{:S(2)}) %copy-start) | copy-done | bytes 8388632
  92.0 0.0 copy-start.4
  92.0 1.0 copy-done.4
  93.0 0.0 copy-start.1
  93.0 6.6 %ladder_tiles.2.refs_4_ = f32[32,64,128]{2,1,0:T(8,128)S(1)} custom-call(s32[4]{0:T(128)S(1)} %get-tuple-element.25.blocks, s32[256]{0:T(256)S(1)} %fusion.5.cols, f32[256]{0:T(256)S(1)} %compare_convert_fusion.live, bf16[8,32,128,128]{3,2,1,0:T(8,128)(2,1)S(1)} %bitcast.18, bf16[32,64,128]{2,1,0:T(8,128)(2,1)S(1)} %get-tuple-element.19.refs_0_, ...), custom_call_target="tpu_custom_call" | custom-call | flops 268435456 | bytes 6291456 | tf_op jit(solution)/shard_map/ladder_tiles/pallas_call | solution.py:113
  99.6 0.0 collective-permute-done.refs_0_
  99.6 0.0 collective-permute-done.1.refs_1_
  99.6 3.9 %collective-permute-done.2.refs_2_ = bf16[32,64,128]{2,1,0:T(8,128)(2,1)S(1)} collective-permute-done((bf16[32,64,128]{2,1,0:T(8,128)(2,1)}, bf16[32,64,128]{2,1,0:T(8,128)(2,1)S(1)}, u32[]{:S(2)}, u32[]{:S(2)}) %collective-permute-start.2) | collective-permute-done | bytes 524320 | tf_op jit(solution)/shard_map/ppermute | solution.py:162
  103.5 9.1 %collective-permute-done.3.refs_3_ = bf16[32,64,128]{2,1,0:T(8,128)(2,1)} collective-permute-done((bf16[32,64,128]{2,1,0:T(8,128)(2,1)}, bf16[32,64,128]{2,1,0:T(8,128)(2,1)}, u32[]{:S(2)}, u32[]{:S(2)}) %collective-permute-start.3) | collective-permute-done | bytes 524320 | tf_op jit(solution)/shard_map/ppermute | solution.py:162
  112.6 0.0 copy-done.1
  112.6 6.7 %ladder_tiles.3 = (f32[16,64,128]{2,1,0:T(8,128)S(1)}, f32[16,64,128]{2,1,0:T(8,128)S(1)}) custom-call(s32[4]{0:T(128)S(1)} %get-tuple-element.26.blocks, s32[256]{0:T(256)S(1)} %fusion.5.cols, f32[256]{0:T(256)S(1)} %compare_convert_fusion.live, bf16[8,32,128,128]{3,2,1,0:T(8,128)(2,1)S(1)} %bitcast.19, ...), custom_call_target="tpu_custom_call" | custom-call | flops 268435456 | bytes 6291456 | tf_op jit(solution)/shard_map/ladder_tiles/pallas_call | solution.py:113
  119.2 0.1 collective-permute-start.7
  119.3 1.9 %collective-permute-done.7 = f32[16,64,128]{2,1,0:T(8,128)S(1)} collective-permute-done((f32[16,64,128]{2,1,0:T(8,128)S(1)}, f32[16,64,128]{2,1,0:T(8,128)S(1)}, u32[]{:S(2)}, u32[]{:S(2)}) %collective-permute-start.7) | collective-permute-done | bytes 524320 | tf_op jit(solution)/shard_map/ppermute | solution.py:167
  121.2 1.6 %collective-permute-start.8 = (f32[8,64,128]{2,1,0:T(8,128)S(1)}, f32[8,64,128]{2,1,0:T(8,128)S(1)}, u32[]{:S(2)}, u32[]{:S(2)}) collective-permute-start(f32[8,64,128]{2,1,0:T(8,128)S(1)} %slice_add_fusion), channel_id=1, source_target_pairs={{0,2},{1,3},{2,0},{3,1},{4,6},{5,7},{6,4},{7,5},{8,10},{9,11},{10,... | collective-permute-start | bytes 786440 | tf_op jit(solution)/shard_map/ppermute | solution.py:172
  122.8 6.9 %collective-permute-done.8 = f32[8,64,128]{2,1,0:T(8,128)S(1)} collective-permute-done((f32[8,64,128]{2,1,0:T(8,128)S(1)}, f32[8,64,128]{2,1,0:T(8,128)S(1)}, u32[]{:S(2)}, u32[]{:S(2)}) %collective-permute-start.8) | collective-permute-done | bytes 262176 | tf_op jit(solution)/shard_map/ppermute | solution.py:172
  129.7 0.7 copy_bitcast_fusion
  (6 shorter events, 0.1 us)
Async XLA Ops:
  1.4 11.2 %all-to-all-start = ((s32[8,1,32]{2,1,0:T(1,128)}), s32[8,1,32]{2,1,0:T(1,128)S(1)}, u32[]{:S(2)}, u32[]{:S(2)}) async-start(s32[8,1,32]{2,1,0:T(1,128)} %broadcast_subtract_fusion), calls=%async_computation | async-start | bytes 8192 | tf_op jit(solution)/shard_map/all_to_all | solution.py:142
  13.3 2.2 %copy-start.2 = (bf16[64,32768]{1,0:T(8,128)(2,1)S(1)}, bf16[64,32768]{1,0:T(8,128)(2,1)}, u32[]{:S(2)}) copy-start(bf16[64,32768]{1,0:T(8,128)(2,1)} %amp.1) | copy-start | bytes 12582916
  18.8 12.2 %collective-permute-start.4 = (bf16[32,64,128]{2,1,0:T(8,128)(2,1)S(1)}, bf16[32,64,128]{2,1,0:T(8,128)(2,1)S(1)}, u32[]{:S(2)}, u32[]{:S(2)}) collective-permute-start(bf16[32,64,128]{2,1,0:T(8,128)(2,1)S(1)} %get-tuple-element.20), channel_id=1, source_target_pairs={{0,4},{4,0},{8,12},{12,8},{16,20},{20,16},{24,28},{28,24},{1,5},{5... | collective-permute-start | bytes 1572872 | tf_op jit(solution)/shard_map/ppermute | solution.py:162
  19.4 20.7 %collective-permute-start.5 = (bf16[32,64,128]{2,1,0:T(8,128)(2,1)S(1)}, bf16[32,64,128]{2,1,0:T(8,128)(2,1)S(1)}, u32[]{:S(2)}, u32[]{:S(2)}) collective-permute-start(bf16[32,64,128]{2,1,0:T(8,128)(2,1)S(1)} %get-tuple-element.21), channel_id=1, source_target_pairs={{0,8},{4,12},{8,0},{12,4},{16,24},{20,28},{24,16},{28,20},{1,9},{5... | collective-permute-start | bytes 1572872 | tf_op jit(solution)/shard_map/ppermute | solution.py:162
  20.9 78.6 %collective-permute-start = (bf16[32,64,128]{2,1,0:T(8,128)(2,1)}, bf16[32,64,128]{2,1,0:T(8,128)(2,1)S(1)}, u32[]{:S(2)}, u32[]{:S(2)}) collective-permute-start(bf16[32,64,128]{2,1,0:T(8,128)(2,1)} %get-tuple-element.15), channel_id=1, source_target_pairs={{0,16},{4,20},{8,24},{12,28},{16,0},{20,4},{24,8},{28,12},{1,17},{... | collective-permute-start | bytes 1572872 | tf_op jit(solution)/shard_map/ppermute | solution.py:162
  21.5 78.1 %collective-permute-start.1 = (bf16[32,64,128]{2,1,0:T(8,128)(2,1)}, bf16[32,64,128]{2,1,0:T(8,128)(2,1)S(1)}, u32[]{:S(2)}, u32[]{:S(2)}) collective-permute-start(bf16[32,64,128]{2,1,0:T(8,128)(2,1)} %get-tuple-element.16), channel_id=1, source_target_pairs={{0,20},{4,16},{8,28},{12,24},{16,4},{20,0},{24,12},{28,8},{1,21},{... | collective-permute-start | bytes 1572872 | tf_op jit(solution)/shard_map/ppermute | solution.py:162
  24.8 78.7 %collective-permute-start.2 = (bf16[32,64,128]{2,1,0:T(8,128)(2,1)}, bf16[32,64,128]{2,1,0:T(8,128)(2,1)S(1)}, u32[]{:S(2)}, u32[]{:S(2)}) collective-permute-start(bf16[32,64,128]{2,1,0:T(8,128)(2,1)} %get-tuple-element.17), channel_id=1, source_target_pairs={{0,24},{4,28},{8,16},{12,20},{16,8},{20,12},{24,0},{28,4},{1,25},{... | collective-permute-start | bytes 1572872 | tf_op jit(solution)/shard_map/ppermute | solution.py:162
  31.1 81.5 %collective-permute-start.3 = (bf16[32,64,128]{2,1,0:T(8,128)(2,1)}, bf16[32,64,128]{2,1,0:T(8,128)(2,1)}, u32[]{:S(2)}, u32[]{:S(2)}) collective-permute-start(bf16[32,64,128]{2,1,0:T(8,128)(2,1)} %get-tuple-element.18), channel_id=1, source_target_pairs={{0,28},{4,24},{8,20},{12,16},{16,12},{20,8},{24,4},{28,0},{1,29},{... | collective-permute-start | bytes 1572872 | tf_op jit(solution)/shard_map/ppermute | solution.py:162
  40.1 0.8 copy-start.3
  40.9 47.6 %collective-permute-start.6 = (bf16[32,64,128]{2,1,0:T(8,128)(2,1)}, bf16[32,64,128]{2,1,0:T(8,128)(2,1)}, u32[]{:S(2)}, u32[]{:S(2)}) collective-permute-start(bf16[32,64,128]{2,1,0:T(8,128)(2,1)} %get-tuple-element.22), channel_id=1, source_target_pairs={{0,12},{4,8},{8,4},{12,0},{16,28},{20,24},{24,20},{28,16},{1,13},{... | collective-permute-start | bytes 1572872 | tf_op jit(solution)/shard_map/ppermute | solution.py:162
  88.6 3.4 %copy-start = (bf16[256,128,128]{2,1,0:T(8,128)(2,1)S(1)}, bf16[256,128,128]{2,1,0:T(8,128)(2,1)}, u32[]{:S(2)}) copy-start(bf16[256,128,128]{2,1,0:T(8,128)(2,1)} %param.7) | copy-start | bytes 25165828
  92.0 1.0 copy-start.4
  93.0 19.6 %copy-start.1 = (bf16[256,128,128]{2,1,0:T(8,128)(2,1)S(1)}, bf16[256,128,128]{2,1,0:T(8,128)(2,1)}, u32[]{:S(2)}) copy-start(bf16[256,128,128]{2,1,0:T(8,128)(2,1)} %param.7) | copy-start | bytes 25165828
  119.2 2.0 %collective-permute-start.7 = (f32[16,64,128]{2,1,0:T(8,128)S(1)}, f32[16,64,128]{2,1,0:T(8,128)S(1)}, u32[]{:S(2)}, u32[]{:S(2)}) collective-permute-start(f32[16,64,128]{2,1,0:T(8,128)S(1)} %get-tuple-element.24), channel_id=1, source_target_pairs={{0,1},{1,0},{2,3},{3,2},{4,5},{5,4},{6,7},{7,6},{8,9},{9,8},{10,11... | collective-permute-start | bytes 1572872 | tf_op jit(solution)/shard_map/ppermute | solution.py:167
  121.2 8.4 %collective-permute-start.8 = (f32[8,64,128]{2,1,0:T(8,128)S(1)}, f32[8,64,128]{2,1,0:T(8,128)S(1)}, u32[]{:S(2)}, u32[]{:S(2)}) collective-permute-start(f32[8,64,128]{2,1,0:T(8,128)S(1)} %slice_add_fusion), channel_id=1, source_target_pairs={{0,2},{1,3},{2,0},{3,1},{4,6},{5,7},{6,4},{7,5},{8,10},{9,11},{10,... | collective-permute-start | bytes 786440 | tf_op jit(solution)/shard_map/ppermute | solution.py:172

commit v2 on v0

v2 whole, which is shorter than its diff:
```python
import functools

import jax
import jax.numpy as jnp
from jax import lax
from jax.experimental import pallas as pl
from jax.experimental.pallas import tpu as pltpu
from jax.sharding import PartitionSpec as P

V = 1024
BLK = 128
ABT_X = 32
CORES = 2
UNROLL = 16
MIB = 1024 * 1024

VMEM_SPEC = pl.BlockSpec(memory_space=pltpu.VMEM)
SMEM_SPEC = pl.BlockSpec(memory_space=pltpu.SMEM)
ANY_SPEC = pl.BlockSpec(memory_space=pl.ANY)


def pair_irrep(tile, virt_irreps):
    first = tile * BLK // V // BLK
    second = tile * BLK % V // BLK
    return jnp.bitwise_xor(virt_irreps[first], virt_irreps[second])


def stage_kernel(source, held, sem):
    copy = pltpu.make_async_copy(source, held, sem)
    copy.start()
    copy.wait()


def stage(x):
    return pl.pallas_call(
        stage_kernel,
        out_shape=pltpu.VMEM(x.shape, x.dtype),
        in_specs=[ANY_SPEC],
        out_specs=VMEM_SPEC,
        scratch_shapes=[pltpu.SemaphoreType.DMA],
        compiler_params=pltpu.CompilerParams(vmem_limit_bytes=8 * MIB),
        cost_estimate=pl.CostEstimate(flops=0, bytes_accessed=2 * x.size, transcendentals=0),
        name="stage_amplitudes",
    )(pltpu.with_memory_space_constraint(x, pltpu.HBM))


def pick_kernel(per, local_tiles, me, before, rows, amp, out, after):
    base = me[0] * per
    origin = me[0] * local_tiles
    after[0] = before[0]

    def step(i, carry):
        lane = pl.multiple_of((rows[base + i] - origin) * BLK, BLK)
        out[i] = amp[:, pl.ds(lane, BLK)]
        return carry

    lax.fori_loop(0, per, step, 0, unroll=8)


def pick(me, before, rows, amp, per):
    occupied, width = amp.shape
    return pl.pallas_call(
        functools.partial(pick_kernel, per, width // BLK),
        out_shape=[
            jax.ShapeDtypeStruct((per, occupied, BLK), amp.dtype),
            jax.ShapeDtypeStruct((1,), jnp.int32),
        ],
        in_specs=[SMEM_SPEC] * 3 + [VMEM_SPEC],
        out_specs=[VMEM_SPEC, SMEM_SPEC],
        compiler_params=pltpu.CompilerParams(vmem_limit_bytes=8 * MIB),
        cost_estimate=pl.CostEstimate(
            flops=0, bytes_accessed=4 * per * occupied * BLK, transcendentals=0
        ),
        name="pick_tiles",
    )(me, before, rows, amp)


def add_products(per, base, cols, live, piece, weights, total):
    unroll = min(UNROLL, per)

    def step(i, carry):
        slots = [i * unroll + u for u in range(unroll)]
        products = [
            jnp.dot(piece[s], weights[s], preferred_element_type=jnp.float32) for s in slots
        ]
        for s, product in zip(slots, products):
            total[cols[base + s]] += product * live[base + s]
        return carry

    lax.fori_loop(0, per // unroll, step, 0)


def near_kernel(near, per, order, cols, live, w, *refs):
    pieces = refs[:near]
    total, far_w, near_w, sems = refs[near:]
    count = far_w.shape[0]
    copies = []
    for j in range(near + count):
        target = near_w.at[j] if j < near else far_w.at[j - near]
        copies.append(pltpu.make_async_copy(w.at[order[j]], target, sems.at[j]))
        copies[-1].start()
    total[...] = jnp.zeros_like(total)
    for j in range(near):
        copies[j].wait()
        add_products(per, order[j] * per, cols, live, pieces[j], near_w.at[j], total)
    for copy in copies[near:]:
        copy.wait()


def near_part(order, cols, live, w, pieces):
    near = len(pieces)
    peers = w.shape[0]
    per, occupied, _ = pieces[0].shape
    return pl.pallas_call(
        functools.partial(near_kernel, near, per),
        out_shape=[
            pltpu.VMEM((ABT_X, occupied, BLK), jnp.float32),
            pltpu.VMEM((peers - near, per, BLK, BLK), w.dtype),
        ],
        in_specs=[SMEM_SPEC] * 3 + [ANY_SPEC] + [VMEM_SPEC] * near,
        out_specs=[VMEM_SPEC, VMEM_SPEC],
        scratch_shapes=[
            pltpu.VMEM((near, per, BLK, BLK), w.dtype),
            pltpu.SemaphoreType.DMA((peers,)),
        ],
        compiler_params=pltpu.CompilerParams(vmem_limit_bytes=12 * MIB),
        cost_estimate=pl.CostEstimate(
            flops=2 * near * per * occupied * BLK * BLK,
            bytes_accessed=2 * w.size,
            transcendentals=0,
        ),
        name="near_products",
    )(order, cols, live, pltpu.with_memory_space_constraint(w, pltpu.HBM), *pieces)


def far_kernel(count, skip, per, last, order, cols, live, w, start, *refs):
    pieces = refs[:count]
    outs = refs[count:]
    total = start if last else outs[0]
    for j in range(count):
        base = order[order.shape[0] - w.shape[0] + skip + j] * per
        add_products(per, base, cols, live, pieces[j], w.at[skip + j], total)
    if last:
        at = 0
        for out in outs:
            out[...] = total[at : at + out.shape[0]]
            at += out.shape[0]


def far_part(order, cols, live, w, skip, start, pieces, last):
    count = len(pieces)
    per, occupied, _ = pieces[0].shape
    if last:
        out_shape = [jax.ShapeDtypeStruct((n, occupied, BLK), jnp.float32) for n in last]
        aliases = {}
    else:
        out_shape = [pltpu.VMEM(start.shape, start.dtype)]
        aliases = {4: 0}
    return pl.pallas_call(
        functools.partial(far_kernel, count, skip, per, last),
        out_shape=out_shape,
        in_specs=[SMEM_SPEC] * 3 + [VMEM_SPEC] * (2 + count),
        out_specs=[VMEM_SPEC] * len(out_shape),
        input_output_aliases=aliases,
        compiler_params=pltpu.CompilerParams(vmem_limit_bytes=8 * MIB),
        cost_estimate=pl.CostEstimate(
            flops=2 * count * per * occupied * BLK * BLK,
            bytes_accessed=4 * start.size,
            transcendentals=0,
        ),
        name="far_products",
    )(order, cols, live, w, start, *pieces)


def per_device(amplitudes, virt_irreps, w_tiles, tile_rows, tile_cols):
    occupied = amplitudes.shape[0]
    peers = lax.axis_size("gx")
    groups = lax.axis_size("gy")
    me = lax.axis_index("gx")
    mine = lax.axis_index("gy")
    row_count = amplitudes.shape[1] // BLK * peers
    per = tile_rows.shape[0] // peers
    near = peers // 2

    def swap(x, k):
        return lax.ppermute(x, "gx", [(i, i ^ k) for i in range(peers)])

    amp = stage(amplitudes)
    here = me.reshape(1)
    zero = jnp.zeros((1,), jnp.int32)
    arrived = {}
    for group in (range(near, peers), range(1, near)):
        rows = tile_rows + zero
        rows_of = [swap(rows, k) for k in group]
        for k, wanted in zip(group, rows_of):
            picked, zero = pick(here, zero, wanted, amp, per)
            arrived[k] = swap(picked, k)
    arrived[0], _ = pick(here, zero, tile_rows, amp, per)

    row_tile = mine * row_count + tile_rows
    col_tile = me * ABT_X + tile_cols
    live = (pair_irrep(row_tile, virt_irreps) == pair_irrep(col_tile, virt_irreps)).astype(
        jnp.float32
    )
    share = ABT_X // groups
    xs = groups // CORES
    owner = tile_cols // share
    other_core = (owner % CORES) ^ (mine % CORES)
    other_x = (owner // CORES) ^ (mine // CORES)
    cols = other_core * (ABT_X // CORES) + other_x * share + tile_cols % share
    order = jnp.arange(peers, dtype=jnp.int32) ^ me

    w = w_tiles.reshape(peers, per, BLK, BLK)
    total, far_w = near_part(order, cols, live, w, [arrived[k] for k in range(near)])
    half = near // 2
    (total,) = far_part(
        order, cols, live, far_w, 0, total, [arrived[near + k] for k in range(half)], None
    )
    sizes = (share, (xs - 1) * share) * CORES
    keep, keep_rest, give, give_rest = far_part(
        order, cols, live, far_w, half, total, [arrived[near + k] for k in range(half, near)], sizes
    )

    def swap_gy(x, k):
        return lax.ppermute(x, "gy", [(i, i ^ k) for i in range(groups)])

    rest = (keep_rest + swap_gy(give_rest, 1)).reshape(xs - 1, share, occupied, BLK)
    result = keep + swap_gy(give, 1)
    for k in range(1, xs):
        result = result + swap_gy(rest[k - 1], k * CORES)
    return jnp.transpose(result, (1, 0, 2)).reshape(occupied, share * BLK)


def solution(mesh):
    in_specs = (
        P(None, ("gy", "gx")),
        P(),
        P(("gx", "gy"), None, None),
        P(("gx", "gy")),
        P(("gx", "gy")),
    )
    out_specs = P(None, ("gx", "gy"))
    return jax.shard_map(
        per_device, mesh=mesh, in_specs=in_specs, out_specs=out_specs, check_vma=False
    )
```

time: 761 us -> 147 us (0.19)
  the two profiles are of different devices: /device:TPU:8 before, /device:TPU:0 now
where the time goes in v2:
time: 147 us
  waiting for transfers between devices  82.2 us (56%)
  starting transfers between devices  29 us (20%)
  Pallas kernels  26.2 us (18%)
  other arithmetic  6.49 us (4%)
  local copies, waits for them, and re-layouts  2.89 us (2%)
    ppermute x14, waiting for transfers between devices, swap(): return lax.ppermute(x, 'gx', [(i, i ^ k) for i in range(peers)])  74.3 us
    ppermute x14, starting transfers between devices, swap(): return lax.ppermute(x, 'gx', [(i, i ^ k) for i in range(peers)])  26.8 us
    pallas_call x8, Pallas kernels, pick(): pl.pallas_call(functools.partial(pick_kernel, per, width // BLK), out_sha...  16 us
    ppermute x3, waiting for transfers between devices, swap_gy(): return lax.ppermute(x, 'gy', [(i, i ^ k) for i in range(groups)])  7.88 us
    convert_element_type x1, other arithmetic, per_device(): (pair_irrep(row_tile, virt_irreps) == pair_irrep(col_tile, virt_irreps))....  5.11 us
    pallas_call x1, Pallas kernels, near_part(): pl.pallas_call(functools.partial(near_kernel, near, per), out_shape=[pltp...  4.1 us
    pallas_call x2, Pallas kernels, far_part(): pl.pallas_call(functools.partial(far_kernel, count, skip, per, last), out...  3.94 us
  transfers between devices with their start and end apart: 17, of which 8 were waited for; matrix products, arithmetic and copies ran while one was open for 4% of the time, Pallas kernels for 14%

profile of v2, /device:TPU:0, one launch (start us, length us, event | category | flops | bytes accessed | tf_op | source)
XLA Modules:
  0.0 146.9 jit_solution(17301603467054322573)
XLA Ops:
  0.0 4.0 %collective-permute-start = (s32[256]{0:T(256)}, s32[256]{0:T(256)S(1)}, u32[]{:S(2)}, u32[]{:S(2)}) collective-permute-start(s32[256]{0:T(256)} %rows.1), channel_id=1, source_target_pairs={{0,16},{4,20},{8,24},{12,28},{16,0},{20,4},{24,8},{28,12},{1,17},{... | collective-permute-start | bytes 3080 | tf_op jit(solution)/shard_map/ppermute | solution.py:186
  4.0 1.3 collective-permute-start.1
  5.3 3.6 %collective-permute-start.2 = (s32[256]{0:T(256)}, s32[256]{0:T(256)S(1)}, u32[]{:S(2)}, u32[]{:S(2)}) collective-permute-start(s32[256]{0:T(256)} %rows.1), channel_id=1, source_target_pairs={{0,24},{4,28},{8,16},{12,20},{16,8},{20,12},{24,0},{28,4},{1,25},{... | collective-permute-start | bytes 3080 | tf_op jit(solution)/shard_map/ppermute | solution.py:186
  8.9 0.0 collective-permute-start.3
  8.9 2.2 %stage_amplitudes.1.amp = bf16[64,32768]{1,0:T(8,128)(2,1)S(1)} custom-call(bf16[64,32768]{1,0:T(8,128)(2,1)} %source.1), custom_call_target="tpu_custom_call" | custom-call | bytes 4194304 | tf_op jit(solution)/shard_map/stage_amplitudes/pallas_call | solution.py:35
  11.1 0.0 collective-permute-done.rows
  11.2 2.0 %pick_tiles.8 = (bf16[32,64,128]{2,1,0:T(8,128)(2,1)}, s32[1]{0:T(128)}) custom-call(s32[1]{0:T(128)} %bitcast.9.me, s32[1]{0:T(128)} %constant.144.clone.1.before, s32[256]{0:T(256)S(1)} %collective-permute-done.rows, bf16[64,32768]{1,0:T(8,128)(2,1)S(1)} %stage_amplitudes.1.amp), custom_call_target="tpu_custom_call" | custom-call | bytes 1048576 | tf_op jit(solution)/shard_map/pick_tiles/pallas_call | solution.py:62
  13.2 2.2 %pick_tiles.9 = (bf16[32,64,128]{2,1,0:T(8,128)(2,1)}, s32[1]{0:T(128)}) custom-call(s32[1]{0:T(128)} %bitcast.9.me, s32[1]{0:T(128)} %get-tuple-element.26.before, s32[256]{0:T(256)S(1)} %collective-permute-done.1.rows, bf16[64,32768]{1,0:T(8,128)(2,1)S(1)} %stage_amplitudes.1.amp), custom_call_target="tpu_custom_call" | custom-call | bytes 1048576 | tf_op jit(solution)/shard_map/pick_tiles/pallas_call | solution.py:62
  15.3 0.0 copy-start.2
  15.4 2.2 %pick_tiles.10 = (bf16[32,64,128]{2,1,0:T(8,128)(2,1)}, s32[1]{0:T(128)}) custom-call(s32[1]{0:T(128)} %bitcast.9.me, s32[1]{0:T(128)} %get-tuple-element.27.before, s32[256]{0:T(256)S(1)} %collective-permute-done.2.rows, bf16[64,32768]{1,0:T(8,128)(2,1)S(1)} %stage_amplitudes.1.amp), custom_call_target="tpu_custom_call" | custom-call | bytes 1048576 | tf_op jit(solution)/shard_map/pick_tiles/pallas_call | solution.py:62
  17.5 2.1 %pick_tiles.11 = (bf16[32,64,128]{2,1,0:T(8,128)(2,1)}, s32[1]{0:T(128)}) custom-call(s32[1]{0:T(128)} %bitcast.9.me, s32[1]{0:T(128)} %get-tuple-element.28.before, s32[256]{0:T(256)S(1)} %collective-permute-done.3.rows, bf16[64,32768]{1,0:T(8,128)(2,1)S(1)} %stage_amplitudes.1.amp), custom_call_target="tpu_custom_call" | custom-call | bytes 1048576 | tf_op jit(solution)/shard_map/pick_tiles/pallas_call | solution.py:62
  19.6 0.6 broadcast_add_fusion
  20.2 1.7 %collective-permute-start.4 = (s32[256]{0:T(256)S(1)}, s32[256]{0:T(256)S(1)}, u32[]{:S(2)}, u32[]{:S(2)}) collective-permute-start(s32[256]{0:T(256)S(1)} %broadcast_add_fusion), channel_id=1, source_target_pairs={{0,4},{4,0},{8,12},{12,8},{16,20},{20,16},{24,28},{28,24},{1,5},{5... | collective-permute-start | bytes 3080 | tf_op jit(solution)/shard_map/ppermute | solution.py:186
  22.0 0.0 collective-permute-start.5
  22.0 1.8 %collective-permute-start.6 = (s32[256]{0:T(256)S(1)}, s32[256]{0:T(256)S(1)}, u32[]{:S(2)}, u32[]{:S(2)}) collective-permute-start(s32[256]{0:T(256)S(1)} %broadcast_add_fusion), channel_id=1, source_target_pairs={{0,12},{4,8},{8,4},{12,0},{16,28},{20,24},{24,20},{28,16},{1,13},{... | collective-permute-start | bytes 3080 | tf_op jit(solution)/shard_map/ppermute | solution.py:186
  23.8 0.1 collective-permute-done.4.rows
  23.9 2.1 %pick_tiles.12 = (bf16[32,64,128]{2,1,0:T(8,128)(2,1)}, s32[1]{0:T(128)}) custom-call(s32[1]{0:T(128)} %bitcast.9.me, s32[1]{0:T(128)} %get-tuple-element.29.before, s32[256]{0:T(256)S(1)} %collective-permute-done.4.rows, bf16[64,32768]{1,0:T(8,128)(2,1)S(1)} %stage_amplitudes.1.amp), custom_call_target="tpu_custom_call" | custom-call | bytes 1048576 | tf_op jit(solution)/shard_map/pick_tiles/pallas_call | solution.py:62
  26.0 0.0 collective-permute-done.5.rows
  26.0 0.0 copy-start.3
  26.0 0.0 copy-start.4
  26.0 1.8 %pick_tiles.13 = (bf16[32,64,128]{2,1,0:T(8,128)(2,1)S(1)}, s32[1]{0:T(128)}) custom-call(s32[1]{0:T(128)} %bitcast.9.me, s32[1]{0:T(128)} %get-tuple-element.30.before, s32[256]{0:T(256)S(1)} %collective-permute-done.5.rows, bf16[64,32768]{1,0:T(8,128)(2,1)S(1)} %stage_amplitudes.1.amp), custom_call_target="tpu_custom_call" | custom-call | bytes 1048576 | tf_op jit(solution)/shard_map/pick_tiles/pallas_call | solution.py:62
  27.8 0.0 collective-permute-done.6.rows
  27.9 1.8 %pick_tiles.14 = (bf16[32,64,128]{2,1,0:T(8,128)(2,1)S(1)}, s32[1]{0:T(128)}) custom-call(s32[1]{0:T(128)} %bitcast.9.me, s32[1]{0:T(128)} %get-tuple-element.31.before, s32[256]{0:T(256)S(1)} %collective-permute-done.6.rows, bf16[64,32768]{1,0:T(8,128)(2,1)S(1)} %stage_amplitudes.1.amp), custom_call_target="tpu_custom_call" | custom-call | bytes 1048576 | tf_op jit(solution)/shard_map/pick_tiles/pallas_call | solution.py:62
  29.7 1.1 collective-permute-start.9
  30.8 2.1 %collective-permute-start.8 = (bf16[32,64,128]{2,1,0:T(8,128)(2,1)S(1)}, bf16[32,64,128]{2,1,0:T(8,128)(2,1)S(1)}, u32[]{:S(2)}, u32[]{:S(2)}) collective-permute-start(bf16[32,64,128]{2,1,0:T(8,128)(2,1)S(1)} %get-tuple-element.35), channel_id=1, source_target_pairs={{0,8},{4,12},{8,0},{12,4},{16,24},{20,28},{24,16},{28,20},{1,9},{5... | collective-permute-start | bytes 1572872 | tf_op jit(solution)/shard_map/ppermute | solution.py:186
  32.9 0.7 fusion.4
  33.6 3.5 %collective-permute-start.13 = (bf16[32,64,128]{2,1,0:T(8,128)(2,1)}, bf16[32,64,128]{2,1,0:T(8,128)(2,1)S(1)}, u32[]{:S(2)}, u32[]{:S(2)}) collective-permute-start(bf16[32,64,128]{2,1,0:T(8,128)(2,1)} %get-tuple-element.42), channel_id=1, source_target_pairs={{0,28},{4,24},{8,20},{12,16},{16,12},{20,8},{24,4},{28,0},{1,29},{... | collective-permute-start | bytes 1572872 | tf_op jit(solution)/shard_map/ppermute | solution.py:186
  37.1 0.1 collective-permute-start.12
  37.2 1.4 collective-permute-start.11
  38.6 8.7 %collective-permute-done.9.refs_3_ = bf16[32,64,128]{2,1,0:T(8,128)(2,1)S(1)} collective-permute-done((bf16[32,64,128]{2,1,0:T(8,128)(2,1)S(1)}, bf16[32,64,128]{2,1,0:T(8,128)(2,1)S(1)}, u32[]{:S(2)}, u32[]{:S(2)}) %collective-permute-start.9) | collective-permute-done | bytes 524320 | tf_op jit(solution)/shard_map/ppermute | solution.py:186
  47.3 5.6 %collective-permute-start.10 = (bf16[32,64,128]{2,1,0:T(8,128)(2,1)}, bf16[32,64,128]{2,1,0:T(8,128)(2,1)}, u32[]{:S(2)}, u32[]{:S(2)}) collective-permute-start(bf16[32,64,128]{2,1,0:T(8,128)(2,1)} %get-tuple-element.39), channel_id=1, source_target_pairs={{0,16},{4,20},{8,24},{12,28},{16,0},{20,4},{24,8},{28,12},{1,17},{... | collective-permute-start | bytes 1572872 | tf_op jit(solution)/shard_map/ppermute | solution.py:186
  52.9 5.7 %collective-permute-done.8.refs_2_ = bf16[32,64,128]{2,1,0:T(8,128)(2,1)S(1)} collective-permute-done((bf16[32,64,128]{2,1,0:T(8,128)(2,1)S(1)}, bf16[32,64,128]{2,1,0:T(8,128)(2,1)S(1)}, u32[]{:S(2)}, u32[]{:S(2)}) %collective-permute-start.8) | collective-permute-done | bytes 524320 | tf_op jit(solution)/shard_map/ppermute | solution.py:186
  58.5 0.5 collective-permute-start.7
  59.0 5.1 %compare_convert_fusion.live = f32[256]{0:T(256)S(1)} fusion(s32[256]{0:T(256)S(1)} %copy-done.4, s32[256]{0:T(256)S(1)} %copy-done.2, s32[]{:T(128)} %bitcast, s32[]{:T(128)} %bitcast.1, s32[]{:T(128)} %bitcast.2, s32[]{:T(128)} %bitcast.3, s32[]{:T(128)} %bitcast.4, s32[]{:T(128)} %bitcast.5, s32[]{:T(128)} %bitcast.6, s32[]{:T(128)} %bitcast.7, ...), kind=kLoop, calls=%fused_computation.34 | loop fusion | flops 44544 | bytes 3112 | tf_op jit(solution)/shard_map/convert_element_type | solution.py:202
  64.2 2.2 %copy-done.1 = bf16[64,32768]{1,0:T(8,128)(2,1)S(1)} copy-done((bf16[64,32768]{1,0:T(8,128)(2,1)S(1)}, bf16[64,32768]{1,0:T(8,128)(2,1)}, u32[]{:S(2)}) %copy-start.1) | copy-done | bytes 4194328
  66.3 1.8 %pick_tiles.15 = (bf16[32,64,128]{2,1,0:T(8,128)(2,1)S(1)}, s32[1]{0:T(128)}) custom-call(s32[1]{0:T(128)} %bitcast.9.me, s32[1]{0:T(128)} %get-tuple-element.32.before, s32[256]{0:T(256)S(1)} %copy-done.2, bf16[64,32768]{1,0:T(8,128)(2,1)S(1)} %copy-done.1), custom_call_target="tpu_custom_call" | custom-call | bytes 1048576 | tf_op jit(solution)/shard_map/pick_tiles/pallas_call | solution.py:62
  68.2 10.1 %collective-permute-done.7.refs_1_ = bf16[32,64,128]{2,1,0:T(8,128)(2,1)S(1)} collective-permute-done((bf16[32,64,128]{2,1,0:T(8,128)(2,1)}, bf16[32,64,128]{2,1,0:T(8,128)(2,1)S(1)}, u32[]{:S(2)}, u32[]{:S(2)}) %collective-permute-start.7) | collective-permute-done | bytes 524320 | tf_op jit(solution)/shard_map/ppermute | solution.py:186
  78.3 4.1 %near_products.1 = (f32[32,64,128]{2,1,0:T(8,128)S(1)}, bf16[4,32,128,128]{3,2,1,0:T(8,128)(2,1)S(1)}) custom-call(s32[8]{0:T(128)S(1)} %iota_xor_fusion.order, s32[256]{0:T(256)S(1)} %fusion.3.cols, f32[256]{0:T(256)S(1)} %compare_convert_fusion.live, bf16[8,32,128,128]{3,2,1,0:T(8,128)(2,1)} %bitcast.17, ...), custom_call_target="tpu_custom_call" | custom-call | flops 268435456 | bytes 8388608 | tf_op jit(solution)/shard_map/near_products/pallas_call | solution.py:114
  82.4 40.8 %collective-permute-done.11.refs_1_ = bf16[32,64,128]{2,1,0:T(8,128)(2,1)S(1)} collective-permute-done((bf16[32,64,128]{2,1,0:T(8,128)(2,1)}, bf16[32,64,128]{2,1,0:T(8,128)(2,1)S(1)}, u32[]{:S(2)}, u32[]{:S(2)}) %collective-permute-start.11) | collective-permute-done | bytes 524320 | tf_op jit(solution)/shard_map/ppermute | solution.py:186
  123.1 9.0 %collective-permute-done.10.refs_0_ = bf16[32,64,128]{2,1,0:T(8,128)(2,1)} collective-permute-done((bf16[32,64,128]{2,1,0:T(8,128)(2,1)}, bf16[32,64,128]{2,1,0:T(8,128)(2,1)}, u32[]{:S(2)}, u32[]{:S(2)}) %collective-permute-start.10) | collective-permute-done | bytes 524320 | tf_op jit(solution)/shard_map/ppermute | solution.py:186
  132.2 2.2 %far_products.2.start = f32[32,64,128]{2,1,0:T(8,128)S(1)} custom-call(s32[8]{0:T(128)S(1)} %iota_xor_fusion.order, s32[256]{0:T(256)S(1)} %fusion.3.cols, f32[256]{0:T(256)S(1)} %compare_convert_fusion.live, bf16[4,32,128,128]{3,2,1,0:T(8,128)(2,1)S(1)} %get-tuple-element.37.w, ...), custom_call_target="tpu_custom_call", output_to_operand_aliasing={{}: (4, {})} | custom-call | flops 134217728 | bytes 1048576 | tf_op jit(solution)/shard_map/far_products/pallas_call | solution.py:159
  134.4 1.8 %far_products.3 = (f32[8,64,128]{2,1,0:T(8,128)S(1)}, f32[8,64,128]{2,1,0:T(8,128)S(1)}, f32[8,64,128]{2,1,0:T(8,128)S(1)}, f32[8,64,128]{2,1,0:T(8,128)S(1)}) custom-call(s32[8]{0:T(128)S(1)} %iota_xor_fusion.order, s32[256]{0:T(256)S(1)} %fusion.3.cols, f32[256]{0:T(256)S(1)} %compare_convert_fusion.live, ...), custom_call_target="tpu_custom_call" | custom-call | flops 134217728 | bytes 1048576 | tf_op jit(solution)/shard_map/far_products/pallas_call | solution.py:159
  136.2 0.1 collective-permute-start.15
  136.2 0.5 collective-permute-start.14
  136.7 1.0 collective-permute-done.15
  137.8 1.6 %collective-permute-start.16 = (f32[8,64,128]{2,1,0:T(8,128)S(1)}, f32[8,64,128]{2,1,0:T(8,128)S(1)}, u32[]{:S(2)}, u32[]{:S(2)}) collective-permute-start(f32[8,64,128]{2,1,0:T(8,128)S(1)} %add.99), channel_id=1, source_target_pairs={{0,2},{1,3},{2,0},{3,1},{4,6},{5,7},{6,4},{7,5},{8,10},{9,11},{10,... | collective-permute-start | bytes 786440 | tf_op jit(solution)/shard_map/ppermute | solution.py:225
  139.4 6.9 %collective-permute-done.16 = f32[8,64,128]{2,1,0:T(8,128)S(1)} collective-permute-done((f32[8,64,128]{2,1,0:T(8,128)S(1)}, f32[8,64,128]{2,1,0:T(8,128)S(1)}, u32[]{:S(2)}, u32[]{:S(2)}) %collective-permute-start.16) | collective-permute-done | bytes 262176 | tf_op jit(solution)/shard_map/ppermute | solution.py:225
  146.2 0.7 copy_bitcast_fusion
  (15 shorter events, 0.1 us)
Async XLA Ops:
  0.0 11.2 %collective-permute-start = (s32[256]{0:T(256)}, s32[256]{0:T(256)S(1)}, u32[]{:S(2)}, u32[]{:S(2)}) collective-permute-start(s32[256]{0:T(256)} %rows.1), channel_id=1, source_target_pairs={{0,16},{4,20},{8,24},{12,28},{16,0},{20,4},{24,8},{28,12},{1,17},{... | collective-permute-start | bytes 3080 | tf_op jit(solution)/shard_map/ppermute | solution.py:186
  4.0 9.1 %collective-permute-start.1 = (s32[256]{0:T(256)}, s32[256]{0:T(256)S(1)}, u32[]{:S(2)}, u32[]{:S(2)}) collective-permute-start(s32[256]{0:T(256)} %rows.1), channel_id=1, source_target_pairs={{0,20},{4,16},{8,28},{12,24},{16,4},{20,0},{24,12},{28,8},{1,21},{... | collective-permute-start | bytes 3080 | tf_op jit(solution)/shard_map/ppermute | solution.py:186
  5.3 10.0 %collective-permute-start.2 = (s32[256]{0:T(256)}, s32[256]{0:T(256)S(1)}, u32[]{:S(2)}, u32[]{:S(2)}) collective-permute-start(s32[256]{0:T(256)} %rows.1), channel_id=1, source_target_pairs={{0,24},{4,28},{8,16},{12,20},{16,8},{20,12},{24,0},{28,4},{1,25},{... | collective-permute-start | bytes 3080 | tf_op jit(solution)/shard_map/ppermute | solution.py:186
  8.9 8.6 %collective-permute-start.3 = (s32[256]{0:T(256)}, s32[256]{0:T(256)S(1)}, u32[]{:S(2)}, u32[]{:S(2)}) collective-permute-start(s32[256]{0:T(256)} %rows.1), channel_id=1, source_target_pairs={{0,28},{4,24},{8,20},{12,16},{16,12},{20,8},{24,4},{28,0},{1,29},{... | collective-permute-start | bytes 3080 | tf_op jit(solution)/shard_map/ppermute | solution.py:186
  11.1 16.7 %copy-start = (bf16[64,32768]{1,0:T(8,128)(2,1)}, bf16[64,32768]{1,0:T(8,128)(2,1)S(1)}, u32[]{:S(2)}) copy-start(bf16[64,32768]{1,0:T(8,128)(2,1)S(1)} %stage_amplitudes.1.amp) | copy-start | bytes 12582916
  15.3 4.3 %copy-start.2 = (s32[256]{0:T(256)S(1)}, s32[256]{0:T(256)}, u32[]{:S(2)}) copy-start(s32[256]{0:T(256)} %rows.1) | copy-start | bytes 3076
  20.2 3.6 %collective-permute-start.4 = (s32[256]{0:T(256)S(1)}, s32[256]{0:T(256)S(1)}, u32[]{:S(2)}, u32[]{:S(2)}) collective-permute-start(s32[256]{0:T(256)S(1)} %broadcast_add_fusion), channel_id=1, source_target_pairs={{0,4},{4,0},{8,12},{12,8},{16,20},{20,16},{24,28},{28,24},{1,5},{5... | collective-permute-start | bytes 3080 | tf_op jit(solution)/shard_map/ppermute | solution.py:186
  22.0 4.0 %collective-permute-start.5 = (s32[256]{0:T(256)S(1)}, s32[256]{0:T(256)S(1)}, u32[]{:S(2)}, u32[]{:S(2)}) collective-permute-start(s32[256]{0:T(256)S(1)} %broadcast_add_fusion), channel_id=1, source_target_pairs={{0,8},{4,12},{8,0},{12,4},{16,24},{20,28},{24,16},{28,20},{1,9},{5... | collective-permute-start | bytes 3080 | tf_op jit(solution)/shard_map/ppermute | solution.py:186
  22.0 5.9 %collective-permute-start.6 = (s32[256]{0:T(256)S(1)}, s32[256]{0:T(256)S(1)}, u32[]{:S(2)}, u32[]{:S(2)}) collective-permute-start(s32[256]{0:T(256)S(1)} %broadcast_add_fusion), channel_id=1, source_target_pairs={{0,12},{4,8},{8,4},{12,0},{16,28},{20,24},{24,20},{28,16},{1,13},{... | collective-permute-start | bytes 3080 | tf_op jit(solution)/shard_map/ppermute | solution.py:186
  26.0 6.9 %copy-start.3 = (s32[8]{0:T(128)S(1)}, s32[8]{0:T(128)}, u32[]{:S(2)}) copy-start(s32[8]{0:T(128)} %param.6) | copy-start | bytes 100
  26.0 33.0 %copy-start.4 = (s32[256]{0:T(256)S(1)}, s32[256]{0:T(256)}, u32[]{:S(2)}) copy-start(s32[256]{0:T(256)} %param.9) | copy-start | bytes 3076
  29.7 17.6 %collective-permute-start.9 = (bf16[32,64,128]{2,1,0:T(8,128)(2,1)S(1)}, bf16[32,64,128]{2,1,0:T(8,128)(2,1)S(1)}, u32[]{:S(2)}, u32[]{:S(2)}) collective-permute-start(bf16[32,64,128]{2,1,0:T(8,128)(2,1)S(1)} %get-tuple-element.36), channel_id=1, source_target_pairs={{0,12},{4,8},{8,4},{12,0},{16,28},{20,24},{24,20},{28,16},{1,13},{... | collective-permute-start | bytes 1572872 | tf_op jit(solution)/shard_map/ppermute | solution.py:186
  30.8 27.8 %collective-permute-start.8 = (bf16[32,64,128]{2,1,0:T(8,128)(2,1)S(1)}, bf16[32,64,128]{2,1,0:T(8,128)(2,1)S(1)}, u32[]{:S(2)}, u32[]{:S(2)}) collective-permute-start(bf16[32,64,128]{2,1,0:T(8,128)(2,1)S(1)} %get-tuple-element.35), channel_id=1, source_target_pairs={{0,8},{4,12},{8,0},{12,4},{16,24},{20,28},{24,16},{28,20},{1,9},{5... | collective-permute-start | bytes 1572872 | tf_op jit(solution)/shard_map/ppermute | solution.py:186
  33.6 100.8 %collective-permute-start.13 = (bf16[32,64,128]{2,1,0:T(8,128)(2,1)}, bf16[32,64,128]{2,1,0:T(8,128)(2,1)S(1)}, u32[]{:S(2)}, u32[]{:S(2)}) collective-permute-start(bf16[32,64,128]{2,1,0:T(8,128)(2,1)} %get-tuple-element.42), channel_id=1, source_target_pairs={{0,28},{4,24},{8,20},{12,16},{16,12},{20,8},{24,4},{28,0},{1,29},{... | collective-permute-start | bytes 1572872 | tf_op jit(solution)/shard_map/ppermute | solution.py:186
  37.1 97.3 %collective-permute-start.12 = (bf16[32,64,128]{2,1,0:T(8,128)(2,1)}, bf16[32,64,128]{2,1,0:T(8,128)(2,1)S(1)}, u32[]{:S(2)}, u32[]{:S(2)}) collective-permute-start(bf16[32,64,128]{2,1,0:T(8,128)(2,1)} %get-tuple-element.41), channel_id=1, source_target_pairs={{0,24},{4,28},{8,16},{12,20},{16,8},{20,12},{24,0},{28,4},{1,25},{... | collective-permute-start | bytes 1572872 | tf_op jit(solution)/shard_map/ppermute | solution.py:186
  37.2 85.9 %collective-permute-start.11 = (bf16[32,64,128]{2,1,0:T(8,128)(2,1)}, bf16[32,64,128]{2,1,0:T(8,128)(2,1)S(1)}, u32[]{:S(2)}, u32[]{:S(2)}) collective-permute-start(bf16[32,64,128]{2,1,0:T(8,128)(2,1)} %get-tuple-element.40), channel_id=1, source_target_pairs={{0,20},{4,16},{8,28},{12,24},{16,4},{20,0},{24,12},{28,8},{1,21},{... | collective-permute-start | bytes 1572872 | tf_op jit(solution)/shard_map/ppermute | solution.py:186
  47.3 84.9 %collective-permute-start.10 = (bf16[32,64,128]{2,1,0:T(8,128)(2,1)}, bf16[32,64,128]{2,1,0:T(8,128)(2,1)}, u32[]{:S(2)}, u32[]{:S(2)}) collective-permute-start(bf16[32,64,128]{2,1,0:T(8,128)(2,1)} %get-tuple-element.39), channel_id=1, source_target_pairs={{0,16},{4,20},{8,24},{12,28},{16,0},{20,4},{24,8},{28,12},{1,17},{... | collective-permute-start | bytes 1572872 | tf_op jit(solution)/shard_map/ppermute | solution.py:186
  58.5 19.7 %collective-permute-start.7 = (bf16[32,64,128]{2,1,0:T(8,128)(2,1)}, bf16[32,64,128]{2,1,0:T(8,128)(2,1)S(1)}, u32[]{:S(2)}, u32[]{:S(2)}) collective-permute-start(bf16[32,64,128]{2,1,0:T(8,128)(2,1)} %get-tuple-element.34), channel_id=1, source_target_pairs={{0,4},{4,0},{8,12},{12,8},{16,20},{20,16},{24,28},{28,24},{1,5},{5... | collective-permute-start | bytes 1572872 | tf_op jit(solution)/shard_map/ppermute | solution.py:186
  64.2 2.2 %copy-start.1 = (bf16[64,32768]{1,0:T(8,128)(2,1)S(1)}, bf16[64,32768]{1,0:T(8,128)(2,1)}, u32[]{:S(2)}) copy-start(bf16[64,32768]{1,0:T(8,128)(2,1)} %copy-done) | copy-start | bytes 12582916
  136.2 1.6 %collective-permute-start.15 = (f32[8,64,128]{2,1,0:T(8,128)S(1)}, f32[8,64,128]{2,1,0:T(8,128)S(1)}, u32[]{:S(2)}, u32[]{:S(2)}) collective-permute-start(f32[8,64,128]{2,1,0:T(8,128)S(1)} %get-tuple-element.46), channel_id=1, source_target_pairs={{0,1},{1,0},{2,3},{3,2},{4,5},{5,4},{6,7},{7,6},{8,9},{9,8},{10,11... | collective-permute-start | bytes 786440 | tf_op jit(solution)/shard_map/ppermute | solution.py:225
  136.2 3.1 %collective-permute-start.14 = (f32[8,64,128]{2,1,0:T(8,128)S(1)}, f32[8,64,128]{2,1,0:T(8,128)S(1)}, u32[]{:S(2)}, u32[]{:S(2)}) collective-permute-start(f32[8,64,128]{2,1,0:T(8,128)S(1)} %get-tuple-element.44), channel_id=1, source_target_pairs={{0,1},{1,0},{2,3},{3,2},{4,5},{5,4},{6,7},{7,6},{8,9},{9,8},{10,11... | collective-permute-start | bytes 786440 | tf_op jit(solution)/shard_map/ppermute | solution.py:225
  137.8 8.4 %collective-permute-start.16 = (f32[8,64,128]{2,1,0:T(8,128)S(1)}, f32[8,64,128]{2,1,0:T(8,128)S(1)}, u32[]{:S(2)}, u32[]{:S(2)}) collective-permute-start(f32[8,64,128]{2,1,0:T(8,128)S(1)} %add.99), channel_id=1, source_target_pairs={{0,2},{1,3},{2,0},{3,1},{4,6},{5,7},{6,4},{7,5},{8,10},{9,11},{10,... | collective-permute-start | bytes 786440 | tf_op jit(solution)/shard_map/ppermute | solution.py:225

commit v3 on v2

--- a/solution.py
+++ b/solution.py
@@ -44,35 +44,49 @@
     )(pltpu.with_memory_space_constraint(x, pltpu.HBM))
 
 
-def pick_kernel(per, local_tiles, me, before, rows, amp, out, after):
-    base = me[0] * per
+def pick_kernel(per, local_tiles, peers_of, me, before, wanted, amp, *refs):
+    outs, after = refs[:-1], refs[-1]
     origin = me[0] * local_tiles
     after[0] = before[0]
-
-    def step(i, carry):
-        lane = pl.multiple_of((rows[base + i] - origin) * BLK, BLK)
-        out[i] = amp[:, pl.ds(lane, BLK)]
-        return carry
-
-    lax.fori_loop(0, per, step, 0, unroll=8)
-
-
-def pick(me, before, rows, amp, per):
-    occupied, width = amp.shape
-    return pl.pallas_call(
-        functools.partial(pick_kernel, per, width // BLK),
-        out_shape=[
-            jax.ShapeDtypeStruct((per, occupied, BLK), amp.dtype),
-            jax.ShapeDtypeStruct((1,), jnp.int32),
-        ],
+    for peer, out in zip(peers_of(me[0]), outs):
+
+        def step(i, carry):
+            lane = pl.multiple_of((wanted[peer, i] - origin) * BLK, BLK)
+            out[i] = amp[:, pl.ds(lane, BLK)]
+            return carry
+
+        lax.fori_loop(0, per, step, 0, unroll=8)
+
+
+def near_pick_kernel(per, local_tiles, me, before, wanted, amp, out, after):
+    near = out.shape[0]
+    first = me[0] // near * near
+    pick_kernel(
+        per,
+        local_tiles,
+        lambda _: [first + j for j in range(near)],
+        me,
+        before,
+        wanted,
+        amp,
+        *[out.at[j] for j in range(near)],
+        after,
+    )
+
+
+def pick(kernel, shapes, me, before, wanted, amp):
+    shapes = [jax.ShapeDtypeStruct(s, amp.dtype) for s in shapes]
+    return pl.pallas_call(
+        kernel,
+        out_shape=shapes + [jax.ShapeDtypeStruct((1,), jnp.int32)],
         in_specs=[SMEM_SPEC] * 3 + [VMEM_SPEC],
-        out_specs=[VMEM_SPEC, SMEM_SPEC],
+        out_specs=[VMEM_SPEC] * len(shapes) + [SMEM_SPEC],
         compiler_params=pltpu.CompilerParams(vmem_limit_bytes=8 * MIB),
         cost_estimate=pl.CostEstimate(
-            flops=0, bytes_accessed=4 * per * occupied * BLK, transcendentals=0
+            flops=0, bytes_accessed=4 * sum(s.size for s in shapes), transcendentals=0
         ),
         name="pick_tiles",
-    )(me, before, rows, amp)
+    )(me, before, wanted, amp)
 
 
 def add_products(per, base, cols, live, piece, weights, total):
@@ -90,34 +104,34 @@
     lax.fori_loop(0, per // unroll, step, 0)
 
 
-def near_kernel(near, per, order, cols, live, w, *refs):
-    pieces = refs[:near]
-    total, far_w, near_w, sems = refs[near:]
-    count = far_w.shape[0]
+def near_kernel(per, order, cols, live, w, pieces, total, far_w, near_w, sems):
+    near = pieces.shape[0]
+    first = order[0] // near * near
     copies = []
-    for j in range(near + count):
-        target = near_w.at[j] if j < near else far_w.at[j - near]
-        copies.append(pltpu.make_async_copy(w.at[order[j]], target, sems.at[j]))
-        copies[-1].start()
+    for j in range(near):
+        copies.append(pltpu.make_async_copy(w.at[first + j], near_w.at[j], sems.at[j]))
+    for j in range(far_w.shape[0]):
+        copies.append(pltpu.make_async_copy(w.at[order[near + j]], far_w.at[j], sems.at[near + j]))
+    for copy in copies:
+        copy.start()
     total[...] = jnp.zeros_like(total)
     for j in range(near):
         copies[j].wait()
-        add_products(per, order[j] * per, cols, live, pieces[j], near_w.at[j], total)
+        add_products(per, (first + j) * per, cols, live, pieces.at[j], near_w.at[j], total)
     for copy in copies[near:]:
         copy.wait()
 
 
 def near_part(order, cols, live, w, pieces):
-    near = len(pieces)
+    near, per, occupied, _ = pieces.shape
     peers = w.shape[0]
-    per, occupied, _ = pieces[0].shape
-    return pl.pallas_call(
-        functools.partial(near_kernel, near, per),
+    return pl.pallas_call(
+        functools.partial(near_kernel, per),
         out_shape=[
             pltpu.VMEM((ABT_X, occupied, BLK), jnp.float32),
             pltpu.VMEM((peers - near, per, BLK, BLK), w.dtype),
         ],
-        in_specs=[SMEM_SPEC] * 3 + [ANY_SPEC] + [VMEM_SPEC] * near,
+        in_specs=[SMEM_SPEC] * 3 + [ANY_SPEC, VMEM_SPEC],
         out_specs=[VMEM_SPEC, VMEM_SPEC],
         scratch_shapes=[
             pltpu.VMEM((near, per, BLK, BLK), w.dtype),
@@ -130,7 +144,7 @@
             transcendentals=0,
         ),
         name="near_products",
-    )(order, cols, live, pltpu.with_memory_space_constraint(w, pltpu.HBM), *pieces)
+    )(order, cols, live, pltpu.with_memory_space_constraint(w, pltpu.HBM), pieces)
 
 
 def far_kernel(count, skip, per, last, order, cols, live, w, start, *refs):
@@ -178,24 +192,28 @@
     groups = lax.axis_size("gy")
     me = lax.axis_index("gx")
     mine = lax.axis_index("gy")
-    row_count = amplitudes.shape[1] // BLK * peers
+    local_tiles = amplitudes.shape[1] // BLK
+    row_count = local_tiles * peers
     per = tile_rows.shape[0] // peers
     near = peers // 2
 
-    def swap(x, k):
-        return lax.ppermute(x, "gx", [(i, i ^ k) for i in range(peers)])
-
+    wanted = lax.all_to_all(tile_rows.reshape(peers, per), "gx", 0, 0)
     amp = stage(amplitudes)
     here = me.reshape(1)
     zero = jnp.zeros((1,), jnp.int32)
-    arrived = {}
-    for group in (range(near, peers), range(1, near)):
-        rows = tile_rows + zero
-        rows_of = [swap(rows, k) for k in group]
-        for k, wanted in zip(group, rows_of):
-            picked, zero = pick(here, zero, wanted, amp, per)
-            arrived[k] = swap(picked, k)
-    arrived[0], _ = pick(here, zero, tile_rows, amp, per)
+    shape = (per, occupied, BLK)
+    far_kernel_of = functools.partial(
+        pick_kernel, per, local_tiles, lambda i: [i ^ k for k in range(near, peers)]
+    )
+    *picked, zero = pick(far_kernel_of, [shape] * near, here, zero, wanted, amp)
+    arrived = [
+        lax.ppermute(x, "gx", [(i, i ^ k) for i in range(peers)])
+        for k, x in zip(range(near, peers), picked)
+    ]
+    near_kernel_of = functools.partial(near_pick_kernel, per, local_tiles)
+    picked, _ = pick(near_kernel_of, [(near, *shape)], here, zero, wanted, amp)
+    halves = [list(range(near)), list(range(near, peers))]
+    near_pieces = lax.all_to_all(picked, "gx", 0, 0, axis_index_groups=halves)
 
     row_tile = mine * row_count + tile_rows
     col_tile = me * ABT_X + tile_cols
@@ -211,14 +229,14 @@
     order = jnp.arange(peers, dtype=jnp.int32) ^ me
 
     w = w_tiles.reshape(peers, per, BLK, BLK)
-    total, far_w = near_part(order, cols, live, w, [arrived[k] for k in range(near)])
+    total, far_w = near_part(order, cols, live, w, near_pieces)
     half = near // 2
     (total,) = far_part(
-        order, cols, live, far_w, 0, total, [arrived[near + k] for k in range(half)], None
+        order, cols, live, far_w, 0, total, arrived[:half], None
     )
     sizes = (share, (xs - 1) * share) * CORES
     keep, keep_rest, give, give_rest = far_part(
-        order, cols, live, far_w, half, total, [arrived[near + k] for k in range(half, near)], sizes
+        order, cols, live, far_w, half, total, arrived[half:], sizes
     )
 
     def swap_gy(x, k):

time: 147 us -> 132 us (0.90)
  the two profiles are of different devices: /device:TPU:0 before, /device:TPU:8 now
where the time goes in v3:
time: 132 us
  waiting for transfers between devices  83 us (63%)
  starting transfers between devices  19.3 us (15%)
  Pallas kernels  15.3 us (12%)
  local copies, waits for them, and re-layouts  8.27 us (6%)
  other arithmetic  5.91 us (4%)
    ppermute x4, waiting for transfers between devices, per_device(): lax.ppermute(x, 'gx', [(i, i ^ k) for i in range(peers)])  43.7 us
    all_to_all x1, waiting for transfers between devices, per_device(): near_pieces = lax.all_to_all(picked, 'gx', 0, 0, axis_index_groups=halves)  30.6 us
    ppermute x3, waiting for transfers between devices, swap_gy(): return lax.ppermute(x, 'gy', [(i, i ^ k) for i in range(groups)])  7.88 us
    all_to_all x1, starting transfers between devices, per_device(): wanted = lax.all_to_all(tile_rows.reshape(peers, per), 'gx', 0, 0)  6.28 us
    unnamed x14, local copies, waits for them, and re-layouts  6.24 us
    ppermute x4, starting transfers between devices, per_device(): lax.ppermute(x, 'gx', [(i, i ^ k) for i in range(peers)])  5.85 us
    convert_element_type x1, other arithmetic, per_device(): (pair_irrep(row_tile, virt_irreps) == pair_irrep(col_tile, virt_irreps))....  5.11 us
    all_to_all x1, starting transfers between devices, per_device(): near_pieces = lax.all_to_all(picked, 'gx', 0, 0, axis_index_groups=halves)  5.06 us
  transfers between devices with their start and end apart: 9, of which 7 were waited for; matrix products, arithmetic and copies ran while one was open for 4% of the time, Pallas kernels for 7%

profile of v3, /device:TPU:8, one launch (start us, length us, event | category | flops | bytes accessed | tf_op | source)
XLA Modules:
  0.0 131.8 jit_solution(12795891275010082573)
XLA Ops:
  0.0 1.4 %all_to_all.10 = s32[8,1,32]{2,1,0:T(1,128)} reshape(s32[256]{0:T(256)} %param.8) | data formatting | bytes 2048 | tf_op jit(solution)/shard_map/all_to_all | solution.py:200
  1.4 6.3 %all-to-all-start = ((s32[8,1,32]{2,1,0:T(1,128)}), s32[8,1,32]{2,1,0:T(1,128)S(1)}, u32[]{:S(2)}, u32[]{:S(2)}) async-start(s32[8,1,32]{2,1,0:T(1,128)} %all_to_all.10), calls=%async_computation | async-start | bytes 8192 | tf_op jit(solution)/shard_map/all_to_all | solution.py:200
  7.6 2.2 %stage_amplitudes.1.amp = bf16[64,32768]{1,0:T(8,128)(2,1)S(1)} custom-call(bf16[64,32768]{1,0:T(8,128)(2,1)} %source.1), custom_call_target="tpu_custom_call" | custom-call | bytes 4194304 | tf_op jit(solution)/shard_map/stage_amplitudes/pallas_call | solution.py:35
  9.8 0.0 copy-start
  9.8 1.9 %copy-done = bf16[64,32768]{1,0:T(8,128)(2,1)} copy-done((bf16[64,32768]{1,0:T(8,128)(2,1)}, bf16[64,32768]{1,0:T(8,128)(2,1)S(1)}, u32[]{:S(2)}) %copy-start) | copy-done | bytes 4194328
  11.8 0.8 all-to-all-done
  12.5 0.0 copy-start.1
  12.5 2.2 %copy-done.1 = bf16[64,32768]{1,0:T(8,128)(2,1)S(1)} copy-done((bf16[64,32768]{1,0:T(8,128)(2,1)S(1)}, bf16[64,32768]{1,0:T(8,128)(2,1)}, u32[]{:S(2)}) %copy-start.1) | copy-done | bytes 4194328
  14.7 2.4 %pick_tiles.2 = (bf16[32,64,128]{2,1,0:T(8,128)(2,1)}, bf16[32,64,128]{2,1,0:T(8,128)(2,1)}, bf16[32,64,128]{2,1,0:T(8,128)(2,1)}, bf16[32,64,128]{2,1,0:T(8,128)(2,1)S(1)}, s32[1]{0:T(128)}) custom-call(s32[1]{0:T(128)} %bitcast.9.me, s32[1]{0:T(128)} %constant.144.clone.1.before, s32[8,32]{1,0:T(8,128)S(1)} %bitcast.17, bf16[64,32768]{1,0:T(8,128)(2,1)S(1)} %copy-done.1), custom_call_target="tpu_custom_call" | custom-call | bytes 4194304 | tf_op jit(solution)/shard_map/pick_tiles/pallas_call | solution.py:79
  17.2 0.0 copy-start.3
  17.2 0.8 copy-done.3
  18.0 0.0 copy-start.4
  18.0 0.0 copy-start.5
  18.0 0.0 copy-start.6
  18.0 2.5 %pick_tiles.3 = (bf16[4,32,64,128]{3,2,1,0:T(8,128)(2,1)S(1)}, s32[1]{0:T(128)}) custom-call(s32[1]{0:T(128)} %bitcast.9.me, s32[1]{0:T(128)} %get-tuple-element.17.before, s32[8,32]{1,0:T(8,128)S(1)} %bitcast.18, bf16[64,32768]{1,0:T(8,128)(2,1)S(1)} %copy-done.1), custom_call_target="tpu_custom_call" | custom-call | bytes 4194304 | tf_op jit(solution)/shard_map/pick_tiles/pallas_call | solution.py:79
  20.4 0.0 copy-start.2
  20.5 1.3 %copy-done.2 = bf16[4,32,64,128]{3,2,1,0:T(8,128)(2,1)} copy-done((bf16[4,32,64,128]{3,2,1,0:T(8,128)(2,1)}, bf16[4,32,64,128]{3,2,1,0:T(8,128)(2,1)S(1)}, u32[]{:S(2)}) %copy-start.2) | copy-done | bytes 2097176
  21.8 5.1 %all-to-all-start.1 = ((bf16[4,32,64,128]{3,2,1,0:T(8,128)(2,1)}), bf16[4,32,64,128]{3,2,1,0:T(8,128)(2,1)S(1)}, u32[]{:S(2)}, u32[]{:S(2)}) async-start(bf16[4,32,64,128]{3,2,1,0:T(8,128)(2,1)} %copy-done.2), calls=%async_computation.1 | async-start | bytes 4194304 | tf_op jit(solution)/shard_map/all_to_all | solution.py:216
  26.8 0.0 copy-done.4
  26.8 0.7 fusion.4
  27.5 0.7 collective-permute-start
  28.2 3.1 %collective-permute-start.1 = (bf16[32,64,128]{2,1,0:T(8,128)(2,1)}, bf16[32,64,128]{2,1,0:T(8,128)(2,1)}, u32[]{:S(2)}, u32[]{:S(2)}) collective-permute-start(bf16[32,64,128]{2,1,0:T(8,128)(2,1)} %get-tuple-element.22), channel_id=1, source_target_pairs={{0,20},{4,16},{8,28},{12,24},{16,4},{20,0},{24,12},{28,8},{1,21},{... | collective-permute-start | bytes 1572872 | tf_op jit(solution)/shard_map/ppermute | solution.py:210
  31.3 0.0 collective-permute-start.2
  31.3 2.0 %collective-permute-start.3 = (bf16[32,64,128]{2,1,0:T(8,128)(2,1)}, bf16[32,64,128]{2,1,0:T(8,128)(2,1)S(1)}, u32[]{:S(2)}, u32[]{:S(2)}) collective-permute-start(bf16[32,64,128]{2,1,0:T(8,128)(2,1)} %copy-done.3), channel_id=1, source_target_pairs={{0,28},{4,24},{8,20},{12,16},{16,12},{20,8},{24,4},{28,0},{1,29},{... | collective-permute-start | bytes 1572872 | tf_op jit(solution)/shard_map/ppermute | solution.py:210
  33.4 0.0 copy-done.5
  33.4 0.0 copy-done.6
  33.4 5.1 %compare_convert_fusion.live = f32[256]{0:T(256)S(1)} fusion(s32[256]{0:T(256)S(1)} %copy-done.5, s32[256]{0:T(256)S(1)} %copy-done.6, s32[]{:T(128)} %bitcast, s32[]{:T(128)} %bitcast.1, s32[]{:T(128)} %bitcast.2, s32[]{:T(128)} %bitcast.3, s32[]{:T(128)} %bitcast.4, s32[]{:T(128)} %bitcast.5, s32[]{:T(128)} %bitcast.6, s32[]{:T(128)} %bitcast.7, ...), kind=kLoop, calls=%fused_computation.34 | loop fusion | flops 44544 | bytes 3112 | tf_op jit(solution)/shard_map/convert_element_type | solution.py:220
  38.5 30.6 %all-to-all-done.1.pieces = bf16[4,32,64,128]{3,2,1,0:T(8,128)(2,1)S(1)} async-done(((bf16[4,32,64,128]{3,2,1,0:T(8,128)(2,1)}), bf16[4,32,64,128]{3,2,1,0:T(8,128)(2,1)S(1)}, u32[]{:S(2)}, u32[]{:S(2)}) %all-to-all-start.1) | async-done | bytes 2097184 | tf_op jit(solution)/shard_map/all_to_all | solution.py:216
  69.1 4.1 %near_products.1 = (f32[32,64,128]{2,1,0:T(8,128)S(1)}, bf16[4,32,128,128]{3,2,1,0:T(8,128)(2,1)S(1)}) custom-call(s32[8]{0:T(128)S(1)} %iota_xor_fusion.order, s32[256]{0:T(256)S(1)} %fusion.3.cols, f32[256]{0:T(256)S(1)} %compare_convert_fusion.live, bf16[8,32,128,128]{3,2,1,0:T(8,128)(2,1)} %bitcast.19, bf16[4,32,64,128]{3,2,1,0:T(8,128)(2,1)S(1)} %all-to-all-done.1.pieces), custom_call_target="tpu_custom_call" | custom-call | flops 268435456 | bytes 8388608 | tf_op jit(solution)/shard_map/near_products/pallas_call | solution.py:128
  73.2 0.0 collective-permute-done.refs_0_
  73.2 23.9 %collective-permute-done.1.refs_1_ = bf16[32,64,128]{2,1,0:T(8,128)(2,1)} collective-permute-done((bf16[32,64,128]{2,1,0:T(8,128)(2,1)}, bf16[32,64,128]{2,1,0:T(8,128)(2,1)}, u32[]{:S(2)}, u32[]{:S(2)}) %collective-permute-start.1) | collective-permute-done | bytes 524320 | tf_op jit(solution)/shard_map/ppermute | solution.py:210
  97.1 2.3 %far_products.2.start = f32[32,64,128]{2,1,0:T(8,128)S(1)} custom-call(s32[8]{0:T(128)S(1)} %iota_xor_fusion.order, s32[256]{0:T(256)S(1)} %fusion.3.cols, f32[256]{0:T(256)S(1)} %compare_convert_fusion.live, bf16[4,32,128,128]{3,2,1,0:T(8,128)(2,1)S(1)} %get-tuple-element.19.w, ...), custom_call_target="tpu_custom_call", output_to_operand_aliasing={{}: (4, {})} | custom-call | flops 134217728 | bytes 1048576 | tf_op jit(solution)/shard_map/far_products/pallas_call | solution.py:173
  99.4 10.0 %collective-permute-done.2.refs_0_ = bf16[32,64,128]{2,1,0:T(8,128)(2,1)S(1)} collective-permute-done((bf16[32,64,128]{2,1,0:T(8,128)(2,1)}, bf16[32,64,128]{2,1,0:T(8,128)(2,1)S(1)}, u32[]{:S(2)}, u32[]{:S(2)}) %collective-permute-start.2) | collective-permute-done | bytes 524320 | tf_op jit(solution)/shard_map/ppermute | solution.py:210
  109.5 9.8 %collective-permute-done.3.refs_1_ = bf16[32,64,128]{2,1,0:T(8,128)(2,1)S(1)} collective-permute-done((bf16[32,64,128]{2,1,0:T(8,128)(2,1)}, bf16[32,64,128]{2,1,0:T(8,128)(2,1)S(1)}, u32[]{:S(2)}, u32[]{:S(2)}) %collective-permute-start.3) | collective-permute-done | bytes 524320 | tf_op jit(solution)/shard_map/ppermute | solution.py:210
  119.3 1.7 %far_products.3 = (f32[8,64,128]{2,1,0:T(8,128)S(1)}, f32[8,64,128]{2,1,0:T(8,128)S(1)}, f32[8,64,128]{2,1,0:T(8,128)S(1)}, f32[8,64,128]{2,1,0:T(8,128)S(1)}) custom-call(s32[8]{0:T(128)S(1)} %iota_xor_fusion.order, s32[256]{0:T(256)S(1)} %fusion.3.cols, f32[256]{0:T(256)S(1)} %compare_convert_fusion.live, ...), custom_call_target="tpu_custom_call" | custom-call | flops 134217728 | bytes 1048576 | tf_op jit(solution)/shard_map/far_products/pallas_call | solution.py:173
  121.0 0.1 collective-permute-start.5
  121.1 0.5 collective-permute-start.4
  121.6 1.0 collective-permute-done.5
  122.7 1.6 %collective-permute-start.6 = (f32[8,64,128]{2,1,0:T(8,128)S(1)}, f32[8,64,128]{2,1,0:T(8,128)S(1)}, u32[]{:S(2)}, u32[]{:S(2)}) collective-permute-start(f32[8,64,128]{2,1,0:T(8,128)S(1)} %add.86), channel_id=1, source_target_pairs={{0,2},{1,3},{2,0},{3,1},{4,6},{5,7},{6,4},{7,5},{8,10},{9,11},{10,... | collective-permute-start | bytes 786440 | tf_op jit(solution)/shard_map/ppermute | solution.py:243
  124.2 0.0 collective-permute-done.4
  124.2 6.9 %collective-permute-done.6 = f32[8,64,128]{2,1,0:T(8,128)S(1)} collective-permute-done((f32[8,64,128]{2,1,0:T(8,128)S(1)}, f32[8,64,128]{2,1,0:T(8,128)S(1)}, u32[]{:S(2)}, u32[]{:S(2)}) %collective-permute-start.6) | collective-permute-done | bytes 262176 | tf_op jit(solution)/shard_map/ppermute | solution.py:243
  131.1 0.7 copy_bitcast_fusion
  (3 shorter events, 0.1 us)
Async XLA Ops:
  1.4 11.2 %all-to-all-start = ((s32[8,1,32]{2,1,0:T(1,128)}), s32[8,1,32]{2,1,0:T(1,128)S(1)}, u32[]{:S(2)}, u32[]{:S(2)}) async-start(s32[8,1,32]{2,1,0:T(1,128)} %all_to_all.10), calls=%async_computation | async-start | bytes 8192 | tf_op jit(solution)/shard_map/all_to_all | solution.py:200
  9.8 1.9 %copy-start = (bf16[64,32768]{1,0:T(8,128)(2,1)}, bf16[64,32768]{1,0:T(8,128)(2,1)S(1)}, u32[]{:S(2)}) copy-start(bf16[64,32768]{1,0:T(8,128)(2,1)S(1)} %stage_amplitudes.1.amp) | copy-start | bytes 12582916
  12.5 2.2 %copy-start.1 = (bf16[64,32768]{1,0:T(8,128)(2,1)S(1)}, bf16[64,32768]{1,0:T(8,128)(2,1)}, u32[]{:S(2)}) copy-start(bf16[64,32768]{1,0:T(8,128)(2,1)} %copy-done) | copy-start | bytes 12582916
  17.2 0.8 copy-start.3
  18.0 8.9 %copy-start.4 = (s32[8]{0:T(128)S(1)}, s32[8]{0:T(128)}, u32[]{:S(2)}) copy-start(s32[8]{0:T(128)} %param.6) | copy-start | bytes 100
  18.0 15.4 %copy-start.5 = (s32[256]{0:T(256)S(1)}, s32[256]{0:T(256)}, u32[]{:S(2)}) copy-start(s32[256]{0:T(256)} %param.9) | copy-start | bytes 3076
  18.0 15.4 %copy-start.6 = (s32[256]{0:T(256)S(1)}, s32[256]{0:T(256)}, u32[]{:S(2)}) copy-start(s32[256]{0:T(256)} %param.8) | copy-start | bytes 3076
  20.4 1.3 %copy-start.2 = (bf16[4,32,64,128]{3,2,1,0:T(8,128)(2,1)}, bf16[4,32,64,128]{3,2,1,0:T(8,128)(2,1)S(1)}, u32[]{:S(2)}) copy-start(bf16[4,32,64,128]{3,2,1,0:T(8,128)(2,1)S(1)} %get-tuple-element.18) | copy-start | bytes 6291460
  21.8 47.3 %all-to-all-start.1 = ((bf16[4,32,64,128]{3,2,1,0:T(8,128)(2,1)}), bf16[4,32,64,128]{3,2,1,0:T(8,128)(2,1)S(1)}, u32[]{:S(2)}, u32[]{:S(2)}) async-start(bf16[4,32,64,128]{3,2,1,0:T(8,128)(2,1)} %copy-done.2), calls=%async_computation.1 | async-start | bytes 4194304 | tf_op jit(solution)/shard_map/all_to_all | solution.py:216
  27.5 45.7 %collective-permute-start = (bf16[32,64,128]{2,1,0:T(8,128)(2,1)}, bf16[32,64,128]{2,1,0:T(8,128)(2,1)}, u32[]{:S(2)}, u32[]{:S(2)}) collective-permute-start(bf16[32,64,128]{2,1,0:T(8,128)(2,1)} %get-tuple-element.21), channel_id=1, source_target_pairs={{0,16},{4,20},{8,24},{12,28},{16,0},{20,4},{24,8},{28,12},{1,17},{... | collective-permute-start | bytes 1572872 | tf_op jit(solution)/shard_map/ppermute | solution.py:210
  28.2 68.9 %collective-permute-start.1 = (bf16[32,64,128]{2,1,0:T(8,128)(2,1)}, bf16[32,64,128]{2,1,0:T(8,128)(2,1)}, u32[]{:S(2)}, u32[]{:S(2)}) collective-permute-start(bf16[32,64,128]{2,1,0:T(8,128)(2,1)} %get-tuple-element.22), channel_id=1, source_target_pairs={{0,20},{4,16},{8,28},{12,24},{16,4},{20,0},{24,12},{28,8},{1,21},{... | collective-permute-start | bytes 1572872 | tf_op jit(solution)/shard_map/ppermute | solution.py:210
  31.3 78.1 %collective-permute-start.2 = (bf16[32,64,128]{2,1,0:T(8,128)(2,1)}, bf16[32,64,128]{2,1,0:T(8,128)(2,1)S(1)}, u32[]{:S(2)}, u32[]{:S(2)}) collective-permute-start(bf16[32,64,128]{2,1,0:T(8,128)(2,1)} %get-tuple-element.23), channel_id=1, source_target_pairs={{0,24},{4,28},{8,16},{12,20},{16,8},{20,12},{24,0},{28,4},{1,25},{... | collective-permute-start | bytes 1572872 | tf_op jit(solution)/shard_map/ppermute | solution.py:210
  31.3 87.9 %collective-permute-start.3 = (bf16[32,64,128]{2,1,0:T(8,128)(2,1)}, bf16[32,64,128]{2,1,0:T(8,128)(2,1)S(1)}, u32[]{:S(2)}, u32[]{:S(2)}) collective-permute-start(bf16[32,64,128]{2,1,0:T(8,128)(2,1)} %copy-done.3), channel_id=1, source_target_pairs={{0,28},{4,24},{8,20},{12,16},{16,12},{20,8},{24,4},{28,0},{1,29},{... | collective-permute-start | bytes 1572872 | tf_op jit(solution)/shard_map/ppermute | solution.py:210
  121.0 1.6 %collective-permute-start.5 = (f32[8,64,128]{2,1,0:T(8,128)S(1)}, f32[8,64,128]{2,1,0:T(8,128)S(1)}, u32[]{:S(2)}, u32[]{:S(2)}) collective-permute-start(f32[8,64,128]{2,1,0:T(8,128)S(1)} %get-tuple-element.28), channel_id=1, source_target_pairs={{0,1},{1,0},{2,3},{3,2},{4,5},{5,4},{6,7},{7,6},{8,9},{9,8},{10,11... | collective-permute-start | bytes 786440 | tf_op jit(solution)/shard_map/ppermute | solution.py:243
  121.1 3.1 %collective-permute-start.4 = (f32[8,64,128]{2,1,0:T(8,128)S(1)}, f32[8,64,128]{2,1,0:T(8,128)S(1)}, u32[]{:S(2)}, u32[]{:S(2)}) collective-permute-start(f32[8,64,128]{2,1,0:T(8,128)S(1)} %get-tuple-element.26), channel_id=1, source_target_pairs={{0,1},{1,0},{2,3},{3,2},{4,5},{5,4},{6,7},{7,6},{8,9},{9,8},{10,11... | collective-permute-start | bytes 786440 | tf_op jit(solution)/shard_map/ppermute | solution.py:243
  122.7 8.4 %collective-permute-start.6 = (f32[8,64,128]{2,1,0:T(8,128)S(1)}, f32[8,64,128]{2,1,0:T(8,128)S(1)}, u32[]{:S(2)}, u32[]{:S(2)}) collective-permute-start(f32[8,64,128]{2,1,0:T(8,128)S(1)} %add.86), channel_id=1, source_target_pairs={{0,2},{1,3},{2,0},{3,1},{4,6},{5,7},{6,4},{7,5},{8,10},{9,11},{10,... | collective-permute-start | bytes 786440 | tf_op jit(solution)/shard_map/ppermute | solution.py:243

commit v4 on v2

v4 whole, which is shorter than its diff:
```python
import functools

import jax
import jax.numpy as jnp
from jax import lax
from jax.experimental import pallas as pl
from jax.experimental.pallas import tpu as pltpu
from jax.sharding import PartitionSpec as P

V = 1024
BLK = 128
ABT_X = 32
CORES = 2
UNROLL = 16
MIB = 1024 * 1024

VMEM_SPEC = pl.BlockSpec(memory_space=pltpu.VMEM)
SMEM_SPEC = pl.BlockSpec(memory_space=pltpu.SMEM)
ANY_SPEC = pl.BlockSpec(memory_space=pl.ANY)


def pair_irrep(tile, virt_irreps):
    first = tile * BLK // V // BLK
    second = tile * BLK % V // BLK
    return jnp.bitwise_xor(virt_irreps[first], virt_irreps[second])


def stage_kernel(source, held, sem):
    copy = pltpu.make_async_copy(source, held, sem)
    copy.start()
    copy.wait()


def stage(x):
    return pl.pallas_call(
        stage_kernel,
        out_shape=pltpu.VMEM(x.shape, x.dtype),
        in_specs=[ANY_SPEC],
        out_specs=VMEM_SPEC,
        scratch_shapes=[pltpu.SemaphoreType.DMA],
        compiler_params=pltpu.CompilerParams(vmem_limit_bytes=8 * MIB),
        cost_estimate=pl.CostEstimate(flops=0, bytes_accessed=2 * x.size, transcendentals=0),
        name="stage_amplitudes",
    )(pltpu.with_memory_space_constraint(x, pltpu.HBM))


def pick_kernel(per, local_tiles, me, rows, amp, out):
    base = me[0] * per
    origin = me[0] * local_tiles

    def step(i, carry):
        lane = pl.multiple_of((rows[base + i] - origin) * BLK, BLK)
        out[i] = amp[:, pl.ds(lane, BLK)]
        return carry

    lax.fori_loop(0, per, step, 0, unroll=8)


def pick(me, rows, amp, per):
    occupied, width = amp.shape
    return pl.pallas_call(
        functools.partial(pick_kernel, per, width // BLK),
        out_shape=jax.ShapeDtypeStruct((per, occupied, BLK), amp.dtype),
        in_specs=[SMEM_SPEC, SMEM_SPEC, VMEM_SPEC],
        out_specs=VMEM_SPEC,
        compiler_params=pltpu.CompilerParams(vmem_limit_bytes=8 * MIB),
        cost_estimate=pl.CostEstimate(
            flops=0, bytes_accessed=4 * per * occupied * BLK, transcendentals=0
        ),
        name="pick_tiles",
    )(me, rows, amp)


def add_products(per, base, cols, live, piece, weights, total):
    unroll = min(UNROLL, per)

    def step(i, carry):
        slots = [i * unroll + u for u in range(unroll)]
        products = [
            jnp.dot(piece[s], weights[s], preferred_element_type=jnp.float32) for s in slots
        ]
        for s, product in zip(slots, products):
            total[cols[base + s]] += product * live[base + s]
        return carry

    lax.fori_loop(0, per // unroll, step, 0)


def ladder_kernel(peers_at, per, first, last, order, cols, live, w, *refs):
    count = len(peers_at)
    pieces, refs = refs[:count], refs[count:]
    if not first:
        start, refs = refs[0], refs[1:]
    *outs, held, sems = refs
    total = start if last else outs[0]
    copies = []
    for j, k in enumerate(peers_at):
        copies.append(pltpu.make_async_copy(w.at[order[k]], held.at[j], sems.at[j]))
        copies[-1].start()
    if first:
        total[...] = jnp.zeros_like(total)
    for j, k in enumerate(peers_at):
        copies[j].wait()
        add_products(per, order[k] * per, cols, live, pieces[j], held.at[j], total)
    if last:
        at = 0
        for out in outs:
            out[...] = total[at : at + out.shape[0]]
            at += out.shape[0]


def ladder(order, cols, live, w, start, arrived, peers_at, last=None):
    pieces = [arrived[k] for k in peers_at]
    count = len(pieces)
    per, occupied, _ = pieces[0].shape
    whole = (ABT_X, occupied, BLK)
    first = start is None
    if last:
        out_shape = [jax.ShapeDtypeStruct((n, occupied, BLK), jnp.float32) for n in last]
    else:
        out_shape = [pltpu.VMEM(whole, jnp.float32)]
    out = pl.pallas_call(
        functools.partial(ladder_kernel, peers_at, per, first, bool(last)),
        out_shape=out_shape,
        in_specs=[SMEM_SPEC] * 3 + [ANY_SPEC] + [VMEM_SPEC] * (count + (not first)),
        out_specs=[VMEM_SPEC] * len(out_shape),
        input_output_aliases={} if first or last else {4 + count: 0},
        scratch_shapes=[
            pltpu.VMEM((count, per, BLK, BLK), w.dtype),
            pltpu.SemaphoreType.DMA((count,)),
        ],
        compiler_params=pltpu.CompilerParams(vmem_limit_bytes=8 * MIB),
        cost_estimate=pl.CostEstimate(
            flops=2 * count * per * occupied * BLK * BLK,
            bytes_accessed=2 * count * per * BLK * BLK,
            transcendentals=0,
        ),
        name="ladder_products",
    )(order, cols, live, pltpu.with_memory_space_constraint(w, pltpu.HBM), *pieces, *([] if first else [start]))
    return out if last else out[0]


def per_device(amplitudes, virt_irreps, w_tiles, tile_rows, tile_cols):
    occupied = amplitudes.shape[0]
    peers = lax.axis_size("gx")
    groups = lax.axis_size("gy")
    me = lax.axis_index("gx")
    mine = lax.axis_index("gy")
    row_count = amplitudes.shape[1] // BLK * peers
    per = tile_rows.shape[0] // peers
    near = peers // 2

    def swap(x, k):
        return lax.ppermute(x, "gx", [(i, i ^ k) for i in range(peers)])

    amp = stage(amplitudes)
    here = me.reshape(1)
    arrived = {0: pick(here, tile_rows, amp, per)}
    for k in range(1, peers):
        arrived[k] = swap(pick(here, swap(tile_rows, k), amp, per), k)

    row_tile = mine * row_count + tile_rows
    col_tile = me * ABT_X + tile_cols
    live = (pair_irrep(row_tile, virt_irreps) == pair_irrep(col_tile, virt_irreps)).astype(
        jnp.float32
    )
    share = ABT_X // groups
    xs = groups // CORES
    owner = tile_cols // share
    other_core = (owner % CORES) ^ (mine % CORES)
    other_x = (owner // CORES) ^ (mine // CORES)
    cols = other_core * (ABT_X // CORES) + other_x * share + tile_cols % share
    order = jnp.arange(peers, dtype=jnp.int32) ^ me

    w = w_tiles.reshape(peers, per, BLK, BLK)
    quarter = near // 4
    far = [list(range(near + j * quarter, near + (j + 1) * quarter)) for j in range(4)]
    total = None
    for peers_at in (far[0], far[1], list(range(near)), far[2]):
        total = ladder(order, cols, live, w, total, arrived, peers_at)
    sizes = (share, (xs - 1) * share) * CORES
    keep, keep_rest, give, give_rest = ladder(order, cols, live, w, total, arrived, far[3], sizes)

    def swap_gy(x, k):
        return lax.ppermute(x, "gy", [(i, i ^ k) for i in range(groups)])

    rest = (keep_rest + swap_gy(give_rest, 1)).reshape(xs - 1, share, occupied, BLK)
    result = keep + swap_gy(give, 1)
    for k in range(1, xs):
        result = result + swap_gy(rest[k - 1], k * CORES)
    return jnp.transpose(result, (1, 0, 2)).reshape(occupied, share * BLK)


def solution(mesh):
    in_specs = (
        P(None, ("gy", "gx")),
        P(),
        P(("gx", "gy"), None, None),
        P(("gx", "gy")),
        P(("gx", "gy")),
    )
    out_specs = P(None, ("gx", "gy"))
    return jax.shard_map(
        per_device, mesh=mesh, in_specs=in_specs, out_specs=out_specs, check_vma=False
    )
```

time: 147 us -> 140 us (0.952)
  the two profiles are of different devices: /device:TPU:0 before, /device:TPU:8 now
where the time goes in v4:
time: 140 us
  waiting for transfers between devices  82 us (59%)
  Pallas kernels  25.4 us (18%)
  starting transfers between devices  23.5 us (17%)
  other arithmetic  5.84 us (4%)
  local copies, waits for them, and re-layouts  2.88 us (2%)
    ppermute x14, waiting for transfers between devices, swap(): return lax.ppermute(x, 'gx', [(i, i ^ k) for i in range(peers)])  74.1 us
    ppermute x14, starting transfers between devices, swap(): return lax.ppermute(x, 'gx', [(i, i ^ k) for i in range(peers)])  21.4 us
    pallas_call x5, Pallas kernels, ladder(): pl.pallas_call(functools.partial(ladder_kernel, peers_at, per, first, boo...  14.4 us
    pallas_call x8, Pallas kernels, pick(): pl.pallas_call(functools.partial(pick_kernel, per, width // BLK), out_sha...  8.85 us
    ppermute x3, waiting for transfers between devices, swap_gy(): return lax.ppermute(x, 'gy', [(i, i ^ k) for i in range(groups)])  7.88 us
    convert_element_type x1, other arithmetic, per_device(): (pair_irrep(row_tile, virt_irreps) == pair_irrep(col_tile, virt_irreps))....  5.04 us
  transfers between devices with their start and end apart: 17, of which 5 were waited for; matrix products, arithmetic and copies ran while one was open for 4% of the time, Pallas kernels for 16%

profile of v4, /device:TPU:8, one launch (start us, length us, event | category | flops | bytes accessed | tf_op | source)
XLA Modules:
  0.0 139.8 jit_solution(17888648315215892715)
XLA Ops:
  0.0 3.5 %collective-permute-start.10 = (s32[256]{0:T(256)}, s32[256]{0:T(256)S(1)}, u32[]{:S(2)}, u32[]{:S(2)}) collective-permute-start(s32[256]{0:T(256)} %rows.1), channel_id=1, source_target_pairs={{0,20},{4,16},{8,28},{12,24},{16,4},{20,0},{24,12},{28,8},{1,21},{... | collective-permute-start | bytes 3080 | tf_op jit(solution)/shard_map/ppermute | solution.py:154
  3.5 0.3 collective-permute-start.12
  3.9 2.2 %stage_amplitudes.1.amp = bf16[64,32768]{1,0:T(8,128)(2,1)S(1)} custom-call(bf16[64,32768]{1,0:T(8,128)(2,1)} %source.1), custom_call_target="tpu_custom_call" | custom-call | bytes 4194304 | tf_op jit(solution)/shard_map/stage_amplitudes/pallas_call | solution.py:35
  6.1 0.0 collective-permute-done.10.rows
  6.1 0.0 copy-start.2
  6.1 0.0 copy-start.3
  6.1 0.7 pick_tiles.14
  6.9 3.1 %collective-permute-start.11 = (bf16[32,64,128]{2,1,0:T(8,128)(2,1)S(1)}, bf16[32,64,128]{2,1,0:T(8,128)(2,1)S(1)}, u32[]{:S(2)}, u32[]{:S(2)}) collective-permute-start(bf16[32,64,128]{2,1,0:T(8,128)(2,1)S(1)} %pick_tiles.14), channel_id=1, source_target_pairs={{0,20},{4,16},{8,28},{12,24},{16,4},{20,0},{24,12},{28,8},{1,21},{... | collective-permute-start | bytes 1572872 | tf_op jit(solution)/shard_map/ppermute | solution.py:154
  9.9 0.0 collective-permute-done.12.rows
  9.9 0.7 pick_tiles.15
  10.6 0.4 collective-permute-start.13
  11.0 0.9 collective-permute-start.8
  12.0 3.1 %collective-permute-start = (s32[256]{0:T(256)S(1)}, s32[256]{0:T(256)S(1)}, u32[]{:S(2)}, u32[]{:S(2)}) collective-permute-start(s32[256]{0:T(256)S(1)} %copy-done.2), channel_id=1, source_target_pairs={{0,28},{4,24},{8,20},{12,16},{16,12},{20,8},{24,4},{28,0},{1,29},{... | collective-permute-start | bytes 3080 | tf_op jit(solution)/shard_map/ppermute | solution.py:154
  15.1 1.3 collective-permute-start.6
  16.4 16.8 %collective-permute-done.8.rows = s32[256]{0:T(256)S(1)} collective-permute-done((s32[256]{0:T(256)S(1)}, s32[256]{0:T(256)S(1)}, u32[]{:S(2)}, u32[]{:S(2)}) %collective-permute-start.8) | collective-permute-done | bytes 1056 | tf_op jit(solution)/shard_map/ppermute | solution.py:154
  33.2 0.5 collective-permute-start.4
  33.8 43.3 %collective-permute-done.rows = s32[256]{0:T(256)S(1)} collective-permute-done((s32[256]{0:T(256)S(1)}, s32[256]{0:T(256)S(1)}, u32[]{:S(2)}, u32[]{:S(2)}) %collective-permute-start) | collective-permute-done | bytes 1056 | tf_op jit(solution)/shard_map/ppermute | solution.py:154
  77.0 2.6 %collective-permute-start.2 = (s32[256]{0:T(256)S(1)}, s32[256]{0:T(256)S(1)}, u32[]{:S(2)}, u32[]{:S(2)}) collective-permute-start(s32[256]{0:T(256)S(1)} %copy-done.2), channel_id=1, source_target_pairs={{0,24},{4,28},{8,16},{12,20},{16,8},{20,12},{24,0},{28,4},{1,25},{... | collective-permute-start | bytes 3080 | tf_op jit(solution)/shard_map/ppermute | solution.py:154
  79.6 0.7 fusion.4
  80.3 1.5 %pick_tiles.13 = bf16[32,64,128]{2,1,0:T(8,128)(2,1)} custom-call(s32[1]{0:T(128)} %bitcast.9.me, s32[256]{0:T(256)S(1)} %collective-permute-done.8.rows, bf16[64,32768]{1,0:T(8,128)(2,1)S(1)} %stage_amplitudes.1.amp), custom_call_target="tpu_custom_call" | custom-call | bytes 1048576 | tf_op jit(solution)/shard_map/pick_tiles/pallas_call | solution.py:61
  81.8 0.7 pick_tiles.8
  82.5 0.0 collective-permute-done.2.rows
  82.5 0.6 collective-permute-start.1
  83.1 1.5 %pick_tiles.9 = bf16[32,64,128]{2,1,0:T(8,128)(2,1)} custom-call(s32[1]{0:T(128)} %bitcast.9.me, s32[256]{0:T(256)S(1)} %collective-permute-done.2.rows, bf16[64,32768]{1,0:T(8,128)(2,1)S(1)} %stage_amplitudes.1.amp), custom_call_target="tpu_custom_call" | custom-call | bytes 1048576 | tf_op jit(solution)/shard_map/pick_tiles/pallas_call | solution.py:61
  84.7 0.0 collective-permute-done.4.rows
  84.7 1.4 %collective-permute-start.3 = (bf16[32,64,128]{2,1,0:T(8,128)(2,1)}, bf16[32,64,128]{2,1,0:T(8,128)(2,1)S(1)}, u32[]{:S(2)}, u32[]{:S(2)}) collective-permute-start(bf16[32,64,128]{2,1,0:T(8,128)(2,1)} %pick_tiles.9), channel_id=1, source_target_pairs={{0,24},{4,28},{8,16},{12,20},{16,8},{20,12},{24,0},{28,4},{1,25},{... | collective-permute-start | bytes 1572872 | tf_op jit(solution)/shard_map/ppermute | solution.py:154
  86.1 1.5 %pick_tiles.11 = bf16[32,64,128]{2,1,0:T(8,128)(2,1)} custom-call(s32[1]{0:T(128)} %bitcast.9.me, s32[256]{0:T(256)S(1)} %collective-permute-done.4.rows, bf16[64,32768]{1,0:T(8,128)(2,1)S(1)} %stage_amplitudes.1.amp), custom_call_target="tpu_custom_call" | custom-call | bytes 1048576 | tf_op jit(solution)/shard_map/pick_tiles/pallas_call | solution.py:61
  87.6 1.5 %collective-permute-start.5 = (bf16[32,64,128]{2,1,0:T(8,128)(2,1)}, bf16[32,64,128]{2,1,0:T(8,128)(2,1)}, u32[]{:S(2)}, u32[]{:S(2)}) collective-permute-start(bf16[32,64,128]{2,1,0:T(8,128)(2,1)} %pick_tiles.11), channel_id=1, source_target_pairs={{0,4},{4,0},{8,12},{12,8},{16,20},{20,16},{24,28},{28,24},{1,5},{5... | collective-permute-start | bytes 1572872 | tf_op jit(solution)/shard_map/ppermute | solution.py:154
  89.1 1.5 %pick_tiles.12 = bf16[32,64,128]{2,1,0:T(8,128)(2,1)} custom-call(s32[1]{0:T(128)} %bitcast.9.me, s32[256]{0:T(256)S(1)} %collective-permute-done.6.rows, bf16[64,32768]{1,0:T(8,128)(2,1)S(1)} %stage_amplitudes.1.amp), custom_call_target="tpu_custom_call" | custom-call | bytes 1048576 | tf_op jit(solution)/shard_map/pick_tiles/pallas_call | solution.py:61
  90.6 2.0 %collective-permute-start.9 = (bf16[32,64,128]{2,1,0:T(8,128)(2,1)}, bf16[32,64,128]{2,1,0:T(8,128)(2,1)}, u32[]{:S(2)}, u32[]{:S(2)}) collective-permute-start(bf16[32,64,128]{2,1,0:T(8,128)(2,1)} %pick_tiles.13), channel_id=1, source_target_pairs={{0,12},{4,8},{8,4},{12,0},{16,28},{20,24},{24,20},{28,16},{1,13},{... | collective-permute-start | bytes 1572872 | tf_op jit(solution)/shard_map/ppermute | solution.py:154
  92.6 2.2 %copy-done.1 = bf16[64,32768]{1,0:T(8,128)(2,1)S(1)} copy-done((bf16[64,32768]{1,0:T(8,128)(2,1)S(1)}, bf16[64,32768]{1,0:T(8,128)(2,1)}, u32[]{:S(2)}) %copy-start.1) | copy-done | bytes 4194328
  94.8 0.7 pick_tiles.10.refs_0_
  95.6 5.0 %compare_convert_fusion.live = f32[256]{0:T(256)S(1)} fusion(s32[256]{0:T(256)S(1)} %copy-done.4, s32[256]{0:T(256)S(1)} %copy-done.2, s32[]{:T(128)} %bitcast, s32[]{:T(128)} %bitcast.1, s32[]{:T(128)} %bitcast.2, s32[]{:T(128)} %bitcast.3, s32[]{:T(128)} %bitcast.4, s32[]{:T(128)} %bitcast.5, s32[]{:T(128)} %bitcast.6, s32[]{:T(128)} %bitcast.7, ...), kind=kLoop, calls=%fused_computation.34 | loop fusion | flops 44544 | bytes 3112 | tf_op jit(solution)/shard_map/convert_element_type | solution.py:164
  100.6 2.4 %ladder_products.5.refs_1_ = f32[32,64,128]{2,1,0:T(8,128)S(1)} custom-call(s32[8]{0:T(128)S(1)} %iota_xor_fusion.order, s32[256]{0:T(256)S(1)} %fusion.3.cols, f32[256]{0:T(256)S(1)} %compare_convert_fusion.live, bf16[8,32,128,128]{3,2,1,0:T(8,128)(2,1)} %bitcast.16, bf16[32,64,128]{2,1,0:T(8,128)(2,1)S(1)} %collective-permute-done.13.refs_0_), custom_call_target="tpu_custom_call" | custom-call | flops 67108864 | bytes 1048576 | tf_op jit(solution)/shard_map/ladder_products/pallas_call | solution.py:122
  103.0 2.4 %ladder_products.6.refs_4_ = f32[32,64,128]{2,1,0:T(8,128)S(1)} custom-call(s32[8]{0:T(128)S(1)} %iota_xor_fusion.order, s32[256]{0:T(256)S(1)} %fusion.3.cols, f32[256]{0:T(256)S(1)} %compare_convert_fusion.live, bf16[8,32,128,128]{3,2,1,0:T(8,128)(2,1)} %bitcast.17, ...), custom_call_target="tpu_custom_call", output_to_operand_aliasing={{}: (5, {})} | custom-call | flops 67108864 | bytes 1048576 | tf_op jit(solution)/shard_map/ladder_products/pallas_call | solution.py:122
  105.4 14.0 %collective-permute-done.5.refs_1_ = bf16[32,64,128]{2,1,0:T(8,128)(2,1)} collective-permute-done((bf16[32,64,128]{2,1,0:T(8,128)(2,1)}, bf16[32,64,128]{2,1,0:T(8,128)(2,1)}, u32[]{:S(2)}, u32[]{:S(2)}) %collective-permute-start.5) | collective-permute-done | bytes 524320 | tf_op jit(solution)/shard_map/ppermute | solution.py:154
  119.4 4.9 %ladder_products.7.refs_1_ = f32[32,64,128]{2,1,0:T(8,128)S(1)} custom-call(s32[8]{0:T(128)S(1)} %iota_xor_fusion.order, s32[256]{0:T(256)S(1)} %fusion.3.cols, f32[256]{0:T(256)S(1)} %compare_convert_fusion.live, bf16[8,32,128,128]{3,2,1,0:T(8,128)(2,1)} %bitcast.18, bf16[32,64,128]{2,1,0:T(8,128)(2,1)S(1)} %pick_tiles.10.refs_0_, ...), custom_call_target="tpu_custom_call", output_to_operand_aliasing={{}: (8, {})} | custom-call | flops 268435456 | bytes 4194304 | tf_op jit(solution)/shard_map/ladder_products/pallas_call | solution.py:122
  124.2 0.0 collective-permute-done.3.refs_0_
  124.2 2.4 %ladder_products.8.refs_1_ = f32[32,64,128]{2,1,0:T(8,128)S(1)} custom-call(s32[8]{0:T(128)S(1)} %iota_xor_fusion.order, s32[256]{0:T(256)S(1)} %fusion.3.cols, f32[256]{0:T(256)S(1)} %compare_convert_fusion.live, bf16[8,32,128,128]{3,2,1,0:T(8,128)(2,1)} %bitcast.19, ...), custom_call_target="tpu_custom_call", output_to_operand_aliasing={{}: (5, {})} | custom-call | flops 67108864 | bytes 1048576 | tf_op jit(solution)/shard_map/ladder_products/pallas_call | solution.py:122
  126.6 0.0 collective-permute-done.1.refs_0_
  126.6 2.4 %ladder_products.9 = (f32[8,64,128]{2,1,0:T(8,128)S(1)}, f32[8,64,128]{2,1,0:T(8,128)S(1)}, f32[8,64,128]{2,1,0:T(8,128)S(1)}, f32[8,64,128]{2,1,0:T(8,128)S(1)}) custom-call(s32[8]{0:T(128)S(1)} %iota_xor_fusion.order, s32[256]{0:T(256)S(1)} %fusion.3.cols, f32[256]{0:T(256)S(1)} %compare_convert_fusion.live, bf16[8,32,128,128]{3,2,1,0:T(8,128)(2,1)} %bitcast.20, ...), custom_call_target="tpu_custom_call" | custom-call | flops 67108864 | bytes 1048576 | tf_op jit(solution)/shard_map/ladder_products/pallas_call | solution.py:122
  129.0 0.1 collective-permute-start.15
  129.1 0.5 collective-permute-start.14
  129.6 1.0 collective-permute-done.15
  130.7 1.6 %collective-permute-start.16 = (f32[8,64,128]{2,1,0:T(8,128)S(1)}, f32[8,64,128]{2,1,0:T(8,128)S(1)}, u32[]{:S(2)}, u32[]{:S(2)}) collective-permute-start(f32[8,64,128]{2,1,0:T(8,128)S(1)} %add.86), channel_id=1, source_target_pairs={{0,2},{1,3},{2,0},{3,1},{4,6},{5,7},{6,4},{7,5},{8,10},{9,11},{10,... | collective-permute-start | bytes 786440 | tf_op jit(solution)/shard_map/ppermute | solution.py:185
  132.2 0.0 collective-permute-done.14
  132.2 6.9 %collective-permute-done.16 = f32[8,64,128]{2,1,0:T(8,128)S(1)} collective-permute-done((f32[8,64,128]{2,1,0:T(8,128)S(1)}, f32[8,64,128]{2,1,0:T(8,128)S(1)}, u32[]{:S(2)}, u32[]{:S(2)}) %collective-permute-start.16) | collective-permute-done | bytes 262176 | tf_op jit(solution)/shard_map/ppermute | solution.py:185
  139.1 0.7 copy_bitcast_fusion
  (16 shorter events, 0.1 us)
Async XLA Ops:
  0.0 6.1 %collective-permute-start.10 = (s32[256]{0:T(256)}, s32[256]{0:T(256)S(1)}, u32[]{:S(2)}, u32[]{:S(2)}) collective-permute-start(s32[256]{0:T(256)} %rows.1), channel_id=1, source_target_pairs={{0,20},{4,16},{8,28},{12,24},{16,4},{20,0},{24,12},{28,8},{1,21},{... | collective-permute-start | bytes 3080 | tf_op jit(solution)/shard_map/ppermute | solution.py:154
  3.5 6.4 %collective-permute-start.12 = (s32[256]{0:T(256)}, s32[256]{0:T(256)S(1)}, u32[]{:S(2)}, u32[]{:S(2)}) collective-permute-start(s32[256]{0:T(256)} %rows.1), channel_id=1, source_target_pairs={{0,16},{4,20},{8,24},{12,28},{16,0},{20,4},{24,8},{28,12},{1,17},{... | collective-permute-start | bytes 3080 | tf_op jit(solution)/shard_map/ppermute | solution.py:154
  6.1 83.0 %copy-start = (bf16[64,32768]{1,0:T(8,128)(2,1)}, bf16[64,32768]{1,0:T(8,128)(2,1)S(1)}, u32[]{:S(2)}) copy-start(bf16[64,32768]{1,0:T(8,128)(2,1)S(1)} %stage_amplitudes.1.amp) | copy-start | bytes 12582916
  6.1 4.9 %copy-start.2 = (s32[256]{0:T(256)S(1)}, s32[256]{0:T(256)}, u32[]{:S(2)}) copy-start(s32[256]{0:T(256)} %rows.1) | copy-start | bytes 3076
  6.1 73.5 %copy-start.3 = (s32[8]{0:T(128)S(1)}, s32[8]{0:T(128)}, u32[]{:S(2)}) copy-start(s32[8]{0:T(128)} %param.6) | copy-start | bytes 100
  6.9 83.8 %collective-permute-start.11 = (bf16[32,64,128]{2,1,0:T(8,128)(2,1)S(1)}, bf16[32,64,128]{2,1,0:T(8,128)(2,1)S(1)}, u32[]{:S(2)}, u32[]{:S(2)}) collective-permute-start(bf16[32,64,128]{2,1,0:T(8,128)(2,1)S(1)} %pick_tiles.14), channel_id=1, source_target_pairs={{0,20},{4,16},{8,28},{12,24},{16,4},{20,0},{24,12},{28,8},{1,21},{... | collective-permute-start | bytes 1572872 | tf_op jit(solution)/shard_map/ppermute | solution.py:154
  10.6 80.0 %collective-permute-start.13 = (bf16[32,64,128]{2,1,0:T(8,128)(2,1)S(1)}, bf16[32,64,128]{2,1,0:T(8,128)(2,1)S(1)}, u32[]{:S(2)}, u32[]{:S(2)}) collective-permute-start(bf16[32,64,128]{2,1,0:T(8,128)(2,1)S(1)} %pick_tiles.15), channel_id=1, source_target_pairs={{0,16},{4,20},{8,24},{12,28},{16,0},{20,4},{24,8},{28,12},{1,17},{... | collective-permute-start | bytes 1572872 | tf_op jit(solution)/shard_map/ppermute | solution.py:154
  11.0 22.2 %collective-permute-start.8 = (s32[256]{0:T(256)S(1)}, s32[256]{0:T(256)S(1)}, u32[]{:S(2)}, u32[]{:S(2)}) collective-permute-start(s32[256]{0:T(256)S(1)} %copy-done.2), channel_id=1, source_target_pairs={{0,12},{4,8},{8,4},{12,0},{16,28},{20,24},{24,20},{28,16},{1,13},{... | collective-permute-start | bytes 3080 | tf_op jit(solution)/shard_map/ppermute | solution.py:154
  12.0 65.1 %collective-permute-start = (s32[256]{0:T(256)S(1)}, s32[256]{0:T(256)S(1)}, u32[]{:S(2)}, u32[]{:S(2)}) collective-permute-start(s32[256]{0:T(256)S(1)} %copy-done.2), channel_id=1, source_target_pairs={{0,28},{4,24},{8,20},{12,16},{16,12},{20,8},{24,4},{28,0},{1,29},{... | collective-permute-start | bytes 3080 | tf_op jit(solution)/shard_map/ppermute | solution.py:154
  15.1 72.5 %collective-permute-start.6 = (s32[256]{0:T(256)S(1)}, s32[256]{0:T(256)S(1)}, u32[]{:S(2)}, u32[]{:S(2)}) collective-permute-start(s32[256]{0:T(256)S(1)} %copy-done.2), channel_id=1, source_target_pairs={{0,8},{4,12},{8,0},{12,4},{16,24},{20,28},{24,16},{28,20},{1,9},{5... | collective-permute-start | bytes 3080 | tf_op jit(solution)/shard_map/ppermute | solution.py:154
  33.2 51.4 %collective-permute-start.4 = (s32[256]{0:T(256)S(1)}, s32[256]{0:T(256)S(1)}, u32[]{:S(2)}, u32[]{:S(2)}) collective-permute-start(s32[256]{0:T(256)S(1)} %copy-done.2), channel_id=1, source_target_pairs={{0,4},{4,0},{8,12},{12,8},{16,20},{20,16},{24,28},{28,24},{1,5},{5... | collective-permute-start | bytes 3080 | tf_op jit(solution)/shard_map/ppermute | solution.py:154
  77.0 5.5 %collective-permute-start.2 = (s32[256]{0:T(256)S(1)}, s32[256]{0:T(256)S(1)}, u32[]{:S(2)}, u32[]{:S(2)}) collective-permute-start(s32[256]{0:T(256)S(1)} %copy-done.2), channel_id=1, source_target_pairs={{0,24},{4,28},{8,16},{12,20},{16,8},{20,12},{24,0},{28,4},{1,25},{... | collective-permute-start | bytes 3080 | tf_op jit(solution)/shard_map/ppermute | solution.py:154
  82.5 44.1 %collective-permute-start.1 = (bf16[32,64,128]{2,1,0:T(8,128)(2,1)S(1)}, bf16[32,64,128]{2,1,0:T(8,128)(2,1)S(1)}, u32[]{:S(2)}, u32[]{:S(2)}) collective-permute-start(bf16[32,64,128]{2,1,0:T(8,128)(2,1)S(1)} %pick_tiles.8), channel_id=1, source_target_pairs={{0,28},{4,24},{8,20},{12,16},{16,12},{20,8},{24,4},{28,0},{1,29},{... | collective-permute-start | bytes 1572872 | tf_op jit(solution)/shard_map/ppermute | solution.py:154
  84.7 39.6 %collective-permute-start.3 = (bf16[32,64,128]{2,1,0:T(8,128)(2,1)}, bf16[32,64,128]{2,1,0:T(8,128)(2,1)S(1)}, u32[]{:S(2)}, u32[]{:S(2)}) collective-permute-start(bf16[32,64,128]{2,1,0:T(8,128)(2,1)} %pick_tiles.9), channel_id=1, source_target_pairs={{0,24},{4,28},{8,16},{12,20},{16,8},{20,12},{24,0},{28,4},{1,25},{... | collective-permute-start | bytes 1572872 | tf_op jit(solution)/shard_map/ppermute | solution.py:154
  87.6 7.9 %copy-start.4 = (s32[256]{0:T(256)S(1)}, s32[256]{0:T(256)}, u32[]{:S(2)}) copy-start(s32[256]{0:T(256)} %param.9) | copy-start | bytes 3076
  87.6 31.8 %collective-permute-start.5 = (bf16[32,64,128]{2,1,0:T(8,128)(2,1)}, bf16[32,64,128]{2,1,0:T(8,128)(2,1)}, u32[]{:S(2)}, u32[]{:S(2)}) collective-permute-start(bf16[32,64,128]{2,1,0:T(8,128)(2,1)} %pick_tiles.11), channel_id=1, source_target_pairs={{0,4},{4,0},{8,12},{12,8},{16,20},{20,16},{24,28},{28,24},{1,5},{5... | collective-permute-start | bytes 1572872 | tf_op jit(solution)/shard_map/ppermute | solution.py:154
  90.6 28.7 %collective-permute-start.7 = (bf16[32,64,128]{2,1,0:T(8,128)(2,1)}, bf16[32,64,128]{2,1,0:T(8,128)(2,1)}, u32[]{:S(2)}, u32[]{:S(2)}) collective-permute-start(bf16[32,64,128]{2,1,0:T(8,128)(2,1)} %pick_tiles.12), channel_id=1, source_target_pairs={{0,8},{4,12},{8,0},{12,4},{16,24},{20,28},{24,16},{28,20},{1,9},{5... | collective-permute-start | bytes 1572872 | tf_op jit(solution)/shard_map/ppermute | solution.py:154
  90.6 28.7 %collective-permute-start.9 = (bf16[32,64,128]{2,1,0:T(8,128)(2,1)}, bf16[32,64,128]{2,1,0:T(8,128)(2,1)}, u32[]{:S(2)}, u32[]{:S(2)}) collective-permute-start(bf16[32,64,128]{2,1,0:T(8,128)(2,1)} %pick_tiles.13), channel_id=1, source_target_pairs={{0,12},{4,8},{8,4},{12,0},{16,28},{20,24},{24,20},{28,16},{1,13},{... | collective-permute-start | bytes 1572872 | tf_op jit(solution)/shard_map/ppermute | solution.py:154
  92.6 2.2 %copy-start.1 = (bf16[64,32768]{1,0:T(8,128)(2,1)S(1)}, bf16[64,32768]{1,0:T(8,128)(2,1)}, u32[]{:S(2)}) copy-start(bf16[64,32768]{1,0:T(8,128)(2,1)} %copy-done) | copy-start | bytes 12582916
  129.0 1.6 %collective-permute-start.15 = (f32[8,64,128]{2,1,0:T(8,128)S(1)}, f32[8,64,128]{2,1,0:T(8,128)S(1)}, u32[]{:S(2)}, u32[]{:S(2)}) collective-permute-start(f32[8,64,128]{2,1,0:T(8,128)S(1)} %get-tuple-element.12), channel_id=1, source_target_pairs={{0,1},{1,0},{2,3},{3,2},{4,5},{5,4},{6,7},{7,6},{8,9},{9,8},{10,11... | collective-permute-start | bytes 786440 | tf_op jit(solution)/shard_map/ppermute | solution.py:185
  129.1 3.1 %collective-permute-start.14 = (f32[8,64,128]{2,1,0:T(8,128)S(1)}, f32[8,64,128]{2,1,0:T(8,128)S(1)}, u32[]{:S(2)}, u32[]{:S(2)}) collective-permute-start(f32[8,64,128]{2,1,0:T(8,128)S(1)} %get-tuple-element.10), channel_id=1, source_target_pairs={{0,1},{1,0},{2,3},{3,2},{4,5},{5,4},{6,7},{7,6},{8,9},{9,8},{10,11... | collective-permute-start | bytes 786440 | tf_op jit(solution)/shard_map/ppermute | solution.py:185
  130.7 8.4 %collective-permute-start.16 = (f32[8,64,128]{2,1,0:T(8,128)S(1)}, f32[8,64,128]{2,1,0:T(8,128)S(1)}, u32[]{:S(2)}, u32[]{:S(2)}) collective-permute-start(f32[8,64,128]{2,1,0:T(8,128)S(1)} %add.86), channel_id=1, source_target_pairs={{0,2},{1,3},{2,0},{3,1},{4,6},{5,7},{6,4},{7,5},{8,10},{9,11},{10,... | collective-permute-start | bytes 786440 | tf_op jit(solution)/shard_map/ppermute | solution.py:185

commit v5 on v4

v5 whole, which is shorter than its diff:
```python
import functools

import jax
import jax.numpy as jnp
from jax import lax
from jax.experimental import pallas as pl
from jax.experimental.pallas import tpu as pltpu
from jax.sharding import PartitionSpec as P

V = 1024
BLK = 128
ABT_X = 32
CORES = 2
UNROLL = 16
MIB = 1024 * 1024

VMEM_SPEC = pl.BlockSpec(memory_space=pltpu.VMEM)
SMEM_SPEC = pl.BlockSpec(memory_space=pltpu.SMEM)
ANY_SPEC = pl.BlockSpec(memory_space=pl.ANY)


def pair_irrep(tile, virt_irreps):
    first = tile * BLK // V // BLK
    second = tile * BLK % V // BLK
    return jnp.bitwise_xor(virt_irreps[first], virt_irreps[second])


def pick_kernel(step, per, local_tiles, me, wanted, amp, out, sem):
    peer = me[0] ^ step
    origin = me[0] * local_tiles

    def start(i, carry):
        lane = pl.multiple_of((wanted[peer, i] - origin) * BLK, BLK)
        pltpu.make_async_copy(amp.at[:, pl.ds(lane, BLK)], out.at[i], sem).start()
        return carry

    lax.fori_loop(0, per, start, 0, unroll=8)
    pltpu.make_async_copy(out, out, sem).wait()


def pick(step, me, wanted, amp):
    occupied, width = amp.shape
    peers, per = wanted.shape
    return pl.pallas_call(
        functools.partial(pick_kernel, step, per, width // BLK),
        out_shape=pltpu.HBM((per, occupied, BLK), amp.dtype),
        in_specs=[SMEM_SPEC, SMEM_SPEC, ANY_SPEC],
        out_specs=pl.BlockSpec(memory_space=pltpu.HBM),
        scratch_shapes=[pltpu.SemaphoreType.DMA],
        compiler_params=pltpu.CompilerParams(vmem_limit_bytes=MIB),
        cost_estimate=pl.CostEstimate(
            flops=0, bytes_accessed=4 * per * occupied * BLK, transcendentals=0
        ),
        name="pick_tiles",
    )(me, wanted, pltpu.with_memory_space_constraint(amp, pltpu.HBM))


def add_products(per, base, cols, live, piece, weights, total):
    unroll = min(UNROLL, per)

    def step(i, carry):
        slots = [i * unroll + u for u in range(unroll)]
        products = [
            jnp.dot(piece[s], weights[s], preferred_element_type=jnp.float32) for s in slots
        ]
        for s, product in zip(slots, products):
            total[cols[base + s]] += product * live[base + s]
        return carry

    lax.fori_loop(0, per // unroll, step, 0)


def ladder_kernel(peers_at, ahead, per, first, last, order, cols, live, w, *refs):
    count = len(peers_at)
    pieces, refs = refs[:count], refs[count:]
    if not first:
        start, refs = refs[0], refs[1:]
    if last:
        outs, held, total = refs, w, start
    else:
        *outs, held, sems = refs
        total = outs[0]
    copies = []
    for j, k in enumerate([] if last else peers_at + ahead):
        target = held.at[j] if j < count else outs[1].at[j - count]
        copies.append(pltpu.make_async_copy(w.at[order[k]], target, sems.at[j]))
        copies[-1].start()
    if first:
        total[...] = jnp.zeros_like(total)
    for j, k in enumerate(peers_at):
        if not last:
            copies[j].wait()
        add_products(per, order[k] * per, cols, live, pieces[j], held.at[j], total)
    for copy in copies[count:]:
        copy.wait()
    if last:
        at = 0
        for out in outs:
            out[...] = total[at : at + out.shape[0]]
            at += out.shape[0]


def ladder(order, cols, live, w, start, arrived, peers_at, ahead=(), last=None):
    pieces = [arrived[k] for k in peers_at]
    count = len(pieces)
    per, occupied, _ = pieces[0].shape
    first = start is None
    scratch = []
    if last:
        out_shape = [jax.ShapeDtypeStruct((n, occupied, BLK), jnp.float32) for n in last]
    else:
        out_shape = [pltpu.VMEM((ABT_X, occupied, BLK), jnp.float32)]
        if ahead:
            out_shape.append(pltpu.VMEM((len(ahead), per, BLK, BLK), w.dtype))
        scratch = [
            pltpu.VMEM((count, per, BLK, BLK), w.dtype),
            pltpu.SemaphoreType.DMA((count + len(ahead),)),
        ]
        w = pltpu.with_memory_space_constraint(w, pltpu.HBM)
    return pl.pallas_call(
        functools.partial(ladder_kernel, peers_at, list(ahead), per, first, bool(last)),
        out_shape=out_shape,
        in_specs=[SMEM_SPEC] * 3
        + [VMEM_SPEC if last else ANY_SPEC]
        + [VMEM_SPEC] * (count + (not first)),
        out_specs=[VMEM_SPEC] * len(out_shape),
        input_output_aliases={} if first or last else {4 + count: 0},
        scratch_shapes=scratch,
        compiler_params=pltpu.CompilerParams(vmem_limit_bytes=8 * MIB),
        cost_estimate=pl.CostEstimate(
            flops=2 * count * per * occupied * BLK * BLK,
            bytes_accessed=2 * (count + len(ahead)) * per * BLK * BLK,
            transcendentals=0,
        ),
        name="ladder_products",
    )(order, cols, live, w, *pieces, *([] if first else [start]))


def per_device(amplitudes, virt_irreps, w_tiles, tile_rows, tile_cols):
    occupied = amplitudes.shape[0]
    peers = lax.axis_size("gx")
    groups = lax.axis_size("gy")
    me = lax.axis_index("gx")
    mine = lax.axis_index("gy")
    row_count = amplitudes.shape[1] // BLK * peers
    per = tile_rows.shape[0] // peers
    near = peers // 2

    def swap(x, k):
        return lax.ppermute(x, "gx", [(i, i ^ k) for i in range(peers)])

    wanted = lax.all_to_all(tile_rows.reshape(peers, per), "gx", 0, 0)
    here = me.reshape(1)
    arrived = {0: pick(0, here, wanted, amplitudes)}
    for k in range(1, peers):
        arrived[k] = swap(pick(k, here, wanted, amplitudes), k)

    row_tile = mine * row_count + tile_rows
    col_tile = me * ABT_X + tile_cols
    live = (pair_irrep(row_tile, virt_irreps) == pair_irrep(col_tile, virt_irreps)).astype(
        jnp.float32
    )
    share = ABT_X // groups
    xs = groups // CORES
    owner = tile_cols // share
    other_core = (owner % CORES) ^ (mine % CORES)
    other_x = (owner // CORES) ^ (mine // CORES)
    cols = other_core * (ABT_X // CORES) + other_x * share + tile_cols % share
    order = jnp.arange(peers, dtype=jnp.int32) ^ me

    w = w_tiles.reshape(peers, per, BLK, BLK)
    quarter = near // 4
    far = [list(range(near + j * quarter, near + (j + 1) * quarter)) for j in range(4)]
    args = (order, cols, live, w)
    (total,) = ladder(*args, None, arrived, far[0])
    (total,) = ladder(*args, total, arrived, far[1])
    total, held = ladder(*args, total, arrived, list(range(near)), ahead=far[3])
    (total,) = ladder(*args, total, arrived, far[2])
    sizes = (share, (xs - 1) * share) * CORES
    keep, keep_rest, give, give_rest = ladder(
        order, cols, live, held, total, arrived, far[3], last=sizes
    )

    def swap_gy(x, k):
        return lax.ppermute(x, "gy", [(i, i ^ k) for i in range(groups)])

    rest = (keep_rest + swap_gy(give_rest, 1)).reshape(xs - 1, share, occupied, BLK)
    result = keep + swap_gy(give, 1)
    for k in range(1, xs):
        result = result + swap_gy(rest[k - 1], k * CORES)
    return jnp.transpose(result, (1, 0, 2)).reshape(occupied, share * BLK)


def solution(mesh):
    in_specs = (
        P(None, ("gy", "gx")),
        P(),
        P(("gx", "gy"), None, None),
        P(("gx", "gy")),
        P(("gx", "gy")),
    )
    out_specs = P(None, ("gx", "gy"))
    return jax.shard_map(
        per_device, mesh=mesh, in_specs=in_specs, out_specs=out_specs, check_vma=False
    )
```

time: 140 us -> 204 us (1.46)
  Pallas kernels: 25.4 us -> 154 us
  waiting for transfers between devices: 82 us -> 23.1 us
  starting transfers between devices: 23.5 us -> 17.9 us
    pallas_call x14 -> x13, Pallas kernels: 25.4 us -> 154 us  [the longest x8 141 us: pick(): pl.pallas_call(functools.partial(pick_kernel, step, per, width // BLK), o...]
    ppermute x14 -> x7, waiting for transfers between devices: 74.1 us -> 10.3 us  [swap(): return lax.ppermute(x, 'gx', [(i, i ^ k) for i in range(peers)])]
    ppermute x14 -> x7, starting transfers between devices: 21.4 us -> 9.53 us  [swap(): return lax.ppermute(x, 'gx', [(i, i ^ k) for i in range(peers)])]
    all_to_all x0 -> x1, starting transfers between devices: none -> 6.28 us  [per_device(): wanted = lax.all_to_all(tile_rows.reshape(peers, per), 'gx', 0, 0)]
    all_to_all x0 -> x1, waiting for transfers between devices: none -> 4.91 us  [per_device(): wanted = lax.all_to_all(tile_rows.reshape(peers, per), 'gx', 0, 0)]
    unnamed x10 -> x8, local copies, waits for them, and re-layouts: 2.21 us -> 0.02 us
  transfers between devices with their start and end apart: 17 -> 11, of which waited for: 5 -> 4; matrix products, arithmetic and copies ran while one was open for 4% -> 3% of each run, Pallas kernels for 16% -> 67%
where the time goes in v5:
time: 204 us; the launch traced here: 203 us
  Pallas kernels  154 us (75%)
  waiting for transfers between devices  23.1 us (11%)
  starting transfers between devices  17.9 us (9%)
  other arithmetic  5.76 us (3%)
  local copies, waits for them, and re-layouts  2.05 us (1%)
    pallas_call x8, Pallas kernels, pick(): pl.pallas_call(functools.partial(pick_kernel, step, per, width // BLK), o...  141 us
    pallas_call x5, Pallas kernels, ladder(): pl.pallas_call(functools.partial(ladder_kernel, peers_at, list(ahead), pe...  12.9 us
    ppermute x7, waiting for transfers between devices, swap(): return lax.ppermute(x, 'gx', [(i, i ^ k) for i in range(peers)])  10.3 us
    ppermute x7, starting transfers between devices, swap(): return lax.ppermute(x, 'gx', [(i, i ^ k) for i in range(peers)])  9.53 us
    ppermute x3, waiting for transfers between devices, swap_gy(): return lax.ppermute(x, 'gy', [(i, i ^ k) for i in range(groups)])  7.88 us
    all_to_all x1, starting transfers between devices, per_device(): wanted = lax.all_to_all(tile_rows.reshape(peers, per), 'gx', 0, 0)  6.28 us
    convert_element_type x1, other arithmetic, per_device(): (pair_irrep(row_tile, virt_irreps) == pair_irrep(col_tile, virt_irreps))....  4.96 us
    all_to_all x1, waiting for transfers between devices, per_device(): wanted = lax.all_to_all(tile_rows.reshape(peers, per), 'gx', 0, 0)  4.91 us
  transfers between devices with their start and end apart: 11, of which 4 were waited for; matrix products, arithmetic and copies ran while one was open for 3% of the time, Pallas kernels for 67%

profile of v5, /device:TPU:8, one launch (start us, length us, event | category | flops | bytes accessed | tf_op | source)
XLA Modules:
  0.0 202.8 jit_solution(12597058371025525639)
XLA Ops:
  0.0 0.0 copy-start.1
  0.0 1.4 all_to_all.7
  1.4 6.3 %all-to-all-start = ((s32[8,1,32]{2,1,0:T(1,128)}), s32[8,1,32]{2,1,0:T(1,128)S(1)}, u32[]{:S(2)}, u32[]{:S(2)}) async-start(s32[8,1,32]{2,1,0:T(1,128)} %all_to_all.7), calls=%async_computation | async-start | bytes 8192 | tf_op jit(solution)/shard_map/all_to_all | solution.py:152
  7.6 4.9 %all-to-all-done = s32[8,1,32]{2,1,0:T(1,128)S(1)} async-done(((s32[8,1,32]{2,1,0:T(1,128)}), s32[8,1,32]{2,1,0:T(1,128)S(1)}, u32[]{:S(2)}, u32[]{:S(2)}) %all-to-all-start) | async-done | bytes 1056 | tf_op jit(solution)/shard_map/all_to_all | solution.py:152
  12.6 17.6 %pick_tiles.13 = bf16[32,64,128]{2,1,0:T(8,128)(2,1)} custom-call(s32[1]{0:T(128)} %bitcast.9.me, s32[8,32]{1,0:T(8,128)S(1)} %bitcast.17, bf16[64,32768]{1,0:T(8,128)(2,1)} %amp.15), custom_call_target="tpu_custom_call" | custom-call | bytes 1048576 | tf_op jit(solution)/shard_map/pick_tiles/pallas_call | solution.py:44
  30.2 0.7 collective-permute-start.4
  30.8 17.6 %pick_tiles.12 = bf16[32,64,128]{2,1,0:T(8,128)(2,1)} custom-call(s32[1]{0:T(128)} %bitcast.9.me, s32[8,32]{1,0:T(8,128)S(1)} %bitcast.18, bf16[64,32768]{1,0:T(8,128)(2,1)} %amp.15), custom_call_target="tpu_custom_call" | custom-call | bytes 1048576 | tf_op jit(solution)/shard_map/pick_tiles/pallas_call | solution.py:44
  48.4 2.4 %collective-permute-start.3 = (bf16[32,64,128]{2,1,0:T(8,128)(2,1)}, bf16[32,64,128]{2,1,0:T(8,128)(2,1)S(1)}, u32[]{:S(2)}, u32[]{:S(2)}) collective-permute-start(bf16[32,64,128]{2,1,0:T(8,128)(2,1)} %pick_tiles.12), channel_id=1, source_target_pairs={{0,20},{4,16},{8,28},{12,24},{16,4},{20,0},{24,12},{28,8},{1,21},{... | collective-permute-start | bytes 1572872 | tf_op jit(solution)/shard_map/ppermute | solution.py:150
  50.9 0.0 copy-done.1
  50.9 0.7 fusion.4
  51.5 17.6 %pick_tiles.9 = bf16[32,64,128]{2,1,0:T(8,128)(2,1)} custom-call(s32[1]{0:T(128)} %bitcast.9.me, s32[8,32]{1,0:T(8,128)S(1)} %bitcast.19, bf16[64,32768]{1,0:T(8,128)(2,1)} %amp.15), custom_call_target="tpu_custom_call" | custom-call | bytes 1048576 | tf_op jit(solution)/shard_map/pick_tiles/pallas_call | solution.py:44
  69.1 0.0 copy-start.2
  69.1 0.0 copy-start.3
  69.1 17.6 %pick_tiles.10 = bf16[32,64,128]{2,1,0:T(8,128)(2,1)} custom-call(s32[1]{0:T(128)} %bitcast.9.me, s32[8,32]{1,0:T(8,128)S(1)} %bitcast.20, bf16[64,32768]{1,0:T(8,128)(2,1)} %amp.15), custom_call_target="tpu_custom_call" | custom-call | bytes 1048576 | tf_op jit(solution)/shard_map/pick_tiles/pallas_call | solution.py:44
  86.8 17.6 %pick_tiles.11 = bf16[32,64,128]{2,1,0:T(8,128)(2,1)} custom-call(s32[1]{0:T(128)} %bitcast.9.me, s32[8,32]{1,0:T(8,128)S(1)} %bitcast.21, bf16[64,32768]{1,0:T(8,128)(2,1)} %amp.15), custom_call_target="tpu_custom_call" | custom-call | bytes 1048576 | tf_op jit(solution)/shard_map/pick_tiles/pallas_call | solution.py:44
  104.4 17.6 %pick_tiles.15 = bf16[32,64,128]{2,1,0:T(8,128)(2,1)} custom-call(s32[1]{0:T(128)} %bitcast.9.me, s32[8,32]{1,0:T(8,128)S(1)} %bitcast.22, bf16[64,32768]{1,0:T(8,128)(2,1)} %amp.15), custom_call_target="tpu_custom_call" | custom-call | bytes 1048576 | tf_op jit(solution)/shard_map/pick_tiles/pallas_call | solution.py:44
  122.0 17.6 %pick_tiles.14 = bf16[32,64,128]{2,1,0:T(8,128)(2,1)} custom-call(s32[1]{0:T(128)} %bitcast.9.me, s32[8,32]{1,0:T(8,128)S(1)} %bitcast.23, bf16[64,32768]{1,0:T(8,128)(2,1)} %amp.15), custom_call_target="tpu_custom_call" | custom-call | bytes 1048576 | tf_op jit(solution)/shard_map/pick_tiles/pallas_call | solution.py:44
  139.6 1.5 collective-permute-start
  141.1 1.5 collective-permute-start.1
  142.6 0.6 collective-permute-start.2
  143.1 0.0 collective-permute-done.4.refs_0_
  143.1 0.5 collective-permute-start.6
  143.7 0.0 collective-permute-done.3.refs_0_
  143.7 2.4 %collective-permute-start.5 = (bf16[32,64,128]{2,1,0:T(8,128)(2,1)}, bf16[32,64,128]{2,1,0:T(8,128)(2,1)S(1)}, u32[]{:S(2)}, u32[]{:S(2)}) collective-permute-start(bf16[32,64,128]{2,1,0:T(8,128)(2,1)} %pick_tiles.14), channel_id=1, source_target_pairs={{0,28},{4,24},{8,20},{12,16},{16,12},{20,8},{24,4},{28,0},{1,29},{... | collective-permute-start | bytes 1572872 | tf_op jit(solution)/shard_map/ppermute | solution.py:150
  146.0 0.0 copy-done.2
  146.1 0.0 copy-done.3
  146.1 5.0 %compare_convert_fusion.live = f32[256]{0:T(256)S(1)} fusion(s32[256]{0:T(256)S(1)} %copy-done.2, s32[256]{0:T(256)S(1)} %copy-done.3, s32[]{:T(128)} %bitcast, s32[]{:T(128)} %bitcast.1, s32[]{:T(128)} %bitcast.2, s32[]{:T(128)} %bitcast.3, s32[]{:T(128)} %bitcast.4, s32[]{:T(128)} %bitcast.5, s32[]{:T(128)} %bitcast.6, s32[]{:T(128)} %bitcast.7, ...), kind=kLoop, calls=%fused_computation.34 | loop fusion | flops 44544 | bytes 3112 | tf_op jit(solution)/shard_map/convert_element_type | solution.py:160
  151.0 17.6 %pick_tiles.8.refs_0_ = bf16[32,64,128]{2,1,0:T(8,128)(2,1)} custom-call(s32[1]{0:T(128)} %bitcast.9.me, s32[8,32]{1,0:T(8,128)S(1)} %bitcast.24, bf16[64,32768]{1,0:T(8,128)(2,1)} %amp.15), custom_call_target="tpu_custom_call" | custom-call | bytes 1048576 | tf_op jit(solution)/shard_map/pick_tiles/pallas_call | solution.py:44
  168.7 0.0 copy-start
  168.7 2.4 %ladder_products.5.refs_1_ = f32[32,64,128]{2,1,0:T(8,128)S(1)} custom-call(s32[8]{0:T(128)S(1)} %iota_xor_fusion.order, s32[256]{0:T(256)S(1)} %fusion.3.cols, f32[256]{0:T(256)S(1)} %compare_convert_fusion.live, bf16[8,32,128,128]{3,2,1,0:T(8,128)(2,1)} %bitcast.25, bf16[32,64,128]{2,1,0:T(8,128)(2,1)S(1)} %collective-permute-done.4.refs_0_), custom_call_target="tpu_custom_call" | custom-call | flops 67108864 | bytes 1048576 | tf_op jit(solution)/shard_map/ladder_products/pallas_call | solution.py:120
  171.0 2.4 %ladder_products.6.refs_4_ = f32[32,64,128]{2,1,0:T(8,128)S(1)} custom-call(s32[8]{0:T(128)S(1)} %iota_xor_fusion.order, s32[256]{0:T(256)S(1)} %fusion.3.cols, f32[256]{0:T(256)S(1)} %compare_convert_fusion.live, bf16[8,32,128,128]{3,2,1,0:T(8,128)(2,1)} %bitcast.26, ...), custom_call_target="tpu_custom_call", output_to_operand_aliasing={{}: (5, {})} | custom-call | flops 67108864 | bytes 1048576 | tf_op jit(solution)/shard_map/ladder_products/pallas_call | solution.py:120
  173.4 0.0 collective-permute-done.refs_1_
  173.4 0.0 collective-permute-done.1.refs_2_
  173.4 0.0 collective-permute-done.2.refs_3_
  173.5 0.0 copy-done
  173.5 4.1 %ladder_products.7 = (f32[32,64,128]{2,1,0:T(8,128)S(1)}, bf16[1,32,128,128]{3,2,1,0:T(8,128)(2,1)S(1)}) custom-call(s32[8]{0:T(128)S(1)} %iota_xor_fusion.order, s32[256]{0:T(256)S(1)} %fusion.3.cols, f32[256]{0:T(256)S(1)} %compare_convert_fusion.live, bf16[8,32,128,128]{3,2,1,0:T(8,128)(2,1)} %bitcast.27, ...), custom_call_target="tpu_custom_call", output_to_operand_aliasing={{0}: (8, {})} | custom-call | flops 268435456 | bytes 5242880 | tf_op jit(solution)/shard_map/ladder_products/pallas_call | solution.py:120
  177.6 0.0 collective-permute-done.6.refs_0_
  177.6 2.8 %ladder_products.8.refs_1_ = f32[32,64,128]{2,1,0:T(8,128)S(1)} custom-call(s32[8]{0:T(128)S(1)} %iota_xor_fusion.order, s32[256]{0:T(256)S(1)} %fusion.3.cols, f32[256]{0:T(256)S(1)} %compare_convert_fusion.live, bf16[8,32,128,128]{3,2,1,0:T(8,128)(2,1)} %bitcast.28, ...), custom_call_target="tpu_custom_call", output_to_operand_aliasing={{}: (5, {})} | custom-call | flops 67108864 | bytes 1048576 | tf_op jit(solution)/shard_map/ladder_products/pallas_call | solution.py:120
  180.4 10.3 %collective-permute-done.5.refs_0_ = bf16[32,64,128]{2,1,0:T(8,128)(2,1)S(1)} collective-permute-done((bf16[32,64,128]{2,1,0:T(8,128)(2,1)}, bf16[32,64,128]{2,1,0:T(8,128)(2,1)S(1)}, u32[]{:S(2)}, u32[]{:S(2)}) %collective-permute-start.5) | collective-permute-done | bytes 524320 | tf_op jit(solution)/shard_map/ppermute | solution.py:150
  190.8 1.2 ladder_products.9
  192.0 0.1 collective-permute-start.8
  192.0 0.5 collective-permute-start.7
  192.5 1.0 collective-permute-done.8
  193.6 1.6 collective-permute-start.9
  195.2 0.0 collective-permute-done.7
  195.2 6.9 %collective-permute-done.9 = f32[8,64,128]{2,1,0:T(8,128)S(1)} collective-permute-done((f32[8,64,128]{2,1,0:T(8,128)S(1)}, f32[8,64,128]{2,1,0:T(8,128)S(1)}, u32[]{:S(2)}, u32[]{:S(2)}) %collective-permute-start.9) | collective-permute-done | bytes 262176 | tf_op jit(solution)/shard_map/ppermute | solution.py:185
  202.0 0.7 copy_bitcast_fusion
  (3 shorter events, 0.1 us)
Async XLA Ops:
  0.0 50.9 %copy-start.1 = (s32[8]{0:T(128)S(1)}, s32[8]{0:T(128)}, u32[]{:S(2)}) copy-start(s32[8]{0:T(128)} %param.6) | copy-start | bytes 100
  1.4 11.2 %all-to-all-start = ((s32[8,1,32]{2,1,0:T(1,128)}), s32[8,1,32]{2,1,0:T(1,128)S(1)}, u32[]{:S(2)}, u32[]{:S(2)}) async-start(s32[8,1,32]{2,1,0:T(1,128)} %all_to_all.7), calls=%async_computation | async-start | bytes 8192 | tf_op jit(solution)/shard_map/all_to_all | solution.py:152
  30.2 113.0 %collective-permute-start.4 = (bf16[32,64,128]{2,1,0:T(8,128)(2,1)}, bf16[32,64,128]{2,1,0:T(8,128)(2,1)S(1)}, u32[]{:S(2)}, u32[]{:S(2)}) collective-permute-start(bf16[32,64,128]{2,1,0:T(8,128)(2,1)} %pick_tiles.13), channel_id=1, source_target_pairs={{0,16},{4,20},{8,24},{12,28},{16,0},{20,4},{24,8},{28,12},{1,17},{... | collective-permute-start | bytes 1572872 | tf_op jit(solution)/shard_map/ppermute | solution.py:150
  48.4 95.3 %collective-permute-start.3 = (bf16[32,64,128]{2,1,0:T(8,128)(2,1)}, bf16[32,64,128]{2,1,0:T(8,128)(2,1)S(1)}, u32[]{:S(2)}, u32[]{:S(2)}) collective-permute-start(bf16[32,64,128]{2,1,0:T(8,128)(2,1)} %pick_tiles.12), channel_id=1, source_target_pairs={{0,20},{4,16},{8,28},{12,24},{16,4},{20,0},{24,12},{28,8},{1,21},{... | collective-permute-start | bytes 1572872 | tf_op jit(solution)/shard_map/ppermute | solution.py:150
  69.1 76.9 %copy-start.2 = (s32[256]{0:T(256)S(1)}, s32[256]{0:T(256)}, u32[]{:S(2)}) copy-start(s32[256]{0:T(256)} %param.9) | copy-start | bytes 3076
  69.1 76.9 %copy-start.3 = (s32[256]{0:T(256)S(1)}, s32[256]{0:T(256)}, u32[]{:S(2)}) copy-start(s32[256]{0:T(256)} %param.8) | copy-start | bytes 3076
  139.6 33.9 %collective-permute-start = (bf16[32,64,128]{2,1,0:T(8,128)(2,1)}, bf16[32,64,128]{2,1,0:T(8,128)(2,1)S(1)}, u32[]{:S(2)}, u32[]{:S(2)}) collective-permute-start(bf16[32,64,128]{2,1,0:T(8,128)(2,1)} %pick_tiles.9), channel_id=1, source_target_pairs={{0,4},{4,0},{8,12},{12,8},{16,20},{20,16},{24,28},{28,24},{1,5},{5... | collective-permute-start | bytes 1572872 | tf_op jit(solution)/shard_map/ppermute | solution.py:150
  141.1 32.4 %collective-permute-start.1 = (bf16[32,64,128]{2,1,0:T(8,128)(2,1)}, bf16[32,64,128]{2,1,0:T(8,128)(2,1)S(1)}, u32[]{:S(2)}, u32[]{:S(2)}) collective-permute-start(bf16[32,64,128]{2,1,0:T(8,128)(2,1)} %pick_tiles.10), channel_id=1, source_target_pairs={{0,8},{4,12},{8,0},{12,4},{16,24},{20,28},{24,16},{28,20},{1,9},{5... | collective-permute-start | bytes 1572872 | tf_op jit(solution)/shard_map/ppermute | solution.py:150
  142.6 30.9 %collective-permute-start.2 = (bf16[32,64,128]{2,1,0:T(8,128)(2,1)}, bf16[32,64,128]{2,1,0:T(8,128)(2,1)S(1)}, u32[]{:S(2)}, u32[]{:S(2)}) collective-permute-start(bf16[32,64,128]{2,1,0:T(8,128)(2,1)} %pick_tiles.11), channel_id=1, source_target_pairs={{0,12},{4,8},{8,4},{12,0},{16,28},{20,24},{24,20},{28,16},{1,13},{... | collective-permute-start | bytes 1572872 | tf_op jit(solution)/shard_map/ppermute | solution.py:150
  143.1 34.4 %collective-permute-start.6 = (bf16[32,64,128]{2,1,0:T(8,128)(2,1)}, bf16[32,64,128]{2,1,0:T(8,128)(2,1)}, u32[]{:S(2)}, u32[]{:S(2)}) collective-permute-start(bf16[32,64,128]{2,1,0:T(8,128)(2,1)} %pick_tiles.15), channel_id=1, source_target_pairs={{0,24},{4,28},{8,16},{12,20},{16,8},{20,12},{24,0},{28,4},{1,25},{... | collective-permute-start | bytes 1572872 | tf_op jit(solution)/shard_map/ppermute | solution.py:150
  143.7 47.1 %collective-permute-start.5 = (bf16[32,64,128]{2,1,0:T(8,128)(2,1)}, bf16[32,64,128]{2,1,0:T(8,128)(2,1)S(1)}, u32[]{:S(2)}, u32[]{:S(2)}) collective-permute-start(bf16[32,64,128]{2,1,0:T(8,128)(2,1)} %pick_tiles.14), channel_id=1, source_target_pairs={{0,28},{4,24},{8,20},{12,16},{16,12},{20,8},{24,4},{28,0},{1,29},{... | collective-permute-start | bytes 1572872 | tf_op jit(solution)/shard_map/ppermute | solution.py:150
  168.7 4.8 %copy-start = (bf16[32,64,128]{2,1,0:T(8,128)(2,1)S(1)}, bf16[32,64,128]{2,1,0:T(8,128)(2,1)}, u32[]{:S(2)}) copy-start(bf16[32,64,128]{2,1,0:T(8,128)(2,1)} %pick_tiles.8.refs_0_) | copy-start | bytes 1572868
  192.0 1.6 collective-permute-start.8
  192.0 3.1 %collective-permute-start.7 = (f32[8,64,128]{2,1,0:T(8,128)S(1)}, f32[8,64,128]{2,1,0:T(8,128)S(1)}, u32[]{:S(2)}, u32[]{:S(2)}) collective-permute-start(f32[8,64,128]{2,1,0:T(8,128)S(1)} %get-tuple-element.14), channel_id=1, source_target_pairs={{0,1},{1,0},{2,3},{3,2},{4,5},{5,4},{6,7},{7,6},{8,9},{9,8},{10,11... | collective-permute-start | bytes 786440 | tf_op jit(solution)/shard_map/ppermute | solution.py:185
  193.6 8.4 %collective-permute-start.9 = (f32[8,64,128]{2,1,0:T(8,128)S(1)}, f32[8,64,128]{2,1,0:T(8,128)S(1)}, u32[]{:S(2)}, u32[]{:S(2)}) collective-permute-start(f32[8,64,128]{2,1,0:T(8,128)S(1)} %add.86), channel_id=1, source_target_pairs={{0,2},{1,3},{2,0},{3,1},{4,6},{5,7},{6,4},{7,5},{8,10},{9,11},{10,... | collective-permute-start | bytes 786440 | tf_op jit(solution)/shard_map/ppermute | solution.py:185

commit v6 on v5

--- a/solution.py
+++ b/solution.py
@@ -25,34 +25,51 @@
     return jnp.bitwise_xor(virt_irreps[first], virt_irreps[second])
 
 
-def pick_kernel(step, per, local_tiles, me, wanted, amp, out, sem):
-    peer = me[0] ^ step
+def stage_kernel(source, held, sem):
+    copy = pltpu.make_async_copy(source, held, sem)
+    copy.start()
+    copy.wait()
+
+
+def stage(x):
+    return pl.pallas_call(
+        stage_kernel,
+        out_shape=pltpu.VMEM(x.shape, x.dtype),
+        in_specs=[ANY_SPEC],
+        out_specs=VMEM_SPEC,
+        scratch_shapes=[pltpu.SemaphoreType.DMA],
+        compiler_params=pltpu.CompilerParams(vmem_limit_bytes=8 * MIB),
+        cost_estimate=pl.CostEstimate(flops=0, bytes_accessed=2 * x.size, transcendentals=0),
+        name="stage_amplitudes",
+    )(pltpu.with_memory_space_constraint(x, pltpu.HBM))
+
+
+def pick_kernel(per, local_tiles, me, rows, amp, *refs):
+    out = refs[-1]
+    base = me[0] * per
     origin = me[0] * local_tiles
 
-    def start(i, carry):
-        lane = pl.multiple_of((wanted[peer, i] - origin) * BLK, BLK)
-        pltpu.make_async_copy(amp.at[:, pl.ds(lane, BLK)], out.at[i], sem).start()
+    def step(i, carry):
+        lane = pl.multiple_of((rows[base + i] - origin) * BLK, BLK)
+        out[i] = amp[:, pl.ds(lane, BLK)]
         return carry
 
-    lax.fori_loop(0, per, start, 0, unroll=8)
-    pltpu.make_async_copy(out, out, sem).wait()
-
-
-def pick(step, me, wanted, amp):
+    lax.fori_loop(0, per, step, 0, unroll=8)
+
+
+def pick(me, rows, amp, per, after=()):
     occupied, width = amp.shape
-    peers, per = wanted.shape
     return pl.pallas_call(
-        functools.partial(pick_kernel, step, per, width // BLK),
-        out_shape=pltpu.HBM((per, occupied, BLK), amp.dtype),
-        in_specs=[SMEM_SPEC, SMEM_SPEC, ANY_SPEC],
-        out_specs=pl.BlockSpec(memory_space=pltpu.HBM),
-        scratch_shapes=[pltpu.SemaphoreType.DMA],
-        compiler_params=pltpu.CompilerParams(vmem_limit_bytes=MIB),
+        functools.partial(pick_kernel, per, width // BLK),
+        out_shape=jax.ShapeDtypeStruct((per, occupied, BLK), amp.dtype),
+        in_specs=[SMEM_SPEC, SMEM_SPEC, VMEM_SPEC] + [ANY_SPEC] * len(after),
+        out_specs=VMEM_SPEC,
+        compiler_params=pltpu.CompilerParams(vmem_limit_bytes=8 * MIB),
         cost_estimate=pl.CostEstimate(
             flops=0, bytes_accessed=4 * per * occupied * BLK, transcendentals=0
         ),
         name="pick_tiles",
-    )(me, wanted, pltpu.with_memory_space_constraint(amp, pltpu.HBM))
+    )(me, rows, amp, *after)
 
 
 def add_products(per, base, cols, live, piece, weights, total):
@@ -149,11 +166,13 @@
     def swap(x, k):
         return lax.ppermute(x, "gx", [(i, i ^ k) for i in range(peers)])
 
-    wanted = lax.all_to_all(tile_rows.reshape(peers, per), "gx", 0, 0)
+    rows = [tile_rows] + [swap(tile_rows, k) for k in range(1, peers)]
+    amp = stage(amplitudes)
     here = me.reshape(1)
-    arrived = {0: pick(0, here, wanted, amplitudes)}
+    arrived = {0: pick(here, tile_rows, amp, per)}
     for k in range(1, peers):
-        arrived[k] = swap(pick(k, here, wanted, amplitudes), k)
+        after = [rows[j] for j in range(1, peers) if j != k] if k >= near else ()
+        arrived[k] = swap(pick(here, rows[k], amp, per, after), k)
 
     row_tile = mine * row_count + tile_rows
     col_tile = me * ABT_X + tile_cols

time: 204 us -> 122 us (0.60)
  Pallas kernels: 154 us -> 24.9 us
  waiting for transfers between devices: 23.1 us -> 64.5 us
  starting transfers between devices: 17.9 us -> 22.6 us
    pallas_call x8 -> x9, Pallas kernels: 141 us -> 11.1 us  [the longest x8 8.9 us: pick(): pl.pallas_call(functools.partial(pick_kernel, per, width // BLK), out_sha...]
    ppermute x7 -> x14, waiting for transfers between devices: 10.3 us -> 56.6 us  [swap(): return lax.ppermute(x, 'gx', [(i, i ^ k) for i in range(peers)])]
    ppermute x7 -> x14, starting transfers between devices: 9.53 us -> 20.4 us  [swap(): return lax.ppermute(x, 'gx', [(i, i ^ k) for i in range(peers)])]
    all_to_all x1 -> x0, starting transfers between devices: 6.28 us -> none  [per_device(): wanted = lax.all_to_all(tile_rows.reshape(peers, per), 'gx', 0, 0)]
    all_to_all x1 -> x0, waiting for transfers between devices: 4.91 us -> none  [per_device(): wanted = lax.all_to_all(tile_rows.reshape(peers, per), 'gx', 0, 0)]
    unnamed x8 -> x10, local copies, waits for them, and re-layouts: 0.02 us -> 2.2 us
  transfers between devices with their start and end apart: 11 -> 17, of which waited for: 4 -> 9; matrix products, arithmetic and copies ran while one was open for 3% -> 5% of each run, Pallas kernels for 67% -> 19%
where the time goes in v6:
time: 122 us; the launch traced here: 121 us
  waiting for transfers between devices  64.5 us (53%)
  Pallas kernels  24.9 us (20%)
  starting transfers between devices  22.6 us (19%)
  other arithmetic  5.85 us (5%)
  local copies, waits for them, and re-layouts  2.87 us (2%)
    ppermute x14, waiting for transfers between devices, swap(): return lax.ppermute(x, 'gx', [(i, i ^ k) for i in range(peers)])  56.6 us
    ppermute x14, starting transfers between devices, swap(): return lax.ppermute(x, 'gx', [(i, i ^ k) for i in range(peers)])  20.4 us
    pallas_call x5, Pallas kernels, ladder(): pl.pallas_call(functools.partial(ladder_kernel, peers_at, list(ahead), pe...  13.8 us
    pallas_call x8, Pallas kernels, pick(): pl.pallas_call(functools.partial(pick_kernel, per, width // BLK), out_sha...  8.9 us
    ppermute x3, waiting for transfers between devices, swap_gy(): return lax.ppermute(x, 'gy', [(i, i ^ k) for i in range(groups)])  7.88 us
    convert_element_type x1, other arithmetic, per_device(): (pair_irrep(row_tile, virt_irreps) == pair_irrep(col_tile, virt_irreps))....  5.05 us
  transfers between devices with their start and end apart: 17, of which 9 were waited for; matrix products, arithmetic and copies ran while one was open for 5% of the time, Pallas kernels for 19%

profile of v6, /device:TPU:8, one launch (start us, length us, event | category | flops | bytes accessed | tf_op | source)
XLA Modules:
  0.0 120.9 jit_solution(12707429116717515693)
XLA Ops:
  0.0 2.6 %collective-permute-start.7 = (s32[256]{0:T(256)}, s32[256]{0:T(256)S(1)}, u32[]{:S(2)}, u32[]{:S(2)}) collective-permute-start(s32[256]{0:T(256)} %rows.1), channel_id=1, source_target_pairs={{0,16},{4,20},{8,24},{12,28},{16,0},{20,4},{24,8},{28,12},{1,17},{... | collective-permute-start | bytes 3080 | tf_op jit(solution)/shard_map/ppermute | solution.py:167
  2.6 1.3 %collective-permute-start.6 = (s32[256]{0:T(256)}, s32[256]{0:T(256)S(1)}, u32[]{:S(2)}, u32[]{:S(2)}) collective-permute-start(s32[256]{0:T(256)} %rows.1), channel_id=1, source_target_pairs={{0,20},{4,16},{8,28},{12,24},{16,4},{20,0},{24,12},{28,8},{1,21},{... | collective-permute-start | bytes 3080 | tf_op jit(solution)/shard_map/ppermute | solution.py:167
  3.9 0.1 collective-permute-start.4
  4.0 1.9 %collective-permute-start.2 = (s32[256]{0:T(256)}, s32[256]{0:T(256)S(1)}, u32[]{:S(2)}, u32[]{:S(2)}) collective-permute-start(s32[256]{0:T(256)} %rows.1), channel_id=1, source_target_pairs={{0,8},{4,12},{8,0},{12,4},{16,24},{20,28},{24,16},{28,20},{1,9},{5... | collective-permute-start | bytes 3080 | tf_op jit(solution)/shard_map/ppermute | solution.py:167
  5.9 1.5 %collective-permute-start = (s32[256]{0:T(256)}, s32[256]{0:T(256)S(1)}, u32[]{:S(2)}, u32[]{:S(2)}) collective-permute-start(s32[256]{0:T(256)} %rows.1), channel_id=1, source_target_pairs={{0,4},{4,0},{8,12},{12,8},{16,20},{20,16},{24,28},{28,24},{1,5},{5... | collective-permute-start | bytes 3080 | tf_op jit(solution)/shard_map/ppermute | solution.py:167
  7.4 1.5 %collective-permute-start.9 = (s32[256]{0:T(256)}, s32[256]{0:T(256)S(1)}, u32[]{:S(2)}, u32[]{:S(2)}) collective-permute-start(s32[256]{0:T(256)} %rows.1), channel_id=1, source_target_pairs={{0,28},{4,24},{8,20},{12,16},{16,12},{20,8},{24,4},{28,0},{1,29},{... | collective-permute-start | bytes 3080 | tf_op jit(solution)/shard_map/ppermute | solution.py:167
  8.9 0.0 collective-permute-done.6.rows.refs_3_.refs_4_
  8.9 0.5 collective-permute-start.8
  9.3 2.2 %stage_amplitudes.1.amp = bf16[64,32768]{1,0:T(8,128)(2,1)S(1)} custom-call(bf16[64,32768]{1,0:T(8,128)(2,1)} %source.1), custom_call_target="tpu_custom_call" | custom-call | bytes 4194304 | tf_op jit(solution)/shard_map/stage_amplitudes/pallas_call | solution.py:35
  11.6 0.0 collective-permute-done.rows.refs_0_
  11.6 0.5 collective-permute-done.9.refs_5_.rows
  12.1 0.6 collective-permute-done.8.refs_4_.refs_5_.rows
  12.7 0.7 pick_tiles.12
  13.4 4.4 %collective-permute-start.10 = (bf16[32,64,128]{2,1,0:T(8,128)(2,1)S(1)}, bf16[32,64,128]{2,1,0:T(8,128)(2,1)S(1)}, u32[]{:S(2)}, u32[]{:S(2)}) collective-permute-start(bf16[32,64,128]{2,1,0:T(8,128)(2,1)S(1)} %pick_tiles.12), channel_id=1, source_target_pairs={{0,20},{4,16},{8,28},{12,24},{16,4},{20,0},{24,12},{28,8},{1,21},{... | collective-permute-start | bytes 1572872 | tf_op jit(solution)/shard_map/ppermute | solution.py:167
  17.8 0.7 pick_tiles.13
  18.5 0.1 collective-permute-start.11
  18.6 0.7 fusion.4
  19.2 1.5 %pick_tiles.9 = bf16[32,64,128]{2,1,0:T(8,128)(2,1)} custom-call(s32[1]{0:T(128)} %bitcast.9.me, s32[256]{0:T(256)S(1)} %collective-permute-done.rows.refs_0_, bf16[64,32768]{1,0:T(8,128)(2,1)S(1)} %stage_amplitudes.1.amp), custom_call_target="tpu_custom_call" | custom-call | bytes 1048576 | tf_op jit(solution)/shard_map/pick_tiles/pallas_call | solution.py:62
  20.8 0.9 collective-permute-start.1
  21.7 1.5 %pick_tiles.10 = bf16[32,64,128]{2,1,0:T(8,128)(2,1)} custom-call(s32[1]{0:T(128)} %bitcast.9.me, s32[256]{0:T(256)S(1)} %collective-permute-done.2.rows.refs_1_, bf16[64,32768]{1,0:T(8,128)(2,1)S(1)} %stage_amplitudes.1.amp), custom_call_target="tpu_custom_call" | custom-call | bytes 1048576 | tf_op jit(solution)/shard_map/pick_tiles/pallas_call | solution.py:62
  23.2 3.4 %collective-permute-start.3 = (bf16[32,64,128]{2,1,0:T(8,128)(2,1)}, bf16[32,64,128]{2,1,0:T(8,128)(2,1)S(1)}, u32[]{:S(2)}, u32[]{:S(2)}) collective-permute-start(bf16[32,64,128]{2,1,0:T(8,128)(2,1)} %pick_tiles.10), channel_id=1, source_target_pairs={{0,8},{4,12},{8,0},{12,4},{16,24},{20,28},{24,16},{28,20},{1,9},{5... | collective-permute-start | bytes 1572872 | tf_op jit(solution)/shard_map/ppermute | solution.py:167
  26.6 1.5 %pick_tiles.11 = bf16[32,64,128]{2,1,0:T(8,128)(2,1)} custom-call(s32[1]{0:T(128)} %bitcast.9.me, s32[256]{0:T(256)S(1)} %collective-permute-done.4.rows.refs_2_, bf16[64,32768]{1,0:T(8,128)(2,1)S(1)} %stage_amplitudes.1.amp), custom_call_target="tpu_custom_call" | custom-call | bytes 1048576 | tf_op jit(solution)/shard_map/pick_tiles/pallas_call | solution.py:62
  28.1 1.0 collective-permute-start.5
  29.1 1.5 %pick_tiles.15 = bf16[32,64,128]{2,1,0:T(8,128)(2,1)} custom-call(s32[1]{0:T(128)} %bitcast.9.me, s32[256]{0:T(256)S(1)} %collective-permute-done.8.refs_4_.refs_5_.rows, bf16[64,32768]{1,0:T(8,128)(2,1)S(1)} %stage_amplitudes.1.amp, s32[256]{0:T(256)S(1)} %collective-permute-done.rows.refs_0_, s32[256]{0:T(256)S(1)} %collective-permute-done.2.rows.refs_1_, ...), custom_call_target="tpu_custom_call" | custom-call | bytes 1048576 | tf_op jit(solution)/shard_map/pick_tiles/pallas_call | solution.py:62
  30.6 0.7 pick_tiles.14
  31.3 17.4 %collective-permute-done.10.refs_0_ = bf16[32,64,128]{2,1,0:T(8,128)(2,1)S(1)} collective-permute-done((bf16[32,64,128]{2,1,0:T(8,128)(2,1)S(1)}, bf16[32,64,128]{2,1,0:T(8,128)(2,1)S(1)}, u32[]{:S(2)}, u32[]{:S(2)}) %collective-permute-start.10) | collective-permute-done | bytes 524320 | tf_op jit(solution)/shard_map/ppermute | solution.py:167
  48.7 1.2 collective-permute-start.12
  49.9 13.2 %collective-permute-done.11.refs_0_ = bf16[32,64,128]{2,1,0:T(8,128)(2,1)S(1)} collective-permute-done((bf16[32,64,128]{2,1,0:T(8,128)(2,1)S(1)}, bf16[32,64,128]{2,1,0:T(8,128)(2,1)S(1)}, u32[]{:S(2)}, u32[]{:S(2)}) %collective-permute-start.11) | collective-permute-done | bytes 524320 | tf_op jit(solution)/shard_map/ppermute | solution.py:167
  63.1 0.2 collective-permute-start.13
  63.3 2.2 %copy-done.1 = bf16[64,32768]{1,0:T(8,128)(2,1)S(1)} copy-done((bf16[64,32768]{1,0:T(8,128)(2,1)S(1)}, bf16[64,32768]{1,0:T(8,128)(2,1)}, u32[]{:S(2)}) %copy-start.1) | copy-done | bytes 4194328
  65.5 0.7 pick_tiles.8.refs_0_
  66.3 5.0 %compare_convert_fusion.live = f32[256]{0:T(256)S(1)} fusion(s32[256]{0:T(256)S(1)} %copy-done.4, s32[256]{0:T(256)S(1)} %copy-done.2, s32[]{:T(128)} %bitcast, s32[]{:T(128)} %bitcast.1, s32[]{:T(128)} %bitcast.2, s32[]{:T(128)} %bitcast.3, s32[]{:T(128)} %bitcast.4, s32[]{:T(128)} %bitcast.5, s32[]{:T(128)} %bitcast.6, s32[]{:T(128)} %bitcast.7, ...), kind=kLoop, calls=%fused_computation.34 | loop fusion | flops 44544 | bytes 3112 | tf_op jit(solution)/shard_map/convert_element_type | solution.py:179
  71.3 2.4 %ladder_products.5.refs_1_ = f32[32,64,128]{2,1,0:T(8,128)S(1)} custom-call(s32[8]{0:T(128)S(1)} %iota_xor_fusion.order, s32[256]{0:T(256)S(1)} %fusion.3.cols, f32[256]{0:T(256)S(1)} %compare_convert_fusion.live, bf16[8,32,128,128]{3,2,1,0:T(8,128)(2,1)} %bitcast.16, bf16[32,64,128]{2,1,0:T(8,128)(2,1)S(1)} %collective-permute-done.11.refs_0_), custom_call_target="tpu_custom_call" | custom-call | flops 67108864 | bytes 1048576 | tf_op jit(solution)/shard_map/ladder_products/pallas_call | solution.py:137
  73.7 2.4 %ladder_products.6.refs_4_ = f32[32,64,128]{2,1,0:T(8,128)S(1)} custom-call(s32[8]{0:T(128)S(1)} %iota_xor_fusion.order, s32[256]{0:T(256)S(1)} %fusion.3.cols, f32[256]{0:T(256)S(1)} %compare_convert_fusion.live, bf16[8,32,128,128]{3,2,1,0:T(8,128)(2,1)} %bitcast.17, ...), custom_call_target="tpu_custom_call", output_to_operand_aliasing={{}: (5, {})} | custom-call | flops 67108864 | bytes 1048576 | tf_op jit(solution)/shard_map/ladder_products/pallas_call | solution.py:137
  76.1 0.0 collective-permute-done.1.refs_1_
  76.1 8.0 %collective-permute-done.3.refs_2_ = bf16[32,64,128]{2,1,0:T(8,128)(2,1)S(1)} collective-permute-done((bf16[32,64,128]{2,1,0:T(8,128)(2,1)}, bf16[32,64,128]{2,1,0:T(8,128)(2,1)S(1)}, u32[]{:S(2)}, u32[]{:S(2)}) %collective-permute-start.3) | collective-permute-done | bytes 524320 | tf_op jit(solution)/shard_map/ppermute | solution.py:167
  84.1 6.7 %collective-permute-done.5.refs_3_ = bf16[32,64,128]{2,1,0:T(8,128)(2,1)} collective-permute-done((bf16[32,64,128]{2,1,0:T(8,128)(2,1)}, bf16[32,64,128]{2,1,0:T(8,128)(2,1)}, u32[]{:S(2)}, u32[]{:S(2)}) %collective-permute-start.5) | collective-permute-done | bytes 524320 | tf_op jit(solution)/shard_map/ppermute | solution.py:167
  90.8 4.5 %ladder_products.7 = (f32[32,64,128]{2,1,0:T(8,128)S(1)}, bf16[1,32,128,128]{3,2,1,0:T(8,128)(2,1)S(1)}) custom-call(s32[8]{0:T(128)S(1)} %iota_xor_fusion.order, s32[256]{0:T(256)S(1)} %fusion.3.cols, f32[256]{0:T(256)S(1)} %compare_convert_fusion.live, bf16[8,32,128,128]{3,2,1,0:T(8,128)(2,1)} %bitcast.18, ...), custom_call_target="tpu_custom_call", output_to_operand_aliasing={{0}: (8, {})} | custom-call | flops 268435456 | bytes 5242880 | tf_op jit(solution)/shard_map/ladder_products/pallas_call | solution.py:137
  95.3 10.2 %collective-permute-done.13.refs_0_ = bf16[32,64,128]{2,1,0:T(8,128)(2,1)} collective-permute-done((bf16[32,64,128]{2,1,0:T(8,128)(2,1)}, bf16[32,64,128]{2,1,0:T(8,128)(2,1)}, u32[]{:S(2)}, u32[]{:S(2)}) %collective-permute-start.13) | collective-permute-done | bytes 524320 | tf_op jit(solution)/shard_map/ppermute | solution.py:167
  105.6 2.8 %ladder_products.8.refs_1_ = f32[32,64,128]{2,1,0:T(8,128)S(1)} custom-call(s32[8]{0:T(128)S(1)} %iota_xor_fusion.order, s32[256]{0:T(256)S(1)} %fusion.3.cols, f32[256]{0:T(256)S(1)} %compare_convert_fusion.live, bf16[8,32,128,128]{3,2,1,0:T(8,128)(2,1)} %bitcast.19, ...), custom_call_target="tpu_custom_call", output_to_operand_aliasing={{}: (5, {})} | custom-call | flops 67108864 | bytes 1048576 | tf_op jit(solution)/shard_map/ladder_products/pallas_call | solution.py:137
  108.4 1.7 %ladder_products.9 = (f32[8,64,128]{2,1,0:T(8,128)S(1)}, f32[8,64,128]{2,1,0:T(8,128)S(1)}, f32[8,64,128]{2,1,0:T(8,128)S(1)}, f32[8,64,128]{2,1,0:T(8,128)S(1)}) custom-call(s32[8]{0:T(128)S(1)} %iota_xor_fusion.order, s32[256]{0:T(256)S(1)} %fusion.3.cols, f32[256]{0:T(256)S(1)} %compare_convert_fusion.live, ...), custom_call_target="tpu_custom_call" | custom-call | flops 67108864 | bytes 1048576 | tf_op jit(solution)/shard_map/ladder_products/pallas_call | solution.py:137
  110.1 0.1 collective-permute-start.15
  110.2 0.5 collective-permute-start.14
  110.7 1.0 collective-permute-done.15
  111.8 1.6 %collective-permute-start.16 = (f32[8,64,128]{2,1,0:T(8,128)S(1)}, f32[8,64,128]{2,1,0:T(8,128)S(1)}, u32[]{:S(2)}, u32[]{:S(2)}) collective-permute-start(f32[8,64,128]{2,1,0:T(8,128)S(1)} %add.86), channel_id=1, source_target_pairs={{0,2},{1,3},{2,0},{3,1},{4,6},{5,7},{6,4},{7,5},{8,10},{9,11},{10,... | collective-permute-start | bytes 786440 | tf_op jit(solution)/shard_map/ppermute | solution.py:204
  113.3 0.0 collective-permute-done.14
  113.3 6.9 %collective-permute-done.16 = f32[8,64,128]{2,1,0:T(8,128)S(1)} collective-permute-done((f32[8,64,128]{2,1,0:T(8,128)S(1)}, f32[8,64,128]{2,1,0:T(8,128)S(1)}, u32[]{:S(2)}, u32[]{:S(2)}) %collective-permute-start.16) | collective-permute-done | bytes 262176 | tf_op jit(solution)/shard_map/ppermute | solution.py:204
  120.2 0.7 copy_bitcast_fusion
  (16 shorter events, 0.1 us)
Async XLA Ops:
  0.0 7.4 %collective-permute-start.7 = (s32[256]{0:T(256)}, s32[256]{0:T(256)S(1)}, u32[]{:S(2)}, u32[]{:S(2)}) collective-permute-start(s32[256]{0:T(256)} %rows.1), channel_id=1, source_target_pairs={{0,16},{4,20},{8,24},{12,28},{16,0},{20,4},{24,8},{28,12},{1,17},{... | collective-permute-start | bytes 3080 | tf_op jit(solution)/shard_map/ppermute | solution.py:167
  2.6 6.3 %collective-permute-start.6 = (s32[256]{0:T(256)}, s32[256]{0:T(256)S(1)}, u32[]{:S(2)}, u32[]{:S(2)}) collective-permute-start(s32[256]{0:T(256)} %rows.1), channel_id=1, source_target_pairs={{0,20},{4,16},{8,28},{12,24},{16,4},{20,0},{24,12},{28,8},{1,21},{... | collective-permute-start | bytes 3080 | tf_op jit(solution)/shard_map/ppermute | solution.py:167
  3.9 7.7 %collective-permute-start.4 = (s32[256]{0:T(256)}, s32[256]{0:T(256)S(1)}, u32[]{:S(2)}, u32[]{:S(2)}) collective-permute-start(s32[256]{0:T(256)} %rows.1), channel_id=1, source_target_pairs={{0,12},{4,8},{8,4},{12,0},{16,28},{20,24},{24,20},{28,16},{1,13},{... | collective-permute-start | bytes 3080 | tf_op jit(solution)/shard_map/ppermute | solution.py:167
  4.0 7.6 %collective-permute-start.2 = (s32[256]{0:T(256)}, s32[256]{0:T(256)S(1)}, u32[]{:S(2)}, u32[]{:S(2)}) collective-permute-start(s32[256]{0:T(256)} %rows.1), channel_id=1, source_target_pairs={{0,8},{4,12},{8,0},{12,4},{16,24},{20,28},{24,16},{28,20},{1,9},{5... | collective-permute-start | bytes 3080 | tf_op jit(solution)/shard_map/ppermute | solution.py:167
  5.9 5.7 %collective-permute-start = (s32[256]{0:T(256)}, s32[256]{0:T(256)S(1)}, u32[]{:S(2)}, u32[]{:S(2)}) collective-permute-start(s32[256]{0:T(256)} %rows.1), channel_id=1, source_target_pairs={{0,4},{4,0},{8,12},{12,8},{16,20},{20,16},{24,28},{28,24},{1,5},{5... | collective-permute-start | bytes 3080 | tf_op jit(solution)/shard_map/ppermute | solution.py:167
  7.4 4.7 %collective-permute-start.9 = (s32[256]{0:T(256)}, s32[256]{0:T(256)S(1)}, u32[]{:S(2)}, u32[]{:S(2)}) collective-permute-start(s32[256]{0:T(256)} %rows.1), channel_id=1, source_target_pairs={{0,28},{4,24},{8,20},{12,16},{16,12},{20,8},{24,4},{28,0},{1,29},{... | collective-permute-start | bytes 3080 | tf_op jit(solution)/shard_map/ppermute | solution.py:167
  8.9 3.8 %collective-permute-start.8 = (s32[256]{0:T(256)}, s32[256]{0:T(256)S(1)}, u32[]{:S(2)}, u32[]{:S(2)}) collective-permute-start(s32[256]{0:T(256)} %rows.1), channel_id=1, source_target_pairs={{0,24},{4,28},{8,16},{12,20},{16,8},{20,12},{24,0},{28,4},{1,25},{... | collective-permute-start | bytes 3080 | tf_op jit(solution)/shard_map/ppermute | solution.py:167
  11.6 19.0 %copy-start = (bf16[64,32768]{1,0:T(8,128)(2,1)}, bf16[64,32768]{1,0:T(8,128)(2,1)S(1)}, u32[]{:S(2)}) copy-start(bf16[64,32768]{1,0:T(8,128)(2,1)S(1)} %stage_amplitudes.1.amp) | copy-start | bytes 12582916
  12.7 5.9 %copy-start.3 = (s32[8]{0:T(128)S(1)}, s32[8]{0:T(128)}, u32[]{:S(2)}) copy-start(s32[8]{0:T(128)} %param.6) | copy-start | bytes 100
  13.4 35.3 %collective-permute-start.10 = (bf16[32,64,128]{2,1,0:T(8,128)(2,1)S(1)}, bf16[32,64,128]{2,1,0:T(8,128)(2,1)S(1)}, u32[]{:S(2)}, u32[]{:S(2)}) collective-permute-start(bf16[32,64,128]{2,1,0:T(8,128)(2,1)S(1)} %pick_tiles.12), channel_id=1, source_target_pairs={{0,20},{4,16},{8,28},{12,24},{16,4},{20,0},{24,12},{28,8},{1,21},{... | collective-permute-start | bytes 1572872 | tf_op jit(solution)/shard_map/ppermute | solution.py:167
  18.5 44.6 %collective-permute-start.11 = (bf16[32,64,128]{2,1,0:T(8,128)(2,1)S(1)}, bf16[32,64,128]{2,1,0:T(8,128)(2,1)S(1)}, u32[]{:S(2)}, u32[]{:S(2)}) collective-permute-start(bf16[32,64,128]{2,1,0:T(8,128)(2,1)S(1)} %pick_tiles.13), channel_id=1, source_target_pairs={{0,16},{4,20},{8,24},{12,28},{16,0},{20,4},{24,8},{28,12},{1,17},{... | collective-permute-start | bytes 1572872 | tf_op jit(solution)/shard_map/ppermute | solution.py:167
  20.8 55.3 %collective-permute-start.1 = (bf16[32,64,128]{2,1,0:T(8,128)(2,1)}, bf16[32,64,128]{2,1,0:T(8,128)(2,1)S(1)}, u32[]{:S(2)}, u32[]{:S(2)}) collective-permute-start(bf16[32,64,128]{2,1,0:T(8,128)(2,1)} %pick_tiles.9), channel_id=1, source_target_pairs={{0,4},{4,0},{8,12},{12,8},{16,20},{20,16},{24,28},{28,24},{1,5},{5... | collective-permute-start | bytes 1572872 | tf_op jit(solution)/shard_map/ppermute | solution.py:167
  23.2 60.9 %collective-permute-start.3 = (bf16[32,64,128]{2,1,0:T(8,128)(2,1)}, bf16[32,64,128]{2,1,0:T(8,128)(2,1)S(1)}, u32[]{:S(2)}, u32[]{:S(2)}) collective-permute-start(bf16[32,64,128]{2,1,0:T(8,128)(2,1)} %pick_tiles.10), channel_id=1, source_target_pairs={{0,8},{4,12},{8,0},{12,4},{16,24},{20,28},{24,16},{28,20},{1,9},{5... | collective-permute-start | bytes 1572872 | tf_op jit(solution)/shard_map/ppermute | solution.py:167
  28.1 35.2 %copy-start.2 = (s32[256]{0:T(256)S(1)}, s32[256]{0:T(256)}, u32[]{:S(2)}) copy-start(s32[256]{0:T(256)} %rows.1) | copy-start | bytes 3076
  28.1 62.6 %collective-permute-start.5 = (bf16[32,64,128]{2,1,0:T(8,128)(2,1)}, bf16[32,64,128]{2,1,0:T(8,128)(2,1)}, u32[]{:S(2)}, u32[]{:S(2)}) collective-permute-start(bf16[32,64,128]{2,1,0:T(8,128)(2,1)} %pick_tiles.11), channel_id=1, source_target_pairs={{0,12},{4,8},{8,4},{12,0},{16,28},{20,24},{24,20},{28,16},{1,13},{... | collective-permute-start | bytes 1572872 | tf_op jit(solution)/shard_map/ppermute | solution.py:167
  30.6 35.6 %copy-start.4 = (s32[256]{0:T(256)S(1)}, s32[256]{0:T(256)}, u32[]{:S(2)}) copy-start(s32[256]{0:T(256)} %param.9) | copy-start | bytes 3076
  48.7 59.7 %collective-permute-start.12 = (bf16[32,64,128]{2,1,0:T(8,128)(2,1)S(1)}, bf16[32,64,128]{2,1,0:T(8,128)(2,1)}, u32[]{:S(2)}, u32[]{:S(2)}) collective-permute-start(bf16[32,64,128]{2,1,0:T(8,128)(2,1)S(1)} %pick_tiles.14), channel_id=1, source_target_pairs={{0,28},{4,24},{8,20},{12,16},{16,12},{20,8},{24,4},{28,0},{1,29},{... | collective-permute-start | bytes 1572872 | tf_op jit(solution)/shard_map/ppermute | solution.py:167
  63.1 42.5 %collective-permute-start.13 = (bf16[32,64,128]{2,1,0:T(8,128)(2,1)}, bf16[32,64,128]{2,1,0:T(8,128)(2,1)}, u32[]{:S(2)}, u32[]{:S(2)}) collective-permute-start(bf16[32,64,128]{2,1,0:T(8,128)(2,1)} %pick_tiles.15), channel_id=1, source_target_pairs={{0,24},{4,28},{8,16},{12,20},{16,8},{20,12},{24,0},{28,4},{1,25},{... | collective-permute-start | bytes 1572872 | tf_op jit(solution)/shard_map/ppermute | solution.py:167
  63.3 2.2 %copy-start.1 = (bf16[64,32768]{1,0:T(8,128)(2,1)S(1)}, bf16[64,32768]{1,0:T(8,128)(2,1)}, u32[]{:S(2)}) copy-start(bf16[64,32768]{1,0:T(8,128)(2,1)} %copy-done) | copy-start | bytes 12582916
  110.1 1.6 %collective-permute-start.15 = (f32[8,64,128]{2,1,0:T(8,128)S(1)}, f32[8,64,128]{2,1,0:T(8,128)S(1)}, u32[]{:S(2)}, u32[]{:S(2)}) collective-permute-start(f32[8,64,128]{2,1,0:T(8,128)S(1)} %get-tuple-element.16), channel_id=1, source_target_pairs={{0,1},{1,0},{2,3},{3,2},{4,5},{5,4},{6,7},{7,6},{8,9},{9,8},{10,11... | collective-permute-start | bytes 786440 | tf_op jit(solution)/shard_map/ppermute | solution.py:204
  110.2 3.1 %collective-permute-start.14 = (f32[8,64,128]{2,1,0:T(8,128)S(1)}, f32[8,64,128]{2,1,0:T(8,128)S(1)}, u32[]{:S(2)}, u32[]{:S(2)}) collective-permute-start(f32[8,64,128]{2,1,0:T(8,128)S(1)} %get-tuple-element.14), channel_id=1, source_target_pairs={{0,1},{1,0},{2,3},{3,2},{4,5},{5,4},{6,7},{7,6},{8,9},{9,8},{10,11... | collective-permute-start | bytes 786440 | tf_op jit(solution)/shard_map/ppermute | solution.py:204
  111.8 8.4 %collective-permute-start.16 = (f32[8,64,128]{2,1,0:T(8,128)S(1)}, f32[8,64,128]{2,1,0:T(8,128)S(1)}, u32[]{:S(2)}, u32[]{:S(2)}) collective-permute-start(f32[8,64,128]{2,1,0:T(8,128)S(1)} %add.86), channel_id=1, source_target_pairs={{0,2},{1,3},{2,0},{3,1},{4,6},{5,7},{6,4},{7,5},{8,10},{9,11},{10,... | collective-permute-start | bytes 786440 | tf_op jit(solution)/shard_map/ppermute | solution.py:204

commit v7 on v6

--- a/solution.py
+++ b/solution.py
@@ -44,9 +44,9 @@
     )(pltpu.with_memory_space_constraint(x, pltpu.HBM))
 
 
-def pick_kernel(per, local_tiles, me, rows, amp, *refs):
+def pick_kernel(first, per, local_tiles, me, rows, amp, *refs):
     out = refs[-1]
-    base = me[0] * per
+    base = first + me[0] * per
     origin = me[0] * local_tiles
 
     def step(i, carry):
@@ -57,10 +57,10 @@
     lax.fori_loop(0, per, step, 0, unroll=8)
 
 
-def pick(me, rows, amp, per, after=()):
+def pick(me, rows, first, amp, per, after=()):
     occupied, width = amp.shape
     return pl.pallas_call(
-        functools.partial(pick_kernel, per, width // BLK),
+        functools.partial(pick_kernel, first, per, width // BLK),
         out_shape=jax.ShapeDtypeStruct((per, occupied, BLK), amp.dtype),
         in_specs=[SMEM_SPEC, SMEM_SPEC, VMEM_SPEC] + [ANY_SPEC] * len(after),
         out_specs=VMEM_SPEC,
@@ -166,13 +166,26 @@
     def swap(x, k):
         return lax.ppermute(x, "gx", [(i, i ^ k) for i in range(peers)])
 
-    rows = [tile_rows] + [swap(tile_rows, k) for k in range(1, peers)]
+    slots = tile_rows.shape[0]
+    rows, bit = tile_rows, 1
+    while bit < near:
+        rows = jnp.concatenate([rows, swap(rows, bit)])
+        bit *= 2
+    far_rows = swap(rows, near)
+
     amp = stage(amplitudes)
     here = me.reshape(1)
-    arrived = {0: pick(here, tile_rows, amp, per)}
-    for k in range(1, peers):
-        after = [rows[j] for j in range(1, peers) if j != k] if k >= near else ()
-        arrived[k] = swap(pick(here, rows[k], amp, per, after), k)
+    quarter = near // 4
+    far = [list(range(near + j * quarter, near + (j + 1) * quarter)) for j in range(4)]
+    arrived = {0: pick(here, tile_rows, 0, amp, per)}
+    for k in far[0] + far[1] + list(range(1, near)) + far[2] + far[3]:
+        source, first = (far_rows, (k - near) * slots) if k >= near else (rows, k * slots)
+        after = ()
+        if k in far[2]:
+            after = (arrived[k - quarter],)
+        if k in far[3]:
+            after = (arrived[k - 2 * quarter], arrived[k - 3 * quarter])
+        arrived[k] = swap(pick(here, source, first, amp, per, after), k)
 
     row_tile = mine * row_count + tile_rows
     col_tile = me * ABT_X + tile_cols
@@ -188,8 +201,6 @@
     order = jnp.arange(peers, dtype=jnp.int32) ^ me
 
     w = w_tiles.reshape(peers, per, BLK, BLK)
-    quarter = near // 4
-    far = [list(range(near + j * quarter, near + (j + 1) * quarter)) for j in range(4)]
     args = (order, cols, live, w)
     (total,) = ladder(*args, None, arrived, far[0])
     (total,) = ladder(*args, total, arrived, far[1])

time: 122 us -> 117 us (0.959)
  starting transfers between devices: 22.6 us -> 16.1 us
    ppermute x14 -> x10, starting transfers between devices: 20.4 us -> 14 us  [swap(): return lax.ppermute(x, 'gx', [(i, i ^ k) for i in range(peers)])]
    unnamed x10 -> x12, local copies, waits for them, and re-layouts: 2.2 us -> 2.93 us
    ppermute x14 -> x10, waiting for transfers between devices: 56.6 us -> 56.7 us  [swap(): return lax.ppermute(x, 'gx', [(i, i ^ k) for i in range(peers)])]
  transfers between devices with their start and end apart: 17 -> 13, of which waited for: 9 -> 9; matrix products, arithmetic and copies ran while one was open for 5% -> 5% of each run, Pallas kernels for 19% -> 20%
where the time goes in v7:
time: 117 us; the launch traced here: 116 us
  waiting for transfers between devices  64.6 us (55%)
  Pallas kernels  25.6 us (22%)
  starting transfers between devices  16.1 us (14%)
  other arithmetic  6.27 us (5%)
  local copies, waits for them, and re-layouts  3.61 us (3%)
    ppermute x10, waiting for transfers between devices, swap(): return lax.ppermute(x, 'gx', [(i, i ^ k) for i in range(peers)])  56.7 us
    ppermute x10, starting transfers between devices, swap(): return lax.ppermute(x, 'gx', [(i, i ^ k) for i in range(peers)])  14 us
    pallas_call x5, Pallas kernels, ladder(): pl.pallas_call(functools.partial(ladder_kernel, peers_at, list(ahead), pe...  13.3 us
    pallas_call x8, Pallas kernels, pick(): pl.pallas_call(functools.partial(pick_kernel, first, per, width // BLK),...  10.1 us
    ppermute x3, waiting for transfers between devices, swap_gy(): return lax.ppermute(x, 'gy', [(i, i ^ k) for i in range(groups)])  7.88 us
    convert_element_type x1, other arithmetic, per_device(): (pair_irrep(row_tile, virt_irreps) == pair_irrep(col_tile, virt_irreps))....  4.77 us
    unnamed x12, local copies, waits for them, and re-layouts  2.93 us
  transfers between devices with their start and end apart: 13, of which 9 were waited for; matrix products, arithmetic and copies ran while one was open for 5% of the time, Pallas kernels for 20%

profile of v7, /device:TPU:8, one launch (start us, length us, event | category | flops | bytes accessed | tf_op | source)
XLA Modules:
  0.0 116.3 jit_solution(14177975673033766581)
XLA Ops:
  0.0 1.5 %collective-permute-start = (s32[256]{0:T(256)}, s32[256]{0:T(256)S(1)}, u32[]{:S(2)}, u32[]{:S(2)}) collective-permute-start(s32[256]{0:T(256)} %rows.1), channel_id=1, source_target_pairs={{0,4},{4,0},{8,12},{12,8},{16,20},{20,16},{24,28},{28,24},{1,5},{5... | collective-permute-start | bytes 3080 | tf_op jit(solution)/shard_map/ppermute | solution.py:167
  1.5 0.7 constant_dynamic-update-slice_fusion.2
  2.2 1.5 %collective-permute-done = s32[256]{0:T(256)S(1)} collective-permute-done((s32[256]{0:T(256)}, s32[256]{0:T(256)S(1)}, u32[]{:S(2)}, u32[]{:S(2)}) %collective-permute-start) | collective-permute-done | bytes 1056 | tf_op jit(solution)/shard_map/ppermute | solution.py:167
  3.8 0.7 pad_add_fusion
  4.5 0.0 collective-permute-start.1
  4.5 3.6 %collective-permute-done.1 = s32[512]{0:T(512)S(1)} collective-permute-done((s32[512]{0:T(512)S(1)}, s32[512]{0:T(512)S(1)}, u32[]{:S(2)}, u32[]{:S(2)}) %collective-permute-start.1) | collective-permute-done | bytes 2080 | tf_op jit(solution)/shard_map/ppermute | solution.py:167
  8.1 2.6 %collective-permute-start.5 = (s32[1024]{0:T(1024)S(1)}, s32[1024]{0:T(1024)S(1)}, u32[]{:S(2)}, u32[]{:S(2)}) collective-permute-start(s32[1024]{0:T(1024)S(1)} %constant_dynamic-update-slice_fusion.rows), channel_id=1, source_target_pairs={{0,16},{4,20},{8,24},{12,28},{16,0},{20,4},{24,8},{28,12},{1,17},{... | collective-permute-start | bytes 12296 | tf_op jit(solution)/shard_map/ppermute | solution.py:167
  10.6 2.2 %stage_amplitudes.1.amp = bf16[64,32768]{1,0:T(8,128)(2,1)S(1)} custom-call(bf16[64,32768]{1,0:T(8,128)(2,1)} %source.1), custom_call_target="tpu_custom_call" | custom-call | bytes 4194304 | tf_op jit(solution)/shard_map/stage_amplitudes/pallas_call | solution.py:35
  12.8 0.0 copy-start
  12.9 0.0 collective-permute-done.5.rows
  12.9 0.0 copy-start.3
  12.9 0.8 pick_tiles.12
  13.7 3.3 %collective-permute-start.6 = (bf16[32,64,128]{2,1,0:T(8,128)(2,1)S(1)}, bf16[32,64,128]{2,1,0:T(8,128)(2,1)S(1)}, u32[]{:S(2)}, u32[]{:S(2)}) collective-permute-start(bf16[32,64,128]{2,1,0:T(8,128)(2,1)S(1)} %pick_tiles.12), channel_id=1, source_target_pairs={{0,20},{4,16},{8,28},{12,24},{16,4},{20,0},{24,12},{28,8},{1,21},{... | collective-permute-start | bytes 1572872 | tf_op jit(solution)/shard_map/ppermute | solution.py:167
  16.9 0.8 pick_tiles.13
  17.7 0.7 collective-permute-start.7
  18.4 0.7 fusion.4
  19.1 1.6 %pick_tiles.11 = bf16[32,64,128]{2,1,0:T(8,128)(2,1)} custom-call(s32[1]{0:T(128)} %bitcast.9.me, s32[1024]{0:T(1024)S(1)} %constant_dynamic-update-slice_fusion.rows, bf16[64,32768]{1,0:T(8,128)(2,1)S(1)} %stage_amplitudes.1.amp), custom_call_target="tpu_custom_call" | custom-call | bytes 1048576 | tf_op jit(solution)/shard_map/pick_tiles/pallas_call | solution.py:62
  20.7 1.6 %pick_tiles.10 = bf16[32,64,128]{2,1,0:T(8,128)(2,1)} custom-call(s32[1]{0:T(128)} %bitcast.9.me, s32[1024]{0:T(1024)S(1)} %constant_dynamic-update-slice_fusion.rows, bf16[64,32768]{1,0:T(8,128)(2,1)S(1)} %stage_amplitudes.1.amp), custom_call_target="tpu_custom_call" | custom-call | bytes 1048576 | tf_op jit(solution)/shard_map/pick_tiles/pallas_call | solution.py:62
  22.2 1.6 %pick_tiles.9 = bf16[32,64,128]{2,1,0:T(8,128)(2,1)} custom-call(s32[1]{0:T(128)} %bitcast.9.me, s32[1024]{0:T(1024)S(1)} %constant_dynamic-update-slice_fusion.rows, bf16[64,32768]{1,0:T(8,128)(2,1)S(1)} %stage_amplitudes.1.amp), custom_call_target="tpu_custom_call" | custom-call | bytes 1048576 | tf_op jit(solution)/shard_map/pick_tiles/pallas_call | solution.py:62
  23.8 0.5 collective-permute-start.2
  24.3 0.4 collective-permute-start.3
  24.8 2.5 %collective-permute-start.4 = (bf16[32,64,128]{2,1,0:T(8,128)(2,1)}, bf16[32,64,128]{2,1,0:T(8,128)(2,1)}, u32[]{:S(2)}, u32[]{:S(2)}) collective-permute-start(bf16[32,64,128]{2,1,0:T(8,128)(2,1)} %pick_tiles.11), channel_id=1, source_target_pairs={{0,12},{4,8},{8,4},{12,0},{16,28},{20,24},{24,20},{28,16},{1,13},{... | collective-permute-start | bytes 1572872 | tf_op jit(solution)/shard_map/ppermute | solution.py:167
  27.3 19.9 %collective-permute-done.6.refs_0_ = bf16[32,64,128]{2,1,0:T(8,128)(2,1)S(1)} collective-permute-done((bf16[32,64,128]{2,1,0:T(8,128)(2,1)S(1)}, bf16[32,64,128]{2,1,0:T(8,128)(2,1)S(1)}, u32[]{:S(2)}, u32[]{:S(2)}) %collective-permute-start.6) | collective-permute-done | bytes 524320 | tf_op jit(solution)/shard_map/ppermute | solution.py:167
  47.2 1.6 %pick_tiles.15 = bf16[32,64,128]{2,1,0:T(8,128)(2,1)} custom-call(s32[1]{0:T(128)} %bitcast.9.me, s32[1024]{0:T(1024)S(1)} %collective-permute-done.5.rows, bf16[64,32768]{1,0:T(8,128)(2,1)S(1)} %stage_amplitudes.1.amp, bf16[32,64,128]{2,1,0:T(8,128)(2,1)S(1)} %collective-permute-done.6.refs_0_), custom_call_target="tpu_custom_call" | custom-call | bytes 1048576 | tf_op jit(solution)/shard_map/pick_tiles/pallas_call | solution.py:62
  48.7 1.7 %collective-permute-start.9 = (bf16[32,64,128]{2,1,0:T(8,128)(2,1)}, bf16[32,64,128]{2,1,0:T(8,128)(2,1)}, u32[]{:S(2)}, u32[]{:S(2)}) collective-permute-start(bf16[32,64,128]{2,1,0:T(8,128)(2,1)} %pick_tiles.15), channel_id=1, source_target_pairs={{0,24},{4,28},{8,16},{12,20},{16,8},{20,12},{24,0},{28,4},{1,25},{... | collective-permute-start | bytes 1572872 | tf_op jit(solution)/shard_map/ppermute | solution.py:167
  50.4 12.3 %collective-permute-done.7.refs_0_.refs_1_ = bf16[32,64,128]{2,1,0:T(8,128)(2,1)S(1)} collective-permute-done((bf16[32,64,128]{2,1,0:T(8,128)(2,1)S(1)}, bf16[32,64,128]{2,1,0:T(8,128)(2,1)S(1)}, u32[]{:S(2)}, u32[]{:S(2)}) %collective-permute-start.7) | collective-permute-done | bytes 524320 | tf_op jit(solution)/shard_map/ppermute | solution.py:167
  62.8 1.6 %pick_tiles.14 = bf16[32,64,128]{2,1,0:T(8,128)(2,1)} custom-call(s32[1]{0:T(128)} %bitcast.9.me, s32[1024]{0:T(1024)S(1)} %collective-permute-done.5.rows, bf16[64,32768]{1,0:T(8,128)(2,1)S(1)} %stage_amplitudes.1.amp, bf16[32,64,128]{2,1,0:T(8,128)(2,1)S(1)} %collective-permute-done.6.refs_0_, bf16[32,64,128]{2,1,0:T(8,128)(2,1)S(1)} %collective-permute-done.7.refs_0_.refs_1_), custom_call_target="tpu_custom_call" | custom-call | bytes 1048576 | tf_op jit(solution)/shard_map/pick_tiles/pallas_call | solution.py:62
  64.3 0.7 collective-permute-start.8
  65.0 2.2 %copy-done.1 = bf16[64,32768]{1,0:T(8,128)(2,1)S(1)} copy-done((bf16[64,32768]{1,0:T(8,128)(2,1)S(1)}, bf16[64,32768]{1,0:T(8,128)(2,1)}, u32[]{:S(2)}) %copy-start.1) | copy-done | bytes 4194328
  67.2 0.7 pick_tiles.8.refs_0_
  68.0 4.8 %compare_convert_fusion.live = f32[256]{0:T(256)S(1)} fusion(s32[256]{0:T(256)S(1)} %copy-done.4, s32[256]{0:T(256)S(1)} %copy-done.2, s32[]{:T(128)} %bitcast, s32[]{:T(128)} %bitcast.1, s32[]{:T(128)} %bitcast.2, s32[]{:T(128)} %bitcast.3, s32[]{:T(128)} %bitcast.4, s32[]{:T(128)} %bitcast.5, s32[]{:T(128)} %bitcast.6, s32[]{:T(128)} %bitcast.7, ...), kind=kLoop, calls=%fused_computation.38 | loop fusion | flops 44544 | bytes 3112 | tf_op jit(solution)/shard_map/convert_element_type | solution.py:192
  72.8 2.4 %ladder_products.5.refs_1_ = f32[32,64,128]{2,1,0:T(8,128)S(1)} custom-call(s32[8]{0:T(128)S(1)} %iota_xor_fusion.order, s32[256]{0:T(256)S(1)} %fusion.3.cols, f32[256]{0:T(256)S(1)} %compare_convert_fusion.live, bf16[8,32,128,128]{3,2,1,0:T(8,128)(2,1)} %bitcast.16, bf16[32,64,128]{2,1,0:T(8,128)(2,1)S(1)} %collective-permute-done.7.refs_0_.refs_1_), custom_call_target="tpu_custom_call" | custom-call | flops 67108864 | bytes 1048576 | tf_op jit(solution)/shard_map/ladder_products/pallas_call | solution.py:137
  75.1 2.4 %ladder_products.6.refs_4_ = f32[32,64,128]{2,1,0:T(8,128)S(1)} custom-call(s32[8]{0:T(128)S(1)} %iota_xor_fusion.order, s32[256]{0:T(256)S(1)} %fusion.3.cols, f32[256]{0:T(256)S(1)} %compare_convert_fusion.live, bf16[8,32,128,128]{3,2,1,0:T(8,128)(2,1)} %bitcast.17, ...), custom_call_target="tpu_custom_call", output_to_operand_aliasing={{}: (5, {})} | custom-call | flops 67108864 | bytes 1048576 | tf_op jit(solution)/shard_map/ladder_products/pallas_call | solution.py:137
  77.5 0.0 collective-permute-done.2.refs_1_
  77.5 0.0 collective-permute-done.3.refs_2_
  77.5 4.8 %collective-permute-done.4.refs_3_ = bf16[32,64,128]{2,1,0:T(8,128)(2,1)} collective-permute-done((bf16[32,64,128]{2,1,0:T(8,128)(2,1)}, bf16[32,64,128]{2,1,0:T(8,128)(2,1)}, u32[]{:S(2)}, u32[]{:S(2)}) %collective-permute-start.4) | collective-permute-done | bytes 524320 | tf_op jit(solution)/shard_map/ppermute | solution.py:167
  82.3 4.5 %ladder_products.7 = (f32[32,64,128]{2,1,0:T(8,128)S(1)}, bf16[1,32,128,128]{3,2,1,0:T(8,128)(2,1)S(1)}) custom-call(s32[8]{0:T(128)S(1)} %iota_xor_fusion.order, s32[256]{0:T(256)S(1)} %fusion.3.cols, f32[256]{0:T(256)S(1)} %compare_convert_fusion.live, bf16[8,32,128,128]{3,2,1,0:T(8,128)(2,1)} %bitcast.18, ...), custom_call_target="tpu_custom_call", output_to_operand_aliasing={{0}: (8, {})} | custom-call | flops 268435456 | bytes 5242880 | tf_op jit(solution)/shard_map/ladder_products/pallas_call | solution.py:137
  86.9 7.5 %collective-permute-done.9.refs_0_ = bf16[32,64,128]{2,1,0:T(8,128)(2,1)} collective-permute-done((bf16[32,64,128]{2,1,0:T(8,128)(2,1)}, bf16[32,64,128]{2,1,0:T(8,128)(2,1)}, u32[]{:S(2)}, u32[]{:S(2)}) %collective-permute-start.9) | collective-permute-done | bytes 524320 | tf_op jit(solution)/shard_map/ppermute | solution.py:167
  94.4 2.8 %ladder_products.8.refs_1_ = f32[32,64,128]{2,1,0:T(8,128)S(1)} custom-call(s32[8]{0:T(128)S(1)} %iota_xor_fusion.order, s32[256]{0:T(256)S(1)} %fusion.3.cols, f32[256]{0:T(256)S(1)} %compare_convert_fusion.live, bf16[8,32,128,128]{3,2,1,0:T(8,128)(2,1)} %bitcast.19, ...), custom_call_target="tpu_custom_call", output_to_operand_aliasing={{}: (5, {})} | custom-call | flops 67108864 | bytes 1048576 | tf_op jit(solution)/shard_map/ladder_products/pallas_call | solution.py:137
  97.2 7.1 %collective-permute-done.8.refs_0_ = bf16[32,64,128]{2,1,0:T(8,128)(2,1)S(1)} collective-permute-done((bf16[32,64,128]{2,1,0:T(8,128)(2,1)}, bf16[32,64,128]{2,1,0:T(8,128)(2,1)S(1)}, u32[]{:S(2)}, u32[]{:S(2)}) %collective-permute-start.8) | collective-permute-done | bytes 524320 | tf_op jit(solution)/shard_map/ppermute | solution.py:167
  104.3 1.2 %ladder_products.9 = (f32[8,64,128]{2,1,0:T(8,128)S(1)}, f32[8,64,128]{2,1,0:T(8,128)S(1)}, f32[8,64,128]{2,1,0:T(8,128)S(1)}, f32[8,64,128]{2,1,0:T(8,128)S(1)}) custom-call(s32[8]{0:T(128)S(1)} %iota_xor_fusion.order, s32[256]{0:T(256)S(1)} %fusion.3.cols, f32[256]{0:T(256)S(1)} %compare_convert_fusion.live, ...), custom_call_target="tpu_custom_call" | custom-call | flops 67108864 | bytes 1048576 | tf_op jit(solution)/shard_map/ladder_products/pallas_call | solution.py:137
  105.5 0.1 collective-permute-start.11
  105.6 0.5 collective-permute-start.10
  106.1 1.0 collective-permute-done.11
  107.1 1.6 %collective-permute-start.12 = (f32[8,64,128]{2,1,0:T(8,128)S(1)}, f32[8,64,128]{2,1,0:T(8,128)S(1)}, u32[]{:S(2)}, u32[]{:S(2)}) collective-permute-start(f32[8,64,128]{2,1,0:T(8,128)S(1)} %add.86), channel_id=1, source_target_pairs={{0,2},{1,3},{2,0},{3,1},{4,6},{5,7},{6,4},{7,5},{8,10},{9,11},{10,... | collective-permute-start | bytes 786440 | tf_op jit(solution)/shard_map/ppermute | solution.py:215
  108.7 0.0 collective-permute-done.10
  108.7 6.9 %collective-permute-done.12 = f32[8,64,128]{2,1,0:T(8,128)S(1)} collective-permute-done((f32[8,64,128]{2,1,0:T(8,128)S(1)}, f32[8,64,128]{2,1,0:T(8,128)S(1)}, u32[]{:S(2)}, u32[]{:S(2)}) %collective-permute-start.12) | collective-permute-done | bytes 262176 | tf_op jit(solution)/shard_map/ppermute | solution.py:215
  115.5 0.7 copy_bitcast_fusion
  (13 shorter events, 0.1 us)
Async XLA Ops:
  0.0 3.8 %collective-permute-start = (s32[256]{0:T(256)}, s32[256]{0:T(256)S(1)}, u32[]{:S(2)}, u32[]{:S(2)}) collective-permute-start(s32[256]{0:T(256)} %rows.1), channel_id=1, source_target_pairs={{0,4},{4,0},{8,12},{12,8},{16,20},{20,16},{24,28},{28,24},{1,5},{5... | collective-permute-start | bytes 3080 | tf_op jit(solution)/shard_map/ppermute | solution.py:167
  4.5 3.6 %collective-permute-start.1 = (s32[512]{0:T(512)S(1)}, s32[512]{0:T(512)S(1)}, u32[]{:S(2)}, u32[]{:S(2)}) collective-permute-start(s32[512]{0:T(512)S(1)} %pad_add_fusion), channel_id=1, source_target_pairs={{0,8},{4,12},{8,0},{12,4},{16,24},{20,28},{24,16},{28,20},{1,9},{5... | collective-permute-start | bytes 6152 | tf_op jit(solution)/shard_map/ppermute | solution.py:167
  8.1 4.8 %collective-permute-start.5 = (s32[1024]{0:T(1024)S(1)}, s32[1024]{0:T(1024)S(1)}, u32[]{:S(2)}, u32[]{:S(2)}) collective-permute-start(s32[1024]{0:T(1024)S(1)} %constant_dynamic-update-slice_fusion.rows), channel_id=1, source_target_pairs={{0,16},{4,20},{8,24},{12,28},{16,0},{20,4},{24,8},{28,12},{1,17},{... | collective-permute-start | bytes 12296 | tf_op jit(solution)/shard_map/ppermute | solution.py:167
  12.8 49.9 %copy-start = (bf16[64,32768]{1,0:T(8,128)(2,1)}, bf16[64,32768]{1,0:T(8,128)(2,1)S(1)}, u32[]{:S(2)}) copy-start(bf16[64,32768]{1,0:T(8,128)(2,1)S(1)} %stage_amplitudes.1.amp) | copy-start | bytes 12582916
  12.9 5.6 %copy-start.3 = (s32[8]{0:T(128)S(1)}, s32[8]{0:T(128)}, u32[]{:S(2)}) copy-start(s32[8]{0:T(128)} %param.6) | copy-start | bytes 100
  13.7 33.5 %collective-permute-start.6 = (bf16[32,64,128]{2,1,0:T(8,128)(2,1)S(1)}, bf16[32,64,128]{2,1,0:T(8,128)(2,1)S(1)}, u32[]{:S(2)}, u32[]{:S(2)}) collective-permute-start(bf16[32,64,128]{2,1,0:T(8,128)(2,1)S(1)} %pick_tiles.12), channel_id=1, source_target_pairs={{0,20},{4,16},{8,28},{12,24},{16,4},{20,0},{24,12},{28,8},{1,21},{... | collective-permute-start | bytes 1572872 | tf_op jit(solution)/shard_map/ppermute | solution.py:167
  17.7 45.1 %collective-permute-start.7 = (bf16[32,64,128]{2,1,0:T(8,128)(2,1)S(1)}, bf16[32,64,128]{2,1,0:T(8,128)(2,1)S(1)}, u32[]{:S(2)}, u32[]{:S(2)}) collective-permute-start(bf16[32,64,128]{2,1,0:T(8,128)(2,1)S(1)} %pick_tiles.13), channel_id=1, source_target_pairs={{0,16},{4,20},{8,24},{12,28},{16,0},{20,4},{24,8},{28,12},{1,17},{... | collective-permute-start | bytes 1572872 | tf_op jit(solution)/shard_map/ppermute | solution.py:167
  23.8 53.7 %collective-permute-start.2 = (bf16[32,64,128]{2,1,0:T(8,128)(2,1)}, bf16[32,64,128]{2,1,0:T(8,128)(2,1)S(1)}, u32[]{:S(2)}, u32[]{:S(2)}) collective-permute-start(bf16[32,64,128]{2,1,0:T(8,128)(2,1)} %pick_tiles.9), channel_id=1, source_target_pairs={{0,4},{4,0},{8,12},{12,8},{16,20},{20,16},{24,28},{28,24},{1,5},{5... | collective-permute-start | bytes 1572872 | tf_op jit(solution)/shard_map/ppermute | solution.py:167
  24.3 53.2 %collective-permute-start.3 = (bf16[32,64,128]{2,1,0:T(8,128)(2,1)}, bf16[32,64,128]{2,1,0:T(8,128)(2,1)S(1)}, u32[]{:S(2)}, u32[]{:S(2)}) collective-permute-start(bf16[32,64,128]{2,1,0:T(8,128)(2,1)} %pick_tiles.10), channel_id=1, source_target_pairs={{0,8},{4,12},{8,0},{12,4},{16,24},{20,28},{24,16},{28,20},{1,9},{5... | collective-permute-start | bytes 1572872 | tf_op jit(solution)/shard_map/ppermute | solution.py:167
  24.8 57.5 %collective-permute-start.4 = (bf16[32,64,128]{2,1,0:T(8,128)(2,1)}, bf16[32,64,128]{2,1,0:T(8,128)(2,1)}, u32[]{:S(2)}, u32[]{:S(2)}) collective-permute-start(bf16[32,64,128]{2,1,0:T(8,128)(2,1)} %pick_tiles.11), channel_id=1, source_target_pairs={{0,12},{4,8},{8,4},{12,0},{16,28},{20,24},{24,20},{28,16},{1,13},{... | collective-permute-start | bytes 1572872 | tf_op jit(solution)/shard_map/ppermute | solution.py:167
  48.7 16.3 %copy-start.2 = (s32[256]{0:T(256)S(1)}, s32[256]{0:T(256)}, u32[]{:S(2)}) copy-start(s32[256]{0:T(256)} %rows.1) | copy-start | bytes 3076
  48.7 19.2 %copy-start.4 = (s32[256]{0:T(256)S(1)}, s32[256]{0:T(256)}, u32[]{:S(2)}) copy-start(s32[256]{0:T(256)} %param.9) | copy-start | bytes 3076
  48.7 45.6 %collective-permute-start.9 = (bf16[32,64,128]{2,1,0:T(8,128)(2,1)}, bf16[32,64,128]{2,1,0:T(8,128)(2,1)}, u32[]{:S(2)}, u32[]{:S(2)}) collective-permute-start(bf16[32,64,128]{2,1,0:T(8,128)(2,1)} %pick_tiles.15), channel_id=1, source_target_pairs={{0,24},{4,28},{8,16},{12,20},{16,8},{20,12},{24,0},{28,4},{1,25},{... | collective-permute-start | bytes 1572872 | tf_op jit(solution)/shard_map/ppermute | solution.py:167
  64.3 39.9 %collective-permute-start.8 = (bf16[32,64,128]{2,1,0:T(8,128)(2,1)}, bf16[32,64,128]{2,1,0:T(8,128)(2,1)S(1)}, u32[]{:S(2)}, u32[]{:S(2)}) collective-permute-start(bf16[32,64,128]{2,1,0:T(8,128)(2,1)} %pick_tiles.14), channel_id=1, source_target_pairs={{0,28},{4,24},{8,20},{12,16},{16,12},{20,8},{24,4},{28,0},{1,29},{... | collective-permute-start | bytes 1572872 | tf_op jit(solution)/shard_map/ppermute | solution.py:167
  65.0 2.2 %copy-start.1 = (bf16[64,32768]{1,0:T(8,128)(2,1)S(1)}, bf16[64,32768]{1,0:T(8,128)(2,1)}, u32[]{:S(2)}) copy-start(bf16[64,32768]{1,0:T(8,128)(2,1)} %copy-done) | copy-start | bytes 12582916
  105.5 1.6 %collective-permute-start.11 = (f32[8,64,128]{2,1,0:T(8,128)S(1)}, f32[8,64,128]{2,1,0:T(8,128)S(1)}, u32[]{:S(2)}, u32[]{:S(2)}) collective-permute-start(f32[8,64,128]{2,1,0:T(8,128)S(1)} %get-tuple-element.16), channel_id=1, source_target_pairs={{0,1},{1,0},{2,3},{3,2},{4,5},{5,4},{6,7},{7,6},{8,9},{9,8},{10,11... | collective-permute-start | bytes 786440 | tf_op jit(solution)/shard_map/ppermute | solution.py:215
  105.6 3.1 %collective-permute-start.10 = (f32[8,64,128]{2,1,0:T(8,128)S(1)}, f32[8,64,128]{2,1,0:T(8,128)S(1)}, u32[]{:S(2)}, u32[]{:S(2)}) collective-permute-start(f32[8,64,128]{2,1,0:T(8,128)S(1)} %get-tuple-element.14), channel_id=1, source_target_pairs={{0,1},{1,0},{2,3},{3,2},{4,5},{5,4},{6,7},{7,6},{8,9},{9,8},{10,11... | collective-permute-start | bytes 786440 | tf_op jit(solution)/shard_map/ppermute | solution.py:215
  107.1 8.4 %collective-permute-start.12 = (f32[8,64,128]{2,1,0:T(8,128)S(1)}, f32[8,64,128]{2,1,0:T(8,128)S(1)}, u32[]{:S(2)}, u32[]{:S(2)}) collective-permute-start(f32[8,64,128]{2,1,0:T(8,128)S(1)} %add.86), channel_id=1, source_target_pairs={{0,2},{1,3},{2,0},{3,1},{4,6},{5,7},{6,4},{7,5},{8,10},{9,11},{10,... | collective-permute-start | bytes 786440 | tf_op jit(solution)/shard_map/ppermute | solution.py:215

commit v8 on v7

--- a/solution.py
+++ b/solution.py
@@ -167,25 +167,29 @@
         return lax.ppermute(x, "gx", [(i, i ^ k) for i in range(peers)])
 
     slots = tile_rows.shape[0]
-    rows, bit = tile_rows, 1
+    near_even, bit = tile_rows, 2
     while bit < near:
-        rows = jnp.concatenate([rows, swap(rows, bit)])
+        near_even = jnp.concatenate([near_even, swap(near_even, bit)])
         bit *= 2
-    far_rows = swap(rows, near)
+    far_even = swap(near_even, near)
+    odd = swap(jnp.concatenate([near_even, far_even]), 1)
 
     amp = stage(amplitudes)
     here = me.reshape(1)
     quarter = near // 4
-    far = [list(range(near + j * quarter, near + (j + 1) * quarter)) for j in range(4)]
+    far_order = list(range(near, peers, 2)) + list(range(near + 1, peers, 2))
+    far = [far_order[j * quarter : (j + 1) * quarter] for j in range(4)]
     arrived = {0: pick(here, tile_rows, 0, amp, per)}
     for k in far[0] + far[1] + list(range(1, near)) + far[2] + far[3]:
-        source, first = (far_rows, (k - near) * slots) if k >= near else (rows, k * slots)
+        source, first = (odd, k // 2) if k % 2 else (near_even, k // 2)
+        if k % 2 == 0 and k >= near:
+            source, first = far_even, (k - near) // 2
         after = ()
         if k in far[2]:
-            after = (arrived[k - quarter],)
+            after = (arrived[far[1][far[2].index(k)]],)
         if k in far[3]:
-            after = (arrived[k - 2 * quarter], arrived[k - 3 * quarter])
-        arrived[k] = swap(pick(here, source, first, amp, per, after), k)
+            after = (arrived[far[1][far[3].index(k)]], arrived[far[0][far[3].index(k)]])
+        arrived[k] = swap(pick(here, source, first * slots, amp, per, after), k)
 
     row_tile = mine * row_count + tile_rows
     col_tile = me * ABT_X + tile_cols

time: 117 us -> 114 us (0.974)
  starting transfers between devices: 16.1 us -> 13.4 us
  waiting for transfers between devices: 64.6 us -> 65.9 us
    ppermute x10, starting transfers between devices: 14 us -> 11.3 us  [swap(): return lax.ppermute(x, 'gx', [(i, i ^ k) for i in range(peers)])]
    ppermute x10, waiting for transfers between devices: 56.7 us -> 58 us  [swap(): return lax.ppermute(x, 'gx', [(i, i ^ k) for i in range(peers)])]
    unnamed x12 -> x11, local copies, waits for them, and re-layouts: 2.93 us -> 2.93 us
  transfers between devices with their start and end apart: 13 -> 13, of which waited for: 9 -> 7; matrix products, arithmetic and copies ran while one was open for 5% -> 5% of each run, Pallas kernels for 20% -> 20%
where the time goes in v8:
time: 114 us
  waiting for transfers between devices  65.9 us (58%)
  Pallas kernels  25.1 us (22%)
  starting transfers between devices  13.4 us (12%)
  other arithmetic  5.59 us (5%)
  local copies, waits for them, and re-layouts  3.62 us (3%)
    ppermute x10, waiting for transfers between devices, swap(): return lax.ppermute(x, 'gx', [(i, i ^ k) for i in range(peers)])  58 us
    pallas_call x5, Pallas kernels, ladder(): pl.pallas_call(functools.partial(ladder_kernel, peers_at, list(ahead), pe...  13.8 us
    ppermute x10, starting transfers between devices, swap(): return lax.ppermute(x, 'gx', [(i, i ^ k) for i in range(peers)])  11.3 us
    pallas_call x8, Pallas kernels, pick(): pl.pallas_call(functools.partial(pick_kernel, first, per, width // BLK),...  9.15 us
    ppermute x3, waiting for transfers between devices, swap_gy(): return lax.ppermute(x, 'gy', [(i, i ^ k) for i in range(groups)])  7.88 us
    convert_element_type x1, other arithmetic, per_device(): (pair_irrep(row_tile, virt_irreps) == pair_irrep(col_tile, virt_irreps))....  4.77 us
    unnamed x11, local copies, waits for them, and re-layouts  2.93 us
  transfers between devices with their start and end apart: 13, of which 7 were waited for; matrix products, arithmetic and copies ran while one was open for 5% of the time, Pallas kernels for 20%

profile of v8, /device:TPU:8, one launch (start us, length us, event | category | flops | bytes accessed | tf_op | source)
XLA Modules:
  0.0 113.9 jit_solution(5262813366632948677)
XLA Ops:
  0.0 0.0 collective-permute-start
  0.0 0.7 constant_dynamic-update-slice_fusion.1
  0.7 3.1 %collective-permute-done = s32[256]{0:T(256)S(1)} collective-permute-done((s32[256]{0:T(256)}, s32[256]{0:T(256)S(1)}, u32[]{:S(2)}, u32[]{:S(2)}) %collective-permute-start) | collective-permute-done | bytes 1056 | tf_op jit(solution)/shard_map/ppermute | solution.py:167
  3.8 2.6 %collective-permute-start.1 = (s32[512]{0:T(512)S(1)}, s32[512]{0:T(512)S(1)}, u32[]{:S(2)}, u32[]{:S(2)}) collective-permute-start(s32[512]{0:T(512)S(1)} %constant_dynamic-update-slice_fusion.rows), channel_id=1, source_target_pairs={{0,16},{4,20},{8,24},{12,28},{16,0},{20,4},{24,8},{28,12},{1,17},{... | collective-permute-start | bytes 6152 | tf_op jit(solution)/shard_map/ppermute | solution.py:167
  6.4 2.2 %stage_amplitudes.1.amp = bf16[64,32768]{1,0:T(8,128)(2,1)S(1)} custom-call(bf16[64,32768]{1,0:T(8,128)(2,1)} %source.1), custom_call_target="tpu_custom_call" | custom-call | bytes 4194304 | tf_op jit(solution)/shard_map/stage_amplitudes/pallas_call | solution.py:35
  8.6 0.0 collective-permute-done.1.rows
  8.6 0.0 copy-start.2
  8.6 0.0 copy-start.3
  8.6 0.7 pick_tiles.12
  9.4 1.3 %collective-permute-start.6 = (bf16[32,64,128]{2,1,0:T(8,128)(2,1)S(1)}, bf16[32,64,128]{2,1,0:T(8,128)(2,1)S(1)}, u32[]{:S(2)}, u32[]{:S(2)}) collective-permute-start(bf16[32,64,128]{2,1,0:T(8,128)(2,1)S(1)} %pick_tiles.12), channel_id=1, source_target_pairs={{0,24},{4,28},{8,16},{12,20},{16,8},{20,12},{24,0},{28,4},{1,25},{... | collective-permute-start | bytes 1572872 | tf_op jit(solution)/shard_map/ppermute | solution.py:167
  10.7 0.7 pick_tiles.13
  11.4 1.6 %collective-permute-start.7 = (bf16[32,64,128]{2,1,0:T(8,128)(2,1)S(1)}, bf16[32,64,128]{2,1,0:T(8,128)(2,1)S(1)}, u32[]{:S(2)}, u32[]{:S(2)}) collective-permute-start(bf16[32,64,128]{2,1,0:T(8,128)(2,1)S(1)} %pick_tiles.13), channel_id=1, source_target_pairs={{0,16},{4,20},{8,24},{12,28},{16,0},{20,4},{24,8},{28,12},{1,17},{... | collective-permute-start | bytes 1572872 | tf_op jit(solution)/shard_map/ppermute | solution.py:167
  13.1 1.6 %collective-permute-start.2 = (s32[1024]{0:T(1024)S(1)}, s32[1024]{0:T(1024)S(1)}, u32[]{:S(2)}, u32[]{:S(2)}) collective-permute-start(s32[1024]{0:T(1024)S(1)} %pad_add_fusion), channel_id=1, source_target_pairs={{0,4},{4,0},{8,12},{12,8},{16,20},{20,16},{24,28},{28,24},{1,5},{5... | collective-permute-start | bytes 12296 | tf_op jit(solution)/shard_map/ppermute | solution.py:167
  14.7 0.7 fusion.4
  15.3 0.7 pick_tiles.10
  16.1 1.0 collective-permute-start.4
  17.0 0.0 collective-permute-done.2.rows
  17.1 1.6 %pick_tiles.9 = bf16[32,64,128]{2,1,0:T(8,128)(2,1)} custom-call(s32[1]{0:T(128)} %bitcast.9.me, s32[1024]{0:T(1024)S(1)} %collective-permute-done.2.rows, bf16[64,32768]{1,0:T(8,128)(2,1)S(1)} %stage_amplitudes.1.amp), custom_call_target="tpu_custom_call" | custom-call | bytes 1048576 | tf_op jit(solution)/shard_map/pick_tiles/pallas_call | solution.py:62
  18.6 1.2 %collective-permute-start.3 = (bf16[32,64,128]{2,1,0:T(8,128)(2,1)}, bf16[32,64,128]{2,1,0:T(8,128)(2,1)S(1)}, u32[]{:S(2)}, u32[]{:S(2)}) collective-permute-start(bf16[32,64,128]{2,1,0:T(8,128)(2,1)} %pick_tiles.9), channel_id=1, source_target_pairs={{0,4},{4,0},{8,12},{12,8},{16,20},{20,16},{24,28},{28,24},{1,5},{5... | collective-permute-start | bytes 1572872 | tf_op jit(solution)/shard_map/ppermute | solution.py:167
  19.8 1.6 %pick_tiles.11 = bf16[32,64,128]{2,1,0:T(8,128)(2,1)} custom-call(s32[1]{0:T(128)} %bitcast.9.me, s32[1024]{0:T(1024)S(1)} %collective-permute-done.2.rows, bf16[64,32768]{1,0:T(8,128)(2,1)S(1)} %stage_amplitudes.1.amp), custom_call_target="tpu_custom_call" | custom-call | bytes 1048576 | tf_op jit(solution)/shard_map/pick_tiles/pallas_call | solution.py:62
  21.4 1.4 %collective-permute-start.5 = (bf16[32,64,128]{2,1,0:T(8,128)(2,1)}, bf16[32,64,128]{2,1,0:T(8,128)(2,1)}, u32[]{:S(2)}, u32[]{:S(2)}) collective-permute-start(bf16[32,64,128]{2,1,0:T(8,128)(2,1)} %pick_tiles.11), channel_id=1, source_target_pairs={{0,12},{4,8},{8,4},{12,0},{16,28},{20,24},{24,20},{28,16},{1,13},{... | collective-permute-start | bytes 1572872 | tf_op jit(solution)/shard_map/ppermute | solution.py:167
  22.7 22.3 %collective-permute-done.6.refs_0_ = bf16[32,64,128]{2,1,0:T(8,128)(2,1)S(1)} collective-permute-done((bf16[32,64,128]{2,1,0:T(8,128)(2,1)S(1)}, bf16[32,64,128]{2,1,0:T(8,128)(2,1)S(1)}, u32[]{:S(2)}, u32[]{:S(2)}) %collective-permute-start.6) | collective-permute-done | bytes 524320 | tf_op jit(solution)/shard_map/ppermute | solution.py:167
  45.1 1.6 %pick_tiles.15 = bf16[32,64,128]{2,1,0:T(8,128)(2,1)} custom-call(s32[1]{0:T(128)} %bitcast.9.me, s32[1024]{0:T(1024)S(1)} %collective-permute-done.2.rows, bf16[64,32768]{1,0:T(8,128)(2,1)S(1)} %stage_amplitudes.1.amp, bf16[32,64,128]{2,1,0:T(8,128)(2,1)S(1)} %collective-permute-done.6.refs_0_), custom_call_target="tpu_custom_call" | custom-call | bytes 1048576 | tf_op jit(solution)/shard_map/pick_tiles/pallas_call | solution.py:62
  46.7 0.0 collective-permute-start.9
  46.7 11.8 %collective-permute-done.7.refs_0_.refs_1_ = bf16[32,64,128]{2,1,0:T(8,128)(2,1)S(1)} collective-permute-done((bf16[32,64,128]{2,1,0:T(8,128)(2,1)S(1)}, bf16[32,64,128]{2,1,0:T(8,128)(2,1)S(1)}, u32[]{:S(2)}, u32[]{:S(2)}) %collective-permute-start.7) | collective-permute-done | bytes 524320 | tf_op jit(solution)/shard_map/ppermute | solution.py:167
  58.4 0.0 copy-done
  58.4 1.6 %pick_tiles.14 = bf16[32,64,128]{2,1,0:T(8,128)(2,1)} custom-call(s32[1]{0:T(128)} %bitcast.9.me, s32[1024]{0:T(1024)S(1)} %collective-permute-done.2.rows, bf16[64,32768]{1,0:T(8,128)(2,1)S(1)} %stage_amplitudes.1.amp, bf16[32,64,128]{2,1,0:T(8,128)(2,1)S(1)} %collective-permute-done.6.refs_0_, bf16[32,64,128]{2,1,0:T(8,128)(2,1)S(1)} %collective-permute-done.7.refs_0_.refs_1_), custom_call_target="tpu_custom_call" | custom-call | bytes 1048576 | tf_op jit(solution)/shard_map/pick_tiles/pallas_call | solution.py:62
  60.0 0.6 collective-permute-start.8
  60.6 2.2 %copy-done.1 = bf16[64,32768]{1,0:T(8,128)(2,1)S(1)} copy-done((bf16[64,32768]{1,0:T(8,128)(2,1)S(1)}, bf16[64,32768]{1,0:T(8,128)(2,1)}, u32[]{:S(2)}) %copy-start.1) | copy-done | bytes 4194328
  62.8 0.7 pick_tiles.8.refs_0_
  63.6 4.8 %compare_convert_fusion.live = f32[256]{0:T(256)S(1)} fusion(s32[256]{0:T(256)S(1)} %copy-done.4, s32[256]{0:T(256)S(1)} %copy-done.2, s32[]{:T(128)} %bitcast, s32[]{:T(128)} %bitcast.1, s32[]{:T(128)} %bitcast.2, s32[]{:T(128)} %bitcast.3, s32[]{:T(128)} %bitcast.4, s32[]{:T(128)} %bitcast.5, s32[]{:T(128)} %bitcast.6, s32[]{:T(128)} %bitcast.7, ...), kind=kLoop, calls=%fused_computation.37 | loop fusion | flops 44544 | bytes 3112 | tf_op jit(solution)/shard_map/convert_element_type | solution.py:196
  68.4 2.4 %ladder_products.5.refs_1_ = f32[32,64,128]{2,1,0:T(8,128)S(1)} custom-call(s32[8]{0:T(128)S(1)} %iota_xor_fusion.order, s32[256]{0:T(256)S(1)} %fusion.3.cols, f32[256]{0:T(256)S(1)} %compare_convert_fusion.live, bf16[8,32,128,128]{3,2,1,0:T(8,128)(2,1)} %bitcast.16, bf16[32,64,128]{2,1,0:T(8,128)(2,1)S(1)} %collective-permute-done.7.refs_0_.refs_1_), custom_call_target="tpu_custom_call" | custom-call | flops 67108864 | bytes 1048576 | tf_op jit(solution)/shard_map/ladder_products/pallas_call | solution.py:137
  70.8 2.4 %ladder_products.6.refs_4_ = f32[32,64,128]{2,1,0:T(8,128)S(1)} custom-call(s32[8]{0:T(128)S(1)} %iota_xor_fusion.order, s32[256]{0:T(256)S(1)} %fusion.3.cols, f32[256]{0:T(256)S(1)} %compare_convert_fusion.live, bf16[8,32,128,128]{3,2,1,0:T(8,128)(2,1)} %bitcast.17, ...), custom_call_target="tpu_custom_call", output_to_operand_aliasing={{}: (5, {})} | custom-call | flops 67108864 | bytes 1048576 | tf_op jit(solution)/shard_map/ladder_products/pallas_call | solution.py:137
  73.1 0.0 collective-permute-done.4.refs_2_
  73.1 0.0 collective-permute-done.3.refs_1_
  73.1 0.0 collective-permute-done.5.refs_3_
  73.2 4.6 %ladder_products.7 = (f32[32,64,128]{2,1,0:T(8,128)S(1)}, bf16[1,32,128,128]{3,2,1,0:T(8,128)(2,1)S(1)}) custom-call(s32[8]{0:T(128)S(1)} %iota_xor_fusion.order, s32[256]{0:T(256)S(1)} %fusion.3.cols, f32[256]{0:T(256)S(1)} %compare_convert_fusion.live, bf16[8,32,128,128]{3,2,1,0:T(8,128)(2,1)} %bitcast.18, ...), custom_call_target="tpu_custom_call", output_to_operand_aliasing={{0}: (8, {})} | custom-call | flops 268435456 | bytes 5242880 | tf_op jit(solution)/shard_map/ladder_products/pallas_call | solution.py:137
  77.7 11.5 %collective-permute-done.9.refs_0_ = bf16[32,64,128]{2,1,0:T(8,128)(2,1)} collective-permute-done((bf16[32,64,128]{2,1,0:T(8,128)(2,1)}, bf16[32,64,128]{2,1,0:T(8,128)(2,1)}, u32[]{:S(2)}, u32[]{:S(2)}) %collective-permute-start.9) | collective-permute-done | bytes 524320 | tf_op jit(solution)/shard_map/ppermute | solution.py:167
  89.2 2.8 %ladder_products.8.refs_1_ = f32[32,64,128]{2,1,0:T(8,128)S(1)} custom-call(s32[8]{0:T(128)S(1)} %iota_xor_fusion.order, s32[256]{0:T(256)S(1)} %fusion.3.cols, f32[256]{0:T(256)S(1)} %compare_convert_fusion.live, bf16[8,32,128,128]{3,2,1,0:T(8,128)(2,1)} %bitcast.19, ...), custom_call_target="tpu_custom_call", output_to_operand_aliasing={{}: (5, {})} | custom-call | flops 67108864 | bytes 1048576 | tf_op jit(solution)/shard_map/ladder_products/pallas_call | solution.py:137
  92.0 9.4 %collective-permute-done.8.refs_0_ = bf16[32,64,128]{2,1,0:T(8,128)(2,1)} collective-permute-done((bf16[32,64,128]{2,1,0:T(8,128)(2,1)}, bf16[32,64,128]{2,1,0:T(8,128)(2,1)}, u32[]{:S(2)}, u32[]{:S(2)}) %collective-permute-start.8) | collective-permute-done | bytes 524320 | tf_op jit(solution)/shard_map/ppermute | solution.py:167
  101.4 1.7 %ladder_products.9 = (f32[8,64,128]{2,1,0:T(8,128)S(1)}, f32[8,64,128]{2,1,0:T(8,128)S(1)}, f32[8,64,128]{2,1,0:T(8,128)S(1)}, f32[8,64,128]{2,1,0:T(8,128)S(1)}) custom-call(s32[8]{0:T(128)S(1)} %iota_xor_fusion.order, s32[256]{0:T(256)S(1)} %fusion.3.cols, f32[256]{0:T(256)S(1)} %compare_convert_fusion.live, ...), custom_call_target="tpu_custom_call" | custom-call | flops 67108864 | bytes 1048576 | tf_op jit(solution)/shard_map/ladder_products/pallas_call | solution.py:137
  103.1 0.1 collective-permute-start.11
  103.2 0.5 collective-permute-start.10
  103.7 1.0 collective-permute-done.11
  104.7 1.6 %collective-permute-start.12 = (f32[8,64,128]{2,1,0:T(8,128)S(1)}, f32[8,64,128]{2,1,0:T(8,128)S(1)}, u32[]{:S(2)}, u32[]{:S(2)}) collective-permute-start(f32[8,64,128]{2,1,0:T(8,128)S(1)} %add.86), channel_id=1, source_target_pairs={{0,2},{1,3},{2,0},{3,1},{4,6},{5,7},{6,4},{7,5},{8,10},{9,11},{10,... | collective-permute-start | bytes 786440 | tf_op jit(solution)/shard_map/ppermute | solution.py:219
  106.3 0.0 collective-permute-done.10
  106.3 6.9 %collective-permute-done.12 = f32[8,64,128]{2,1,0:T(8,128)S(1)} collective-permute-done((f32[8,64,128]{2,1,0:T(8,128)S(1)}, f32[8,64,128]{2,1,0:T(8,128)S(1)}, u32[]{:S(2)}, u32[]{:S(2)}) %collective-permute-start.12) | collective-permute-done | bytes 262176 | tf_op jit(solution)/shard_map/ppermute | solution.py:219
  113.2 0.7 copy_bitcast_fusion
  (12 shorter events, 0.1 us)
Async XLA Ops:
  0.0 3.8 %collective-permute-start = (s32[256]{0:T(256)}, s32[256]{0:T(256)S(1)}, u32[]{:S(2)}, u32[]{:S(2)}) collective-permute-start(s32[256]{0:T(256)} %rows.1), channel_id=1, source_target_pairs={{0,8},{4,12},{8,0},{12,4},{16,24},{20,28},{24,16},{28,20},{1,9},{5... | collective-permute-start | bytes 3080 | tf_op jit(solution)/shard_map/ppermute | solution.py:167
  3.8 4.8 %collective-permute-start.1 = (s32[512]{0:T(512)S(1)}, s32[512]{0:T(512)S(1)}, u32[]{:S(2)}, u32[]{:S(2)}) collective-permute-start(s32[512]{0:T(512)S(1)} %constant_dynamic-update-slice_fusion.rows), channel_id=1, source_target_pairs={{0,16},{4,20},{8,24},{12,28},{16,0},{20,4},{24,8},{28,12},{1,17},{... | collective-permute-start | bytes 6152 | tf_op jit(solution)/shard_map/ppermute | solution.py:167
  8.6 49.9 %copy-start = (bf16[64,32768]{1,0:T(8,128)(2,1)}, bf16[64,32768]{1,0:T(8,128)(2,1)S(1)}, u32[]{:S(2)}) copy-start(bf16[64,32768]{1,0:T(8,128)(2,1)S(1)} %stage_amplitudes.1.amp) | copy-start | bytes 12582916
  8.6 4.4 %copy-start.2 = (s32[256]{0:T(256)S(1)}, s32[256]{0:T(256)}, u32[]{:S(2)}) copy-start(s32[256]{0:T(256)} %rows.1) | copy-start | bytes 3076
  8.6 6.0 %copy-start.3 = (s32[8]{0:T(128)S(1)}, s32[8]{0:T(128)}, u32[]{:S(2)}) copy-start(s32[8]{0:T(128)} %param.6) | copy-start | bytes 100
  9.4 35.7 %collective-permute-start.6 = (bf16[32,64,128]{2,1,0:T(8,128)(2,1)S(1)}, bf16[32,64,128]{2,1,0:T(8,128)(2,1)S(1)}, u32[]{:S(2)}, u32[]{:S(2)}) collective-permute-start(bf16[32,64,128]{2,1,0:T(8,128)(2,1)S(1)} %pick_tiles.12), channel_id=1, source_target_pairs={{0,24},{4,28},{8,16},{12,20},{16,8},{20,12},{24,0},{28,4},{1,25},{... | collective-permute-start | bytes 1572872 | tf_op jit(solution)/shard_map/ppermute | solution.py:167
  11.4 47.0 %collective-permute-start.7 = (bf16[32,64,128]{2,1,0:T(8,128)(2,1)S(1)}, bf16[32,64,128]{2,1,0:T(8,128)(2,1)S(1)}, u32[]{:S(2)}, u32[]{:S(2)}) collective-permute-start(bf16[32,64,128]{2,1,0:T(8,128)(2,1)S(1)} %pick_tiles.13), channel_id=1, source_target_pairs={{0,16},{4,20},{8,24},{12,28},{16,0},{20,4},{24,8},{28,12},{1,17},{... | collective-permute-start | bytes 1572872 | tf_op jit(solution)/shard_map/ppermute | solution.py:167
  13.1 4.0 %collective-permute-start.2 = (s32[1024]{0:T(1024)S(1)}, s32[1024]{0:T(1024)S(1)}, u32[]{:S(2)}, u32[]{:S(2)}) collective-permute-start(s32[1024]{0:T(1024)S(1)} %pad_add_fusion), channel_id=1, source_target_pairs={{0,4},{4,0},{8,12},{12,8},{16,20},{20,16},{24,28},{28,24},{1,5},{5... | collective-permute-start | bytes 12296 | tf_op jit(solution)/shard_map/ppermute | solution.py:167
  16.1 57.1 %collective-permute-start.4 = (bf16[32,64,128]{2,1,0:T(8,128)(2,1)S(1)}, bf16[32,64,128]{2,1,0:T(8,128)(2,1)S(1)}, u32[]{:S(2)}, u32[]{:S(2)}) collective-permute-start(bf16[32,64,128]{2,1,0:T(8,128)(2,1)S(1)} %pick_tiles.10), channel_id=1, source_target_pairs={{0,8},{4,12},{8,0},{12,4},{16,24},{20,28},{24,16},{28,20},{1,9},{5... | collective-permute-start | bytes 1572872 | tf_op jit(solution)/shard_map/ppermute | solution.py:167
  18.6 54.5 %collective-permute-start.3 = (bf16[32,64,128]{2,1,0:T(8,128)(2,1)}, bf16[32,64,128]{2,1,0:T(8,128)(2,1)S(1)}, u32[]{:S(2)}, u32[]{:S(2)}) collective-permute-start(bf16[32,64,128]{2,1,0:T(8,128)(2,1)} %pick_tiles.9), channel_id=1, source_target_pairs={{0,4},{4,0},{8,12},{12,8},{16,20},{20,16},{24,28},{28,24},{1,5},{5... | collective-permute-start | bytes 1572872 | tf_op jit(solution)/shard_map/ppermute | solution.py:167
  21.4 51.8 %collective-permute-start.5 = (bf16[32,64,128]{2,1,0:T(8,128)(2,1)}, bf16[32,64,128]{2,1,0:T(8,128)(2,1)}, u32[]{:S(2)}, u32[]{:S(2)}) collective-permute-start(bf16[32,64,128]{2,1,0:T(8,128)(2,1)} %pick_tiles.11), channel_id=1, source_target_pairs={{0,12},{4,8},{8,4},{12,0},{16,28},{20,24},{24,20},{28,16},{1,13},{... | collective-permute-start | bytes 1572872 | tf_op jit(solution)/shard_map/ppermute | solution.py:167
  46.7 16.9 %copy-start.4 = (s32[256]{0:T(256)S(1)}, s32[256]{0:T(256)}, u32[]{:S(2)}) copy-start(s32[256]{0:T(256)} %param.9) | copy-start | bytes 3076
  46.7 42.5 %collective-permute-start.9 = (bf16[32,64,128]{2,1,0:T(8,128)(2,1)}, bf16[32,64,128]{2,1,0:T(8,128)(2,1)}, u32[]{:S(2)}, u32[]{:S(2)}) collective-permute-start(bf16[32,64,128]{2,1,0:T(8,128)(2,1)} %pick_tiles.15), channel_id=1, source_target_pairs={{0,20},{4,16},{8,28},{12,24},{16,4},{20,0},{24,12},{28,8},{1,21},{... | collective-permute-start | bytes 1572872 | tf_op jit(solution)/shard_map/ppermute | solution.py:167
  60.0 41.4 %collective-permute-start.8 = (bf16[32,64,128]{2,1,0:T(8,128)(2,1)}, bf16[32,64,128]{2,1,0:T(8,128)(2,1)}, u32[]{:S(2)}, u32[]{:S(2)}) collective-permute-start(bf16[32,64,128]{2,1,0:T(8,128)(2,1)} %pick_tiles.14), channel_id=1, source_target_pairs={{0,28},{4,24},{8,20},{12,16},{16,12},{20,8},{24,4},{28,0},{1,29},{... | collective-permute-start | bytes 1572872 | tf_op jit(solution)/shard_map/ppermute | solution.py:167
  60.6 2.2 %copy-start.1 = (bf16[64,32768]{1,0:T(8,128)(2,1)S(1)}, bf16[64,32768]{1,0:T(8,128)(2,1)}, u32[]{:S(2)}) copy-start(bf16[64,32768]{1,0:T(8,128)(2,1)} %copy-done) | copy-start | bytes 12582916
  103.1 1.6 %collective-permute-start.11 = (f32[8,64,128]{2,1,0:T(8,128)S(1)}, f32[8,64,128]{2,1,0:T(8,128)S(1)}, u32[]{:S(2)}, u32[]{:S(2)}) collective-permute-start(f32[8,64,128]{2,1,0:T(8,128)S(1)} %get-tuple-element.16), channel_id=1, source_target_pairs={{0,1},{1,0},{2,3},{3,2},{4,5},{5,4},{6,7},{7,6},{8,9},{9,8},{10,11... | collective-permute-start | bytes 786440 | tf_op jit(solution)/shard_map/ppermute | solution.py:219
  103.2 3.1 %collective-permute-start.10 = (f32[8,64,128]{2,1,0:T(8,128)S(1)}, f32[8,64,128]{2,1,0:T(8,128)S(1)}, u32[]{:S(2)}, u32[]{:S(2)}) collective-permute-start(f32[8,64,128]{2,1,0:T(8,128)S(1)} %get-tuple-element.14), channel_id=1, source_target_pairs={{0,1},{1,0},{2,3},{3,2},{4,5},{5,4},{6,7},{7,6},{8,9},{9,8},{10,11... | collective-permute-start | bytes 786440 | tf_op jit(solution)/shard_map/ppermute | solution.py:219
  104.7 8.4 %collective-permute-start.12 = (f32[8,64,128]{2,1,0:T(8,128)S(1)}, f32[8,64,128]{2,1,0:T(8,128)S(1)}, u32[]{:S(2)}, u32[]{:S(2)}) collective-permute-start(f32[8,64,128]{2,1,0:T(8,128)S(1)} %add.86), channel_id=1, source_target_pairs={{0,2},{1,3},{2,0},{3,1},{4,6},{5,7},{6,4},{7,5},{8,10},{9,11},{10,... | collective-permute-start | bytes 786440 | tf_op jit(solution)/shard_map/ppermute | solution.py:219

commit v9 on v8

--- a/solution.py
+++ b/solution.py
@@ -188,7 +188,7 @@
         if k in far[2]:
             after = (arrived[far[1][far[2].index(k)]],)
         if k in far[3]:
-            after = (arrived[far[1][far[3].index(k)]], arrived[far[0][far[3].index(k)]])
+            after = (arrived[far[1][far[3].index(k)]], arrived[1 + far[3].index(k)])
         arrived[k] = swap(pick(here, source, first * slots, amp, per, after), k)
 
     row_tile = mine * row_count + tile_rows

time: 114 us -> 116 us (1.018)
  starting transfers between devices: 13.4 us -> 15.4 us
  waiting for transfers between devices: 65.9 us -> 64.6 us
    ppermute x10, starting transfers between devices: 11.3 us -> 13.3 us  [swap(): return lax.ppermute(x, 'gx', [(i, i ^ k) for i in range(peers)])]
    ppermute x10, waiting for transfers between devices: 58 us -> 56.8 us  [swap(): return lax.ppermute(x, 'gx', [(i, i ^ k) for i in range(peers)])]
  transfers between devices with their start and end apart: 13 -> 13, of which waited for: 7 -> 8; matrix products, arithmetic and copies ran while one was open for 5% -> 5% of each run, Pallas kernels for 20% -> 21%
where the time goes in v9:
time: 116 us; the launch traced here: 115 us
  waiting for transfers between devices  64.6 us (56%)
  Pallas kernels  25.2 us (22%)
  starting transfers between devices  15.4 us (13%)
  other arithmetic  6.27 us (5%)
  local copies, waits for them, and re-layouts  3.62 us (3%)
    ppermute x10, waiting for transfers between devices, swap(): return lax.ppermute(x, 'gx', [(i, i ^ k) for i in range(peers)])  56.8 us
    pallas_call x5, Pallas kernels, ladder(): pl.pallas_call(functools.partial(ladder_kernel, peers_at, list(ahead), pe...  13.8 us
    ppermute x10, starting transfers between devices, swap(): return lax.ppermute(x, 'gx', [(i, i ^ k) for i in range(peers)])  13.3 us
    pallas_call x8, Pallas kernels, pick(): pl.pallas_call(functools.partial(pick_kernel, first, per, width // BLK),...  9.16 us
    ppermute x3, waiting for transfers between devices, swap_gy(): return lax.ppermute(x, 'gy', [(i, i ^ k) for i in range(groups)])  7.88 us
    convert_element_type x1, other arithmetic, per_device(): (pair_irrep(row_tile, virt_irreps) == pair_irrep(col_tile, virt_irreps))....  4.77 us
    unnamed x11, local copies, waits for them, and re-layouts  2.93 us
  transfers between devices with their start and end apart: 13, of which 8 were waited for; matrix products, arithmetic and copies ran while one was open for 5% of the time, Pallas kernels for 21%

profile of v9, /device:TPU:8, one launch (start us, length us, event | category | flops | bytes accessed | tf_op | source)
XLA Modules:
  0.0 115.2 jit_solution(3869698024321360316)
XLA Ops:
  0.0 0.0 collective-permute-start
  0.0 0.7 constant_dynamic-update-slice_fusion.1
  0.7 3.1 %collective-permute-done = s32[256]{0:T(256)S(1)} collective-permute-done((s32[256]{0:T(256)}, s32[256]{0:T(256)S(1)}, u32[]{:S(2)}, u32[]{:S(2)}) %collective-permute-start) | collective-permute-done | bytes 1056 | tf_op jit(solution)/shard_map/ppermute | solution.py:167
  3.8 2.6 %collective-permute-start.1 = (s32[512]{0:T(512)S(1)}, s32[512]{0:T(512)S(1)}, u32[]{:S(2)}, u32[]{:S(2)}) collective-permute-start(s32[512]{0:T(512)S(1)} %constant_dynamic-update-slice_fusion.rows), channel_id=1, source_target_pairs={{0,16},{4,20},{8,24},{12,28},{16,0},{20,4},{24,8},{28,12},{1,17},{... | collective-permute-start | bytes 6152 | tf_op jit(solution)/shard_map/ppermute | solution.py:167
  6.4 1.9 %collective-permute-done.1.rows = s32[512]{0:T(512)S(1)} collective-permute-done((s32[512]{0:T(512)S(1)}, s32[512]{0:T(512)S(1)}, u32[]{:S(2)}, u32[]{:S(2)}) %collective-permute-start.1) | collective-permute-done | bytes 2080 | tf_op jit(solution)/shard_map/ppermute | solution.py:167
  8.3 0.7 pad_add_fusion
  9.0 1.5 %collective-permute-start.2 = (s32[1024]{0:T(1024)S(1)}, s32[1024]{0:T(1024)S(1)}, u32[]{:S(2)}, u32[]{:S(2)}) collective-permute-start(s32[1024]{0:T(1024)S(1)} %pad_add_fusion), channel_id=1, source_target_pairs={{0,4},{4,0},{8,12},{12,8},{16,20},{20,16},{24,28},{28,24},{1,5},{5... | collective-permute-start | bytes 12296 | tf_op jit(solution)/shard_map/ppermute | solution.py:167
  10.5 2.2 %stage_amplitudes.1.amp = bf16[64,32768]{1,0:T(8,128)(2,1)S(1)} custom-call(bf16[64,32768]{1,0:T(8,128)(2,1)} %source.1), custom_call_target="tpu_custom_call" | custom-call | bytes 4194304 | tf_op jit(solution)/shard_map/stage_amplitudes/pallas_call | solution.py:35
  12.7 0.0 copy-start
  12.7 0.0 copy-start.3
  12.7 0.7 pick_tiles.12
  13.5 1.6 %collective-permute-start.6 = (bf16[32,64,128]{2,1,0:T(8,128)(2,1)S(1)}, bf16[32,64,128]{2,1,0:T(8,128)(2,1)S(1)}, u32[]{:S(2)}, u32[]{:S(2)}) collective-permute-start(bf16[32,64,128]{2,1,0:T(8,128)(2,1)S(1)} %pick_tiles.12), channel_id=1, source_target_pairs={{0,24},{4,28},{8,16},{12,20},{16,8},{20,12},{24,0},{28,4},{1,25},{... | collective-permute-start | bytes 1572872 | tf_op jit(solution)/shard_map/ppermute | solution.py:167
  15.1 0.0 collective-permute-done.2.rows
  15.1 0.8 pick_tiles.9
  15.9 0.6 collective-permute-start.3
  16.4 0.7 fusion.4
  17.1 0.7 pick_tiles.10
  17.9 2.5 %collective-permute-start.4 = (bf16[32,64,128]{2,1,0:T(8,128)(2,1)S(1)}, bf16[32,64,128]{2,1,0:T(8,128)(2,1)S(1)}, u32[]{:S(2)}, u32[]{:S(2)}) collective-permute-start(bf16[32,64,128]{2,1,0:T(8,128)(2,1)S(1)} %pick_tiles.10), channel_id=1, source_target_pairs={{0,8},{4,12},{8,0},{12,4},{16,24},{20,28},{24,16},{28,20},{1,9},{5... | collective-permute-start | bytes 1572872 | tf_op jit(solution)/shard_map/ppermute | solution.py:167
  20.4 1.5 %pick_tiles.13 = bf16[32,64,128]{2,1,0:T(8,128)(2,1)} custom-call(s32[1]{0:T(128)} %bitcast.9.me, s32[512]{0:T(512)S(1)} %collective-permute-done.1.rows, bf16[64,32768]{1,0:T(8,128)(2,1)S(1)} %stage_amplitudes.1.amp), custom_call_target="tpu_custom_call" | custom-call | bytes 1048576 | tf_op jit(solution)/shard_map/pick_tiles/pallas_call | solution.py:62
  21.9 0.0 collective-permute-start.7
  21.9 1.6 %pick_tiles.11 = bf16[32,64,128]{2,1,0:T(8,128)(2,1)} custom-call(s32[1]{0:T(128)} %bitcast.9.me, s32[1024]{0:T(1024)S(1)} %collective-permute-done.2.rows, bf16[64,32768]{1,0:T(8,128)(2,1)S(1)} %stage_amplitudes.1.amp), custom_call_target="tpu_custom_call" | custom-call | bytes 1048576 | tf_op jit(solution)/shard_map/pick_tiles/pallas_call | solution.py:62
  23.5 1.7 %collective-permute-start.5 = (bf16[32,64,128]{2,1,0:T(8,128)(2,1)}, bf16[32,64,128]{2,1,0:T(8,128)(2,1)}, u32[]{:S(2)}, u32[]{:S(2)}) collective-permute-start(bf16[32,64,128]{2,1,0:T(8,128)(2,1)} %pick_tiles.11), channel_id=1, source_target_pairs={{0,12},{4,8},{8,4},{12,0},{16,28},{20,24},{24,20},{28,16},{1,13},{... | collective-permute-start | bytes 1572872 | tf_op jit(solution)/shard_map/ppermute | solution.py:167
  25.2 15.3 %collective-permute-done.6.refs_0_ = bf16[32,64,128]{2,1,0:T(8,128)(2,1)S(1)} collective-permute-done((bf16[32,64,128]{2,1,0:T(8,128)(2,1)S(1)}, bf16[32,64,128]{2,1,0:T(8,128)(2,1)S(1)}, u32[]{:S(2)}, u32[]{:S(2)}) %collective-permute-start.6) | collective-permute-done | bytes 524320 | tf_op jit(solution)/shard_map/ppermute | solution.py:167
  40.5 1.6 %pick_tiles.15 = bf16[32,64,128]{2,1,0:T(8,128)(2,1)} custom-call(s32[1]{0:T(128)} %bitcast.9.me, s32[1024]{0:T(1024)S(1)} %collective-permute-done.2.rows, bf16[64,32768]{1,0:T(8,128)(2,1)S(1)} %stage_amplitudes.1.amp, bf16[32,64,128]{2,1,0:T(8,128)(2,1)S(1)} %collective-permute-done.6.refs_0_), custom_call_target="tpu_custom_call" | custom-call | bytes 1048576 | tf_op jit(solution)/shard_map/pick_tiles/pallas_call | solution.py:62
  42.1 0.0 collective-permute-start.9
  42.1 0.0 collective-permute-done.3.refs_1_
  42.1 1.6 %pick_tiles.14 = bf16[32,64,128]{2,1,0:T(8,128)(2,1)} custom-call(s32[1]{0:T(128)} %bitcast.9.me, s32[1024]{0:T(1024)S(1)} %collective-permute-done.2.rows, bf16[64,32768]{1,0:T(8,128)(2,1)S(1)} %stage_amplitudes.1.amp, bf16[32,64,128]{2,1,0:T(8,128)(2,1)S(1)} %collective-permute-done.6.refs_0_, bf16[32,64,128]{2,1,0:T(8,128)(2,1)S(1)} %collective-permute-done.3.refs_1_), custom_call_target="tpu_custom_call" | custom-call | bytes 1048576 | tf_op jit(solution)/shard_map/pick_tiles/pallas_call | solution.py:62
  43.7 2.6 %collective-permute-start.8 = (bf16[32,64,128]{2,1,0:T(8,128)(2,1)}, bf16[32,64,128]{2,1,0:T(8,128)(2,1)S(1)}, u32[]{:S(2)}, u32[]{:S(2)}) collective-permute-start(bf16[32,64,128]{2,1,0:T(8,128)(2,1)} %pick_tiles.14), channel_id=1, source_target_pairs={{0,28},{4,24},{8,20},{12,16},{16,12},{20,8},{24,4},{28,0},{1,29},{... | collective-permute-start | bytes 1572872 | tf_op jit(solution)/shard_map/ppermute | solution.py:167
  46.3 2.2 %copy-done.1 = bf16[64,32768]{1,0:T(8,128)(2,1)S(1)} copy-done((bf16[64,32768]{1,0:T(8,128)(2,1)S(1)}, bf16[64,32768]{1,0:T(8,128)(2,1)}, u32[]{:S(2)}) %copy-start.1) | copy-done | bytes 4194328
  48.5 0.7 pick_tiles.8.refs_0_
  49.3 4.8 %compare_convert_fusion.live = f32[256]{0:T(256)S(1)} fusion(s32[256]{0:T(256)S(1)} %copy-done.4, s32[256]{0:T(256)S(1)} %copy-done.2, s32[]{:T(128)} %bitcast, s32[]{:T(128)} %bitcast.1, s32[]{:T(128)} %bitcast.2, s32[]{:T(128)} %bitcast.3, s32[]{:T(128)} %bitcast.4, s32[]{:T(128)} %bitcast.5, s32[]{:T(128)} %bitcast.6, s32[]{:T(128)} %bitcast.7, ...), kind=kLoop, calls=%fused_computation.37 | loop fusion | flops 44544 | bytes 3112 | tf_op jit(solution)/shard_map/convert_element_type | solution.py:196
  54.1 8.8 %collective-permute-done.7.refs_0_ = bf16[32,64,128]{2,1,0:T(8,128)(2,1)} collective-permute-done((bf16[32,64,128]{2,1,0:T(8,128)(2,1)}, bf16[32,64,128]{2,1,0:T(8,128)(2,1)}, u32[]{:S(2)}, u32[]{:S(2)}) %collective-permute-start.7) | collective-permute-done | bytes 524320 | tf_op jit(solution)/shard_map/ppermute | solution.py:167
  62.8 2.8 %ladder_products.5.refs_1_ = f32[32,64,128]{2,1,0:T(8,128)S(1)} custom-call(s32[8]{0:T(128)S(1)} %iota_xor_fusion.order, s32[256]{0:T(256)S(1)} %fusion.3.cols, f32[256]{0:T(256)S(1)} %compare_convert_fusion.live, bf16[8,32,128,128]{3,2,1,0:T(8,128)(2,1)} %bitcast.16, bf16[32,64,128]{2,1,0:T(8,128)(2,1)} %collective-permute-done.7.refs_0_), custom_call_target="tpu_custom_call" | custom-call | flops 67108864 | bytes 1048576 | tf_op jit(solution)/shard_map/ladder_products/pallas_call | solution.py:137
  65.7 2.4 %ladder_products.6.refs_4_ = f32[32,64,128]{2,1,0:T(8,128)S(1)} custom-call(s32[8]{0:T(128)S(1)} %iota_xor_fusion.order, s32[256]{0:T(256)S(1)} %fusion.3.cols, f32[256]{0:T(256)S(1)} %compare_convert_fusion.live, bf16[8,32,128,128]{3,2,1,0:T(8,128)(2,1)} %bitcast.17, ...), custom_call_target="tpu_custom_call", output_to_operand_aliasing={{}: (5, {})} | custom-call | flops 67108864 | bytes 1048576 | tf_op jit(solution)/shard_map/ladder_products/pallas_call | solution.py:137
  68.1 0.0 collective-permute-done.4.refs_2_
  68.1 0.0 collective-permute-done.5.refs_3_
  68.1 4.5 %ladder_products.7 = (f32[32,64,128]{2,1,0:T(8,128)S(1)}, bf16[1,32,128,128]{3,2,1,0:T(8,128)(2,1)S(1)}) custom-call(s32[8]{0:T(128)S(1)} %iota_xor_fusion.order, s32[256]{0:T(256)S(1)} %fusion.3.cols, f32[256]{0:T(256)S(1)} %compare_convert_fusion.live, bf16[8,32,128,128]{3,2,1,0:T(8,128)(2,1)} %bitcast.18, ...), custom_call_target="tpu_custom_call", output_to_operand_aliasing={{0}: (8, {})} | custom-call | flops 268435456 | bytes 5242880 | tf_op jit(solution)/shard_map/ladder_products/pallas_call | solution.py:137
  72.6 20.7 %collective-permute-done.9.refs_0_ = bf16[32,64,128]{2,1,0:T(8,128)(2,1)} collective-permute-done((bf16[32,64,128]{2,1,0:T(8,128)(2,1)}, bf16[32,64,128]{2,1,0:T(8,128)(2,1)}, u32[]{:S(2)}, u32[]{:S(2)}) %collective-permute-start.9) | collective-permute-done | bytes 524320 | tf_op jit(solution)/shard_map/ppermute | solution.py:167
  93.3 2.8 %ladder_products.8.refs_1_ = f32[32,64,128]{2,1,0:T(8,128)S(1)} custom-call(s32[8]{0:T(128)S(1)} %iota_xor_fusion.order, s32[256]{0:T(256)S(1)} %fusion.3.cols, f32[256]{0:T(256)S(1)} %compare_convert_fusion.live, bf16[8,32,128,128]{3,2,1,0:T(8,128)(2,1)} %bitcast.19, ...), custom_call_target="tpu_custom_call", output_to_operand_aliasing={{}: (5, {})} | custom-call | flops 67108864 | bytes 1048576 | tf_op jit(solution)/shard_map/ladder_products/pallas_call | solution.py:137
  96.2 7.1 %collective-permute-done.8.refs_0_ = bf16[32,64,128]{2,1,0:T(8,128)(2,1)S(1)} collective-permute-done((bf16[32,64,128]{2,1,0:T(8,128)(2,1)}, bf16[32,64,128]{2,1,0:T(8,128)(2,1)S(1)}, u32[]{:S(2)}, u32[]{:S(2)}) %collective-permute-start.8) | collective-permute-done | bytes 524320 | tf_op jit(solution)/shard_map/ppermute | solution.py:167
  103.2 1.2 %ladder_products.9 = (f32[8,64,128]{2,1,0:T(8,128)S(1)}, f32[8,64,128]{2,1,0:T(8,128)S(1)}, f32[8,64,128]{2,1,0:T(8,128)S(1)}, f32[8,64,128]{2,1,0:T(8,128)S(1)}) custom-call(s32[8]{0:T(128)S(1)} %iota_xor_fusion.order, s32[256]{0:T(256)S(1)} %fusion.3.cols, f32[256]{0:T(256)S(1)} %compare_convert_fusion.live, ...), custom_call_target="tpu_custom_call" | custom-call | flops 67108864 | bytes 1048576 | tf_op jit(solution)/shard_map/ladder_products/pallas_call | solution.py:137
  104.4 0.1 collective-permute-start.11
  104.5 0.5 collective-permute-start.10
  105.0 1.0 collective-permute-done.11
  106.1 1.6 %collective-permute-start.12 = (f32[8,64,128]{2,1,0:T(8,128)S(1)}, f32[8,64,128]{2,1,0:T(8,128)S(1)}, u32[]{:S(2)}, u32[]{:S(2)}) collective-permute-start(f32[8,64,128]{2,1,0:T(8,128)S(1)} %add.86), channel_id=1, source_target_pairs={{0,2},{1,3},{2,0},{3,1},{4,6},{5,7},{6,4},{7,5},{8,10},{9,11},{10,... | collective-permute-start | bytes 786440 | tf_op jit(solution)/shard_map/ppermute | solution.py:219
  107.6 0.0 collective-permute-done.10
  107.6 6.9 %collective-permute-done.12 = f32[8,64,128]{2,1,0:T(8,128)S(1)} collective-permute-done((f32[8,64,128]{2,1,0:T(8,128)S(1)}, f32[8,64,128]{2,1,0:T(8,128)S(1)}, u32[]{:S(2)}, u32[]{:S(2)}) %collective-permute-start.12) | collective-permute-done | bytes 262176 | tf_op jit(solution)/shard_map/ppermute | solution.py:219
  114.5 0.7 copy_bitcast_fusion
  (12 shorter events, 0.1 us)
Async XLA Ops:
  0.0 3.8 %collective-permute-start = (s32[256]{0:T(256)}, s32[256]{0:T(256)S(1)}, u32[]{:S(2)}, u32[]{:S(2)}) collective-permute-start(s32[256]{0:T(256)} %rows.1), channel_id=1, source_target_pairs={{0,8},{4,12},{8,0},{12,4},{16,24},{20,28},{24,16},{28,20},{1,9},{5... | collective-permute-start | bytes 3080 | tf_op jit(solution)/shard_map/ppermute | solution.py:167
  3.8 4.5 %collective-permute-start.1 = (s32[512]{0:T(512)S(1)}, s32[512]{0:T(512)S(1)}, u32[]{:S(2)}, u32[]{:S(2)}) collective-permute-start(s32[512]{0:T(512)S(1)} %constant_dynamic-update-slice_fusion.rows), channel_id=1, source_target_pairs={{0,16},{4,20},{8,24},{12,28},{16,0},{20,4},{24,8},{28,12},{1,17},{... | collective-permute-start | bytes 6152 | tf_op jit(solution)/shard_map/ppermute | solution.py:167
  9.0 6.1 %collective-permute-start.2 = (s32[1024]{0:T(1024)S(1)}, s32[1024]{0:T(1024)S(1)}, u32[]{:S(2)}, u32[]{:S(2)}) collective-permute-start(s32[1024]{0:T(1024)S(1)} %pad_add_fusion), channel_id=1, source_target_pairs={{0,4},{4,0},{8,12},{12,8},{16,20},{20,16},{24,28},{28,24},{1,5},{5... | collective-permute-start | bytes 12296 | tf_op jit(solution)/shard_map/ppermute | solution.py:167
  12.7 29.4 %copy-start = (bf16[64,32768]{1,0:T(8,128)(2,1)}, bf16[64,32768]{1,0:T(8,128)(2,1)S(1)}, u32[]{:S(2)}) copy-start(bf16[64,32768]{1,0:T(8,128)(2,1)S(1)} %stage_amplitudes.1.amp) | copy-start | bytes 12582916
  12.7 3.7 %copy-start.3 = (s32[8]{0:T(128)S(1)}, s32[8]{0:T(128)}, u32[]{:S(2)}) copy-start(s32[8]{0:T(128)} %param.6) | copy-start | bytes 100
  13.5 27.1 %collective-permute-start.6 = (bf16[32,64,128]{2,1,0:T(8,128)(2,1)S(1)}, bf16[32,64,128]{2,1,0:T(8,128)(2,1)S(1)}, u32[]{:S(2)}, u32[]{:S(2)}) collective-permute-start(bf16[32,64,128]{2,1,0:T(8,128)(2,1)S(1)} %pick_tiles.12), channel_id=1, source_target_pairs={{0,24},{4,28},{8,16},{12,20},{16,8},{20,12},{24,0},{28,4},{1,25},{... | collective-permute-start | bytes 1572872 | tf_op jit(solution)/shard_map/ppermute | solution.py:167
  15.9 26.2 %collective-permute-start.3 = (bf16[32,64,128]{2,1,0:T(8,128)(2,1)S(1)}, bf16[32,64,128]{2,1,0:T(8,128)(2,1)S(1)}, u32[]{:S(2)}, u32[]{:S(2)}) collective-permute-start(bf16[32,64,128]{2,1,0:T(8,128)(2,1)S(1)} %pick_tiles.9), channel_id=1, source_target_pairs={{0,4},{4,0},{8,12},{12,8},{16,20},{20,16},{24,28},{28,24},{1,5},{5... | collective-permute-start | bytes 1572872 | tf_op jit(solution)/shard_map/ppermute | solution.py:167
  17.9 50.2 %collective-permute-start.4 = (bf16[32,64,128]{2,1,0:T(8,128)(2,1)S(1)}, bf16[32,64,128]{2,1,0:T(8,128)(2,1)S(1)}, u32[]{:S(2)}, u32[]{:S(2)}) collective-permute-start(bf16[32,64,128]{2,1,0:T(8,128)(2,1)S(1)} %pick_tiles.10), channel_id=1, source_target_pairs={{0,8},{4,12},{8,0},{12,4},{16,24},{20,28},{24,16},{28,20},{1,9},{5... | collective-permute-start | bytes 1572872 | tf_op jit(solution)/shard_map/ppermute | solution.py:167
  21.9 40.9 %collective-permute-start.7 = (bf16[32,64,128]{2,1,0:T(8,128)(2,1)}, bf16[32,64,128]{2,1,0:T(8,128)(2,1)}, u32[]{:S(2)}, u32[]{:S(2)}) collective-permute-start(bf16[32,64,128]{2,1,0:T(8,128)(2,1)} %pick_tiles.13), channel_id=1, source_target_pairs={{0,16},{4,20},{8,24},{12,28},{16,0},{20,4},{24,8},{28,12},{1,17},{... | collective-permute-start | bytes 1572872 | tf_op jit(solution)/shard_map/ppermute | solution.py:167
  23.5 44.6 %collective-permute-start.5 = (bf16[32,64,128]{2,1,0:T(8,128)(2,1)}, bf16[32,64,128]{2,1,0:T(8,128)(2,1)}, u32[]{:S(2)}, u32[]{:S(2)}) collective-permute-start(bf16[32,64,128]{2,1,0:T(8,128)(2,1)} %pick_tiles.11), channel_id=1, source_target_pairs={{0,12},{4,8},{8,4},{12,0},{16,28},{20,24},{24,20},{28,16},{1,13},{... | collective-permute-start | bytes 1572872 | tf_op jit(solution)/shard_map/ppermute | solution.py:167
  42.1 4.2 %copy-start.2 = (s32[256]{0:T(256)S(1)}, s32[256]{0:T(256)}, u32[]{:S(2)}) copy-start(s32[256]{0:T(256)} %rows.1) | copy-start | bytes 3076
  42.1 7.2 %copy-start.4 = (s32[256]{0:T(256)S(1)}, s32[256]{0:T(256)}, u32[]{:S(2)}) copy-start(s32[256]{0:T(256)} %param.9) | copy-start | bytes 3076
  42.1 51.2 %collective-permute-start.9 = (bf16[32,64,128]{2,1,0:T(8,128)(2,1)}, bf16[32,64,128]{2,1,0:T(8,128)(2,1)}, u32[]{:S(2)}, u32[]{:S(2)}) collective-permute-start(bf16[32,64,128]{2,1,0:T(8,128)(2,1)} %pick_tiles.15), channel_id=1, source_target_pairs={{0,20},{4,16},{8,28},{12,24},{16,4},{20,0},{24,12},{28,8},{1,21},{... | collective-permute-start | bytes 1572872 | tf_op jit(solution)/shard_map/ppermute | solution.py:167
  43.7 59.6 %collective-permute-start.8 = (bf16[32,64,128]{2,1,0:T(8,128)(2,1)}, bf16[32,64,128]{2,1,0:T(8,128)(2,1)S(1)}, u32[]{:S(2)}, u32[]{:S(2)}) collective-permute-start(bf16[32,64,128]{2,1,0:T(8,128)(2,1)} %pick_tiles.14), channel_id=1, source_target_pairs={{0,28},{4,24},{8,20},{12,16},{16,12},{20,8},{24,4},{28,0},{1,29},{... | collective-permute-start | bytes 1572872 | tf_op jit(solution)/shard_map/ppermute | solution.py:167
  46.3 2.2 %copy-start.1 = (bf16[64,32768]{1,0:T(8,128)(2,1)S(1)}, bf16[64,32768]{1,0:T(8,128)(2,1)}, u32[]{:S(2)}) copy-start(bf16[64,32768]{1,0:T(8,128)(2,1)} %copy-done) | copy-start | bytes 12582916
  104.4 1.6 %collective-permute-start.11 = (f32[8,64,128]{2,1,0:T(8,128)S(1)}, f32[8,64,128]{2,1,0:T(8,128)S(1)}, u32[]{:S(2)}, u32[]{:S(2)}) collective-permute-start(f32[8,64,128]{2,1,0:T(8,128)S(1)} %get-tuple-element.16), channel_id=1, source_target_pairs={{0,1},{1,0},{2,3},{3,2},{4,5},{5,4},{6,7},{7,6},{8,9},{9,8},{10,11... | collective-permute-start | bytes 786440 | tf_op jit(solution)/shard_map/ppermute | solution.py:219
  104.5 3.1 %collective-permute-start.10 = (f32[8,64,128]{2,1,0:T(8,128)S(1)}, f32[8,64,128]{2,1,0:T(8,128)S(1)}, u32[]{:S(2)}, u32[]{:S(2)}) collective-permute-start(f32[8,64,128]{2,1,0:T(8,128)S(1)} %get-tuple-element.14), channel_id=1, source_target_pairs={{0,1},{1,0},{2,3},{3,2},{4,5},{5,4},{6,7},{7,6},{8,9},{9,8},{10,11... | collective-permute-start | bytes 786440 | tf_op jit(solution)/shard_map/ppermute | solution.py:219
  106.1 8.4 %collective-permute-start.12 = (f32[8,64,128]{2,1,0:T(8,128)S(1)}, f32[8,64,128]{2,1,0:T(8,128)S(1)}, u32[]{:S(2)}, u32[]{:S(2)}) collective-permute-start(f32[8,64,128]{2,1,0:T(8,128)S(1)} %add.86), channel_id=1, source_target_pairs={{0,2},{1,3},{2,0},{3,1},{4,6},{5,7},{6,4},{7,5},{8,10},{9,11},{10,... | collective-permute-start | bytes 786440 | tf_op jit(solution)/shard_map/ppermute | solution.py:219

commit v10 on v9

--- a/solution.py
+++ b/solution.py
@@ -188,7 +188,7 @@
         if k in far[2]:
             after = (arrived[far[1][far[2].index(k)]],)
         if k in far[3]:
-            after = (arrived[far[1][far[3].index(k)]], arrived[1 + far[3].index(k)])
+            after = (arrived[far[1][far[3].index(k)]], arrived[2 + far[3].index(k)])
         arrived[k] = swap(pick(here, source, first * slots, amp, per, after), k)
 
     row_tile = mine * row_count + tile_rows

time: 116 us -> 114 us (0.983)
  waiting for transfers between devices: 64.6 us -> 62.5 us
    ppermute x10, waiting for transfers between devices: 56.8 us -> 54.6 us  [swap(): return lax.ppermute(x, 'gx', [(i, i ^ k) for i in range(peers)])]
  transfers between devices with their start and end apart: 13 -> 13, of which waited for: 8 -> 7; matrix products, arithmetic and copies ran while one was open for 5% -> 6% of each run, Pallas kernels for 21% -> 21%
where the time goes in v10:
time: 114 us; the launch traced here: 113 us
  waiting for transfers between devices  62.5 us (55%)
  Pallas kernels  25.5 us (22%)
  starting transfers between devices  16 us (14%)
  other arithmetic  5.59 us (5%)
  local copies, waits for them, and re-layouts  3.62 us (3%)
    ppermute x10, waiting for transfers between devices, swap(): return lax.ppermute(x, 'gx', [(i, i ^ k) for i in range(peers)])  54.6 us
    ppermute x10, starting transfers between devices, swap(): return lax.ppermute(x, 'gx', [(i, i ^ k) for i in range(peers)])  13.9 us
    pallas_call x5, Pallas kernels, ladder(): pl.pallas_call(functools.partial(ladder_kernel, peers_at, list(ahead), pe...  13.3 us
    pallas_call x8, Pallas kernels, pick(): pl.pallas_call(functools.partial(pick_kernel, first, per, width // BLK),...  9.96 us
    ppermute x3, waiting for transfers between devices, swap_gy(): return lax.ppermute(x, 'gy', [(i, i ^ k) for i in range(groups)])  7.88 us
    convert_element_type x1, other arithmetic, per_device(): (pair_irrep(row_tile, virt_irreps) == pair_irrep(col_tile, virt_irreps))....  4.77 us
    unnamed x11, local copies, waits for them, and re-layouts  2.93 us
  transfers between devices with their start and end apart: 13, of which 7 were waited for; matrix products, arithmetic and copies ran while one was open for 6% of the time, Pallas kernels for 21%

profile of v10, /device:TPU:8, one launch (start us, length us, event | category | flops | bytes accessed | tf_op | source)
XLA Modules:
  0.0 113.3 jit_solution(504518408511116323)
XLA Ops:
  0.0 0.0 collective-permute-start
  0.0 0.7 constant_dynamic-update-slice_fusion.1
  0.7 3.1 %collective-permute-done = s32[256]{0:T(256)S(1)} collective-permute-done((s32[256]{0:T(256)}, s32[256]{0:T(256)S(1)}, u32[]{:S(2)}, u32[]{:S(2)}) %collective-permute-start) | collective-permute-done | bytes 1056 | tf_op jit(solution)/shard_map/ppermute | solution.py:167
  3.8 2.6 %collective-permute-start.1 = (s32[512]{0:T(512)S(1)}, s32[512]{0:T(512)S(1)}, u32[]{:S(2)}, u32[]{:S(2)}) collective-permute-start(s32[512]{0:T(512)S(1)} %constant_dynamic-update-slice_fusion.rows), channel_id=1, source_target_pairs={{0,16},{4,20},{8,24},{12,28},{16,0},{20,4},{24,8},{28,12},{1,17},{... | collective-permute-start | bytes 6152 | tf_op jit(solution)/shard_map/ppermute | solution.py:167
  6.4 2.2 %stage_amplitudes.1.amp = bf16[64,32768]{1,0:T(8,128)(2,1)S(1)} custom-call(bf16[64,32768]{1,0:T(8,128)(2,1)} %source.1), custom_call_target="tpu_custom_call" | custom-call | bytes 4194304 | tf_op jit(solution)/shard_map/stage_amplitudes/pallas_call | solution.py:35
  8.6 0.0 collective-permute-done.1.rows
  8.6 0.0 copy-start.2
  8.6 0.0 copy-start.3
  8.6 0.7 pick_tiles.12
  9.4 1.3 %collective-permute-start.6 = (bf16[32,64,128]{2,1,0:T(8,128)(2,1)S(1)}, bf16[32,64,128]{2,1,0:T(8,128)(2,1)S(1)}, u32[]{:S(2)}, u32[]{:S(2)}) collective-permute-start(bf16[32,64,128]{2,1,0:T(8,128)(2,1)S(1)} %pick_tiles.12), channel_id=1, source_target_pairs={{0,24},{4,28},{8,16},{12,20},{16,8},{20,12},{24,0},{28,4},{1,25},{... | collective-permute-start | bytes 1572872 | tf_op jit(solution)/shard_map/ppermute | solution.py:167
  10.7 0.7 pick_tiles.10
  11.4 2.5 %collective-permute-start.4 = (bf16[32,64,128]{2,1,0:T(8,128)(2,1)S(1)}, bf16[32,64,128]{2,1,0:T(8,128)(2,1)S(1)}, u32[]{:S(2)}, u32[]{:S(2)}) collective-permute-start(bf16[32,64,128]{2,1,0:T(8,128)(2,1)S(1)} %pick_tiles.10), channel_id=1, source_target_pairs={{0,8},{4,12},{8,0},{12,4},{16,24},{20,28},{24,16},{28,20},{1,9},{5... | collective-permute-start | bytes 1572872 | tf_op jit(solution)/shard_map/ppermute | solution.py:167
  13.9 0.0 copy-done.2
  14.0 1.6 %collective-permute-start.2 = (s32[1024]{0:T(1024)S(1)}, s32[1024]{0:T(1024)S(1)}, u32[]{:S(2)}, u32[]{:S(2)}) collective-permute-start(s32[1024]{0:T(1024)S(1)} %pad_add_fusion), channel_id=1, source_target_pairs={{0,4},{4,0},{8,12},{12,8},{16,20},{20,16},{24,28},{28,24},{1,5},{5... | collective-permute-start | bytes 12296 | tf_op jit(solution)/shard_map/ppermute | solution.py:167
  15.5 0.7 fusion.4
  16.2 1.5 %pick_tiles.13 = bf16[32,64,128]{2,1,0:T(8,128)(2,1)} custom-call(s32[1]{0:T(128)} %bitcast.9.me, s32[512]{0:T(512)S(1)} %collective-permute-done.1.rows, bf16[64,32768]{1,0:T(8,128)(2,1)S(1)} %stage_amplitudes.1.amp), custom_call_target="tpu_custom_call" | custom-call | bytes 1048576 | tf_op jit(solution)/shard_map/pick_tiles/pallas_call | solution.py:62
  17.8 0.0 collective-permute-start.7
  17.8 0.0 collective-permute-done.2.rows
  17.8 1.6 %pick_tiles.9 = bf16[32,64,128]{2,1,0:T(8,128)(2,1)} custom-call(s32[1]{0:T(128)} %bitcast.9.me, s32[1024]{0:T(1024)S(1)} %collective-permute-done.2.rows, bf16[64,32768]{1,0:T(8,128)(2,1)S(1)} %stage_amplitudes.1.amp), custom_call_target="tpu_custom_call" | custom-call | bytes 1048576 | tf_op jit(solution)/shard_map/pick_tiles/pallas_call | solution.py:62
  19.3 1.4 %collective-permute-start.3 = (bf16[32,64,128]{2,1,0:T(8,128)(2,1)}, bf16[32,64,128]{2,1,0:T(8,128)(2,1)S(1)}, u32[]{:S(2)}, u32[]{:S(2)}) collective-permute-start(bf16[32,64,128]{2,1,0:T(8,128)(2,1)} %pick_tiles.9), channel_id=1, source_target_pairs={{0,4},{4,0},{8,12},{12,8},{16,20},{20,16},{24,28},{28,24},{1,5},{5... | collective-permute-start | bytes 1572872 | tf_op jit(solution)/shard_map/ppermute | solution.py:167
  20.7 1.6 %pick_tiles.11 = bf16[32,64,128]{2,1,0:T(8,128)(2,1)} custom-call(s32[1]{0:T(128)} %bitcast.9.me, s32[1024]{0:T(1024)S(1)} %collective-permute-done.2.rows, bf16[64,32768]{1,0:T(8,128)(2,1)S(1)} %stage_amplitudes.1.amp), custom_call_target="tpu_custom_call" | custom-call | bytes 1048576 | tf_op jit(solution)/shard_map/pick_tiles/pallas_call | solution.py:62
  22.3 1.2 %collective-permute-start.5 = (bf16[32,64,128]{2,1,0:T(8,128)(2,1)}, bf16[32,64,128]{2,1,0:T(8,128)(2,1)S(1)}, u32[]{:S(2)}, u32[]{:S(2)}) collective-permute-start(bf16[32,64,128]{2,1,0:T(8,128)(2,1)} %pick_tiles.11), channel_id=1, source_target_pairs={{0,12},{4,8},{8,4},{12,0},{16,28},{20,24},{24,20},{28,16},{1,13},{... | collective-permute-start | bytes 1572872 | tf_op jit(solution)/shard_map/ppermute | solution.py:167
  23.5 13.0 %collective-permute-done.6.refs_0_ = bf16[32,64,128]{2,1,0:T(8,128)(2,1)S(1)} collective-permute-done((bf16[32,64,128]{2,1,0:T(8,128)(2,1)S(1)}, bf16[32,64,128]{2,1,0:T(8,128)(2,1)S(1)}, u32[]{:S(2)}, u32[]{:S(2)}) %collective-permute-start.6) | collective-permute-done | bytes 524320 | tf_op jit(solution)/shard_map/ppermute | solution.py:167
  36.4 1.6 %pick_tiles.15 = bf16[32,64,128]{2,1,0:T(8,128)(2,1)} custom-call(s32[1]{0:T(128)} %bitcast.9.me, s32[1024]{0:T(1024)S(1)} %collective-permute-done.2.rows, bf16[64,32768]{1,0:T(8,128)(2,1)S(1)} %stage_amplitudes.1.amp, bf16[32,64,128]{2,1,0:T(8,128)(2,1)S(1)} %collective-permute-done.6.refs_0_), custom_call_target="tpu_custom_call" | custom-call | bytes 1048576 | tf_op jit(solution)/shard_map/pick_tiles/pallas_call | solution.py:62
  38.0 0.0 collective-permute-start.9
  38.0 0.0 collective-permute-done.4.refs_2_.refs_1_
  38.0 1.6 %pick_tiles.14 = bf16[32,64,128]{2,1,0:T(8,128)(2,1)} custom-call(s32[1]{0:T(128)} %bitcast.9.me, s32[1024]{0:T(1024)S(1)} %collective-permute-done.2.rows, bf16[64,32768]{1,0:T(8,128)(2,1)S(1)} %stage_amplitudes.1.amp, bf16[32,64,128]{2,1,0:T(8,128)(2,1)S(1)} %collective-permute-done.6.refs_0_, bf16[32,64,128]{2,1,0:T(8,128)(2,1)S(1)} %collective-permute-done.4.refs_2_.refs_1_), custom_call_target="tpu_custom_call" | custom-call | bytes 1048576 | tf_op jit(solution)/shard_map/pick_tiles/pallas_call | solution.py:62
  39.6 3.3 %collective-permute-start.8 = (bf16[32,64,128]{2,1,0:T(8,128)(2,1)}, bf16[32,64,128]{2,1,0:T(8,128)(2,1)S(1)}, u32[]{:S(2)}, u32[]{:S(2)}) collective-permute-start(bf16[32,64,128]{2,1,0:T(8,128)(2,1)} %pick_tiles.14), channel_id=1, source_target_pairs={{0,28},{4,24},{8,20},{12,16},{16,12},{20,8},{24,4},{28,0},{1,29},{... | collective-permute-start | bytes 1572872 | tf_op jit(solution)/shard_map/ppermute | solution.py:167
  42.9 2.2 %copy-done.1 = bf16[64,32768]{1,0:T(8,128)(2,1)S(1)} copy-done((bf16[64,32768]{1,0:T(8,128)(2,1)S(1)}, bf16[64,32768]{1,0:T(8,128)(2,1)}, u32[]{:S(2)}) %copy-start.1) | copy-done | bytes 4194328
  45.0 0.7 pick_tiles.8.refs_0_
  45.8 4.8 %compare_convert_fusion.live = f32[256]{0:T(256)S(1)} fusion(s32[256]{0:T(256)S(1)} %copy-done.4, s32[256]{0:T(256)S(1)} %copy-done.2, s32[]{:T(128)} %bitcast, s32[]{:T(128)} %bitcast.1, s32[]{:T(128)} %bitcast.2, s32[]{:T(128)} %bitcast.3, s32[]{:T(128)} %bitcast.4, s32[]{:T(128)} %bitcast.5, s32[]{:T(128)} %bitcast.6, s32[]{:T(128)} %bitcast.7, ...), kind=kLoop, calls=%fused_computation.37 | loop fusion | flops 44544 | bytes 3112 | tf_op jit(solution)/shard_map/convert_element_type | solution.py:196
  50.6 7.9 %collective-permute-done.7.refs_0_ = bf16[32,64,128]{2,1,0:T(8,128)(2,1)} collective-permute-done((bf16[32,64,128]{2,1,0:T(8,128)(2,1)}, bf16[32,64,128]{2,1,0:T(8,128)(2,1)}, u32[]{:S(2)}, u32[]{:S(2)}) %collective-permute-start.7) | collective-permute-done | bytes 524320 | tf_op jit(solution)/shard_map/ppermute | solution.py:167
  58.5 2.8 %ladder_products.5.refs_1_ = f32[32,64,128]{2,1,0:T(8,128)S(1)} custom-call(s32[8]{0:T(128)S(1)} %iota_xor_fusion.order, s32[256]{0:T(256)S(1)} %fusion.3.cols, f32[256]{0:T(256)S(1)} %compare_convert_fusion.live, bf16[8,32,128,128]{3,2,1,0:T(8,128)(2,1)} %bitcast.16, bf16[32,64,128]{2,1,0:T(8,128)(2,1)} %collective-permute-done.7.refs_0_), custom_call_target="tpu_custom_call" | custom-call | flops 67108864 | bytes 1048576 | tf_op jit(solution)/shard_map/ladder_products/pallas_call | solution.py:137
  61.3 2.4 %ladder_products.6.refs_4_ = f32[32,64,128]{2,1,0:T(8,128)S(1)} custom-call(s32[8]{0:T(128)S(1)} %iota_xor_fusion.order, s32[256]{0:T(256)S(1)} %fusion.3.cols, f32[256]{0:T(256)S(1)} %compare_convert_fusion.live, bf16[8,32,128,128]{3,2,1,0:T(8,128)(2,1)} %bitcast.17, ...), custom_call_target="tpu_custom_call", output_to_operand_aliasing={{}: (5, {})} | custom-call | flops 67108864 | bytes 1048576 | tf_op jit(solution)/shard_map/ladder_products/pallas_call | solution.py:137
  63.7 0.0 collective-permute-done.3.refs_1_
  63.7 0.0 collective-permute-done.5.refs_3_
  63.7 4.1 %ladder_products.7 = (f32[32,64,128]{2,1,0:T(8,128)S(1)}, bf16[1,32,128,128]{3,2,1,0:T(8,128)(2,1)S(1)}) custom-call(s32[8]{0:T(128)S(1)} %iota_xor_fusion.order, s32[256]{0:T(256)S(1)} %fusion.3.cols, f32[256]{0:T(256)S(1)} %compare_convert_fusion.live, bf16[8,32,128,128]{3,2,1,0:T(8,128)(2,1)} %bitcast.18, ...), custom_call_target="tpu_custom_call", output_to_operand_aliasing={{0}: (8, {})} | custom-call | flops 268435456 | bytes 5242880 | tf_op jit(solution)/shard_map/ladder_products/pallas_call | solution.py:137
  67.8 21.4 %collective-permute-done.9.refs_0_ = bf16[32,64,128]{2,1,0:T(8,128)(2,1)} collective-permute-done((bf16[32,64,128]{2,1,0:T(8,128)(2,1)}, bf16[32,64,128]{2,1,0:T(8,128)(2,1)}, u32[]{:S(2)}, u32[]{:S(2)}) %collective-permute-start.9) | collective-permute-done | bytes 524320 | tf_op jit(solution)/shard_map/ppermute | solution.py:167
  89.2 2.8 %ladder_products.8.refs_1_ = f32[32,64,128]{2,1,0:T(8,128)S(1)} custom-call(s32[8]{0:T(128)S(1)} %iota_xor_fusion.order, s32[256]{0:T(256)S(1)} %fusion.3.cols, f32[256]{0:T(256)S(1)} %compare_convert_fusion.live, bf16[8,32,128,128]{3,2,1,0:T(8,128)(2,1)} %bitcast.19, ...), custom_call_target="tpu_custom_call", output_to_operand_aliasing={{}: (5, {})} | custom-call | flops 67108864 | bytes 1048576 | tf_op jit(solution)/shard_map/ladder_products/pallas_call | solution.py:137
  92.0 9.3 %collective-permute-done.8.refs_0_ = bf16[32,64,128]{2,1,0:T(8,128)(2,1)S(1)} collective-permute-done((bf16[32,64,128]{2,1,0:T(8,128)(2,1)}, bf16[32,64,128]{2,1,0:T(8,128)(2,1)S(1)}, u32[]{:S(2)}, u32[]{:S(2)}) %collective-permute-start.8) | collective-permute-done | bytes 524320 | tf_op jit(solution)/shard_map/ppermute | solution.py:167
  101.3 1.2 %ladder_products.9 = (f32[8,64,128]{2,1,0:T(8,128)S(1)}, f32[8,64,128]{2,1,0:T(8,128)S(1)}, f32[8,64,128]{2,1,0:T(8,128)S(1)}, f32[8,64,128]{2,1,0:T(8,128)S(1)}) custom-call(s32[8]{0:T(128)S(1)} %iota_xor_fusion.order, s32[256]{0:T(256)S(1)} %fusion.3.cols, f32[256]{0:T(256)S(1)} %compare_convert_fusion.live, ...), custom_call_target="tpu_custom_call" | custom-call | flops 67108864 | bytes 1048576 | tf_op jit(solution)/shard_map/ladder_products/pallas_call | solution.py:137
  102.5 0.1 collective-permute-start.11
  102.6 0.5 collective-permute-start.10
  103.1 1.0 collective-permute-done.11
  104.2 1.6 %collective-permute-start.12 = (f32[8,64,128]{2,1,0:T(8,128)S(1)}, f32[8,64,128]{2,1,0:T(8,128)S(1)}, u32[]{:S(2)}, u32[]{:S(2)}) collective-permute-start(f32[8,64,128]{2,1,0:T(8,128)S(1)} %add.86), channel_id=1, source_target_pairs={{0,2},{1,3},{2,0},{3,1},{4,6},{5,7},{6,4},{7,5},{8,10},{9,11},{10,... | collective-permute-start | bytes 786440 | tf_op jit(solution)/shard_map/ppermute | solution.py:219
  105.7 0.0 collective-permute-done.10
  105.7 6.9 %collective-permute-done.12 = f32[8,64,128]{2,1,0:T(8,128)S(1)} collective-permute-done((f32[8,64,128]{2,1,0:T(8,128)S(1)}, f32[8,64,128]{2,1,0:T(8,128)S(1)}, u32[]{:S(2)}, u32[]{:S(2)}) %collective-permute-start.12) | collective-permute-done | bytes 262176 | tf_op jit(solution)/shard_map/ppermute | solution.py:219
  112.6 0.7 copy_bitcast_fusion
  (12 shorter events, 0.1 us)
Async XLA Ops:
  0.0 3.8 %collective-permute-start = (s32[256]{0:T(256)}, s32[256]{0:T(256)S(1)}, u32[]{:S(2)}, u32[]{:S(2)}) collective-permute-start(s32[256]{0:T(256)} %rows.1), channel_id=1, source_target_pairs={{0,8},{4,12},{8,0},{12,4},{16,24},{20,28},{24,16},{28,20},{1,9},{5... | collective-permute-start | bytes 3080 | tf_op jit(solution)/shard_map/ppermute | solution.py:167
  3.8 4.8 %collective-permute-start.1 = (s32[512]{0:T(512)S(1)}, s32[512]{0:T(512)S(1)}, u32[]{:S(2)}, u32[]{:S(2)}) collective-permute-start(s32[512]{0:T(512)S(1)} %constant_dynamic-update-slice_fusion.rows), channel_id=1, source_target_pairs={{0,16},{4,20},{8,24},{12,28},{16,0},{20,4},{24,8},{28,12},{1,17},{... | collective-permute-start | bytes 6152 | tf_op jit(solution)/shard_map/ppermute | solution.py:167
  8.6 29.4 %copy-start = (bf16[64,32768]{1,0:T(8,128)(2,1)}, bf16[64,32768]{1,0:T(8,128)(2,1)S(1)}, u32[]{:S(2)}) copy-start(bf16[64,32768]{1,0:T(8,128)(2,1)S(1)} %stage_amplitudes.1.amp) | copy-start | bytes 12582916
  8.6 5.3 %copy-start.2 = (s32[256]{0:T(256)S(1)}, s32[256]{0:T(256)}, u32[]{:S(2)}) copy-start(s32[256]{0:T(256)} %rows.1) | copy-start | bytes 3076
  8.6 6.9 %copy-start.3 = (s32[8]{0:T(128)S(1)}, s32[8]{0:T(128)}, u32[]{:S(2)}) copy-start(s32[8]{0:T(128)} %param.6) | copy-start | bytes 100
  9.4 27.1 %collective-permute-start.6 = (bf16[32,64,128]{2,1,0:T(8,128)(2,1)S(1)}, bf16[32,64,128]{2,1,0:T(8,128)(2,1)S(1)}, u32[]{:S(2)}, u32[]{:S(2)}) collective-permute-start(bf16[32,64,128]{2,1,0:T(8,128)(2,1)S(1)} %pick_tiles.12), channel_id=1, source_target_pairs={{0,24},{4,28},{8,16},{12,20},{16,8},{20,12},{24,0},{28,4},{1,25},{... | collective-permute-start | bytes 1572872 | tf_op jit(solution)/shard_map/ppermute | solution.py:167
  11.4 26.6 %collective-permute-start.4 = (bf16[32,64,128]{2,1,0:T(8,128)(2,1)S(1)}, bf16[32,64,128]{2,1,0:T(8,128)(2,1)S(1)}, u32[]{:S(2)}, u32[]{:S(2)}) collective-permute-start(bf16[32,64,128]{2,1,0:T(8,128)(2,1)S(1)} %pick_tiles.10), channel_id=1, source_target_pairs={{0,8},{4,12},{8,0},{12,4},{16,24},{20,28},{24,16},{28,20},{1,9},{5... | collective-permute-start | bytes 1572872 | tf_op jit(solution)/shard_map/ppermute | solution.py:167
  14.0 3.8 %collective-permute-start.2 = (s32[1024]{0:T(1024)S(1)}, s32[1024]{0:T(1024)S(1)}, u32[]{:S(2)}, u32[]{:S(2)}) collective-permute-start(s32[1024]{0:T(1024)S(1)} %pad_add_fusion), channel_id=1, source_target_pairs={{0,4},{4,0},{8,12},{12,8},{16,20},{20,16},{24,28},{28,24},{1,5},{5... | collective-permute-start | bytes 12296 | tf_op jit(solution)/shard_map/ppermute | solution.py:167
  17.8 40.7 %collective-permute-start.7 = (bf16[32,64,128]{2,1,0:T(8,128)(2,1)}, bf16[32,64,128]{2,1,0:T(8,128)(2,1)}, u32[]{:S(2)}, u32[]{:S(2)}) collective-permute-start(bf16[32,64,128]{2,1,0:T(8,128)(2,1)} %pick_tiles.13), channel_id=1, source_target_pairs={{0,16},{4,20},{8,24},{12,28},{16,0},{20,4},{24,8},{28,12},{1,17},{... | collective-permute-start | bytes 1572872 | tf_op jit(solution)/shard_map/ppermute | solution.py:167
  19.3 44.3 %collective-permute-start.3 = (bf16[32,64,128]{2,1,0:T(8,128)(2,1)}, bf16[32,64,128]{2,1,0:T(8,128)(2,1)S(1)}, u32[]{:S(2)}, u32[]{:S(2)}) collective-permute-start(bf16[32,64,128]{2,1,0:T(8,128)(2,1)} %pick_tiles.9), channel_id=1, source_target_pairs={{0,4},{4,0},{8,12},{12,8},{16,20},{20,16},{24,28},{28,24},{1,5},{5... | collective-permute-start | bytes 1572872 | tf_op jit(solution)/shard_map/ppermute | solution.py:167
  22.3 41.4 %collective-permute-start.5 = (bf16[32,64,128]{2,1,0:T(8,128)(2,1)}, bf16[32,64,128]{2,1,0:T(8,128)(2,1)S(1)}, u32[]{:S(2)}, u32[]{:S(2)}) collective-permute-start(bf16[32,64,128]{2,1,0:T(8,128)(2,1)} %pick_tiles.11), channel_id=1, source_target_pairs={{0,12},{4,8},{8,4},{12,0},{16,28},{20,24},{24,20},{28,16},{1,13},{... | collective-permute-start | bytes 1572872 | tf_op jit(solution)/shard_map/ppermute | solution.py:167
  38.0 7.8 %copy-start.4 = (s32[256]{0:T(256)S(1)}, s32[256]{0:T(256)}, u32[]{:S(2)}) copy-start(s32[256]{0:T(256)} %param.9) | copy-start | bytes 3076
  38.0 51.2 %collective-permute-start.9 = (bf16[32,64,128]{2,1,0:T(8,128)(2,1)}, bf16[32,64,128]{2,1,0:T(8,128)(2,1)}, u32[]{:S(2)}, u32[]{:S(2)}) collective-permute-start(bf16[32,64,128]{2,1,0:T(8,128)(2,1)} %pick_tiles.15), channel_id=1, source_target_pairs={{0,20},{4,16},{8,28},{12,24},{16,4},{20,0},{24,12},{28,8},{1,21},{... | collective-permute-start | bytes 1572872 | tf_op jit(solution)/shard_map/ppermute | solution.py:167
  39.6 61.7 %collective-permute-start.8 = (bf16[32,64,128]{2,1,0:T(8,128)(2,1)}, bf16[32,64,128]{2,1,0:T(8,128)(2,1)S(1)}, u32[]{:S(2)}, u32[]{:S(2)}) collective-permute-start(bf16[32,64,128]{2,1,0:T(8,128)(2,1)} %pick_tiles.14), channel_id=1, source_target_pairs={{0,28},{4,24},{8,20},{12,16},{16,12},{20,8},{24,4},{28,0},{1,29},{... | collective-permute-start | bytes 1572872 | tf_op jit(solution)/shard_map/ppermute | solution.py:167
  42.9 2.2 %copy-start.1 = (bf16[64,32768]{1,0:T(8,128)(2,1)S(1)}, bf16[64,32768]{1,0:T(8,128)(2,1)}, u32[]{:S(2)}) copy-start(bf16[64,32768]{1,0:T(8,128)(2,1)} %copy-done) | copy-start | bytes 12582916
  102.5 1.6 %collective-permute-start.11 = (f32[8,64,128]{2,1,0:T(8,128)S(1)}, f32[8,64,128]{2,1,0:T(8,128)S(1)}, u32[]{:S(2)}, u32[]{:S(2)}) collective-permute-start(f32[8,64,128]{2,1,0:T(8,128)S(1)} %get-tuple-element.16), channel_id=1, source_target_pairs={{0,1},{1,0},{2,3},{3,2},{4,5},{5,4},{6,7},{7,6},{8,9},{9,8},{10,11... | collective-permute-start | bytes 786440 | tf_op jit(solution)/shard_map/ppermute | solution.py:219
  102.6 3.1 %collective-permute-start.10 = (f32[8,64,128]{2,1,0:T(8,128)S(1)}, f32[8,64,128]{2,1,0:T(8,128)S(1)}, u32[]{:S(2)}, u32[]{:S(2)}) collective-permute-start(f32[8,64,128]{2,1,0:T(8,128)S(1)} %get-tuple-element.14), channel_id=1, source_target_pairs={{0,1},{1,0},{2,3},{3,2},{4,5},{5,4},{6,7},{7,6},{8,9},{9,8},{10,11... | collective-permute-start | bytes 786440 | tf_op jit(solution)/shard_map/ppermute | solution.py:219
  104.2 8.4 %collective-permute-start.12 = (f32[8,64,128]{2,1,0:T(8,128)S(1)}, f32[8,64,128]{2,1,0:T(8,128)S(1)}, u32[]{:S(2)}, u32[]{:S(2)}) collective-permute-start(f32[8,64,128]{2,1,0:T(8,128)S(1)} %add.86), channel_id=1, source_target_pairs={{0,2},{1,3},{2,0},{3,1},{4,6},{5,7},{6,4},{7,5},{8,10},{9,11},{10,... | collective-permute-start | bytes 786440 | tf_op jit(solution)/shard_map/ppermute | solution.py:219

commit v11 on v7

--- a/solution.py
+++ b/solution.py
@@ -167,25 +167,31 @@
         return lax.ppermute(x, "gx", [(i, i ^ k) for i in range(peers)])
 
     slots = tile_rows.shape[0]
-    rows, bit = tile_rows, 1
+    first_far = swap(tile_rows, near)
+    place = {near: (first_far, 0)}
+    known, rows, bit = [0, near], jnp.concatenate([tile_rows, first_far]), 2
     while bit < near:
         rows = jnp.concatenate([rows, swap(rows, bit)])
+        known = known + [k ^ bit for k in known]
         bit *= 2
-    far_rows = swap(rows, near)
+    odd = swap(rows, 1)
+    for j, k in enumerate(known):
+        place.setdefault(k, (rows, j * slots))
+        place[k ^ 1] = (odd, j * slots)
 
     amp = stage(amplitudes)
     here = me.reshape(1)
     quarter = near // 4
-    far = [list(range(near + j * quarter, near + (j + 1) * quarter)) for j in range(4)]
+    far_order = list(range(near, peers, 2)) + list(range(near + 1, peers, 2))
+    far = [far_order[j * quarter : (j + 1) * quarter] for j in range(4)]
     arrived = {0: pick(here, tile_rows, 0, amp, per)}
     for k in far[0] + far[1] + list(range(1, near)) + far[2] + far[3]:
-        source, first = (far_rows, (k - near) * slots) if k >= near else (rows, k * slots)
         after = ()
         if k in far[2]:
-            after = (arrived[k - quarter],)
+            after = (arrived[far[0][far[2].index(k)]],)
         if k in far[3]:
-            after = (arrived[k - 2 * quarter], arrived[k - 3 * quarter])
-        arrived[k] = swap(pick(here, source, first, amp, per, after), k)
+            after = (arrived[far[0][far[3].index(k)]], arrived[2 + far[3].index(k)])
+        arrived[k] = swap(pick(here, *place[k], amp, per, after), k)
 
     row_tile = mine * row_count + tile_rows
     col_tile = me * ABT_X + tile_cols

time: 117 us -> 113 us (0.966)
  waiting for transfers between devices: 64.6 us -> 53.1 us
  starting transfers between devices: 16.1 us -> 24.5 us
    ppermute x10, waiting for transfers between devices: 56.7 us -> 45.2 us  [swap(): return lax.ppermute(x, 'gx', [(i, i ^ k) for i in range(peers)])]
    ppermute x10, starting transfers between devices: 14 us -> 22.4 us  [swap(): return lax.ppermute(x, 'gx', [(i, i ^ k) for i in range(peers)])]
  transfers between devices with their start and end apart: 13 -> 13, of which waited for: 9 -> 6; matrix products, arithmetic and copies ran while one was open for 5% -> 6% of each run, Pallas kernels for 20% -> 22%
where the time goes in v11:
time: 113 us
  waiting for transfers between devices  53.1 us (47%)
  Pallas kernels  25.5 us (23%)
  starting transfers between devices  24.5 us (22%)
  other arithmetic  5.59 us (5%)
  local copies, waits for them, and re-layouts  3.6 us (3%)
    ppermute x10, waiting for transfers between devices, swap(): return lax.ppermute(x, 'gx', [(i, i ^ k) for i in range(peers)])  45.2 us
    ppermute x10, starting transfers between devices, swap(): return lax.ppermute(x, 'gx', [(i, i ^ k) for i in range(peers)])  22.4 us
    pallas_call x5, Pallas kernels, ladder(): pl.pallas_call(functools.partial(ladder_kernel, peers_at, list(ahead), pe...  13.3 us
    pallas_call x8, Pallas kernels, pick(): pl.pallas_call(functools.partial(pick_kernel, first, per, width // BLK),...  10 us
    ppermute x3, waiting for transfers between devices, swap_gy(): return lax.ppermute(x, 'gy', [(i, i ^ k) for i in range(groups)])  7.88 us
    convert_element_type x1, other arithmetic, per_device(): (pair_irrep(row_tile, virt_irreps) == pair_irrep(col_tile, virt_irreps))....  4.77 us
    unnamed x12, local copies, waits for them, and re-layouts  2.92 us
  transfers between devices with their start and end apart: 13, of which 6 were waited for; matrix products, arithmetic and copies ran while one was open for 6% of the time, Pallas kernels for 22%

profile of v11, /device:TPU:8, one launch (start us, length us, event | category | flops | bytes accessed | tf_op | source)
XLA Modules:
  0.0 112.5 jit_solution(7480369875630140741)
XLA Ops:
  0.0 2.6 %collective-permute-start = (s32[256]{0:T(256)}, s32[256]{0:T(256)S(1)}, u32[]{:S(2)}, u32[]{:S(2)}) collective-permute-start(s32[256]{0:T(256)} %rows.1), channel_id=1, source_target_pairs={{0,16},{4,20},{8,24},{12,28},{16,0},{20,4},{24,8},{28,12},{1,17},{... | collective-permute-start | bytes 3080 | tf_op jit(solution)/shard_map/ppermute | solution.py:167
  2.6 0.7 constant_dynamic-update-slice_fusion.2
  3.3 2.2 %stage_amplitudes.1.amp = bf16[64,32768]{1,0:T(8,128)(2,1)S(1)} custom-call(bf16[64,32768]{1,0:T(8,128)(2,1)} %source.1), custom_call_target="tpu_custom_call" | custom-call | bytes 4194304 | tf_op jit(solution)/shard_map/stage_amplitudes/pallas_call | solution.py:35
  5.5 0.0 collective-permute-done.rows
  5.5 0.0 copy-done.2
  5.6 0.5 collective-permute-start.1
  6.1 0.7 pick_tiles.13
  6.8 1.8 %collective-permute-start.7 = (bf16[32,64,128]{2,1,0:T(8,128)(2,1)S(1)}, bf16[32,64,128]{2,1,0:T(8,128)(2,1)S(1)}, u32[]{:S(2)}, u32[]{:S(2)}) collective-permute-start(bf16[32,64,128]{2,1,0:T(8,128)(2,1)S(1)} %pick_tiles.13), channel_id=1, source_target_pairs={{0,16},{4,20},{8,24},{12,28},{16,0},{20,4},{24,8},{28,12},{1,17},{... | collective-permute-start | bytes 1572872 | tf_op jit(solution)/shard_map/ppermute | solution.py:167
  8.6 0.7 collective-permute-done.1
  9.2 0.8 pick_tiles.10
  10.0 1.0 collective-permute-start.4
  11.0 1.5 %collective-permute-start.2 = (s32[1024]{0:T(1024)S(1)}, s32[1024]{0:T(1024)S(1)}, u32[]{:S(2)}, u32[]{:S(2)}) collective-permute-start(s32[1024]{0:T(1024)S(1)} %constant_dynamic-update-slice_fusion.rows), channel_id=1, source_target_pairs={{0,4},{4,0},{8,12},{12,8},{16,20},{20,16},{24,28},{28,24},{1,5},{5... | collective-permute-start | bytes 12296 | tf_op jit(solution)/shard_map/ppermute | solution.py:167
  12.5 0.0 copy-done.3
  12.5 0.7 fusion.4
  13.2 1.6 %pick_tiles.12 = bf16[32,64,128]{2,1,0:T(8,128)(2,1)} custom-call(s32[1]{0:T(128)} %bitcast.9.me, s32[1024]{0:T(1024)S(1)} %constant_dynamic-update-slice_fusion.rows, bf16[64,32768]{1,0:T(8,128)(2,1)S(1)} %stage_amplitudes.1.amp), custom_call_target="tpu_custom_call" | custom-call | bytes 1048576 | tf_op jit(solution)/shard_map/pick_tiles/pallas_call | solution.py:62
  14.8 1.5 %collective-permute-start.6 = (bf16[32,64,128]{2,1,0:T(8,128)(2,1)}, bf16[32,64,128]{2,1,0:T(8,128)(2,1)}, u32[]{:S(2)}, u32[]{:S(2)}) collective-permute-start(bf16[32,64,128]{2,1,0:T(8,128)(2,1)} %pick_tiles.12), channel_id=1, source_target_pairs={{0,24},{4,28},{8,16},{12,20},{16,8},{20,12},{24,0},{28,4},{1,25},{... | collective-permute-start | bytes 1572872 | tf_op jit(solution)/shard_map/ppermute | solution.py:167
  16.3 0.0 collective-permute-done.2.rows
  16.3 1.6 %pick_tiles.9 = bf16[32,64,128]{2,1,0:T(8,128)(2,1)} custom-call(s32[1]{0:T(128)} %bitcast.9.me, s32[1024]{0:T(1024)S(1)} %collective-permute-done.2.rows, bf16[64,32768]{1,0:T(8,128)(2,1)S(1)} %stage_amplitudes.1.amp), custom_call_target="tpu_custom_call" | custom-call | bytes 1048576 | tf_op jit(solution)/shard_map/pick_tiles/pallas_call | solution.py:62
  17.9 0.5 collective-permute-start.3
  18.4 1.6 %pick_tiles.11 = bf16[32,64,128]{2,1,0:T(8,128)(2,1)} custom-call(s32[1]{0:T(128)} %bitcast.9.me, s32[1024]{0:T(1024)S(1)} %collective-permute-done.2.rows, bf16[64,32768]{1,0:T(8,128)(2,1)S(1)} %stage_amplitudes.1.amp), custom_call_target="tpu_custom_call" | custom-call | bytes 1048576 | tf_op jit(solution)/shard_map/pick_tiles/pallas_call | solution.py:62
  20.0 2.1 %collective-permute-start.5 = (bf16[32,64,128]{2,1,0:T(8,128)(2,1)}, bf16[32,64,128]{2,1,0:T(8,128)(2,1)S(1)}, u32[]{:S(2)}, u32[]{:S(2)}) collective-permute-start(bf16[32,64,128]{2,1,0:T(8,128)(2,1)} %pick_tiles.11), channel_id=1, source_target_pairs={{0,12},{4,8},{8,4},{12,0},{16,28},{20,24},{24,20},{28,16},{1,13},{... | collective-permute-start | bytes 1572872 | tf_op jit(solution)/shard_map/ppermute | solution.py:167
  22.1 11.0 %collective-permute-done.7.refs_0_ = bf16[32,64,128]{2,1,0:T(8,128)(2,1)S(1)} collective-permute-done((bf16[32,64,128]{2,1,0:T(8,128)(2,1)S(1)}, bf16[32,64,128]{2,1,0:T(8,128)(2,1)S(1)}, u32[]{:S(2)}, u32[]{:S(2)}) %collective-permute-start.7) | collective-permute-done | bytes 524320 | tf_op jit(solution)/shard_map/ppermute | solution.py:167
  33.0 1.6 %pick_tiles.15 = bf16[32,64,128]{2,1,0:T(8,128)(2,1)} custom-call(s32[1]{0:T(128)} %bitcast.9.me, s32[1024]{0:T(1024)S(1)} %collective-permute-done.2.rows, bf16[64,32768]{1,0:T(8,128)(2,1)S(1)} %stage_amplitudes.1.amp, bf16[32,64,128]{2,1,0:T(8,128)(2,1)S(1)} %collective-permute-done.7.refs_0_), custom_call_target="tpu_custom_call" | custom-call | bytes 1048576 | tf_op jit(solution)/shard_map/pick_tiles/pallas_call | solution.py:62
  34.6 10.8 %collective-permute-start.9 = (bf16[32,64,128]{2,1,0:T(8,128)(2,1)}, bf16[32,64,128]{2,1,0:T(8,128)(2,1)}, u32[]{:S(2)}, u32[]{:S(2)}) collective-permute-start(bf16[32,64,128]{2,1,0:T(8,128)(2,1)} %pick_tiles.15), channel_id=1, source_target_pairs={{0,20},{4,16},{8,28},{12,24},{16,4},{20,0},{24,12},{28,8},{1,21},{... | collective-permute-start | bytes 1572872 | tf_op jit(solution)/shard_map/ppermute | solution.py:167
  45.5 0.0 collective-permute-done.4.refs_2_.refs_1_
  45.5 0.0 copy-done
  45.5 1.6 %pick_tiles.14 = bf16[32,64,128]{2,1,0:T(8,128)(2,1)} custom-call(s32[1]{0:T(128)} %bitcast.9.me, s32[1024]{0:T(1024)S(1)} %collective-permute-done.2.rows, bf16[64,32768]{1,0:T(8,128)(2,1)S(1)} %stage_amplitudes.1.amp, bf16[32,64,128]{2,1,0:T(8,128)(2,1)S(1)} %collective-permute-done.7.refs_0_, bf16[32,64,128]{2,1,0:T(8,128)(2,1)S(1)} %collective-permute-done.4.refs_2_.refs_1_), custom_call_target="tpu_custom_call" | custom-call | bytes 1048576 | tf_op jit(solution)/shard_map/pick_tiles/pallas_call | solution.py:62
  47.0 0.0 collective-permute-start.8
  47.0 2.2 %copy-done.1 = bf16[64,32768]{1,0:T(8,128)(2,1)S(1)} copy-done((bf16[64,32768]{1,0:T(8,128)(2,1)S(1)}, bf16[64,32768]{1,0:T(8,128)(2,1)}, u32[]{:S(2)}) %copy-start.1) | copy-done | bytes 4194328
  49.2 0.7 pick_tiles.8.refs_0_
  50.0 4.8 %compare_convert_fusion.live = f32[256]{0:T(256)S(1)} fusion(s32[256]{0:T(256)S(1)} %copy-done.4, s32[256]{0:T(256)S(1)} %copy-done.2, s32[]{:T(128)} %bitcast, s32[]{:T(128)} %bitcast.1, s32[]{:T(128)} %bitcast.2, s32[]{:T(128)} %bitcast.3, s32[]{:T(128)} %bitcast.4, s32[]{:T(128)} %bitcast.5, s32[]{:T(128)} %bitcast.6, s32[]{:T(128)} %bitcast.7, ...), kind=kLoop, calls=%fused_computation.38 | loop fusion | flops 44544 | bytes 3112 | tf_op jit(solution)/shard_map/convert_element_type | solution.py:198
  54.8 2.4 %ladder_products.5.refs_1_ = f32[32,64,128]{2,1,0:T(8,128)S(1)} custom-call(s32[8]{0:T(128)S(1)} %iota_xor_fusion.order, s32[256]{0:T(256)S(1)} %fusion.3.cols, f32[256]{0:T(256)S(1)} %compare_convert_fusion.live, bf16[8,32,128,128]{3,2,1,0:T(8,128)(2,1)} %bitcast.16, bf16[32,64,128]{2,1,0:T(8,128)(2,1)S(1)} %collective-permute-done.7.refs_0_), custom_call_target="tpu_custom_call" | custom-call | flops 67108864 | bytes 1048576 | tf_op jit(solution)/shard_map/ladder_products/pallas_call | solution.py:137
  57.1 0.0 collective-permute-done.6.refs_0_
  57.1 2.8 %ladder_products.6.refs_4_ = f32[32,64,128]{2,1,0:T(8,128)S(1)} custom-call(s32[8]{0:T(128)S(1)} %iota_xor_fusion.order, s32[256]{0:T(256)S(1)} %fusion.3.cols, f32[256]{0:T(256)S(1)} %compare_convert_fusion.live, bf16[8,32,128,128]{3,2,1,0:T(8,128)(2,1)} %bitcast.17, ...), custom_call_target="tpu_custom_call", output_to_operand_aliasing={{}: (5, {})} | custom-call | flops 67108864 | bytes 1048576 | tf_op jit(solution)/shard_map/ladder_products/pallas_call | solution.py:137
  60.0 0.0 collective-permute-done.3.refs_1_
  60.0 0.0 collective-permute-done.5.refs_3_
  60.0 4.1 %ladder_products.7 = (f32[32,64,128]{2,1,0:T(8,128)S(1)}, bf16[1,32,128,128]{3,2,1,0:T(8,128)(2,1)S(1)}) custom-call(s32[8]{0:T(128)S(1)} %iota_xor_fusion.order, s32[256]{0:T(256)S(1)} %fusion.3.cols, f32[256]{0:T(256)S(1)} %compare_convert_fusion.live, bf16[8,32,128,128]{3,2,1,0:T(8,128)(2,1)} %bitcast.18, ...), custom_call_target="tpu_custom_call", output_to_operand_aliasing={{0}: (8, {})} | custom-call | flops 268435456 | bytes 5242880 | tf_op jit(solution)/shard_map/ladder_products/pallas_call | solution.py:137
  64.1 23.0 %collective-permute-done.9.refs_0_ = bf16[32,64,128]{2,1,0:T(8,128)(2,1)} collective-permute-done((bf16[32,64,128]{2,1,0:T(8,128)(2,1)}, bf16[32,64,128]{2,1,0:T(8,128)(2,1)}, u32[]{:S(2)}, u32[]{:S(2)}) %collective-permute-start.9) | collective-permute-done | bytes 524320 | tf_op jit(solution)/shard_map/ppermute | solution.py:167
  87.1 2.8 %ladder_products.8.refs_1_ = f32[32,64,128]{2,1,0:T(8,128)S(1)} custom-call(s32[8]{0:T(128)S(1)} %iota_xor_fusion.order, s32[256]{0:T(256)S(1)} %fusion.3.cols, f32[256]{0:T(256)S(1)} %compare_convert_fusion.live, bf16[8,32,128,128]{3,2,1,0:T(8,128)(2,1)} %bitcast.19, ...), custom_call_target="tpu_custom_call", output_to_operand_aliasing={{}: (5, {})} | custom-call | flops 67108864 | bytes 1048576 | tf_op jit(solution)/shard_map/ladder_products/pallas_call | solution.py:137
  89.9 10.6 %collective-permute-done.8.refs_0_ = bf16[32,64,128]{2,1,0:T(8,128)(2,1)S(1)} collective-permute-done((bf16[32,64,128]{2,1,0:T(8,128)(2,1)}, bf16[32,64,128]{2,1,0:T(8,128)(2,1)S(1)}, u32[]{:S(2)}, u32[]{:S(2)}) %collective-permute-start.8) | collective-permute-done | bytes 524320 | tf_op jit(solution)/shard_map/ppermute | solution.py:167
  100.5 1.2 %ladder_products.9 = (f32[8,64,128]{2,1,0:T(8,128)S(1)}, f32[8,64,128]{2,1,0:T(8,128)S(1)}, f32[8,64,128]{2,1,0:T(8,128)S(1)}, f32[8,64,128]{2,1,0:T(8,128)S(1)}) custom-call(s32[8]{0:T(128)S(1)} %iota_xor_fusion.order, s32[256]{0:T(256)S(1)} %fusion.3.cols, f32[256]{0:T(256)S(1)} %compare_convert_fusion.live, ...), custom_call_target="tpu_custom_call" | custom-call | flops 67108864 | bytes 1048576 | tf_op jit(solution)/shard_map/ladder_products/pallas_call | solution.py:137
  101.7 0.1 collective-permute-start.11
  101.8 0.5 collective-permute-start.10
  102.3 1.0 collective-permute-done.11
  103.4 1.6 %collective-permute-start.12 = (f32[8,64,128]{2,1,0:T(8,128)S(1)}, f32[8,64,128]{2,1,0:T(8,128)S(1)}, u32[]{:S(2)}, u32[]{:S(2)}) collective-permute-start(f32[8,64,128]{2,1,0:T(8,128)S(1)} %add.86), channel_id=1, source_target_pairs={{0,2},{1,3},{2,0},{3,1},{4,6},{5,7},{6,4},{7,5},{8,10},{9,11},{10,... | collective-permute-start | bytes 786440 | tf_op jit(solution)/shard_map/ppermute | solution.py:221
  104.9 0.0 collective-permute-done.10
  104.9 6.9 %collective-permute-done.12 = f32[8,64,128]{2,1,0:T(8,128)S(1)} collective-permute-done((f32[8,64,128]{2,1,0:T(8,128)S(1)}, f32[8,64,128]{2,1,0:T(8,128)S(1)}, u32[]{:S(2)}, u32[]{:S(2)}) %collective-permute-start.12) | collective-permute-done | bytes 262176 | tf_op jit(solution)/shard_map/ppermute | solution.py:221
  111.8 0.7 copy_bitcast_fusion
  (13 shorter events, 0.1 us)
Async XLA Ops:
  0.0 5.5 %collective-permute-start = (s32[256]{0:T(256)}, s32[256]{0:T(256)S(1)}, u32[]{:S(2)}, u32[]{:S(2)}) collective-permute-start(s32[256]{0:T(256)} %rows.1), channel_id=1, source_target_pairs={{0,16},{4,20},{8,24},{12,28},{16,0},{20,4},{24,8},{28,12},{1,17},{... | collective-permute-start | bytes 3080 | tf_op jit(solution)/shard_map/ppermute | solution.py:167
  3.3 2.2 %copy-start.2 = (s32[256]{0:T(256)S(1)}, s32[256]{0:T(256)}, u32[]{:S(2)}) copy-start(s32[256]{0:T(256)} %rows.1) | copy-start | bytes 3076
  5.5 39.9 %copy-start = (bf16[64,32768]{1,0:T(8,128)(2,1)}, bf16[64,32768]{1,0:T(8,128)(2,1)S(1)}, u32[]{:S(2)}) copy-start(bf16[64,32768]{1,0:T(8,128)(2,1)S(1)} %stage_amplitudes.1.amp) | copy-start | bytes 12582916
  5.6 3.7 %collective-permute-start.1 = (s32[512]{0:T(512)S(1)}, s32[512]{0:T(512)S(1)}, u32[]{:S(2)}, u32[]{:S(2)}) collective-permute-start(s32[512]{0:T(512)S(1)} %pad_add_fusion), channel_id=1, source_target_pairs={{0,8},{4,12},{8,0},{12,4},{16,24},{20,28},{24,16},{28,20},{1,9},{5... | collective-permute-start | bytes 6152 | tf_op jit(solution)/shard_map/ppermute | solution.py:167
  6.1 6.5 %copy-start.3 = (s32[8]{0:T(128)S(1)}, s32[8]{0:T(128)}, u32[]{:S(2)}) copy-start(s32[8]{0:T(128)} %param.6) | copy-start | bytes 100
  6.8 26.2 %collective-permute-start.7 = (bf16[32,64,128]{2,1,0:T(8,128)(2,1)S(1)}, bf16[32,64,128]{2,1,0:T(8,128)(2,1)S(1)}, u32[]{:S(2)}, u32[]{:S(2)}) collective-permute-start(bf16[32,64,128]{2,1,0:T(8,128)(2,1)S(1)} %pick_tiles.13), channel_id=1, source_target_pairs={{0,16},{4,20},{8,24},{12,28},{16,0},{20,4},{24,8},{28,12},{1,17},{... | collective-permute-start | bytes 1572872 | tf_op jit(solution)/shard_map/ppermute | solution.py:167
  10.0 35.4 %collective-permute-start.4 = (bf16[32,64,128]{2,1,0:T(8,128)(2,1)S(1)}, bf16[32,64,128]{2,1,0:T(8,128)(2,1)S(1)}, u32[]{:S(2)}, u32[]{:S(2)}) collective-permute-start(bf16[32,64,128]{2,1,0:T(8,128)(2,1)S(1)} %pick_tiles.10), channel_id=1, source_target_pairs={{0,8},{4,12},{8,0},{12,4},{16,24},{20,28},{24,16},{28,20},{1,9},{5... | collective-permute-start | bytes 1572872 | tf_op jit(solution)/shard_map/ppermute | solution.py:167
  11.0 5.3 %collective-permute-start.2 = (s32[1024]{0:T(1024)S(1)}, s32[1024]{0:T(1024)S(1)}, u32[]{:S(2)}, u32[]{:S(2)}) collective-permute-start(s32[1024]{0:T(1024)S(1)} %constant_dynamic-update-slice_fusion.rows), channel_id=1, source_target_pairs={{0,4},{4,0},{8,12},{12,8},{16,20},{20,16},{24,28},{28,24},{1,5},{5... | collective-permute-start | bytes 12296 | tf_op jit(solution)/shard_map/ppermute | solution.py:167
  14.8 42.3 %collective-permute-start.6 = (bf16[32,64,128]{2,1,0:T(8,128)(2,1)}, bf16[32,64,128]{2,1,0:T(8,128)(2,1)}, u32[]{:S(2)}, u32[]{:S(2)}) collective-permute-start(bf16[32,64,128]{2,1,0:T(8,128)(2,1)} %pick_tiles.12), channel_id=1, source_target_pairs={{0,24},{4,28},{8,16},{12,20},{16,8},{20,12},{24,0},{28,4},{1,25},{... | collective-permute-start | bytes 1572872 | tf_op jit(solution)/shard_map/ppermute | solution.py:167
  17.9 42.1 %collective-permute-start.3 = (bf16[32,64,128]{2,1,0:T(8,128)(2,1)}, bf16[32,64,128]{2,1,0:T(8,128)(2,1)S(1)}, u32[]{:S(2)}, u32[]{:S(2)}) collective-permute-start(bf16[32,64,128]{2,1,0:T(8,128)(2,1)} %pick_tiles.9), channel_id=1, source_target_pairs={{0,4},{4,0},{8,12},{12,8},{16,20},{20,16},{24,28},{28,24},{1,5},{5... | collective-permute-start | bytes 1572872 | tf_op jit(solution)/shard_map/ppermute | solution.py:167
  20.0 40.1 %collective-permute-start.5 = (bf16[32,64,128]{2,1,0:T(8,128)(2,1)}, bf16[32,64,128]{2,1,0:T(8,128)(2,1)S(1)}, u32[]{:S(2)}, u32[]{:S(2)}) collective-permute-start(bf16[32,64,128]{2,1,0:T(8,128)(2,1)} %pick_tiles.11), channel_id=1, source_target_pairs={{0,12},{4,8},{8,4},{12,0},{16,28},{20,24},{24,20},{28,16},{1,13},{... | collective-permute-start | bytes 1572872 | tf_op jit(solution)/shard_map/ppermute | solution.py:167
  34.6 15.4 %copy-start.4 = (s32[256]{0:T(256)S(1)}, s32[256]{0:T(256)}, u32[]{:S(2)}) copy-start(s32[256]{0:T(256)} %param.9) | copy-start | bytes 3076
  34.6 52.5 %collective-permute-start.9 = (bf16[32,64,128]{2,1,0:T(8,128)(2,1)}, bf16[32,64,128]{2,1,0:T(8,128)(2,1)}, u32[]{:S(2)}, u32[]{:S(2)}) collective-permute-start(bf16[32,64,128]{2,1,0:T(8,128)(2,1)} %pick_tiles.15), channel_id=1, source_target_pairs={{0,20},{4,16},{8,28},{12,24},{16,4},{20,0},{24,12},{28,8},{1,21},{... | collective-permute-start | bytes 1572872 | tf_op jit(solution)/shard_map/ppermute | solution.py:167
  47.0 53.5 %collective-permute-start.8 = (bf16[32,64,128]{2,1,0:T(8,128)(2,1)}, bf16[32,64,128]{2,1,0:T(8,128)(2,1)S(1)}, u32[]{:S(2)}, u32[]{:S(2)}) collective-permute-start(bf16[32,64,128]{2,1,0:T(8,128)(2,1)} %pick_tiles.14), channel_id=1, source_target_pairs={{0,28},{4,24},{8,20},{12,16},{16,12},{20,8},{24,4},{28,0},{1,29},{... | collective-permute-start | bytes 1572872 | tf_op jit(solution)/shard_map/ppermute | solution.py:167
  47.0 2.2 %copy-start.1 = (bf16[64,32768]{1,0:T(8,128)(2,1)S(1)}, bf16[64,32768]{1,0:T(8,128)(2,1)}, u32[]{:S(2)}) copy-start(bf16[64,32768]{1,0:T(8,128)(2,1)} %copy-done) | copy-start | bytes 12582916
  101.7 1.6 %collective-permute-start.11 = (f32[8,64,128]{2,1,0:T(8,128)S(1)}, f32[8,64,128]{2,1,0:T(8,128)S(1)}, u32[]{:S(2)}, u32[]{:S(2)}) collective-permute-start(f32[8,64,128]{2,1,0:T(8,128)S(1)} %get-tuple-element.16), channel_id=1, source_target_pairs={{0,1},{1,0},{2,3},{3,2},{4,5},{5,4},{6,7},{7,6},{8,9},{9,8},{10,11... | collective-permute-start | bytes 786440 | tf_op jit(solution)/shard_map/ppermute | solution.py:221
  101.8 3.1 %collective-permute-start.10 = (f32[8,64,128]{2,1,0:T(8,128)S(1)}, f32[8,64,128]{2,1,0:T(8,128)S(1)}, u32[]{:S(2)}, u32[]{:S(2)}) collective-permute-start(f32[8,64,128]{2,1,0:T(8,128)S(1)} %get-tuple-element.14), channel_id=1, source_target_pairs={{0,1},{1,0},{2,3},{3,2},{4,5},{5,4},{6,7},{7,6},{8,9},{9,8},{10,11... | collective-permute-start | bytes 786440 | tf_op jit(solution)/shard_map/ppermute | solution.py:221
  103.4 8.4 %collective-permute-start.12 = (f32[8,64,128]{2,1,0:T(8,128)S(1)}, f32[8,64,128]{2,1,0:T(8,128)S(1)}, u32[]{:S(2)}, u32[]{:S(2)}) collective-permute-start(f32[8,64,128]{2,1,0:T(8,128)S(1)} %add.86), channel_id=1, source_target_pairs={{0,2},{1,3},{2,0},{3,1},{4,6},{5,7},{6,4},{7,5},{8,10},{9,11},{10,... | collective-permute-start | bytes 786440 | tf_op jit(solution)/shard_map/ppermute | solution.py:221

commit v12 on v11

--- a/solution.py
+++ b/solution.py
@@ -11,7 +11,8 @@
 BLK = 128
 ABT_X = 32
 CORES = 2
-UNROLL = 16
+UNROLL = 32
+CODE_TOP = 32000.0
 MIB = 1024 * 1024
 
 VMEM_SPEC = pl.BlockSpec(memory_space=pltpu.VMEM)
@@ -153,6 +154,66 @@
     )(order, cols, live, w, *pieces, *([] if first else [start]))
 
 
+def encode_kernel(kept, got, *outs):
+    share = outs[0].shape[0] - 1
+    lane = lax.broadcasted_iota(jnp.int32, kept.shape[1:], 1)
+    for b, out in enumerate(outs):
+        powers = jnp.zeros(kept.shape[1:], jnp.int32)
+        for j in range(share):
+            value = kept[b * share + j] + got[b * share + j]
+            top = jnp.max(jnp.abs(value), axis=1, keepdims=True)
+            power = jnp.ceil(jnp.log2(jnp.maximum(top, 2.0**-100)))
+            code = jnp.round(value * (jnp.exp2(-power) * CODE_TOP))
+            out[j] = code.astype(jnp.int32).astype(jnp.int16)
+            powers = jnp.where(lane == j, power.astype(jnp.int32), powers)
+        out[share] = powers.astype(jnp.int16)
+
+
+def encode(kept, got, parts):
+    tiles, occupied, _ = kept.shape
+    shape = jax.ShapeDtypeStruct((tiles // parts + 1, occupied, BLK), jnp.int16)
+    return pl.pallas_call(
+        encode_kernel,
+        out_shape=[shape] * parts,
+        in_specs=[VMEM_SPEC] * 2,
+        out_specs=[VMEM_SPEC] * parts,
+        compiler_params=pltpu.CompilerParams(vmem_limit_bytes=8 * MIB),
+        cost_estimate=pl.CostEstimate(
+            flops=8 * kept.size, bytes_accessed=10 * kept.size, transcendentals=0
+        ),
+        name="encode_sums",
+    )(kept, got)
+
+
+def decode_kernel(kept, got, *refs):
+    arrived, out = refs[:-1], refs[-1]
+    share = kept.shape[0]
+    lane = lax.broadcasted_iota(jnp.int32, kept.shape[1:], 1)
+    for j in range(share):
+        value = kept[j] + got[j]
+        for part in arrived:
+            powers = jnp.where(lane == j, part[share].astype(jnp.int32), 0)
+            power = jnp.sum(powers.astype(jnp.float32), axis=1, keepdims=True)
+            code = part[j].astype(jnp.int32).astype(jnp.float32)
+            value = value + code * (jnp.exp2(power) * (1.0 / CODE_TOP))
+        out[:, j * BLK : (j + 1) * BLK] = value
+
+
+def decode(kept, got, arrived):
+    share, occupied, _ = kept.shape
+    return pl.pallas_call(
+        decode_kernel,
+        out_shape=jax.ShapeDtypeStruct((occupied, share * BLK), jnp.float32),
+        in_specs=[VMEM_SPEC] * (2 + len(arrived)),
+        out_specs=VMEM_SPEC,
+        compiler_params=pltpu.CompilerParams(vmem_limit_bytes=8 * MIB),
+        cost_estimate=pl.CostEstimate(
+            flops=8 * kept.size, bytes_accessed=14 * kept.size, transcendentals=0
+        ),
+        name="decode_sums",
+    )(kept, got, *arrived)
+
+
 def per_device(amplitudes, virt_irreps, w_tiles, tile_rows, tile_cols):
     occupied = amplitudes.shape[0]
     peers = lax.axis_size("gx")
@@ -220,11 +281,9 @@
     def swap_gy(x, k):
         return lax.ppermute(x, "gy", [(i, i ^ k) for i in range(groups)])
 
-    rest = (keep_rest + swap_gy(give_rest, 1)).reshape(xs - 1, share, occupied, BLK)
-    result = keep + swap_gy(give, 1)
-    for k in range(1, xs):
-        result = result + swap_gy(rest[k - 1], k * CORES)
-    return jnp.transpose(result, (1, 0, 2)).reshape(occupied, share * BLK)
+    coded = encode(keep_rest, swap_gy(give_rest, 1), xs - 1)
+    got = swap_gy(give, 1)
+    return decode(keep, got, [swap_gy(coded[k - 1], k * CORES) for k in range(1, xs)])
 
 
 def solution(mesh):

time: 113 us -> 111 us (0.982)
  waiting for transfers between devices: 53.1 us -> 51.6 us
    ppermute x3, waiting for transfers between devices: 7.88 us -> 5.42 us  [swap_gy(): return lax.ppermute(x, 'gy', [(i, i ^ k) for i in range(groups)])]
  transfers between devices with their start and end apart: 13 -> 13, of which waited for: 6 -> 6; matrix products, arithmetic and copies ran while one was open for 6% -> 6% of each run, Pallas kernels for 22% -> 21%
where the time goes in v12:
time: 111 us; the launch traced here: 110 us
  waiting for transfers between devices  51.6 us (46%)
  Pallas kernels  25.5 us (23%)
  starting transfers between devices  24.5 us (22%)
  other arithmetic  4.81 us (4%)
  local copies, waits for them, and re-layouts  3.6 us (3%)
    ppermute x10, waiting for transfers between devices, swap(): return lax.ppermute(x, 'gx', [(i, i ^ k) for i in range(peers)])  46.2 us
    ppermute x10, starting transfers between devices, swap(): return lax.ppermute(x, 'gx', [(i, i ^ k) for i in range(peers)])  22.4 us
    pallas_call x5, Pallas kernels, ladder(): pl.pallas_call(functools.partial(ladder_kernel, peers_at, list(ahead), pe...  12.2 us
    pallas_call x8, Pallas kernels, pick(): pl.pallas_call(functools.partial(pick_kernel, first, per, width // BLK),...  10 us
    ppermute x3, waiting for transfers between devices, swap_gy(): return lax.ppermute(x, 'gy', [(i, i ^ k) for i in range(groups)])  5.42 us
    convert_element_type x1, other arithmetic, per_device(): (pair_irrep(row_tile, virt_irreps) == pair_irrep(col_tile, virt_irreps))....  4.77 us
    unnamed x12, local copies, waits for them, and re-layouts  2.92 us
  transfers between devices with their start and end apart: 13, of which 6 were waited for; matrix products, arithmetic and copies ran while one was open for 6% of the time, Pallas kernels for 21%

profile of v12, /device:TPU:8, one launch (start us, length us, event | category | flops | bytes accessed | tf_op | source)
XLA Modules:
  0.0 110.2 jit_solution(5099295697247023877)
XLA Ops:
  0.0 2.6 %collective-permute-start = (s32[256]{0:T(256)}, s32[256]{0:T(256)S(1)}, u32[]{:S(2)}, u32[]{:S(2)}) collective-permute-start(s32[256]{0:T(256)} %rows.1), channel_id=1, source_target_pairs={{0,16},{4,20},{8,24},{12,28},{16,0},{20,4},{24,8},{28,12},{1,17},{... | collective-permute-start | bytes 3080 | tf_op jit(solution)/shard_map/ppermute | solution.py:228
  2.6 0.7 constant_dynamic-update-slice_fusion.2
  3.3 2.2 %stage_amplitudes.1.amp = bf16[64,32768]{1,0:T(8,128)(2,1)S(1)} custom-call(bf16[64,32768]{1,0:T(8,128)(2,1)} %source.1), custom_call_target="tpu_custom_call" | custom-call | bytes 4194304 | tf_op jit(solution)/shard_map/stage_amplitudes/pallas_call | solution.py:36
  5.5 0.0 collective-permute-done.rows
  5.5 0.0 copy-done.2
  5.6 0.5 collective-permute-start.1
  6.1 0.7 pick_tiles.13
  6.8 1.8 %collective-permute-start.7 = (bf16[32,64,128]{2,1,0:T(8,128)(2,1)S(1)}, bf16[32,64,128]{2,1,0:T(8,128)(2,1)S(1)}, u32[]{:S(2)}, u32[]{:S(2)}) collective-permute-start(bf16[32,64,128]{2,1,0:T(8,128)(2,1)S(1)} %pick_tiles.13), channel_id=1, source_target_pairs={{0,16},{4,20},{8,24},{12,28},{16,0},{20,4},{24,8},{28,12},{1,17},{... | collective-permute-start | bytes 1572872 | tf_op jit(solution)/shard_map/ppermute | solution.py:228
  8.6 0.7 collective-permute-done.1
  9.2 0.8 pick_tiles.10
  10.0 1.0 collective-permute-start.4
  11.0 1.5 %collective-permute-start.2 = (s32[1024]{0:T(1024)S(1)}, s32[1024]{0:T(1024)S(1)}, u32[]{:S(2)}, u32[]{:S(2)}) collective-permute-start(s32[1024]{0:T(1024)S(1)} %constant_dynamic-update-slice_fusion.rows), channel_id=1, source_target_pairs={{0,4},{4,0},{8,12},{12,8},{16,20},{20,16},{24,28},{28,24},{1,5},{5... | collective-permute-start | bytes 12296 | tf_op jit(solution)/shard_map/ppermute | solution.py:228
  12.5 0.0 copy-done.3
  12.5 0.7 fusion.4
  13.2 1.6 %pick_tiles.12 = bf16[32,64,128]{2,1,0:T(8,128)(2,1)} custom-call(s32[1]{0:T(128)} %bitcast.9.me, s32[1024]{0:T(1024)S(1)} %constant_dynamic-update-slice_fusion.rows, bf16[64,32768]{1,0:T(8,128)(2,1)S(1)} %stage_amplitudes.1.amp), custom_call_target="tpu_custom_call" | custom-call | bytes 1048576 | tf_op jit(solution)/shard_map/pick_tiles/pallas_call | solution.py:63
  14.8 1.5 %collective-permute-start.6 = (bf16[32,64,128]{2,1,0:T(8,128)(2,1)}, bf16[32,64,128]{2,1,0:T(8,128)(2,1)}, u32[]{:S(2)}, u32[]{:S(2)}) collective-permute-start(bf16[32,64,128]{2,1,0:T(8,128)(2,1)} %pick_tiles.12), channel_id=1, source_target_pairs={{0,24},{4,28},{8,16},{12,20},{16,8},{20,12},{24,0},{28,4},{1,25},{... | collective-permute-start | bytes 1572872 | tf_op jit(solution)/shard_map/ppermute | solution.py:228
  16.3 0.0 collective-permute-done.2.rows
  16.3 1.6 %pick_tiles.9 = bf16[32,64,128]{2,1,0:T(8,128)(2,1)} custom-call(s32[1]{0:T(128)} %bitcast.9.me, s32[1024]{0:T(1024)S(1)} %collective-permute-done.2.rows, bf16[64,32768]{1,0:T(8,128)(2,1)S(1)} %stage_amplitudes.1.amp), custom_call_target="tpu_custom_call" | custom-call | bytes 1048576 | tf_op jit(solution)/shard_map/pick_tiles/pallas_call | solution.py:63
  17.9 0.5 collective-permute-start.3
  18.4 1.6 %pick_tiles.11 = bf16[32,64,128]{2,1,0:T(8,128)(2,1)} custom-call(s32[1]{0:T(128)} %bitcast.9.me, s32[1024]{0:T(1024)S(1)} %collective-permute-done.2.rows, bf16[64,32768]{1,0:T(8,128)(2,1)S(1)} %stage_amplitudes.1.amp), custom_call_target="tpu_custom_call" | custom-call | bytes 1048576 | tf_op jit(solution)/shard_map/pick_tiles/pallas_call | solution.py:63
  20.0 2.1 %collective-permute-start.5 = (bf16[32,64,128]{2,1,0:T(8,128)(2,1)}, bf16[32,64,128]{2,1,0:T(8,128)(2,1)S(1)}, u32[]{:S(2)}, u32[]{:S(2)}) collective-permute-start(bf16[32,64,128]{2,1,0:T(8,128)(2,1)} %pick_tiles.11), channel_id=1, source_target_pairs={{0,12},{4,8},{8,4},{12,0},{16,28},{20,24},{24,20},{28,16},{1,13},{... | collective-permute-start | bytes 1572872 | tf_op jit(solution)/shard_map/ppermute | solution.py:228
  22.1 11.0 %collective-permute-done.7.refs_0_ = bf16[32,64,128]{2,1,0:T(8,128)(2,1)S(1)} collective-permute-done((bf16[32,64,128]{2,1,0:T(8,128)(2,1)S(1)}, bf16[32,64,128]{2,1,0:T(8,128)(2,1)S(1)}, u32[]{:S(2)}, u32[]{:S(2)}) %collective-permute-start.7) | collective-permute-done | bytes 524320 | tf_op jit(solution)/shard_map/ppermute | solution.py:228
  33.0 1.6 %pick_tiles.15 = bf16[32,64,128]{2,1,0:T(8,128)(2,1)} custom-call(s32[1]{0:T(128)} %bitcast.9.me, s32[1024]{0:T(1024)S(1)} %collective-permute-done.2.rows, bf16[64,32768]{1,0:T(8,128)(2,1)S(1)} %stage_amplitudes.1.amp, bf16[32,64,128]{2,1,0:T(8,128)(2,1)S(1)} %collective-permute-done.7.refs_0_), custom_call_target="tpu_custom_call" | custom-call | bytes 1048576 | tf_op jit(solution)/shard_map/pick_tiles/pallas_call | solution.py:63
  34.6 10.8 %collective-permute-start.9 = (bf16[32,64,128]{2,1,0:T(8,128)(2,1)}, bf16[32,64,128]{2,1,0:T(8,128)(2,1)}, u32[]{:S(2)}, u32[]{:S(2)}) collective-permute-start(bf16[32,64,128]{2,1,0:T(8,128)(2,1)} %pick_tiles.15), channel_id=1, source_target_pairs={{0,20},{4,16},{8,28},{12,24},{16,4},{20,0},{24,12},{28,8},{1,21},{... | collective-permute-start | bytes 1572872 | tf_op jit(solution)/shard_map/ppermute | solution.py:228
  45.5 0.0 collective-permute-done.4.refs_2_.refs_1_
  45.5 1.6 %pick_tiles.14 = bf16[32,64,128]{2,1,0:T(8,128)(2,1)} custom-call(s32[1]{0:T(128)} %bitcast.9.me, s32[1024]{0:T(1024)S(1)} %collective-permute-done.2.rows, bf16[64,32768]{1,0:T(8,128)(2,1)S(1)} %stage_amplitudes.1.amp, bf16[32,64,128]{2,1,0:T(8,128)(2,1)S(1)} %collective-permute-done.7.refs_0_, bf16[32,64,128]{2,1,0:T(8,128)(2,1)S(1)} %collective-permute-done.4.refs_2_.refs_1_), custom_call_target="tpu_custom_call" | custom-call | bytes 1048576 | tf_op jit(solution)/shard_map/pick_tiles/pallas_call | solution.py:63
  47.0 0.0 collective-permute-start.8
  47.0 2.2 %copy-done.1 = bf16[64,32768]{1,0:T(8,128)(2,1)S(1)} copy-done((bf16[64,32768]{1,0:T(8,128)(2,1)S(1)}, bf16[64,32768]{1,0:T(8,128)(2,1)}, u32[]{:S(2)}) %copy-start.1) | copy-done | bytes 4194328
  49.2 0.7 pick_tiles.8.refs_0_
  50.0 4.8 %compare_convert_fusion.live = f32[256]{0:T(256)S(1)} fusion(s32[256]{0:T(256)S(1)} %copy-done.4, s32[256]{0:T(256)S(1)} %copy-done.2, s32[]{:T(128)} %bitcast, s32[]{:T(128)} %bitcast.1, s32[]{:T(128)} %bitcast.2, s32[]{:T(128)} %bitcast.3, s32[]{:T(128)} %bitcast.4, s32[]{:T(128)} %bitcast.5, s32[]{:T(128)} %bitcast.6, s32[]{:T(128)} %bitcast.7, ...), kind=kLoop, calls=%fused_computation.36 | loop fusion | flops 44544 | bytes 3112 | tf_op jit(solution)/shard_map/convert_element_type | solution.py:259
  54.8 2.2 %ladder_products.5.refs_1_ = f32[32,64,128]{2,1,0:T(8,128)S(1)} custom-call(s32[8]{0:T(128)S(1)} %iota_xor_fusion.order, s32[256]{0:T(256)S(1)} %fusion.3.cols, f32[256]{0:T(256)S(1)} %compare_convert_fusion.live, bf16[8,32,128,128]{3,2,1,0:T(8,128)(2,1)} %bitcast.10, bf16[32,64,128]{2,1,0:T(8,128)(2,1)S(1)} %collective-permute-done.7.refs_0_), custom_call_target="tpu_custom_call" | custom-call | flops 67108864 | bytes 1048576 | tf_op jit(solution)/shard_map/ladder_products/pallas_call | solution.py:138
  57.0 0.0 collective-permute-done.6.refs_0_
  57.0 2.7 %ladder_products.6.refs_4_ = f32[32,64,128]{2,1,0:T(8,128)S(1)} custom-call(s32[8]{0:T(128)S(1)} %iota_xor_fusion.order, s32[256]{0:T(256)S(1)} %fusion.3.cols, f32[256]{0:T(256)S(1)} %compare_convert_fusion.live, bf16[8,32,128,128]{3,2,1,0:T(8,128)(2,1)} %bitcast.11, ...), custom_call_target="tpu_custom_call", output_to_operand_aliasing={{}: (5, {})} | custom-call | flops 67108864 | bytes 1048576 | tf_op jit(solution)/shard_map/ladder_products/pallas_call | solution.py:138
  59.7 0.0 collective-permute-done.3.refs_1_
  59.7 0.0 collective-permute-done.5.refs_3_
  59.8 3.5 %ladder_products.7 = (f32[32,64,128]{2,1,0:T(8,128)S(1)}, bf16[1,32,128,128]{3,2,1,0:T(8,128)(2,1)S(1)}) custom-call(s32[8]{0:T(128)S(1)} %iota_xor_fusion.order, s32[256]{0:T(256)S(1)} %fusion.3.cols, f32[256]{0:T(256)S(1)} %compare_convert_fusion.live, bf16[8,32,128,128]{3,2,1,0:T(8,128)(2,1)} %bitcast.12, ...), custom_call_target="tpu_custom_call", output_to_operand_aliasing={{0}: (8, {})} | custom-call | flops 268435456 | bytes 5242880 | tf_op jit(solution)/shard_map/ladder_products/pallas_call | solution.py:138
  63.3 23.8 %collective-permute-done.9.refs_0_ = bf16[32,64,128]{2,1,0:T(8,128)(2,1)} collective-permute-done((bf16[32,64,128]{2,1,0:T(8,128)(2,1)}, bf16[32,64,128]{2,1,0:T(8,128)(2,1)}, u32[]{:S(2)}, u32[]{:S(2)}) %collective-permute-start.9) | collective-permute-done | bytes 524320 | tf_op jit(solution)/shard_map/ppermute | solution.py:228
  87.1 2.7 %ladder_products.8.refs_1_ = f32[32,64,128]{2,1,0:T(8,128)S(1)} custom-call(s32[8]{0:T(128)S(1)} %iota_xor_fusion.order, s32[256]{0:T(256)S(1)} %fusion.3.cols, f32[256]{0:T(256)S(1)} %compare_convert_fusion.live, bf16[8,32,128,128]{3,2,1,0:T(8,128)(2,1)} %bitcast.13, ...), custom_call_target="tpu_custom_call", output_to_operand_aliasing={{}: (5, {})} | custom-call | flops 67108864 | bytes 1048576 | tf_op jit(solution)/shard_map/ladder_products/pallas_call | solution.py:138
  89.8 10.7 %collective-permute-done.8.refs_0_ = bf16[32,64,128]{2,1,0:T(8,128)(2,1)S(1)} collective-permute-done((bf16[32,64,128]{2,1,0:T(8,128)(2,1)}, bf16[32,64,128]{2,1,0:T(8,128)(2,1)S(1)}, u32[]{:S(2)}, u32[]{:S(2)}) %collective-permute-start.8) | collective-permute-done | bytes 524320 | tf_op jit(solution)/shard_map/ppermute | solution.py:228
  100.5 1.1 ladder_products.9
  101.6 0.1 collective-permute-start.11
  101.7 0.5 collective-permute-start.10
  102.2 1.0 collective-permute-done.11.got
  103.2 0.2 encode_sums.1
  103.4 1.6 %collective-permute-start.12 = (s16[9,64,128]{2,1,0:T(8,128)(2,1)S(1)}, s16[9,64,128]{2,1,0:T(8,128)(2,1)S(1)}, u32[]{:S(2)}, u32[]{:S(2)}) collective-permute-start(s16[9,64,128]{2,1,0:T(8,128)(2,1)S(1)} %encode_sums.1), channel_id=1, source_target_pairs={{0,2},{1,3},{2,0},{3,1},{4,6},{5,7},{6,4},{7,5},{8,10},{9,11},{10,... | collective-permute-start | bytes 442376 | tf_op jit(solution)/shard_map/ppermute | solution.py:282
  104.9 0.0 collective-permute-done.10.got
  105.0 4.4 %collective-permute-done.12.refs_0_ = s16[9,64,128]{2,1,0:T(8,128)(2,1)S(1)} collective-permute-done((s16[9,64,128]{2,1,0:T(8,128)(2,1)S(1)}, s16[9,64,128]{2,1,0:T(8,128)(2,1)S(1)}, u32[]{:S(2)}, u32[]{:S(2)}) %collective-permute-start.12) | collective-permute-done | bytes 147488 | tf_op jit(solution)/shard_map/ppermute | solution.py:282
  109.3 0.9 decode_sums.1
  (13 shorter events, 0.1 us)
Async XLA Ops:
  0.0 5.5 %collective-permute-start = (s32[256]{0:T(256)}, s32[256]{0:T(256)S(1)}, u32[]{:S(2)}, u32[]{:S(2)}) collective-permute-start(s32[256]{0:T(256)} %rows.1), channel_id=1, source_target_pairs={{0,16},{4,20},{8,24},{12,28},{16,0},{20,4},{24,8},{28,12},{1,17},{... | collective-permute-start | bytes 3080 | tf_op jit(solution)/shard_map/ppermute | solution.py:228
  3.3 2.2 %copy-start.2 = (s32[256]{0:T(256)S(1)}, s32[256]{0:T(256)}, u32[]{:S(2)}) copy-start(s32[256]{0:T(256)} %rows.1) | copy-start | bytes 3076
  5.5 39.9 %copy-start = (bf16[64,32768]{1,0:T(8,128)(2,1)}, bf16[64,32768]{1,0:T(8,128)(2,1)S(1)}, u32[]{:S(2)}) copy-start(bf16[64,32768]{1,0:T(8,128)(2,1)S(1)} %stage_amplitudes.1.amp) | copy-start | bytes 12582916
  5.6 3.7 %collective-permute-start.1 = (s32[512]{0:T(512)S(1)}, s32[512]{0:T(512)S(1)}, u32[]{:S(2)}, u32[]{:S(2)}) collective-permute-start(s32[512]{0:T(512)S(1)} %pad_add_fusion), channel_id=1, source_target_pairs={{0,8},{4,12},{8,0},{12,4},{16,24},{20,28},{24,16},{28,20},{1,9},{5... | collective-permute-start | bytes 6152 | tf_op jit(solution)/shard_map/ppermute | solution.py:228
  6.1 6.5 %copy-start.3 = (s32[8]{0:T(128)S(1)}, s32[8]{0:T(128)}, u32[]{:S(2)}) copy-start(s32[8]{0:T(128)} %param.6) | copy-start | bytes 100
  6.8 26.2 %collective-permute-start.7 = (bf16[32,64,128]{2,1,0:T(8,128)(2,1)S(1)}, bf16[32,64,128]{2,1,0:T(8,128)(2,1)S(1)}, u32[]{:S(2)}, u32[]{:S(2)}) collective-permute-start(bf16[32,64,128]{2,1,0:T(8,128)(2,1)S(1)} %pick_tiles.13), channel_id=1, source_target_pairs={{0,16},{4,20},{8,24},{12,28},{16,0},{20,4},{24,8},{28,12},{1,17},{... | collective-permute-start | bytes 1572872 | tf_op jit(solution)/shard_map/ppermute | solution.py:228
  10.0 35.4 %collective-permute-start.4 = (bf16[32,64,128]{2,1,0:T(8,128)(2,1)S(1)}, bf16[32,64,128]{2,1,0:T(8,128)(2,1)S(1)}, u32[]{:S(2)}, u32[]{:S(2)}) collective-permute-start(bf16[32,64,128]{2,1,0:T(8,128)(2,1)S(1)} %pick_tiles.10), channel_id=1, source_target_pairs={{0,8},{4,12},{8,0},{12,4},{16,24},{20,28},{24,16},{28,20},{1,9},{5... | collective-permute-start | bytes 1572872 | tf_op jit(solution)/shard_map/ppermute | solution.py:228
  11.0 5.3 %collective-permute-start.2 = (s32[1024]{0:T(1024)S(1)}, s32[1024]{0:T(1024)S(1)}, u32[]{:S(2)}, u32[]{:S(2)}) collective-permute-start(s32[1024]{0:T(1024)S(1)} %constant_dynamic-update-slice_fusion.rows), channel_id=1, source_target_pairs={{0,4},{4,0},{8,12},{12,8},{16,20},{20,16},{24,28},{28,24},{1,5},{5... | collective-permute-start | bytes 12296 | tf_op jit(solution)/shard_map/ppermute | solution.py:228
  14.8 42.2 %collective-permute-start.6 = (bf16[32,64,128]{2,1,0:T(8,128)(2,1)}, bf16[32,64,128]{2,1,0:T(8,128)(2,1)}, u32[]{:S(2)}, u32[]{:S(2)}) collective-permute-start(bf16[32,64,128]{2,1,0:T(8,128)(2,1)} %pick_tiles.12), channel_id=1, source_target_pairs={{0,24},{4,28},{8,16},{12,20},{16,8},{20,12},{24,0},{28,4},{1,25},{... | collective-permute-start | bytes 1572872 | tf_op jit(solution)/shard_map/ppermute | solution.py:228
  17.9 41.8 %collective-permute-start.3 = (bf16[32,64,128]{2,1,0:T(8,128)(2,1)}, bf16[32,64,128]{2,1,0:T(8,128)(2,1)S(1)}, u32[]{:S(2)}, u32[]{:S(2)}) collective-permute-start(bf16[32,64,128]{2,1,0:T(8,128)(2,1)} %pick_tiles.9), channel_id=1, source_target_pairs={{0,4},{4,0},{8,12},{12,8},{16,20},{20,16},{24,28},{28,24},{1,5},{5... | collective-permute-start | bytes 1572872 | tf_op jit(solution)/shard_map/ppermute | solution.py:228
  20.0 39.8 %collective-permute-start.5 = (bf16[32,64,128]{2,1,0:T(8,128)(2,1)}, bf16[32,64,128]{2,1,0:T(8,128)(2,1)S(1)}, u32[]{:S(2)}, u32[]{:S(2)}) collective-permute-start(bf16[32,64,128]{2,1,0:T(8,128)(2,1)} %pick_tiles.11), channel_id=1, source_target_pairs={{0,12},{4,8},{8,4},{12,0},{16,28},{20,24},{24,20},{28,16},{1,13},{... | collective-permute-start | bytes 1572872 | tf_op jit(solution)/shard_map/ppermute | solution.py:228
  34.6 15.4 %copy-start.4 = (s32[256]{0:T(256)S(1)}, s32[256]{0:T(256)}, u32[]{:S(2)}) copy-start(s32[256]{0:T(256)} %param.9) | copy-start | bytes 3076
  34.6 52.5 %collective-permute-start.9 = (bf16[32,64,128]{2,1,0:T(8,128)(2,1)}, bf16[32,64,128]{2,1,0:T(8,128)(2,1)}, u32[]{:S(2)}, u32[]{:S(2)}) collective-permute-start(bf16[32,64,128]{2,1,0:T(8,128)(2,1)} %pick_tiles.15), channel_id=1, source_target_pairs={{0,20},{4,16},{8,28},{12,24},{16,4},{20,0},{24,12},{28,8},{1,21},{... | collective-permute-start | bytes 1572872 | tf_op jit(solution)/shard_map/ppermute | solution.py:228
  47.0 53.5 %collective-permute-start.8 = (bf16[32,64,128]{2,1,0:T(8,128)(2,1)}, bf16[32,64,128]{2,1,0:T(8,128)(2,1)S(1)}, u32[]{:S(2)}, u32[]{:S(2)}) collective-permute-start(bf16[32,64,128]{2,1,0:T(8,128)(2,1)} %pick_tiles.14), channel_id=1, source_target_pairs={{0,28},{4,24},{8,20},{12,16},{16,12},{20,8},{24,4},{28,0},{1,29},{... | collective-permute-start | bytes 1572872 | tf_op jit(solution)/shard_map/ppermute | solution.py:228
  47.0 2.2 %copy-start.1 = (bf16[64,32768]{1,0:T(8,128)(2,1)S(1)}, bf16[64,32768]{1,0:T(8,128)(2,1)}, u32[]{:S(2)}) copy-start(bf16[64,32768]{1,0:T(8,128)(2,1)} %copy-done) | copy-start | bytes 12582916
  101.6 1.6 %collective-permute-start.11 = (f32[8,64,128]{2,1,0:T(8,128)S(1)}, f32[8,64,128]{2,1,0:T(8,128)S(1)}, u32[]{:S(2)}, u32[]{:S(2)}) collective-permute-start(f32[8,64,128]{2,1,0:T(8,128)S(1)} %get-tuple-element.16), channel_id=1, source_target_pairs={{0,1},{1,0},{2,3},{3,2},{4,5},{5,4},{6,7},{7,6},{8,9},{9,8},{10,11... | collective-permute-start | bytes 786440 | tf_op jit(solution)/shard_map/ppermute | solution.py:282
  101.7 3.3 %collective-permute-start.10 = (f32[8,64,128]{2,1,0:T(8,128)S(1)}, f32[8,64,128]{2,1,0:T(8,128)S(1)}, u32[]{:S(2)}, u32[]{:S(2)}) collective-permute-start(f32[8,64,128]{2,1,0:T(8,128)S(1)} %get-tuple-element.14), channel_id=1, source_target_pairs={{0,1},{1,0},{2,3},{3,2},{4,5},{5,4},{6,7},{7,6},{8,9},{9,8},{10,11... | collective-permute-start | bytes 786440 | tf_op jit(solution)/shard_map/ppermute | solution.py:282
  103.4 6.0 %collective-permute-start.12 = (s16[9,64,128]{2,1,0:T(8,128)(2,1)S(1)}, s16[9,64,128]{2,1,0:T(8,128)(2,1)S(1)}, u32[]{:S(2)}, u32[]{:S(2)}) collective-permute-start(s16[9,64,128]{2,1,0:T(8,128)(2,1)S(1)} %encode_sums.1), channel_id=1, source_target_pairs={{0,2},{1,3},{2,0},{3,1},{4,6},{5,7},{6,4},{7,5},{8,10},{9,11},{10,... | collective-permute-start | bytes 442376 | tf_op jit(solution)/shard_map/ppermute | solution.py:282

commit v13 on v12

--- a/solution.py
+++ b/solution.py
@@ -13,6 +13,7 @@
 CORES = 2
 UNROLL = 32
 CODE_TOP = 32000.0
+STAGE_ROWS = 16
 MIB = 1024 * 1024
 
 VMEM_SPEC = pl.BlockSpec(memory_space=pltpu.VMEM)
@@ -26,19 +27,24 @@
     return jnp.bitwise_xor(virt_irreps[first], virt_irreps[second])
 
 
-def stage_kernel(source, held, sem):
-    copy = pltpu.make_async_copy(source, held, sem)
-    copy.start()
-    copy.wait()
+def stage_kernel(rows, source, held, sems):
+    copies = []
+    for j in range(held.shape[0] // rows):
+        part = pl.ds(j * rows, rows)
+        copies.append(pltpu.make_async_copy(source.at[part], held.at[part], sems.at[j]))
+        copies[-1].start()
+    for copy in copies:
+        copy.wait()
 
 
 def stage(x):
-    return pl.pallas_call(
-        stage_kernel,
+    rows = STAGE_ROWS if x.shape[0] % STAGE_ROWS == 0 else x.shape[0]
+    return pl.pallas_call(
+        functools.partial(stage_kernel, rows),
         out_shape=pltpu.VMEM(x.shape, x.dtype),
         in_specs=[ANY_SPEC],
         out_specs=VMEM_SPEC,
-        scratch_shapes=[pltpu.SemaphoreType.DMA],
+        scratch_shapes=[pltpu.SemaphoreType.DMA((x.shape[0] // rows,))],
         compiler_params=pltpu.CompilerParams(vmem_limit_bytes=8 * MIB),
         cost_estimate=pl.CostEstimate(flops=0, bytes_accessed=2 * x.size, transcendentals=0),
         name="stage_amplitudes",

time: 111 us -> 111 us (level)
  no operation moved by 1% of the time
where the time goes in v13:
time: 111 us; the launch traced here: 110 us
  waiting for transfers between devices  51.6 us (46%)
  Pallas kernels  25.5 us (23%)
  starting transfers between devices  24.5 us (22%)
  other arithmetic  4.81 us (4%)
  local copies, waits for them, and re-layouts  3.6 us (3%)
    ppermute x10, waiting for transfers between devices, swap(): return lax.ppermute(x, 'gx', [(i, i ^ k) for i in range(peers)])  46.2 us
    ppermute x10, starting transfers between devices, swap(): return lax.ppermute(x, 'gx', [(i, i ^ k) for i in range(peers)])  22.4 us
    pallas_call x5, Pallas kernels, ladder(): pl.pallas_call(functools.partial(ladder_kernel, peers_at, list(ahead), pe...  12.2 us
    pallas_call x8, Pallas kernels, pick(): pl.pallas_call(functools.partial(pick_kernel, first, per, width // BLK),...  10 us
    ppermute x3, waiting for transfers between devices, swap_gy(): return lax.ppermute(x, 'gy', [(i, i ^ k) for i in range(groups)])  5.43 us
    convert_element_type x1, other arithmetic, per_device(): (pair_irrep(row_tile, virt_irreps) == pair_irrep(col_tile, virt_irreps))....  4.77 us
    unnamed x12, local copies, waits for them, and re-layouts  2.92 us
  transfers between devices with their start and end apart: 13, of which 6 were waited for; matrix products, arithmetic and copies ran while one was open for 6% of the time, Pallas kernels for 21%

profile of v13, /device:TPU:8, one launch (start us, length us, event | category | flops | bytes accessed | tf_op | source)
XLA Modules:
  0.0 110.2 jit_solution(14020097816954785914)
XLA Ops:
  0.0 2.6 %collective-permute-start = (s32[256]{0:T(256)}, s32[256]{0:T(256)S(1)}, u32[]{:S(2)}, u32[]{:S(2)}) collective-permute-start(s32[256]{0:T(256)} %rows.1), channel_id=1, source_target_pairs={{0,16},{4,20},{8,24},{12,28},{16,0},{20,4},{24,8},{28,12},{1,17},{... | collective-permute-start | bytes 3080 | tf_op jit(solution)/shard_map/ppermute | solution.py:234
  2.6 0.7 constant_dynamic-update-slice_fusion.2
  3.3 2.2 %stage_amplitudes.1.amp = bf16[64,32768]{1,0:T(8,128)(2,1)S(1)} custom-call(bf16[64,32768]{1,0:T(8,128)(2,1)} %source.1), custom_call_target="tpu_custom_call" | custom-call | bytes 4194304 | tf_op jit(solution)/shard_map/stage_amplitudes/pallas_call | solution.py:42
  5.5 0.0 copy-start
  5.5 0.0 collective-permute-done.rows
  5.6 0.5 collective-permute-start.1
  6.1 0.7 pick_tiles.13
  6.8 1.8 %collective-permute-start.7 = (bf16[32,64,128]{2,1,0:T(8,128)(2,1)S(1)}, bf16[32,64,128]{2,1,0:T(8,128)(2,1)S(1)}, u32[]{:S(2)}, u32[]{:S(2)}) collective-permute-start(bf16[32,64,128]{2,1,0:T(8,128)(2,1)S(1)} %pick_tiles.13), channel_id=1, source_target_pairs={{0,16},{4,20},{8,24},{12,28},{16,0},{20,4},{24,8},{28,12},{1,17},{... | collective-permute-start | bytes 1572872 | tf_op jit(solution)/shard_map/ppermute | solution.py:234
  8.6 0.7 collective-permute-done.1
  9.3 0.8 pick_tiles.10
  10.0 1.0 collective-permute-start.4
  11.0 1.5 %collective-permute-start.2 = (s32[1024]{0:T(1024)S(1)}, s32[1024]{0:T(1024)S(1)}, u32[]{:S(2)}, u32[]{:S(2)}) collective-permute-start(s32[1024]{0:T(1024)S(1)} %constant_dynamic-update-slice_fusion.rows), channel_id=1, source_target_pairs={{0,4},{4,0},{8,12},{12,8},{16,20},{20,16},{24,28},{28,24},{1,5},{5... | collective-permute-start | bytes 12296 | tf_op jit(solution)/shard_map/ppermute | solution.py:234
  12.5 0.0 copy-done.3
  12.5 0.7 fusion.4
  13.2 1.6 %pick_tiles.12 = bf16[32,64,128]{2,1,0:T(8,128)(2,1)} custom-call(s32[1]{0:T(128)} %bitcast.9.me, s32[1024]{0:T(1024)S(1)} %constant_dynamic-update-slice_fusion.rows, bf16[64,32768]{1,0:T(8,128)(2,1)S(1)} %stage_amplitudes.1.amp), custom_call_target="tpu_custom_call" | custom-call | bytes 1048576 | tf_op jit(solution)/shard_map/pick_tiles/pallas_call | solution.py:69
  14.8 1.5 %collective-permute-start.6 = (bf16[32,64,128]{2,1,0:T(8,128)(2,1)}, bf16[32,64,128]{2,1,0:T(8,128)(2,1)}, u32[]{:S(2)}, u32[]{:S(2)}) collective-permute-start(bf16[32,64,128]{2,1,0:T(8,128)(2,1)} %pick_tiles.12), channel_id=1, source_target_pairs={{0,24},{4,28},{8,16},{12,20},{16,8},{20,12},{24,0},{28,4},{1,25},{... | collective-permute-start | bytes 1572872 | tf_op jit(solution)/shard_map/ppermute | solution.py:234
  16.3 0.0 collective-permute-done.2.rows
  16.3 1.6 %pick_tiles.9 = bf16[32,64,128]{2,1,0:T(8,128)(2,1)} custom-call(s32[1]{0:T(128)} %bitcast.9.me, s32[1024]{0:T(1024)S(1)} %collective-permute-done.2.rows, bf16[64,32768]{1,0:T(8,128)(2,1)S(1)} %stage_amplitudes.1.amp), custom_call_target="tpu_custom_call" | custom-call | bytes 1048576 | tf_op jit(solution)/shard_map/pick_tiles/pallas_call | solution.py:69
  17.9 0.5 collective-permute-start.3
  18.4 1.6 %pick_tiles.11 = bf16[32,64,128]{2,1,0:T(8,128)(2,1)} custom-call(s32[1]{0:T(128)} %bitcast.9.me, s32[1024]{0:T(1024)S(1)} %collective-permute-done.2.rows, bf16[64,32768]{1,0:T(8,128)(2,1)S(1)} %stage_amplitudes.1.amp), custom_call_target="tpu_custom_call" | custom-call | bytes 1048576 | tf_op jit(solution)/shard_map/pick_tiles/pallas_call | solution.py:69
  20.0 2.1 %collective-permute-start.5 = (bf16[32,64,128]{2,1,0:T(8,128)(2,1)}, bf16[32,64,128]{2,1,0:T(8,128)(2,1)S(1)}, u32[]{:S(2)}, u32[]{:S(2)}) collective-permute-start(bf16[32,64,128]{2,1,0:T(8,128)(2,1)} %pick_tiles.11), channel_id=1, source_target_pairs={{0,12},{4,8},{8,4},{12,0},{16,28},{20,24},{24,20},{28,16},{1,13},{... | collective-permute-start | bytes 1572872 | tf_op jit(solution)/shard_map/ppermute | solution.py:234
  22.1 11.0 %collective-permute-done.7.refs_0_ = bf16[32,64,128]{2,1,0:T(8,128)(2,1)S(1)} collective-permute-done((bf16[32,64,128]{2,1,0:T(8,128)(2,1)S(1)}, bf16[32,64,128]{2,1,0:T(8,128)(2,1)S(1)}, u32[]{:S(2)}, u32[]{:S(2)}) %collective-permute-start.7) | collective-permute-done | bytes 524320 | tf_op jit(solution)/shard_map/ppermute | solution.py:234
  33.0 1.6 %pick_tiles.15 = bf16[32,64,128]{2,1,0:T(8,128)(2,1)} custom-call(s32[1]{0:T(128)} %bitcast.9.me, s32[1024]{0:T(1024)S(1)} %collective-permute-done.2.rows, bf16[64,32768]{1,0:T(8,128)(2,1)S(1)} %stage_amplitudes.1.amp, bf16[32,64,128]{2,1,0:T(8,128)(2,1)S(1)} %collective-permute-done.7.refs_0_), custom_call_target="tpu_custom_call" | custom-call | bytes 1048576 | tf_op jit(solution)/shard_map/pick_tiles/pallas_call | solution.py:69
  34.6 10.8 %collective-permute-start.9 = (bf16[32,64,128]{2,1,0:T(8,128)(2,1)}, bf16[32,64,128]{2,1,0:T(8,128)(2,1)}, u32[]{:S(2)}, u32[]{:S(2)}) collective-permute-start(bf16[32,64,128]{2,1,0:T(8,128)(2,1)} %pick_tiles.15), channel_id=1, source_target_pairs={{0,20},{4,16},{8,28},{12,24},{16,4},{20,0},{24,12},{28,8},{1,21},{... | collective-permute-start | bytes 1572872 | tf_op jit(solution)/shard_map/ppermute | solution.py:234
  45.5 0.0 collective-permute-done.4.refs_2_.refs_1_
  45.5 1.6 %pick_tiles.14 = bf16[32,64,128]{2,1,0:T(8,128)(2,1)} custom-call(s32[1]{0:T(128)} %bitcast.9.me, s32[1024]{0:T(1024)S(1)} %collective-permute-done.2.rows, bf16[64,32768]{1,0:T(8,128)(2,1)S(1)} %stage_amplitudes.1.amp, bf16[32,64,128]{2,1,0:T(8,128)(2,1)S(1)} %collective-permute-done.7.refs_0_, bf16[32,64,128]{2,1,0:T(8,128)(2,1)S(1)} %collective-permute-done.4.refs_2_.refs_1_), custom_call_target="tpu_custom_call" | custom-call | bytes 1048576 | tf_op jit(solution)/shard_map/pick_tiles/pallas_call | solution.py:69
  47.0 0.0 collective-permute-start.8
  47.0 2.2 %copy-done.1 = bf16[64,32768]{1,0:T(8,128)(2,1)S(1)} copy-done((bf16[64,32768]{1,0:T(8,128)(2,1)S(1)}, bf16[64,32768]{1,0:T(8,128)(2,1)}, u32[]{:S(2)}) %copy-start.1) | copy-done | bytes 4194328
  49.2 0.7 pick_tiles.8.refs_0_
  50.0 4.8 %compare_convert_fusion.live = f32[256]{0:T(256)S(1)} fusion(s32[256]{0:T(256)S(1)} %copy-done.4, s32[256]{0:T(256)S(1)} %copy-done.2, s32[]{:T(128)} %bitcast, s32[]{:T(128)} %bitcast.1, s32[]{:T(128)} %bitcast.2, s32[]{:T(128)} %bitcast.3, s32[]{:T(128)} %bitcast.4, s32[]{:T(128)} %bitcast.5, s32[]{:T(128)} %bitcast.6, s32[]{:T(128)} %bitcast.7, ...), kind=kLoop, calls=%fused_computation.36 | loop fusion | flops 44544 | bytes 3112 | tf_op jit(solution)/shard_map/convert_element_type | solution.py:265
  54.8 2.2 %ladder_products.5.refs_1_ = f32[32,64,128]{2,1,0:T(8,128)S(1)} custom-call(s32[8]{0:T(128)S(1)} %iota_xor_fusion.order, s32[256]{0:T(256)S(1)} %fusion.3.cols, f32[256]{0:T(256)S(1)} %compare_convert_fusion.live, bf16[8,32,128,128]{3,2,1,0:T(8,128)(2,1)} %bitcast.10, bf16[32,64,128]{2,1,0:T(8,128)(2,1)S(1)} %collective-permute-done.7.refs_0_), custom_call_target="tpu_custom_call" | custom-call | flops 67108864 | bytes 1048576 | tf_op jit(solution)/shard_map/ladder_products/pallas_call | solution.py:144
  57.0 0.0 collective-permute-done.6.refs_0_
  57.0 2.7 %ladder_products.6.refs_4_ = f32[32,64,128]{2,1,0:T(8,128)S(1)} custom-call(s32[8]{0:T(128)S(1)} %iota_xor_fusion.order, s32[256]{0:T(256)S(1)} %fusion.3.cols, f32[256]{0:T(256)S(1)} %compare_convert_fusion.live, bf16[8,32,128,128]{3,2,1,0:T(8,128)(2,1)} %bitcast.11, ...), custom_call_target="tpu_custom_call", output_to_operand_aliasing={{}: (5, {})} | custom-call | flops 67108864 | bytes 1048576 | tf_op jit(solution)/shard_map/ladder_products/pallas_call | solution.py:144
  59.7 0.0 collective-permute-done.3.refs_1_
  59.8 0.0 collective-permute-done.5.refs_3_
  59.8 3.5 %ladder_products.7 = (f32[32,64,128]{2,1,0:T(8,128)S(1)}, bf16[1,32,128,128]{3,2,1,0:T(8,128)(2,1)S(1)}) custom-call(s32[8]{0:T(128)S(1)} %iota_xor_fusion.order, s32[256]{0:T(256)S(1)} %fusion.3.cols, f32[256]{0:T(256)S(1)} %compare_convert_fusion.live, bf16[8,32,128,128]{3,2,1,0:T(8,128)(2,1)} %bitcast.12, ...), custom_call_target="tpu_custom_call", output_to_operand_aliasing={{0}: (8, {})} | custom-call | flops 268435456 | bytes 5242880 | tf_op jit(solution)/shard_map/ladder_products/pallas_call | solution.py:144
  63.3 23.8 %collective-permute-done.9.refs_0_ = bf16[32,64,128]{2,1,0:T(8,128)(2,1)} collective-permute-done((bf16[32,64,128]{2,1,0:T(8,128)(2,1)}, bf16[32,64,128]{2,1,0:T(8,128)(2,1)}, u32[]{:S(2)}, u32[]{:S(2)}) %collective-permute-start.9) | collective-permute-done | bytes 524320 | tf_op jit(solution)/shard_map/ppermute | solution.py:234
  87.1 2.7 %ladder_products.8.refs_1_ = f32[32,64,128]{2,1,0:T(8,128)S(1)} custom-call(s32[8]{0:T(128)S(1)} %iota_xor_fusion.order, s32[256]{0:T(256)S(1)} %fusion.3.cols, f32[256]{0:T(256)S(1)} %compare_convert_fusion.live, bf16[8,32,128,128]{3,2,1,0:T(8,128)(2,1)} %bitcast.13, ...), custom_call_target="tpu_custom_call", output_to_operand_aliasing={{}: (5, {})} | custom-call | flops 67108864 | bytes 1048576 | tf_op jit(solution)/shard_map/ladder_products/pallas_call | solution.py:144
  89.8 10.7 %collective-permute-done.8.refs_0_ = bf16[32,64,128]{2,1,0:T(8,128)(2,1)S(1)} collective-permute-done((bf16[32,64,128]{2,1,0:T(8,128)(2,1)}, bf16[32,64,128]{2,1,0:T(8,128)(2,1)S(1)}, u32[]{:S(2)}, u32[]{:S(2)}) %collective-permute-start.8) | collective-permute-done | bytes 524320 | tf_op jit(solution)/shard_map/ppermute | solution.py:234
  100.5 1.1 ladder_products.9
  101.6 0.1 collective-permute-start.11
  101.7 0.5 collective-permute-start.10
  102.2 1.0 collective-permute-done.11.got
  103.2 0.2 encode_sums.1
  103.4 1.6 %collective-permute-start.12 = (s16[9,64,128]{2,1,0:T(8,128)(2,1)S(1)}, s16[9,64,128]{2,1,0:T(8,128)(2,1)S(1)}, u32[]{:S(2)}, u32[]{:S(2)}) collective-permute-start(s16[9,64,128]{2,1,0:T(8,128)(2,1)S(1)} %encode_sums.1), channel_id=1, source_target_pairs={{0,2},{1,3},{2,0},{3,1},{4,6},{5,7},{6,4},{7,5},{8,10},{9,11},{10,... | collective-permute-start | bytes 442376 | tf_op jit(solution)/shard_map/ppermute | solution.py:288
  105.0 0.0 collective-permute-done.10.got
  105.0 4.4 %collective-permute-done.12.refs_0_ = s16[9,64,128]{2,1,0:T(8,128)(2,1)S(1)} collective-permute-done((s16[9,64,128]{2,1,0:T(8,128)(2,1)S(1)}, s16[9,64,128]{2,1,0:T(8,128)(2,1)S(1)}, u32[]{:S(2)}, u32[]{:S(2)}) %collective-permute-start.12) | collective-permute-done | bytes 147488 | tf_op jit(solution)/shard_map/ppermute | solution.py:288
  109.4 0.9 decode_sums.1
  (13 shorter events, 0.1 us)
Async XLA Ops:
  0.0 5.5 %collective-permute-start = (s32[256]{0:T(256)}, s32[256]{0:T(256)S(1)}, u32[]{:S(2)}, u32[]{:S(2)}) collective-permute-start(s32[256]{0:T(256)} %rows.1), channel_id=1, source_target_pairs={{0,16},{4,20},{8,24},{12,28},{16,0},{20,4},{24,8},{28,12},{1,17},{... | collective-permute-start | bytes 3080 | tf_op jit(solution)/shard_map/ppermute | solution.py:234
  3.3 2.3 %copy-start.2 = (s32[256]{0:T(256)S(1)}, s32[256]{0:T(256)}, u32[]{:S(2)}) copy-start(s32[256]{0:T(256)} %rows.1) | copy-start | bytes 3076
  5.5 39.9 %copy-start = (bf16[64,32768]{1,0:T(8,128)(2,1)}, bf16[64,32768]{1,0:T(8,128)(2,1)S(1)}, u32[]{:S(2)}) copy-start(bf16[64,32768]{1,0:T(8,128)(2,1)S(1)} %stage_amplitudes.1.amp) | copy-start | bytes 12582916
  5.6 3.7 %collective-permute-start.1 = (s32[512]{0:T(512)S(1)}, s32[512]{0:T(512)S(1)}, u32[]{:S(2)}, u32[]{:S(2)}) collective-permute-start(s32[512]{0:T(512)S(1)} %pad_add_fusion), channel_id=1, source_target_pairs={{0,8},{4,12},{8,0},{12,4},{16,24},{20,28},{24,16},{28,20},{1,9},{5... | collective-permute-start | bytes 6152 | tf_op jit(solution)/shard_map/ppermute | solution.py:234
  6.1 6.4 %copy-start.3 = (s32[8]{0:T(128)S(1)}, s32[8]{0:T(128)}, u32[]{:S(2)}) copy-start(s32[8]{0:T(128)} %param.6) | copy-start | bytes 100
  6.8 26.2 %collective-permute-start.7 = (bf16[32,64,128]{2,1,0:T(8,128)(2,1)S(1)}, bf16[32,64,128]{2,1,0:T(8,128)(2,1)S(1)}, u32[]{:S(2)}, u32[]{:S(2)}) collective-permute-start(bf16[32,64,128]{2,1,0:T(8,128)(2,1)S(1)} %pick_tiles.13), channel_id=1, source_target_pairs={{0,16},{4,20},{8,24},{12,28},{16,0},{20,4},{24,8},{28,12},{1,17},{... | collective-permute-start | bytes 1572872 | tf_op jit(solution)/shard_map/ppermute | solution.py:234
  10.0 35.4 %collective-permute-start.4 = (bf16[32,64,128]{2,1,0:T(8,128)(2,1)S(1)}, bf16[32,64,128]{2,1,0:T(8,128)(2,1)S(1)}, u32[]{:S(2)}, u32[]{:S(2)}) collective-permute-start(bf16[32,64,128]{2,1,0:T(8,128)(2,1)S(1)} %pick_tiles.10), channel_id=1, source_target_pairs={{0,8},{4,12},{8,0},{12,4},{16,24},{20,28},{24,16},{28,20},{1,9},{5... | collective-permute-start | bytes 1572872 | tf_op jit(solution)/shard_map/ppermute | solution.py:234
  11.0 5.3 %collective-permute-start.2 = (s32[1024]{0:T(1024)S(1)}, s32[1024]{0:T(1024)S(1)}, u32[]{:S(2)}, u32[]{:S(2)}) collective-permute-start(s32[1024]{0:T(1024)S(1)} %constant_dynamic-update-slice_fusion.rows), channel_id=1, source_target_pairs={{0,4},{4,0},{8,12},{12,8},{16,20},{20,16},{24,28},{28,24},{1,5},{5... | collective-permute-start | bytes 12296 | tf_op jit(solution)/shard_map/ppermute | solution.py:234
  14.8 42.2 %collective-permute-start.6 = (bf16[32,64,128]{2,1,0:T(8,128)(2,1)}, bf16[32,64,128]{2,1,0:T(8,128)(2,1)}, u32[]{:S(2)}, u32[]{:S(2)}) collective-permute-start(bf16[32,64,128]{2,1,0:T(8,128)(2,1)} %pick_tiles.12), channel_id=1, source_target_pairs={{0,24},{4,28},{8,16},{12,20},{16,8},{20,12},{24,0},{28,4},{1,25},{... | collective-permute-start | bytes 1572872 | tf_op jit(solution)/shard_map/ppermute | solution.py:234
  17.9 41.9 %collective-permute-start.3 = (bf16[32,64,128]{2,1,0:T(8,128)(2,1)}, bf16[32,64,128]{2,1,0:T(8,128)(2,1)S(1)}, u32[]{:S(2)}, u32[]{:S(2)}) collective-permute-start(bf16[32,64,128]{2,1,0:T(8,128)(2,1)} %pick_tiles.9), channel_id=1, source_target_pairs={{0,4},{4,0},{8,12},{12,8},{16,20},{20,16},{24,28},{28,24},{1,5},{5... | collective-permute-start | bytes 1572872 | tf_op jit(solution)/shard_map/ppermute | solution.py:234
  20.0 39.8 %collective-permute-start.5 = (bf16[32,64,128]{2,1,0:T(8,128)(2,1)}, bf16[32,64,128]{2,1,0:T(8,128)(2,1)S(1)}, u32[]{:S(2)}, u32[]{:S(2)}) collective-permute-start(bf16[32,64,128]{2,1,0:T(8,128)(2,1)} %pick_tiles.11), channel_id=1, source_target_pairs={{0,12},{4,8},{8,4},{12,0},{16,28},{20,24},{24,20},{28,16},{1,13},{... | collective-permute-start | bytes 1572872 | tf_op jit(solution)/shard_map/ppermute | solution.py:234
  34.6 15.4 %copy-start.4 = (s32[256]{0:T(256)S(1)}, s32[256]{0:T(256)}, u32[]{:S(2)}) copy-start(s32[256]{0:T(256)} %param.9) | copy-start | bytes 3076
  34.6 52.5 %collective-permute-start.9 = (bf16[32,64,128]{2,1,0:T(8,128)(2,1)}, bf16[32,64,128]{2,1,0:T(8,128)(2,1)}, u32[]{:S(2)}, u32[]{:S(2)}) collective-permute-start(bf16[32,64,128]{2,1,0:T(8,128)(2,1)} %pick_tiles.15), channel_id=1, source_target_pairs={{0,20},{4,16},{8,28},{12,24},{16,4},{20,0},{24,12},{28,8},{1,21},{... | collective-permute-start | bytes 1572872 | tf_op jit(solution)/shard_map/ppermute | solution.py:234
  47.0 53.5 %collective-permute-start.8 = (bf16[32,64,128]{2,1,0:T(8,128)(2,1)}, bf16[32,64,128]{2,1,0:T(8,128)(2,1)S(1)}, u32[]{:S(2)}, u32[]{:S(2)}) collective-permute-start(bf16[32,64,128]{2,1,0:T(8,128)(2,1)} %pick_tiles.14), channel_id=1, source_target_pairs={{0,28},{4,24},{8,20},{12,16},{16,12},{20,8},{24,4},{28,0},{1,29},{... | collective-permute-start | bytes 1572872 | tf_op jit(solution)/shard_map/ppermute | solution.py:234
  47.0 2.2 %copy-start.1 = (bf16[64,32768]{1,0:T(8,128)(2,1)S(1)}, bf16[64,32768]{1,0:T(8,128)(2,1)}, u32[]{:S(2)}) copy-start(bf16[64,32768]{1,0:T(8,128)(2,1)} %copy-done) | copy-start | bytes 12582916
  101.6 1.6 %collective-permute-start.11 = (f32[8,64,128]{2,1,0:T(8,128)S(1)}, f32[8,64,128]{2,1,0:T(8,128)S(1)}, u32[]{:S(2)}, u32[]{:S(2)}) collective-permute-start(f32[8,64,128]{2,1,0:T(8,128)S(1)} %get-tuple-element.16), channel_id=1, source_target_pairs={{0,1},{1,0},{2,3},{3,2},{4,5},{5,4},{6,7},{7,6},{8,9},{9,8},{10,11... | collective-permute-start | bytes 786440 | tf_op jit(solution)/shard_map/ppermute | solution.py:288
  101.7 3.3 %collective-permute-start.10 = (f32[8,64,128]{2,1,0:T(8,128)S(1)}, f32[8,64,128]{2,1,0:T(8,128)S(1)}, u32[]{:S(2)}, u32[]{:S(2)}) collective-permute-start(f32[8,64,128]{2,1,0:T(8,128)S(1)} %get-tuple-element.14), channel_id=1, source_target_pairs={{0,1},{1,0},{2,3},{3,2},{4,5},{5,4},{6,7},{7,6},{8,9},{9,8},{10,11... | collective-permute-start | bytes 786440 | tf_op jit(solution)/shard_map/ppermute | solution.py:288
  103.4 6.0 %collective-permute-start.12 = (s16[9,64,128]{2,1,0:T(8,128)(2,1)S(1)}, s16[9,64,128]{2,1,0:T(8,128)(2,1)S(1)}, u32[]{:S(2)}, u32[]{:S(2)}) collective-permute-start(s16[9,64,128]{2,1,0:T(8,128)(2,1)S(1)} %encode_sums.1), channel_id=1, source_target_pairs={{0,2},{1,3},{2,0},{3,1},{4,6},{5,7},{6,4},{7,5},{8,10},{9,11},{10,... | collective-permute-start | bytes 442376 | tf_op jit(solution)/shard_map/ppermute | solution.py:288

commit v14 on v12

--- a/solution.py
+++ b/solution.py
@@ -26,23 +26,53 @@
     return jnp.bitwise_xor(virt_irreps[first], virt_irreps[second])
 
 
-def stage_kernel(source, held, sem):
+def stage_kernel(source, *refs):
+    held, sem = refs[-2:]
     copy = pltpu.make_async_copy(source, held, sem)
     copy.start()
     copy.wait()
 
 
-def stage(x):
+def stage(x, after):
     return pl.pallas_call(
         stage_kernel,
         out_shape=pltpu.VMEM(x.shape, x.dtype),
-        in_specs=[ANY_SPEC],
+        in_specs=[ANY_SPEC] * (1 + len(after)),
         out_specs=VMEM_SPEC,
         scratch_shapes=[pltpu.SemaphoreType.DMA],
         compiler_params=pltpu.CompilerParams(vmem_limit_bytes=8 * MIB),
         cost_estimate=pl.CostEstimate(flops=0, bytes_accessed=2 * x.size, transcendentals=0),
         name="stage_amplitudes",
-    )(pltpu.with_memory_space_constraint(x, pltpu.HBM))
+    )(pltpu.with_memory_space_constraint(x, pltpu.HBM), *after)
+
+
+def fetch_kernel(first, per, local_tiles, me, rows, amp, out, sem):
+    base = first + me[0] * per
+    origin = me[0] * local_tiles
+
+    def start(i, carry):
+        lane = pl.multiple_of((rows[base + i] - origin) * BLK, BLK)
+        pltpu.make_async_copy(amp.at[:, pl.ds(lane, BLK)], out.at[i], sem).start()
+        return carry
+
+    lax.fori_loop(0, per, start, 0, unroll=8)
+    pltpu.make_async_copy(out, out, sem).wait()
+
+
+def fetch(me, rows, first, amp, per):
+    occupied, width = amp.shape
+    return pl.pallas_call(
+        functools.partial(fetch_kernel, first, per, width // BLK),
+        out_shape=pltpu.VMEM((per, occupied, BLK), amp.dtype),
+        in_specs=[SMEM_SPEC, SMEM_SPEC, ANY_SPEC],
+        out_specs=VMEM_SPEC,
+        scratch_shapes=[pltpu.SemaphoreType.DMA],
+        compiler_params=pltpu.CompilerParams(vmem_limit_bytes=8 * MIB),
+        cost_estimate=pl.CostEstimate(
+            flops=0, bytes_accessed=4 * per * occupied * BLK, transcendentals=0
+        ),
+        name="fetch_tiles",
+    )(me, rows, pltpu.with_memory_space_constraint(amp, pltpu.HBM))
 
 
 def pick_kernel(first, per, local_tiles, me, rows, amp, *refs):
@@ -240,13 +270,14 @@
         place.setdefault(k, (rows, j * slots))
         place[k ^ 1] = (odd, j * slots)
 
-    amp = stage(amplitudes)
     here = me.reshape(1)
+    fetched = fetch(here, *place[near], amplitudes, per)
+    amp = stage(amplitudes, (fetched,))
     quarter = near // 4
     far_order = list(range(near, peers, 2)) + list(range(near + 1, peers, 2))
     far = [far_order[j * quarter : (j + 1) * quarter] for j in range(4)]
-    arrived = {0: pick(here, tile_rows, 0, amp, per)}
-    for k in far[0] + far[1] + list(range(1, near)) + far[2] + far[3]:
+    arrived = {0: pick(here, tile_rows, 0, amp, per), near: swap(fetched, near)}
+    for k in far[0][1:] + far[1] + list(range(1, near)) + far[2] + far[3]:
         after = ()
         if k in far[2]:
             after = (arrived[far[0][far[2].index(k)]],)

time: 111 us -> 111 us (level)
  waiting for transfers between devices: 51.6 us -> 49.3 us
    ppermute x10, waiting for transfers between devices: 46.2 us -> 43.9 us  [swap(): return lax.ppermute(x, 'gx', [(i, i ^ k) for i in range(peers)])]
    pallas_call x0 -> x1, Pallas kernels: none -> 1.58 us  [fetch(): pl.pallas_call(functools.partial(fetch_kernel, first, per, width // BLK),...]
    pallas_call x8 -> x7, Pallas kernels: 10 us -> 9.3 us  [pick(): pl.pallas_call(functools.partial(pick_kernel, first, per, width // BLK),...]
  transfers between devices with their start and end apart: 13 -> 13, of which waited for: 6 -> 7; matrix products, arithmetic and copies ran while one was open for 6% -> 6% of each run, Pallas kernels for 21% -> 22%
where the time goes in v14:
time: 111 us; the launch traced here: 110 us
  waiting for transfers between devices  49.3 us (44%)
  Pallas kernels  25.9 us (23%)
  starting transfers between devices  25.1 us (23%)
  other arithmetic  5.85 us (5%)
  local copies, waits for them, and re-layouts  3.6 us (3%)
    ppermute x10, waiting for transfers between devices, swap(): return lax.ppermute(x, 'gx', [(i, i ^ k) for i in range(peers)])  43.9 us
    ppermute x10, starting transfers between devices, swap(): return lax.ppermute(x, 'gx', [(i, i ^ k) for i in range(peers)])  23 us
    pallas_call x5, Pallas kernels, ladder(): pl.pallas_call(functools.partial(ladder_kernel, peers_at, list(ahead), pe...  11.8 us
    pallas_call x7, Pallas kernels, pick(): pl.pallas_call(functools.partial(pick_kernel, first, per, width // BLK),...  9.3 us
    ppermute x3, waiting for transfers between devices, swap_gy(): return lax.ppermute(x, 'gy', [(i, i ^ k) for i in range(groups)])  5.42 us
    convert_element_type x1, other arithmetic, per_device(): (pair_irrep(row_tile, virt_irreps) == pair_irrep(col_tile, virt_irreps))....  5.13 us
    unnamed x12, local copies, waits for them, and re-layouts  2.92 us
  transfers between devices with their start and end apart: 13, of which 7 were waited for; matrix products, arithmetic and copies ran while one was open for 6% of the time, Pallas kernels for 22%

profile of v14, /device:TPU:8, one launch (start us, length us, event | category | flops | bytes accessed | tf_op | source)
XLA Modules:
  0.0 110.0 jit_solution(8119007345796248442)
XLA Ops:
  0.0 2.6 %collective-permute-start = (s32[256]{0:T(256)}, s32[256]{0:T(256)S(1)}, u32[]{:S(2)}, u32[]{:S(2)}) collective-permute-start(s32[256]{0:T(256)} %rows.1), channel_id=1, source_target_pairs={{0,16},{4,20},{8,24},{12,28},{16,0},{20,4},{24,8},{28,12},{1,17},{... | collective-permute-start | bytes 3080 | tf_op jit(solution)/shard_map/ppermute | solution.py:258
  2.6 0.7 constant_dynamic-update-slice_fusion.2
  3.3 1.4 %collective-permute-done.rows = s32[256]{0:T(256)S(1)} collective-permute-done((s32[256]{0:T(256)}, s32[256]{0:T(256)S(1)}, u32[]{:S(2)}, u32[]{:S(2)}) %collective-permute-start) | collective-permute-done | bytes 1056 | tf_op jit(solution)/shard_map/ppermute | solution.py:258
  4.7 0.7 pad_add_fusion
  5.4 0.1 collective-permute-start.1
  5.5 1.6 %fetch_tiles.1.refs_0_ = bf16[32,64,128]{2,1,0:T(8,128)(2,1)S(1)} custom-call(s32[1]{0:T(128)} %bitcast.9.me, s32[256]{0:T(256)S(1)} %collective-permute-done.rows, bf16[64,32768]{1,0:T(8,128)(2,1)} %source.1), custom_call_target="tpu_custom_call" | custom-call | bytes 1048576 | tf_op jit(solution)/shard_map/fetch_tiles/pallas_call | solution.py:64
  7.1 3.0 %collective-permute-start.7 = (bf16[32,64,128]{2,1,0:T(8,128)(2,1)S(1)}, bf16[32,64,128]{2,1,0:T(8,128)(2,1)S(1)}, u32[]{:S(2)}, u32[]{:S(2)}) collective-permute-start(bf16[32,64,128]{2,1,0:T(8,128)(2,1)S(1)} %fetch_tiles.1.refs_0_), channel_id=1, source_target_pairs={{0,16},{4,20},{8,24},{12,28},{16,0},{20,4},{24,8},{28,12},{1,17},{... | collective-permute-start | bytes 1572872 | tf_op jit(solution)/shard_map/ppermute | solution.py:258
  10.1 2.2 %stage_amplitudes.1.amp = bf16[64,32768]{1,0:T(8,128)(2,1)S(1)} custom-call(bf16[64,32768]{1,0:T(8,128)(2,1)} %source.1, bf16[32,64,128]{2,1,0:T(8,128)(2,1)S(1)} %fetch_tiles.1.refs_0_), custom_call_target="tpu_custom_call" | custom-call | bytes 4194304 | tf_op jit(solution)/shard_map/stage_amplitudes/pallas_call | solution.py:37
  12.3 0.0 copy-start.3
  12.3 0.0 collective-permute-done.1
  12.3 0.8 pick_tiles.9
  13.1 1.6 %collective-permute-start.4 = (bf16[32,64,128]{2,1,0:T(8,128)(2,1)S(1)}, bf16[32,64,128]{2,1,0:T(8,128)(2,1)S(1)}, u32[]{:S(2)}, u32[]{:S(2)}) collective-permute-start(bf16[32,64,128]{2,1,0:T(8,128)(2,1)S(1)} %pick_tiles.9), channel_id=1, source_target_pairs={{0,8},{4,12},{8,0},{12,4},{16,24},{20,28},{24,16},{28,20},{1,9},{5... | collective-permute-start | bytes 1572872 | tf_op jit(solution)/shard_map/ppermute | solution.py:258
  14.7 1.5 %collective-permute-start.2 = (s32[1024]{0:T(1024)S(1)}, s32[1024]{0:T(1024)S(1)}, u32[]{:S(2)}, u32[]{:S(2)}) collective-permute-start(s32[1024]{0:T(1024)S(1)} %constant_dynamic-update-slice_fusion.rows), channel_id=1, source_target_pairs={{0,4},{4,0},{8,12},{12,8},{16,20},{20,16},{24,28},{28,24},{1,5},{5... | collective-permute-start | bytes 12296 | tf_op jit(solution)/shard_map/ppermute | solution.py:258
  16.3 0.7 fusion.4
  16.9 1.6 %pick_tiles.11 = bf16[32,64,128]{2,1,0:T(8,128)(2,1)} custom-call(s32[1]{0:T(128)} %bitcast.9.me, s32[1024]{0:T(1024)S(1)} %constant_dynamic-update-slice_fusion.rows, bf16[64,32768]{1,0:T(8,128)(2,1)S(1)} %stage_amplitudes.1.amp), custom_call_target="tpu_custom_call" | custom-call | bytes 1048576 | tf_op jit(solution)/shard_map/pick_tiles/pallas_call | solution.py:93
  18.5 0.0 collective-permute-start.6
  18.5 0.0 collective-permute-done.2.rows
  18.5 1.6 %pick_tiles.8 = bf16[32,64,128]{2,1,0:T(8,128)(2,1)} custom-call(s32[1]{0:T(128)} %bitcast.9.me, s32[1024]{0:T(1024)S(1)} %collective-permute-done.2.rows, bf16[64,32768]{1,0:T(8,128)(2,1)S(1)} %stage_amplitudes.1.amp), custom_call_target="tpu_custom_call" | custom-call | bytes 1048576 | tf_op jit(solution)/shard_map/pick_tiles/pallas_call | solution.py:93
  20.1 1.3 %collective-permute-start.3 = (bf16[32,64,128]{2,1,0:T(8,128)(2,1)}, bf16[32,64,128]{2,1,0:T(8,128)(2,1)S(1)}, u32[]{:S(2)}, u32[]{:S(2)}) collective-permute-start(bf16[32,64,128]{2,1,0:T(8,128)(2,1)} %pick_tiles.8), channel_id=1, source_target_pairs={{0,4},{4,0},{8,12},{12,8},{16,20},{20,16},{24,28},{28,24},{1,5},{5... | collective-permute-start | bytes 1572872 | tf_op jit(solution)/shard_map/ppermute | solution.py:258
  21.4 1.6 %pick_tiles.10 = bf16[32,64,128]{2,1,0:T(8,128)(2,1)} custom-call(s32[1]{0:T(128)} %bitcast.9.me, s32[1024]{0:T(1024)S(1)} %collective-permute-done.2.rows, bf16[64,32768]{1,0:T(8,128)(2,1)S(1)} %stage_amplitudes.1.amp), custom_call_target="tpu_custom_call" | custom-call | bytes 1048576 | tf_op jit(solution)/shard_map/pick_tiles/pallas_call | solution.py:93
  23.0 1.9 %collective-permute-start.5 = (bf16[32,64,128]{2,1,0:T(8,128)(2,1)}, bf16[32,64,128]{2,1,0:T(8,128)(2,1)S(1)}, u32[]{:S(2)}, u32[]{:S(2)}) collective-permute-start(bf16[32,64,128]{2,1,0:T(8,128)(2,1)} %pick_tiles.10), channel_id=1, source_target_pairs={{0,12},{4,8},{8,4},{12,0},{16,28},{20,24},{24,20},{28,16},{1,13},{... | collective-permute-start | bytes 1572872 | tf_op jit(solution)/shard_map/ppermute | solution.py:258
  24.9 9.6 %collective-permute-done.7.refs_0_ = bf16[32,64,128]{2,1,0:T(8,128)(2,1)S(1)} collective-permute-done((bf16[32,64,128]{2,1,0:T(8,128)(2,1)S(1)}, bf16[32,64,128]{2,1,0:T(8,128)(2,1)S(1)}, u32[]{:S(2)}, u32[]{:S(2)}) %collective-permute-start.7) | collective-permute-done | bytes 524320 | tf_op jit(solution)/shard_map/ppermute | solution.py:258
  34.5 1.6 %pick_tiles.13 = bf16[32,64,128]{2,1,0:T(8,128)(2,1)} custom-call(s32[1]{0:T(128)} %bitcast.9.me, s32[1024]{0:T(1024)S(1)} %collective-permute-done.2.rows, bf16[64,32768]{1,0:T(8,128)(2,1)S(1)} %stage_amplitudes.1.amp, bf16[32,64,128]{2,1,0:T(8,128)(2,1)S(1)} %collective-permute-done.7.refs_0_), custom_call_target="tpu_custom_call" | custom-call | bytes 1048576 | tf_op jit(solution)/shard_map/pick_tiles/pallas_call | solution.py:93
  36.1 10.8 %collective-permute-start.9 = (bf16[32,64,128]{2,1,0:T(8,128)(2,1)}, bf16[32,64,128]{2,1,0:T(8,128)(2,1)}, u32[]{:S(2)}, u32[]{:S(2)}) collective-permute-start(bf16[32,64,128]{2,1,0:T(8,128)(2,1)} %pick_tiles.13), channel_id=1, source_target_pairs={{0,20},{4,16},{8,28},{12,24},{16,4},{20,0},{24,12},{28,8},{1,21},{... | collective-permute-start | bytes 1572872 | tf_op jit(solution)/shard_map/ppermute | solution.py:258
  46.9 2.6 %collective-permute-done.4.refs_2_.refs_1_ = bf16[32,64,128]{2,1,0:T(8,128)(2,1)S(1)} collective-permute-done((bf16[32,64,128]{2,1,0:T(8,128)(2,1)S(1)}, bf16[32,64,128]{2,1,0:T(8,128)(2,1)S(1)}, u32[]{:S(2)}, u32[]{:S(2)}) %collective-permute-start.4) | collective-permute-done | bytes 524320 | tf_op jit(solution)/shard_map/ppermute | solution.py:258
  49.5 1.6 %pick_tiles.12 = bf16[32,64,128]{2,1,0:T(8,128)(2,1)} custom-call(s32[1]{0:T(128)} %bitcast.9.me, s32[1024]{0:T(1024)S(1)} %collective-permute-done.2.rows, bf16[64,32768]{1,0:T(8,128)(2,1)S(1)} %stage_amplitudes.1.amp, bf16[32,64,128]{2,1,0:T(8,128)(2,1)S(1)} %collective-permute-done.7.refs_0_, bf16[32,64,128]{2,1,0:T(8,128)(2,1)S(1)} %collective-permute-done.4.refs_2_.refs_1_), custom_call_target="tpu_custom_call" | custom-call | bytes 1048576 | tf_op jit(solution)/shard_map/pick_tiles/pallas_call | solution.py:93
  51.0 0.0 collective-permute-start.8
  51.1 5.1 %compare_convert_fusion.live = f32[256]{0:T(256)S(1)} fusion(s32[256]{0:T(256)S(1)} %copy-done.4, s32[256]{0:T(256)S(1)} %copy-done.2, s32[]{:T(128)} %bitcast, s32[]{:T(128)} %bitcast.1, s32[]{:T(128)} %bitcast.2, s32[]{:T(128)} %bitcast.3, s32[]{:T(128)} %bitcast.4, s32[]{:T(128)} %bitcast.5, s32[]{:T(128)} %bitcast.6, s32[]{:T(128)} %bitcast.7, ...), kind=kLoop, calls=%fused_computation.36 | loop fusion | flops 44544 | bytes 3112 | tf_op jit(solution)/shard_map/convert_element_type | solution.py:290
  56.2 2.2 %copy-done.1 = bf16[64,32768]{1,0:T(8,128)(2,1)S(1)} copy-done((bf16[64,32768]{1,0:T(8,128)(2,1)S(1)}, bf16[64,32768]{1,0:T(8,128)(2,1)}, u32[]{:S(2)}) %copy-start.1) | copy-done | bytes 4194328
  58.4 0.7 pick_tiles.7.refs_0_
  59.1 2.2 %ladder_products.5.refs_1_ = f32[32,64,128]{2,1,0:T(8,128)S(1)} custom-call(s32[8]{0:T(128)S(1)} %iota_xor_fusion.order, s32[256]{0:T(256)S(1)} %fusion.3.cols, f32[256]{0:T(256)S(1)} %compare_convert_fusion.live, bf16[8,32,128,128]{3,2,1,0:T(8,128)(2,1)} %bitcast.10, bf16[32,64,128]{2,1,0:T(8,128)(2,1)S(1)} %collective-permute-done.7.refs_0_), custom_call_target="tpu_custom_call" | custom-call | flops 67108864 | bytes 1048576 | tf_op jit(solution)/shard_map/ladder_products/pallas_call | solution.py:168
  61.4 0.0 collective-permute-done.6.refs_0_
  61.4 2.2 %ladder_products.6.refs_4_ = f32[32,64,128]{2,1,0:T(8,128)S(1)} custom-call(s32[8]{0:T(128)S(1)} %iota_xor_fusion.order, s32[256]{0:T(256)S(1)} %fusion.3.cols, f32[256]{0:T(256)S(1)} %compare_convert_fusion.live, bf16[8,32,128,128]{3,2,1,0:T(8,128)(2,1)} %bitcast.11, ...), custom_call_target="tpu_custom_call", output_to_operand_aliasing={{}: (5, {})} | custom-call | flops 67108864 | bytes 1048576 | tf_op jit(solution)/shard_map/ladder_products/pallas_call | solution.py:168
  63.6 0.0 collective-permute-done.3.refs_1_
  63.6 0.0 collective-permute-done.5.refs_3_
  63.6 3.5 %ladder_products.7 = (f32[32,64,128]{2,1,0:T(8,128)S(1)}, bf16[1,32,128,128]{3,2,1,0:T(8,128)(2,1)S(1)}) custom-call(s32[8]{0:T(128)S(1)} %iota_xor_fusion.order, s32[256]{0:T(256)S(1)} %fusion.3.cols, f32[256]{0:T(256)S(1)} %compare_convert_fusion.live, bf16[8,32,128,128]{3,2,1,0:T(8,128)(2,1)} %bitcast.12, ...), custom_call_target="tpu_custom_call", output_to_operand_aliasing={{0}: (8, {})} | custom-call | flops 268435456 | bytes 5242880 | tf_op jit(solution)/shard_map/ladder_products/pallas_call | solution.py:168
  67.2 21.4 %collective-permute-done.9.refs_0_ = bf16[32,64,128]{2,1,0:T(8,128)(2,1)} collective-permute-done((bf16[32,64,128]{2,1,0:T(8,128)(2,1)}, bf16[32,64,128]{2,1,0:T(8,128)(2,1)}, u32[]{:S(2)}, u32[]{:S(2)}) %collective-permute-start.9) | collective-permute-done | bytes 524320 | tf_op jit(solution)/shard_map/ppermute | solution.py:258
  88.5 2.7 %ladder_products.8.refs_1_ = f32[32,64,128]{2,1,0:T(8,128)S(1)} custom-call(s32[8]{0:T(128)S(1)} %iota_xor_fusion.order, s32[256]{0:T(256)S(1)} %fusion.3.cols, f32[256]{0:T(256)S(1)} %compare_convert_fusion.live, bf16[8,32,128,128]{3,2,1,0:T(8,128)(2,1)} %bitcast.13, ...), custom_call_target="tpu_custom_call", output_to_operand_aliasing={{}: (5, {})} | custom-call | flops 67108864 | bytes 1048576 | tf_op jit(solution)/shard_map/ladder_products/pallas_call | solution.py:168
  91.3 9.0 %collective-permute-done.8.refs_0_ = bf16[32,64,128]{2,1,0:T(8,128)(2,1)S(1)} collective-permute-done((bf16[32,64,128]{2,1,0:T(8,128)(2,1)}, bf16[32,64,128]{2,1,0:T(8,128)(2,1)S(1)}, u32[]{:S(2)}, u32[]{:S(2)}) %collective-permute-start.8) | collective-permute-done | bytes 524320 | tf_op jit(solution)/shard_map/ppermute | solution.py:258
  100.2 1.1 ladder_products.9
  101.3 0.1 collective-permute-start.11
  101.4 0.5 collective-permute-start.10
  101.9 1.0 collective-permute-done.11.got
  102.9 0.2 encode_sums.1
  103.1 1.6 %collective-permute-start.12 = (s16[9,64,128]{2,1,0:T(8,128)(2,1)S(1)}, s16[9,64,128]{2,1,0:T(8,128)(2,1)S(1)}, u32[]{:S(2)}, u32[]{:S(2)}) collective-permute-start(s16[9,64,128]{2,1,0:T(8,128)(2,1)S(1)} %encode_sums.1), channel_id=1, source_target_pairs={{0,2},{1,3},{2,0},{3,1},{4,6},{5,7},{6,4},{7,5},{8,10},{9,11},{10,... | collective-permute-start | bytes 442376 | tf_op jit(solution)/shard_map/ppermute | solution.py:313
  104.7 0.0 collective-permute-done.10.got
  104.7 4.4 %collective-permute-done.12.refs_0_ = s16[9,64,128]{2,1,0:T(8,128)(2,1)S(1)} collective-permute-done((s16[9,64,128]{2,1,0:T(8,128)(2,1)S(1)}, s16[9,64,128]{2,1,0:T(8,128)(2,1)S(1)}, u32[]{:S(2)}, u32[]{:S(2)}) %collective-permute-start.12) | collective-permute-done | bytes 147488 | tf_op jit(solution)/shard_map/ppermute | solution.py:313
  109.1 0.9 decode_sums.1
  (13 shorter events, 0.1 us)
Async XLA Ops:
  0.0 4.7 %collective-permute-start = (s32[256]{0:T(256)}, s32[256]{0:T(256)S(1)}, u32[]{:S(2)}, u32[]{:S(2)}) collective-permute-start(s32[256]{0:T(256)} %rows.1), channel_id=1, source_target_pairs={{0,16},{4,20},{8,24},{12,28},{16,0},{20,4},{24,8},{28,12},{1,17},{... | collective-permute-start | bytes 3080 | tf_op jit(solution)/shard_map/ppermute | solution.py:258
  5.4 6.9 %collective-permute-start.1 = (s32[512]{0:T(512)S(1)}, s32[512]{0:T(512)S(1)}, u32[]{:S(2)}, u32[]{:S(2)}) collective-permute-start(s32[512]{0:T(512)S(1)} %pad_add_fusion), channel_id=1, source_target_pairs={{0,8},{4,12},{8,0},{12,4},{16,24},{20,28},{24,16},{28,20},{1,9},{5... | collective-permute-start | bytes 6152 | tf_op jit(solution)/shard_map/ppermute | solution.py:258
  7.1 27.4 %collective-permute-start.7 = (bf16[32,64,128]{2,1,0:T(8,128)(2,1)S(1)}, bf16[32,64,128]{2,1,0:T(8,128)(2,1)S(1)}, u32[]{:S(2)}, u32[]{:S(2)}) collective-permute-start(bf16[32,64,128]{2,1,0:T(8,128)(2,1)S(1)} %fetch_tiles.1.refs_0_), channel_id=1, source_target_pairs={{0,16},{4,20},{8,24},{12,28},{16,0},{20,4},{24,8},{28,12},{1,17},{... | collective-permute-start | bytes 1572872 | tf_op jit(solution)/shard_map/ppermute | solution.py:258
  12.3 37.2 %copy-start = (bf16[64,32768]{1,0:T(8,128)(2,1)}, bf16[64,32768]{1,0:T(8,128)(2,1)S(1)}, u32[]{:S(2)}) copy-start(bf16[64,32768]{1,0:T(8,128)(2,1)S(1)} %stage_amplitudes.1.amp) | copy-start | bytes 12582916
  12.3 4.0 %copy-start.3 = (s32[8]{0:T(128)S(1)}, s32[8]{0:T(128)}, u32[]{:S(2)}) copy-start(s32[8]{0:T(128)} %param.6) | copy-start | bytes 100
  13.1 36.4 %collective-permute-start.4 = (bf16[32,64,128]{2,1,0:T(8,128)(2,1)S(1)}, bf16[32,64,128]{2,1,0:T(8,128)(2,1)S(1)}, u32[]{:S(2)}, u32[]{:S(2)}) collective-permute-start(bf16[32,64,128]{2,1,0:T(8,128)(2,1)S(1)} %pick_tiles.9), channel_id=1, source_target_pairs={{0,8},{4,12},{8,0},{12,4},{16,24},{20,28},{24,16},{28,20},{1,9},{5... | collective-permute-start | bytes 1572872 | tf_op jit(solution)/shard_map/ppermute | solution.py:258
  14.7 3.8 %collective-permute-start.2 = (s32[1024]{0:T(1024)S(1)}, s32[1024]{0:T(1024)S(1)}, u32[]{:S(2)}, u32[]{:S(2)}) collective-permute-start(s32[1024]{0:T(1024)S(1)} %constant_dynamic-update-slice_fusion.rows), channel_id=1, source_target_pairs={{0,4},{4,0},{8,12},{12,8},{16,20},{20,16},{24,28},{28,24},{1,5},{5... | collective-permute-start | bytes 12296 | tf_op jit(solution)/shard_map/ppermute | solution.py:258
  18.5 42.9 %collective-permute-start.6 = (bf16[32,64,128]{2,1,0:T(8,128)(2,1)}, bf16[32,64,128]{2,1,0:T(8,128)(2,1)S(1)}, u32[]{:S(2)}, u32[]{:S(2)}) collective-permute-start(bf16[32,64,128]{2,1,0:T(8,128)(2,1)} %pick_tiles.11), channel_id=1, source_target_pairs={{0,24},{4,28},{8,16},{12,20},{16,8},{20,12},{24,0},{28,4},{1,25},{... | collective-permute-start | bytes 1572872 | tf_op jit(solution)/shard_map/ppermute | solution.py:258
  20.1 43.5 %collective-permute-start.3 = (bf16[32,64,128]{2,1,0:T(8,128)(2,1)}, bf16[32,64,128]{2,1,0:T(8,128)(2,1)S(1)}, u32[]{:S(2)}, u32[]{:S(2)}) collective-permute-start(bf16[32,64,128]{2,1,0:T(8,128)(2,1)} %pick_tiles.8), channel_id=1, source_target_pairs={{0,4},{4,0},{8,12},{12,8},{16,20},{20,16},{24,28},{28,24},{1,5},{5... | collective-permute-start | bytes 1572872 | tf_op jit(solution)/shard_map/ppermute | solution.py:258
  23.0 40.7 %collective-permute-start.5 = (bf16[32,64,128]{2,1,0:T(8,128)(2,1)}, bf16[32,64,128]{2,1,0:T(8,128)(2,1)S(1)}, u32[]{:S(2)}, u32[]{:S(2)}) collective-permute-start(bf16[32,64,128]{2,1,0:T(8,128)(2,1)} %pick_tiles.10), channel_id=1, source_target_pairs={{0,12},{4,8},{8,4},{12,0},{16,28},{20,24},{24,20},{28,16},{1,13},{... | collective-permute-start | bytes 1572872 | tf_op jit(solution)/shard_map/ppermute | solution.py:258
  36.1 15.0 %copy-start.4 = (s32[256]{0:T(256)S(1)}, s32[256]{0:T(256)}, u32[]{:S(2)}) copy-start(s32[256]{0:T(256)} %param.9) | copy-start | bytes 3076
  36.1 15.0 %copy-start.2 = (s32[256]{0:T(256)S(1)}, s32[256]{0:T(256)}, u32[]{:S(2)}) copy-start(s32[256]{0:T(256)} %rows.1) | copy-start | bytes 3076
  36.1 52.5 %collective-permute-start.9 = (bf16[32,64,128]{2,1,0:T(8,128)(2,1)}, bf16[32,64,128]{2,1,0:T(8,128)(2,1)}, u32[]{:S(2)}, u32[]{:S(2)}) collective-permute-start(bf16[32,64,128]{2,1,0:T(8,128)(2,1)} %pick_tiles.13), channel_id=1, source_target_pairs={{0,20},{4,16},{8,28},{12,24},{16,4},{20,0},{24,12},{28,8},{1,21},{... | collective-permute-start | bytes 1572872 | tf_op jit(solution)/shard_map/ppermute | solution.py:258
  51.0 49.2 %collective-permute-start.8 = (bf16[32,64,128]{2,1,0:T(8,128)(2,1)}, bf16[32,64,128]{2,1,0:T(8,128)(2,1)S(1)}, u32[]{:S(2)}, u32[]{:S(2)}) collective-permute-start(bf16[32,64,128]{2,1,0:T(8,128)(2,1)} %pick_tiles.12), channel_id=1, source_target_pairs={{0,28},{4,24},{8,20},{12,16},{16,12},{20,8},{24,4},{28,0},{1,29},{... | collective-permute-start | bytes 1572872 | tf_op jit(solution)/shard_map/ppermute | solution.py:258
  56.2 2.2 %copy-start.1 = (bf16[64,32768]{1,0:T(8,128)(2,1)S(1)}, bf16[64,32768]{1,0:T(8,128)(2,1)}, u32[]{:S(2)}) copy-start(bf16[64,32768]{1,0:T(8,128)(2,1)} %copy-done) | copy-start | bytes 12582916
  101.3 1.6 %collective-permute-start.11 = (f32[8,64,128]{2,1,0:T(8,128)S(1)}, f32[8,64,128]{2,1,0:T(8,128)S(1)}, u32[]{:S(2)}, u32[]{:S(2)}) collective-permute-start(f32[8,64,128]{2,1,0:T(8,128)S(1)} %get-tuple-element.16), channel_id=1, source_target_pairs={{0,1},{1,0},{2,3},{3,2},{4,5},{5,4},{6,7},{7,6},{8,9},{9,8},{10,11... | collective-permute-start | bytes 786440 | tf_op jit(solution)/shard_map/ppermute | solution.py:313
  101.4 3.3 %collective-permute-start.10 = (f32[8,64,128]{2,1,0:T(8,128)S(1)}, f32[8,64,128]{2,1,0:T(8,128)S(1)}, u32[]{:S(2)}, u32[]{:S(2)}) collective-permute-start(f32[8,64,128]{2,1,0:T(8,128)S(1)} %get-tuple-element.14), channel_id=1, source_target_pairs={{0,1},{1,0},{2,3},{3,2},{4,5},{5,4},{6,7},{7,6},{8,9},{9,8},{10,11... | collective-permute-start | bytes 786440 | tf_op jit(solution)/shard_map/ppermute | solution.py:313
  103.1 6.0 %collective-permute-start.12 = (s16[9,64,128]{2,1,0:T(8,128)(2,1)S(1)}, s16[9,64,128]{2,1,0:T(8,128)(2,1)S(1)}, u32[]{:S(2)}, u32[]{:S(2)}) collective-permute-start(s16[9,64,128]{2,1,0:T(8,128)(2,1)S(1)} %encode_sums.1), channel_id=1, source_target_pairs={{0,2},{1,3},{2,0},{3,1},{4,6},{5,7},{6,4},{7,5},{8,10},{9,11},{10,... | collective-permute-start | bytes 442376 | tf_op jit(solution)/shard_map/ppermute | solution.py:313

commit v15 on v12

--- a/solution.py
+++ b/solution.py
@@ -251,7 +251,7 @@
         if k in far[2]:
             after = (arrived[far[0][far[2].index(k)]],)
         if k in far[3]:
-            after = (arrived[far[0][far[3].index(k)]], arrived[2 + far[3].index(k)])
+            after = (arrived[far[0][far[3].index(k)]], arrived[far[1][far[3].index(k)]])
         arrived[k] = swap(pick(here, *place[k], amp, per, after), k)
 
     row_tile = mine * row_count + tile_rows

time: 111 us -> 111 us (level)
  waiting for transfers between devices: 51.6 us -> 35.6 us
  starting transfers between devices: 24.5 us -> 40.4 us
    ppermute x10, waiting for transfers between devices: 46.2 us -> 30.2 us  [swap(): return lax.ppermute(x, 'gx', [(i, i ^ k) for i in range(peers)])]
    ppermute x10, starting transfers between devices: 22.4 us -> 38.3 us  [swap(): return lax.ppermute(x, 'gx', [(i, i ^ k) for i in range(peers)])]
where the time goes in v15:
time: 111 us; the launch traced here: 110 us
  starting transfers between devices  40.4 us (36%)
  waiting for transfers between devices  35.6 us (32%)
  Pallas kernels  25.5 us (23%)
  other arithmetic  4.81 us (4%)
  local copies, waits for them, and re-layouts  3.61 us (3%)
    ppermute x10, starting transfers between devices, swap(): return lax.ppermute(x, 'gx', [(i, i ^ k) for i in range(peers)])  38.3 us
    ppermute x10, waiting for transfers between devices, swap(): return lax.ppermute(x, 'gx', [(i, i ^ k) for i in range(peers)])  30.2 us
    pallas_call x5, Pallas kernels, ladder(): pl.pallas_call(functools.partial(ladder_kernel, peers_at, list(ahead), pe...  12.2 us
    pallas_call x8, Pallas kernels, pick(): pl.pallas_call(functools.partial(pick_kernel, first, per, width // BLK),...  10 us
    ppermute x3, waiting for transfers between devices, swap_gy(): return lax.ppermute(x, 'gy', [(i, i ^ k) for i in range(groups)])  5.42 us
    convert_element_type x1, other arithmetic, per_device(): (pair_irrep(row_tile, virt_irreps) == pair_irrep(col_tile, virt_irreps))....  4.77 us
    unnamed x12, local copies, waits for them, and re-layouts  2.92 us
  transfers between devices with their start and end apart: 13, of which 6 were waited for; matrix products, arithmetic and copies ran while one was open for 6% of the time, Pallas kernels for 21%

profile of v15, /device:TPU:8, one launch (start us, length us, event | category | flops | bytes accessed | tf_op | source)
XLA Modules:
  0.0 110.2 jit_solution(7104744433344750551)
XLA Ops:
  0.0 2.6 %collective-permute-start = (s32[256]{0:T(256)}, s32[256]{0:T(256)S(1)}, u32[]{:S(2)}, u32[]{:S(2)}) collective-permute-start(s32[256]{0:T(256)} %rows.1), channel_id=1, source_target_pairs={{0,16},{4,20},{8,24},{12,28},{16,0},{20,4},{24,8},{28,12},{1,17},{... | collective-permute-start | bytes 3080 | tf_op jit(solution)/shard_map/ppermute | solution.py:228
  2.6 0.7 constant_dynamic-update-slice_fusion.2
  3.3 2.2 %stage_amplitudes.1.amp = bf16[64,32768]{1,0:T(8,128)(2,1)S(1)} custom-call(bf16[64,32768]{1,0:T(8,128)(2,1)} %source.1), custom_call_target="tpu_custom_call" | custom-call | bytes 4194304 | tf_op jit(solution)/shard_map/stage_amplitudes/pallas_call | solution.py:36
  5.5 0.0 copy-start
  5.5 0.0 collective-permute-done.rows
  5.5 0.0 copy-done.2
  5.6 0.5 collective-permute-start.1
  6.1 0.7 pick_tiles.13
  6.8 1.8 %collective-permute-start.7 = (bf16[32,64,128]{2,1,0:T(8,128)(2,1)S(1)}, bf16[32,64,128]{2,1,0:T(8,128)(2,1)S(1)}, u32[]{:S(2)}, u32[]{:S(2)}) collective-permute-start(bf16[32,64,128]{2,1,0:T(8,128)(2,1)S(1)} %pick_tiles.13), channel_id=1, source_target_pairs={{0,16},{4,20},{8,24},{12,28},{16,0},{20,4},{24,8},{28,12},{1,17},{... | collective-permute-start | bytes 1572872 | tf_op jit(solution)/shard_map/ppermute | solution.py:228
  8.6 0.7 collective-permute-done.1
  9.2 0.8 pick_tiles.12
  10.0 0.8 collective-permute-start.6
  10.8 1.5 %collective-permute-start.2 = (s32[1024]{0:T(1024)S(1)}, s32[1024]{0:T(1024)S(1)}, u32[]{:S(2)}, u32[]{:S(2)}) collective-permute-start(s32[1024]{0:T(1024)S(1)} %constant_dynamic-update-slice_fusion.rows), channel_id=1, source_target_pairs={{0,4},{4,0},{8,12},{12,8},{16,20},{20,16},{24,28},{28,24},{1,5},{5... | collective-permute-start | bytes 12296 | tf_op jit(solution)/shard_map/ppermute | solution.py:228
  12.3 0.7 fusion.4
  13.0 1.6 %pick_tiles.10 = bf16[32,64,128]{2,1,0:T(8,128)(2,1)} custom-call(s32[1]{0:T(128)} %bitcast.9.me, s32[1024]{0:T(1024)S(1)} %constant_dynamic-update-slice_fusion.rows, bf16[64,32768]{1,0:T(8,128)(2,1)S(1)} %stage_amplitudes.1.amp), custom_call_target="tpu_custom_call" | custom-call | bytes 1048576 | tf_op jit(solution)/shard_map/pick_tiles/pallas_call | solution.py:63
  14.5 2.7 %collective-permute-start.4 = (bf16[32,64,128]{2,1,0:T(8,128)(2,1)}, bf16[32,64,128]{2,1,0:T(8,128)(2,1)S(1)}, u32[]{:S(2)}, u32[]{:S(2)}) collective-permute-start(bf16[32,64,128]{2,1,0:T(8,128)(2,1)} %pick_tiles.10), channel_id=1, source_target_pairs={{0,8},{4,12},{8,0},{12,4},{16,24},{20,28},{24,16},{28,20},{1,9},{5... | collective-permute-start | bytes 1572872 | tf_op jit(solution)/shard_map/ppermute | solution.py:228
  17.2 0.0 collective-permute-done.2.rows
  17.2 1.6 %pick_tiles.9 = bf16[32,64,128]{2,1,0:T(8,128)(2,1)} custom-call(s32[1]{0:T(128)} %bitcast.9.me, s32[1024]{0:T(1024)S(1)} %collective-permute-done.2.rows, bf16[64,32768]{1,0:T(8,128)(2,1)S(1)} %stage_amplitudes.1.amp), custom_call_target="tpu_custom_call" | custom-call | bytes 1048576 | tf_op jit(solution)/shard_map/pick_tiles/pallas_call | solution.py:63
  18.8 0.5 collective-permute-start.3
  19.3 1.6 %pick_tiles.11 = bf16[32,64,128]{2,1,0:T(8,128)(2,1)} custom-call(s32[1]{0:T(128)} %bitcast.9.me, s32[1024]{0:T(1024)S(1)} %collective-permute-done.2.rows, bf16[64,32768]{1,0:T(8,128)(2,1)S(1)} %stage_amplitudes.1.amp), custom_call_target="tpu_custom_call" | custom-call | bytes 1048576 | tf_op jit(solution)/shard_map/pick_tiles/pallas_call | solution.py:63
  20.9 1.0 collective-permute-start.5
  21.8 20.2 %collective-permute-done.7.refs_0_ = bf16[32,64,128]{2,1,0:T(8,128)(2,1)S(1)} collective-permute-done((bf16[32,64,128]{2,1,0:T(8,128)(2,1)S(1)}, bf16[32,64,128]{2,1,0:T(8,128)(2,1)S(1)}, u32[]{:S(2)}, u32[]{:S(2)}) %collective-permute-start.7) | collective-permute-done | bytes 524320 | tf_op jit(solution)/shard_map/ppermute | solution.py:228
  42.0 1.6 %pick_tiles.15 = bf16[32,64,128]{2,1,0:T(8,128)(2,1)} custom-call(s32[1]{0:T(128)} %bitcast.9.me, s32[1024]{0:T(1024)S(1)} %collective-permute-done.2.rows, bf16[64,32768]{1,0:T(8,128)(2,1)S(1)} %stage_amplitudes.1.amp, bf16[32,64,128]{2,1,0:T(8,128)(2,1)S(1)} %collective-permute-done.7.refs_0_), custom_call_target="tpu_custom_call" | custom-call | bytes 1048576 | tf_op jit(solution)/shard_map/pick_tiles/pallas_call | solution.py:63
  43.6 4.3 %collective-permute-start.9 = (bf16[32,64,128]{2,1,0:T(8,128)(2,1)}, bf16[32,64,128]{2,1,0:T(8,128)(2,1)}, u32[]{:S(2)}, u32[]{:S(2)}) collective-permute-start(bf16[32,64,128]{2,1,0:T(8,128)(2,1)} %pick_tiles.15), channel_id=1, source_target_pairs={{0,20},{4,16},{8,28},{12,24},{16,4},{20,0},{24,12},{28,8},{1,21},{... | collective-permute-start | bytes 1572872 | tf_op jit(solution)/shard_map/ppermute | solution.py:228
  47.9 8.5 %collective-permute-done.6.refs_0_.refs_1_ = bf16[32,64,128]{2,1,0:T(8,128)(2,1)S(1)} collective-permute-done((bf16[32,64,128]{2,1,0:T(8,128)(2,1)S(1)}, bf16[32,64,128]{2,1,0:T(8,128)(2,1)S(1)}, u32[]{:S(2)}, u32[]{:S(2)}) %collective-permute-start.6) | collective-permute-done | bytes 524320 | tf_op jit(solution)/shard_map/ppermute | solution.py:228
  56.5 1.6 %pick_tiles.14 = bf16[32,64,128]{2,1,0:T(8,128)(2,1)} custom-call(s32[1]{0:T(128)} %bitcast.9.me, s32[1024]{0:T(1024)S(1)} %collective-permute-done.2.rows, bf16[64,32768]{1,0:T(8,128)(2,1)S(1)} %stage_amplitudes.1.amp, bf16[32,64,128]{2,1,0:T(8,128)(2,1)S(1)} %collective-permute-done.7.refs_0_, bf16[32,64,128]{2,1,0:T(8,128)(2,1)S(1)} %collective-permute-done.6.refs_0_.refs_1_), custom_call_target="tpu_custom_call" | custom-call | bytes 1048576 | tf_op jit(solution)/shard_map/pick_tiles/pallas_call | solution.py:63
  58.0 22.7 %collective-permute-start.8 = (bf16[32,64,128]{2,1,0:T(8,128)(2,1)}, bf16[32,64,128]{2,1,0:T(8,128)(2,1)S(1)}, u32[]{:S(2)}, u32[]{:S(2)}) collective-permute-start(bf16[32,64,128]{2,1,0:T(8,128)(2,1)} %pick_tiles.14), channel_id=1, source_target_pairs={{0,28},{4,24},{8,20},{12,16},{16,12},{20,8},{24,4},{28,0},{1,29},{... | collective-permute-start | bytes 1572872 | tf_op jit(solution)/shard_map/ppermute | solution.py:228
  80.7 2.2 %copy-done.1 = bf16[64,32768]{1,0:T(8,128)(2,1)S(1)} copy-done((bf16[64,32768]{1,0:T(8,128)(2,1)S(1)}, bf16[64,32768]{1,0:T(8,128)(2,1)}, u32[]{:S(2)}) %copy-start.1) | copy-done | bytes 4194328
  82.9 0.7 pick_tiles.8.refs_0_
  83.7 4.8 %compare_convert_fusion.live = f32[256]{0:T(256)S(1)} fusion(s32[256]{0:T(256)S(1)} %copy-done.4, s32[256]{0:T(256)S(1)} %copy-done.2, s32[]{:T(128)} %bitcast, s32[]{:T(128)} %bitcast.1, s32[]{:T(128)} %bitcast.2, s32[]{:T(128)} %bitcast.3, s32[]{:T(128)} %bitcast.4, s32[]{:T(128)} %bitcast.5, s32[]{:T(128)} %bitcast.6, s32[]{:T(128)} %bitcast.7, ...), kind=kLoop, calls=%fused_computation.36 | loop fusion | flops 44544 | bytes 3112 | tf_op jit(solution)/shard_map/convert_element_type | solution.py:259
  88.5 2.2 %ladder_products.5.refs_1_ = f32[32,64,128]{2,1,0:T(8,128)S(1)} custom-call(s32[8]{0:T(128)S(1)} %iota_xor_fusion.order, s32[256]{0:T(256)S(1)} %fusion.3.cols, f32[256]{0:T(256)S(1)} %compare_convert_fusion.live, bf16[8,32,128,128]{3,2,1,0:T(8,128)(2,1)} %bitcast.10, bf16[32,64,128]{2,1,0:T(8,128)(2,1)S(1)} %collective-permute-done.7.refs_0_), custom_call_target="tpu_custom_call" | custom-call | flops 67108864 | bytes 1048576 | tf_op jit(solution)/shard_map/ladder_products/pallas_call | solution.py:138
  90.7 2.2 %ladder_products.6.refs_4_ = f32[32,64,128]{2,1,0:T(8,128)S(1)} custom-call(s32[8]{0:T(128)S(1)} %iota_xor_fusion.order, s32[256]{0:T(256)S(1)} %fusion.3.cols, f32[256]{0:T(256)S(1)} %compare_convert_fusion.live, bf16[8,32,128,128]{3,2,1,0:T(8,128)(2,1)} %bitcast.11, ...), custom_call_target="tpu_custom_call", output_to_operand_aliasing={{}: (5, {})} | custom-call | flops 67108864 | bytes 1048576 | tf_op jit(solution)/shard_map/ladder_products/pallas_call | solution.py:138
  92.9 0.0 collective-permute-done.4.refs_2_
  93.0 0.0 collective-permute-done.3.refs_1_
  93.0 0.0 collective-permute-done.5.refs_3_
  93.0 4.0 %ladder_products.7 = (f32[32,64,128]{2,1,0:T(8,128)S(1)}, bf16[1,32,128,128]{3,2,1,0:T(8,128)(2,1)S(1)}) custom-call(s32[8]{0:T(128)S(1)} %iota_xor_fusion.order, s32[256]{0:T(256)S(1)} %fusion.3.cols, f32[256]{0:T(256)S(1)} %compare_convert_fusion.live, bf16[8,32,128,128]{3,2,1,0:T(8,128)(2,1)} %bitcast.12, ...), custom_call_target="tpu_custom_call", output_to_operand_aliasing={{0}: (8, {})} | custom-call | flops 268435456 | bytes 5242880 | tf_op jit(solution)/shard_map/ladder_products/pallas_call | solution.py:138
  97.0 0.0 collective-permute-done.9.refs_0_
  97.0 2.7 %ladder_products.8.refs_1_ = f32[32,64,128]{2,1,0:T(8,128)S(1)} custom-call(s32[8]{0:T(128)S(1)} %iota_xor_fusion.order, s32[256]{0:T(256)S(1)} %fusion.3.cols, f32[256]{0:T(256)S(1)} %compare_convert_fusion.live, bf16[8,32,128,128]{3,2,1,0:T(8,128)(2,1)} %bitcast.13, ...), custom_call_target="tpu_custom_call", output_to_operand_aliasing={{}: (5, {})} | custom-call | flops 67108864 | bytes 1048576 | tf_op jit(solution)/shard_map/ladder_products/pallas_call | solution.py:138
  99.7 0.8 collective-permute-done.8.refs_0_
  100.5 1.1 ladder_products.9
  101.6 0.1 collective-permute-start.11
  101.7 0.5 collective-permute-start.10
  102.2 1.0 collective-permute-done.11.got
  103.2 0.2 encode_sums.1
  103.4 1.6 %collective-permute-start.12 = (s16[9,64,128]{2,1,0:T(8,128)(2,1)S(1)}, s16[9,64,128]{2,1,0:T(8,128)(2,1)S(1)}, u32[]{:S(2)}, u32[]{:S(2)}) collective-permute-start(s16[9,64,128]{2,1,0:T(8,128)(2,1)S(1)} %encode_sums.1), channel_id=1, source_target_pairs={{0,2},{1,3},{2,0},{3,1},{4,6},{5,7},{6,4},{7,5},{8,10},{9,11},{10,... | collective-permute-start | bytes 442376 | tf_op jit(solution)/shard_map/ppermute | solution.py:282
  104.9 0.0 collective-permute-done.10.got
  105.0 4.4 %collective-permute-done.12.refs_0_ = s16[9,64,128]{2,1,0:T(8,128)(2,1)S(1)} collective-permute-done((s16[9,64,128]{2,1,0:T(8,128)(2,1)S(1)}, s16[9,64,128]{2,1,0:T(8,128)(2,1)S(1)}, u32[]{:S(2)}, u32[]{:S(2)}) %collective-permute-start.12) | collective-permute-done | bytes 147488 | tf_op jit(solution)/shard_map/ppermute | solution.py:282
  109.3 0.9 decode_sums.1
  (13 shorter events, 0.1 us)
Async XLA Ops:
  0.0 5.5 %collective-permute-start = (s32[256]{0:T(256)}, s32[256]{0:T(256)S(1)}, u32[]{:S(2)}, u32[]{:S(2)}) collective-permute-start(s32[256]{0:T(256)} %rows.1), channel_id=1, source_target_pairs={{0,16},{4,20},{8,24},{12,28},{16,0},{20,4},{24,8},{28,12},{1,17},{... | collective-permute-start | bytes 3080 | tf_op jit(solution)/shard_map/ppermute | solution.py:228
  3.3 2.2 %copy-start.2 = (s32[256]{0:T(256)S(1)}, s32[256]{0:T(256)}, u32[]{:S(2)}) copy-start(s32[256]{0:T(256)} %rows.1) | copy-start | bytes 3076
  5.5 51.0 %copy-start = (bf16[64,32768]{1,0:T(8,128)(2,1)}, bf16[64,32768]{1,0:T(8,128)(2,1)S(1)}, u32[]{:S(2)}) copy-start(bf16[64,32768]{1,0:T(8,128)(2,1)S(1)} %stage_amplitudes.1.amp) | copy-start | bytes 12582916
  5.6 3.7 %collective-permute-start.1 = (s32[512]{0:T(512)S(1)}, s32[512]{0:T(512)S(1)}, u32[]{:S(2)}, u32[]{:S(2)}) collective-permute-start(s32[512]{0:T(512)S(1)} %pad_add_fusion), channel_id=1, source_target_pairs={{0,8},{4,12},{8,0},{12,4},{16,24},{20,28},{24,16},{28,20},{1,9},{5... | collective-permute-start | bytes 6152 | tf_op jit(solution)/shard_map/ppermute | solution.py:228
  6.1 6.2 %copy-start.3 = (s32[8]{0:T(128)S(1)}, s32[8]{0:T(128)}, u32[]{:S(2)}) copy-start(s32[8]{0:T(128)} %param.6) | copy-start | bytes 100
  6.8 35.2 %collective-permute-start.7 = (bf16[32,64,128]{2,1,0:T(8,128)(2,1)S(1)}, bf16[32,64,128]{2,1,0:T(8,128)(2,1)S(1)}, u32[]{:S(2)}, u32[]{:S(2)}) collective-permute-start(bf16[32,64,128]{2,1,0:T(8,128)(2,1)S(1)} %pick_tiles.13), channel_id=1, source_target_pairs={{0,16},{4,20},{8,24},{12,28},{16,0},{20,4},{24,8},{28,12},{1,17},{... | collective-permute-start | bytes 1572872 | tf_op jit(solution)/shard_map/ppermute | solution.py:228
  10.0 46.5 %collective-permute-start.6 = (bf16[32,64,128]{2,1,0:T(8,128)(2,1)S(1)}, bf16[32,64,128]{2,1,0:T(8,128)(2,1)S(1)}, u32[]{:S(2)}, u32[]{:S(2)}) collective-permute-start(bf16[32,64,128]{2,1,0:T(8,128)(2,1)S(1)} %pick_tiles.12), channel_id=1, source_target_pairs={{0,24},{4,28},{8,16},{12,20},{16,8},{20,12},{24,0},{28,4},{1,25},{... | collective-permute-start | bytes 1572872 | tf_op jit(solution)/shard_map/ppermute | solution.py:228
  10.8 6.4 %collective-permute-start.2 = (s32[1024]{0:T(1024)S(1)}, s32[1024]{0:T(1024)S(1)}, u32[]{:S(2)}, u32[]{:S(2)}) collective-permute-start(s32[1024]{0:T(1024)S(1)} %constant_dynamic-update-slice_fusion.rows), channel_id=1, source_target_pairs={{0,4},{4,0},{8,12},{12,8},{16,20},{20,16},{24,28},{28,24},{1,5},{5... | collective-permute-start | bytes 12296 | tf_op jit(solution)/shard_map/ppermute | solution.py:228
  14.5 78.4 %collective-permute-start.4 = (bf16[32,64,128]{2,1,0:T(8,128)(2,1)}, bf16[32,64,128]{2,1,0:T(8,128)(2,1)S(1)}, u32[]{:S(2)}, u32[]{:S(2)}) collective-permute-start(bf16[32,64,128]{2,1,0:T(8,128)(2,1)} %pick_tiles.10), channel_id=1, source_target_pairs={{0,8},{4,12},{8,0},{12,4},{16,24},{20,28},{24,16},{28,20},{1,9},{5... | collective-permute-start | bytes 1572872 | tf_op jit(solution)/shard_map/ppermute | solution.py:228
  18.8 74.2 %collective-permute-start.3 = (bf16[32,64,128]{2,1,0:T(8,128)(2,1)}, bf16[32,64,128]{2,1,0:T(8,128)(2,1)S(1)}, u32[]{:S(2)}, u32[]{:S(2)}) collective-permute-start(bf16[32,64,128]{2,1,0:T(8,128)(2,1)} %pick_tiles.9), channel_id=1, source_target_pairs={{0,4},{4,0},{8,12},{12,8},{16,20},{20,16},{24,28},{28,24},{1,5},{5... | collective-permute-start | bytes 1572872 | tf_op jit(solution)/shard_map/ppermute | solution.py:228
  20.9 72.1 %collective-permute-start.5 = (bf16[32,64,128]{2,1,0:T(8,128)(2,1)}, bf16[32,64,128]{2,1,0:T(8,128)(2,1)}, u32[]{:S(2)}, u32[]{:S(2)}) collective-permute-start(bf16[32,64,128]{2,1,0:T(8,128)(2,1)} %pick_tiles.11), channel_id=1, source_target_pairs={{0,12},{4,8},{8,4},{12,0},{16,28},{20,24},{24,20},{28,16},{1,13},{... | collective-permute-start | bytes 1572872 | tf_op jit(solution)/shard_map/ppermute | solution.py:228
  43.6 40.1 %copy-start.4 = (s32[256]{0:T(256)S(1)}, s32[256]{0:T(256)}, u32[]{:S(2)}) copy-start(s32[256]{0:T(256)} %param.9) | copy-start | bytes 3076
  43.6 53.4 %collective-permute-start.9 = (bf16[32,64,128]{2,1,0:T(8,128)(2,1)}, bf16[32,64,128]{2,1,0:T(8,128)(2,1)}, u32[]{:S(2)}, u32[]{:S(2)}) collective-permute-start(bf16[32,64,128]{2,1,0:T(8,128)(2,1)} %pick_tiles.15), channel_id=1, source_target_pairs={{0,20},{4,16},{8,28},{12,24},{16,4},{20,0},{24,12},{28,8},{1,21},{... | collective-permute-start | bytes 1572872 | tf_op jit(solution)/shard_map/ppermute | solution.py:228
  58.0 42.5 %collective-permute-start.8 = (bf16[32,64,128]{2,1,0:T(8,128)(2,1)}, bf16[32,64,128]{2,1,0:T(8,128)(2,1)S(1)}, u32[]{:S(2)}, u32[]{:S(2)}) collective-permute-start(bf16[32,64,128]{2,1,0:T(8,128)(2,1)} %pick_tiles.14), channel_id=1, source_target_pairs={{0,28},{4,24},{8,20},{12,16},{16,12},{20,8},{24,4},{28,0},{1,29},{... | collective-permute-start | bytes 1572872 | tf_op jit(solution)/shard_map/ppermute | solution.py:228
  80.7 2.2 %copy-start.1 = (bf16[64,32768]{1,0:T(8,128)(2,1)S(1)}, bf16[64,32768]{1,0:T(8,128)(2,1)}, u32[]{:S(2)}) copy-start(bf16[64,32768]{1,0:T(8,128)(2,1)} %copy-done) | copy-start | bytes 12582916
  101.6 1.6 %collective-permute-start.11 = (f32[8,64,128]{2,1,0:T(8,128)S(1)}, f32[8,64,128]{2,1,0:T(8,128)S(1)}, u32[]{:S(2)}, u32[]{:S(2)}) collective-permute-start(f32[8,64,128]{2,1,0:T(8,128)S(1)} %get-tuple-element.16), channel_id=1, source_target_pairs={{0,1},{1,0},{2,3},{3,2},{4,5},{5,4},{6,7},{7,6},{8,9},{9,8},{10,11... | collective-permute-start | bytes 786440 | tf_op jit(solution)/shard_map/ppermute | solution.py:282
  101.7 3.3 %collective-permute-start.10 = (f32[8,64,128]{2,1,0:T(8,128)S(1)}, f32[8,64,128]{2,1,0:T(8,128)S(1)}, u32[]{:S(2)}, u32[]{:S(2)}) collective-permute-start(f32[8,64,128]{2,1,0:T(8,128)S(1)} %get-tuple-element.14), channel_id=1, source_target_pairs={{0,1},{1,0},{2,3},{3,2},{4,5},{5,4},{6,7},{7,6},{8,9},{9,8},{10,11... | collective-permute-start | bytes 786440 | tf_op jit(solution)/shard_map/ppermute | solution.py:282
  103.4 6.0 %collective-permute-start.12 = (s16[9,64,128]{2,1,0:T(8,128)(2,1)S(1)}, s16[9,64,128]{2,1,0:T(8,128)(2,1)S(1)}, u32[]{:S(2)}, u32[]{:S(2)}) collective-permute-start(s16[9,64,128]{2,1,0:T(8,128)(2,1)S(1)} %encode_sums.1), channel_id=1, source_target_pairs={{0,2},{1,3},{2,0},{3,1},{4,6},{5,7},{6,4},{7,5},{8,10},{9,11},{10,... | collective-permute-start | bytes 442376 | tf_op jit(solution)/shard_map/ppermute | solution.py:282

commit v16 on v12

--- a/solution.py
+++ b/solution.py
@@ -26,23 +26,31 @@
     return jnp.bitwise_xor(virt_irreps[first], virt_irreps[second])
 
 
-def stage_kernel(source, held, sem):
-    copy = pltpu.make_async_copy(source, held, sem)
-    copy.start()
-    copy.wait()
-
-
-def stage(x):
+def stage_kernel(source, rows, held, pair, sems):
+    copies = [
+        pltpu.make_async_copy(source, held, sems.at[0]),
+        pltpu.make_async_copy(rows, pair.at[pl.ds(0, rows.shape[0])], sems.at[1]),
+    ]
+    for copy in copies:
+        copy.start()
+    for copy in copies:
+        copy.wait()
+
+
+def stage(x, rows):
     return pl.pallas_call(
         stage_kernel,
-        out_shape=pltpu.VMEM(x.shape, x.dtype),
-        in_specs=[ANY_SPEC],
-        out_specs=VMEM_SPEC,
-        scratch_shapes=[pltpu.SemaphoreType.DMA],
+        out_shape=[
+            pltpu.VMEM(x.shape, x.dtype),
+            pltpu.VMEM((2 * rows.shape[0],), rows.dtype),
+        ],
+        in_specs=[ANY_SPEC] * 2,
+        out_specs=[VMEM_SPEC] * 2,
+        scratch_shapes=[pltpu.SemaphoreType.DMA((2,))],
         compiler_params=pltpu.CompilerParams(vmem_limit_bytes=8 * MIB),
         cost_estimate=pl.CostEstimate(flops=0, bytes_accessed=2 * x.size, transcendentals=0),
         name="stage_amplitudes",
-    )(pltpu.with_memory_space_constraint(x, pltpu.HBM))
+    )(*[pltpu.with_memory_space_constraint(a, pltpu.HBM) for a in (x, rows)])
 
 
 def pick_kernel(first, per, local_tiles, me, rows, amp, *refs):
@@ -230,7 +238,8 @@
     slots = tile_rows.shape[0]
     first_far = swap(tile_rows, near)
     place = {near: (first_far, 0)}
-    known, rows, bit = [0, near], jnp.concatenate([tile_rows, first_far]), 2
+    amp, pair = stage(amplitudes, tile_rows)
+    known, rows, bit = [0, near], lax.dynamic_update_slice(pair, first_far, (slots,)), 2
     while bit < near:
         rows = jnp.concatenate([rows, swap(rows, bit)])
         known = known + [k ^ bit for k in known]
@@ -240,7 +249,6 @@
         place.setdefault(k, (rows, j * slots))
         place[k ^ 1] = (odd, j * slots)
 
-    amp = stage(amplitudes)
     here = me.reshape(1)
     quarter = near // 4
     far_order = list(range(near, peers, 2)) + list(range(near + 1, peers, 2))

time: 111 us -> 114 us (1.027)
  local copies, waits for them, and re-layouts: 3.6 us -> 7.92 us
  waiting for transfers between devices: 51.6 us -> 49.2 us
  starting transfers between devices: 24.5 us -> 25.7 us
    unnamed x12 -> x14, local copies, waits for them, and re-layouts: 2.92 us -> 7.23 us
    ppermute x10, waiting for transfers between devices: 46.2 us -> 43.8 us  [swap(): return lax.ppermute(x, 'gx', [(i, i ^ k) for i in range(peers)])]
    ppermute x10, starting transfers between devices: 22.4 us -> 23.6 us  [swap(): return lax.ppermute(x, 'gx', [(i, i ^ k) for i in range(peers)])]
  transfers between devices with their start and end apart: 13 -> 13, of which waited for: 6 -> 5; matrix products, arithmetic and copies ran while one was open for 6% -> 5% of each run, Pallas kernels for 21% -> 21%
where the time goes in v16:
time: 114 us
  waiting for transfers between devices  49.2 us (43%)
  starting transfers between devices  25.7 us (23%)
  Pallas kernels  25.5 us (22%)
  local copies, waits for them, and re-layouts  7.92 us (7%)
  other arithmetic  5.08 us (4%)
    ppermute x10, waiting for transfers between devices, swap(): return lax.ppermute(x, 'gx', [(i, i ^ k) for i in range(peers)])  43.8 us
    ppermute x10, starting transfers between devices, swap(): return lax.ppermute(x, 'gx', [(i, i ^ k) for i in range(peers)])  23.6 us
    pallas_call x5, Pallas kernels, ladder(): pl.pallas_call(functools.partial(ladder_kernel, peers_at, list(ahead), pe...  12.2 us
    pallas_call x8, Pallas kernels, pick(): pl.pallas_call(functools.partial(pick_kernel, first, per, width // BLK),...  9.96 us
    unnamed x14, local copies, waits for them, and re-layouts  7.23 us
    ppermute x3, waiting for transfers between devices, swap_gy(): return lax.ppermute(x, 'gy', [(i, i ^ k) for i in range(groups)])  5.42 us
    convert_element_type x1, other arithmetic, per_device(): (pair_irrep(row_tile, virt_irreps) == pair_irrep(col_tile, virt_irreps))....  5.04 us
  transfers between devices with their start and end apart: 13, of which 5 were waited for; matrix products, arithmetic and copies ran while one was open for 5% of the time, Pallas kernels for 21%

profile of v16, /device:TPU:8, one launch (start us, length us, event | category | flops | bytes accessed | tf_op | source)
XLA Modules:
  0.0 113.6 jit_solution(6876845558413274884)
XLA Ops:
  0.0 2.6 %collective-permute-start = (s32[256]{0:T(256)}, s32[256]{0:T(256)S(1)}, u32[]{:S(2)}, u32[]{:S(2)}) collective-permute-start(s32[256]{0:T(256)} %rows.3), channel_id=1, source_target_pairs={{0,16},{4,20},{8,24},{12,28},{16,0},{20,4},{24,8},{28,12},{1,17},{... | collective-permute-start | bytes 3080 | tf_op jit(solution)/shard_map/ppermute | solution.py:236
  2.6 2.2 %stage_amplitudes.1 = (bf16[64,32768]{1,0:T(8,128)(2,1)S(1)}, s32[512]{0:T(512)S(1)}) custom-call(bf16[64,32768]{1,0:T(8,128)(2,1)} %source.1, s32[256]{0:T(256)} %rows.3), custom_call_target="tpu_custom_call" | custom-call | bytes 4194304 | tf_op jit(solution)/shard_map/stage_amplitudes/pallas_call | solution.py:41
  4.8 1.9 %copy-done = bf16[64,32768]{1,0:T(8,128)(2,1)} copy-done((bf16[64,32768]{1,0:T(8,128)(2,1)}, bf16[64,32768]{1,0:T(8,128)(2,1)S(1)}, u32[]{:S(2)}) %copy-start) | copy-done | bytes 4194328
  6.7 0.0 collective-permute-done.rows
  6.8 0.5 collective-permute-start.1
  7.3 2.2 %copy-done.1 = bf16[64,32768]{1,0:T(8,128)(2,1)S(1)} copy-done((bf16[64,32768]{1,0:T(8,128)(2,1)S(1)}, bf16[64,32768]{1,0:T(8,128)(2,1)}, u32[]{:S(2)}) %copy-start.1) | copy-done | bytes 4194328
  9.5 0.7 pick_tiles.13
  10.2 0.5 collective-permute-start.7
  10.7 0.0 collective-permute-done.1
  10.7 0.9 copy-done.2
  11.6 0.8 pick_tiles.10
  12.4 1.6 %collective-permute-start.4 = (bf16[32,64,128]{2,1,0:T(8,128)(2,1)S(1)}, bf16[32,64,128]{2,1,0:T(8,128)(2,1)S(1)}, u32[]{:S(2)}, u32[]{:S(2)}) collective-permute-start(bf16[32,64,128]{2,1,0:T(8,128)(2,1)S(1)} %pick_tiles.10), channel_id=1, source_target_pairs={{0,8},{4,12},{8,0},{12,4},{16,24},{20,28},{24,16},{28,20},{1,9},{5... | collective-permute-start | bytes 1572872 | tf_op jit(solution)/shard_map/ppermute | solution.py:236
  14.1 1.5 %collective-permute-start.2 = (s32[1024]{0:T(1024)S(1)}, s32[1024]{0:T(1024)S(1)}, u32[]{:S(2)}, u32[]{:S(2)}) collective-permute-start(s32[1024]{0:T(1024)S(1)} %pad_add_fusion.rows), channel_id=1, source_target_pairs={{0,4},{4,0},{8,12},{12,8},{16,20},{20,16},{24,28},{28,24},{1,5},{5... | collective-permute-start | bytes 12296 | tf_op jit(solution)/shard_map/ppermute | solution.py:236
  15.6 0.7 fusion.4
  16.3 1.6 %pick_tiles.12 = bf16[32,64,128]{2,1,0:T(8,128)(2,1)} custom-call(s32[1]{0:T(128)} %bitcast.9.me, s32[1024]{0:T(1024)S(1)} %pad_add_fusion.rows, bf16[64,32768]{1,0:T(8,128)(2,1)S(1)} %copy-done.2), custom_call_target="tpu_custom_call" | custom-call | bytes 1048576 | tf_op jit(solution)/shard_map/pick_tiles/pallas_call | solution.py:71
  17.8 0.5 collective-permute-start.6
  18.3 0.0 collective-permute-done.2.rows
  18.4 1.6 %pick_tiles.9 = bf16[32,64,128]{2,1,0:T(8,128)(2,1)} custom-call(s32[1]{0:T(128)} %bitcast.9.me, s32[1024]{0:T(1024)S(1)} %collective-permute-done.2.rows, bf16[64,32768]{1,0:T(8,128)(2,1)S(1)} %copy-done.2), custom_call_target="tpu_custom_call" | custom-call | bytes 1048576 | tf_op jit(solution)/shard_map/pick_tiles/pallas_call | solution.py:71
  19.9 0.8 collective-permute-start.3
  20.7 1.5 %pick_tiles.11 = bf16[32,64,128]{2,1,0:T(8,128)(2,1)} custom-call(s32[1]{0:T(128)} %bitcast.9.me, s32[1024]{0:T(1024)S(1)} %collective-permute-done.2.rows, bf16[64,32768]{1,0:T(8,128)(2,1)S(1)} %copy-done.2), custom_call_target="tpu_custom_call" | custom-call | bytes 1048576 | tf_op jit(solution)/shard_map/pick_tiles/pallas_call | solution.py:71
  22.3 3.1 %collective-permute-start.5 = (bf16[32,64,128]{2,1,0:T(8,128)(2,1)}, bf16[32,64,128]{2,1,0:T(8,128)(2,1)S(1)}, u32[]{:S(2)}, u32[]{:S(2)}) collective-permute-start(bf16[32,64,128]{2,1,0:T(8,128)(2,1)} %pick_tiles.11), channel_id=1, source_target_pairs={{0,12},{4,8},{8,4},{12,0},{16,28},{20,24},{24,20},{28,16},{1,13},{... | collective-permute-start | bytes 1572872 | tf_op jit(solution)/shard_map/ppermute | solution.py:236
  25.4 9.8 %collective-permute-done.7.refs_0_ = bf16[32,64,128]{2,1,0:T(8,128)(2,1)S(1)} collective-permute-done((bf16[32,64,128]{2,1,0:T(8,128)(2,1)S(1)}, bf16[32,64,128]{2,1,0:T(8,128)(2,1)S(1)}, u32[]{:S(2)}, u32[]{:S(2)}) %collective-permute-start.7) | collective-permute-done | bytes 524320 | tf_op jit(solution)/shard_map/ppermute | solution.py:236
  35.2 1.6 %pick_tiles.15 = bf16[32,64,128]{2,1,0:T(8,128)(2,1)} custom-call(s32[1]{0:T(128)} %bitcast.9.me, s32[1024]{0:T(1024)S(1)} %collective-permute-done.2.rows, bf16[64,32768]{1,0:T(8,128)(2,1)S(1)} %copy-done.2, bf16[32,64,128]{2,1,0:T(8,128)(2,1)S(1)} %collective-permute-done.7.refs_0_), custom_call_target="tpu_custom_call" | custom-call | bytes 1048576 | tf_op jit(solution)/shard_map/pick_tiles/pallas_call | solution.py:71
  36.7 12.3 %collective-permute-start.9 = (bf16[32,64,128]{2,1,0:T(8,128)(2,1)}, bf16[32,64,128]{2,1,0:T(8,128)(2,1)}, u32[]{:S(2)}, u32[]{:S(2)}) collective-permute-start(bf16[32,64,128]{2,1,0:T(8,128)(2,1)} %pick_tiles.15), channel_id=1, source_target_pairs={{0,20},{4,16},{8,28},{12,24},{16,4},{20,0},{24,12},{28,8},{1,21},{... | collective-permute-start | bytes 1572872 | tf_op jit(solution)/shard_map/ppermute | solution.py:236
  49.0 0.0 collective-permute-done.4.refs_2_.refs_1_
  49.1 1.6 %pick_tiles.14 = bf16[32,64,128]{2,1,0:T(8,128)(2,1)} custom-call(s32[1]{0:T(128)} %bitcast.9.me, s32[1024]{0:T(1024)S(1)} %collective-permute-done.2.rows, bf16[64,32768]{1,0:T(8,128)(2,1)S(1)} %copy-done.2, bf16[32,64,128]{2,1,0:T(8,128)(2,1)S(1)} %collective-permute-done.7.refs_0_, bf16[32,64,128]{2,1,0:T(8,128)(2,1)S(1)} %collective-permute-done.4.refs_2_.refs_1_), custom_call_target="tpu_custom_call" | custom-call | bytes 1048576 | tf_op jit(solution)/shard_map/pick_tiles/pallas_call | solution.py:71
  50.6 0.0 collective-permute-start.8
  50.6 2.2 %copy-done.3 = bf16[64,32768]{1,0:T(8,128)(2,1)S(1)} copy-done((bf16[64,32768]{1,0:T(8,128)(2,1)S(1)}, bf16[64,32768]{1,0:T(8,128)(2,1)}, u32[]{:S(2)}) %copy-start.3) | copy-done | bytes 4194328
  52.8 0.7 pick_tiles.8.refs_0_
  53.6 5.0 %compare_convert_fusion.live = f32[256]{0:T(256)S(1)} fusion(s32[256]{0:T(256)S(1)} %copy-done.6, s32[256]{0:T(256)S(1)} %copy-done.4, s32[]{:T(128)} %bitcast, s32[]{:T(128)} %bitcast.1, s32[]{:T(128)} %bitcast.2, s32[]{:T(128)} %bitcast.3, s32[]{:T(128)} %bitcast.4, s32[]{:T(128)} %bitcast.5, s32[]{:T(128)} %bitcast.6, s32[]{:T(128)} %bitcast.7, ...), kind=kLoop, calls=%fused_computation.33 | loop fusion | flops 44544 | bytes 3112 | tf_op jit(solution)/shard_map/convert_element_type | solution.py:267
  58.6 2.2 %ladder_products.5.refs_1_ = f32[32,64,128]{2,1,0:T(8,128)S(1)} custom-call(s32[8]{0:T(128)S(1)} %iota_xor_fusion.order, s32[256]{0:T(256)S(1)} %fusion.3.cols, f32[256]{0:T(256)S(1)} %compare_convert_fusion.live, bf16[8,32,128,128]{3,2,1,0:T(8,128)(2,1)} %bitcast.10, bf16[32,64,128]{2,1,0:T(8,128)(2,1)S(1)} %collective-permute-done.7.refs_0_), custom_call_target="tpu_custom_call" | custom-call | flops 67108864 | bytes 1048576 | tf_op jit(solution)/shard_map/ladder_products/pallas_call | solution.py:146
  60.9 0.0 collective-permute-done.6.refs_0_
  60.9 2.7 %ladder_products.6.refs_4_ = f32[32,64,128]{2,1,0:T(8,128)S(1)} custom-call(s32[8]{0:T(128)S(1)} %iota_xor_fusion.order, s32[256]{0:T(256)S(1)} %fusion.3.cols, f32[256]{0:T(256)S(1)} %compare_convert_fusion.live, bf16[8,32,128,128]{3,2,1,0:T(8,128)(2,1)} %bitcast.11, ...), custom_call_target="tpu_custom_call", output_to_operand_aliasing={{}: (5, {})} | custom-call | flops 67108864 | bytes 1048576 | tf_op jit(solution)/shard_map/ladder_products/pallas_call | solution.py:146
  63.6 0.0 collective-permute-done.3.refs_1_
  63.6 0.0 collective-permute-done.5.refs_3_
  63.6 3.5 %ladder_products.7 = (f32[32,64,128]{2,1,0:T(8,128)S(1)}, bf16[1,32,128,128]{3,2,1,0:T(8,128)(2,1)S(1)}) custom-call(s32[8]{0:T(128)S(1)} %iota_xor_fusion.order, s32[256]{0:T(256)S(1)} %fusion.3.cols, f32[256]{0:T(256)S(1)} %compare_convert_fusion.live, bf16[8,32,128,128]{3,2,1,0:T(8,128)(2,1)} %bitcast.12, ...), custom_call_target="tpu_custom_call", output_to_operand_aliasing={{0}: (8, {})} | custom-call | flops 268435456 | bytes 5242880 | tf_op jit(solution)/shard_map/ladder_products/pallas_call | solution.py:146
  67.2 22.8 %collective-permute-done.9.refs_0_ = bf16[32,64,128]{2,1,0:T(8,128)(2,1)} collective-permute-done((bf16[32,64,128]{2,1,0:T(8,128)(2,1)}, bf16[32,64,128]{2,1,0:T(8,128)(2,1)}, u32[]{:S(2)}, u32[]{:S(2)}) %collective-permute-start.9) | collective-permute-done | bytes 524320 | tf_op jit(solution)/shard_map/ppermute | solution.py:236
  89.9 2.7 %ladder_products.8.refs_1_ = f32[32,64,128]{2,1,0:T(8,128)S(1)} custom-call(s32[8]{0:T(128)S(1)} %iota_xor_fusion.order, s32[256]{0:T(256)S(1)} %fusion.3.cols, f32[256]{0:T(256)S(1)} %compare_convert_fusion.live, bf16[8,32,128,128]{3,2,1,0:T(8,128)(2,1)} %bitcast.13, ...), custom_call_target="tpu_custom_call", output_to_operand_aliasing={{}: (5, {})} | custom-call | flops 67108864 | bytes 1048576 | tf_op jit(solution)/shard_map/ladder_products/pallas_call | solution.py:146
  92.7 11.2 %collective-permute-done.8.refs_0_ = bf16[32,64,128]{2,1,0:T(8,128)(2,1)S(1)} collective-permute-done((bf16[32,64,128]{2,1,0:T(8,128)(2,1)}, bf16[32,64,128]{2,1,0:T(8,128)(2,1)S(1)}, u32[]{:S(2)}, u32[]{:S(2)}) %collective-permute-start.8) | collective-permute-done | bytes 524320 | tf_op jit(solution)/shard_map/ppermute | solution.py:236
  103.9 1.1 ladder_products.9
  105.0 0.1 collective-permute-start.11
  105.0 0.5 collective-permute-start.10
  105.5 1.0 collective-permute-done.11.got
  106.6 0.2 encode_sums.1
  106.8 1.6 %collective-permute-start.12 = (s16[9,64,128]{2,1,0:T(8,128)(2,1)S(1)}, s16[9,64,128]{2,1,0:T(8,128)(2,1)S(1)}, u32[]{:S(2)}, u32[]{:S(2)}) collective-permute-start(s16[9,64,128]{2,1,0:T(8,128)(2,1)S(1)} %encode_sums.1), channel_id=1, source_target_pairs={{0,2},{1,3},{2,0},{3,1},{4,6},{5,7},{6,4},{7,5},{8,10},{9,11},{10,... | collective-permute-start | bytes 442376 | tf_op jit(solution)/shard_map/ppermute | solution.py:290
  108.3 0.0 collective-permute-done.10.got
  108.3 4.4 %collective-permute-done.12.refs_0_ = s16[9,64,128]{2,1,0:T(8,128)(2,1)S(1)} collective-permute-done((s16[9,64,128]{2,1,0:T(8,128)(2,1)S(1)}, s16[9,64,128]{2,1,0:T(8,128)(2,1)S(1)}, u32[]{:S(2)}, u32[]{:S(2)}) %collective-permute-start.12) | collective-permute-done | bytes 147488 | tf_op jit(solution)/shard_map/ppermute | solution.py:290
  112.7 0.9 decode_sums.1
  (14 shorter events, 0.1 us)
Async XLA Ops:
  0.0 6.7 %collective-permute-start = (s32[256]{0:T(256)}, s32[256]{0:T(256)S(1)}, u32[]{:S(2)}, u32[]{:S(2)}) collective-permute-start(s32[256]{0:T(256)} %rows.3), channel_id=1, source_target_pairs={{0,16},{4,20},{8,24},{12,28},{16,0},{20,4},{24,8},{28,12},{1,17},{... | collective-permute-start | bytes 3080 | tf_op jit(solution)/shard_map/ppermute | solution.py:236
  4.8 1.9 %copy-start = (bf16[64,32768]{1,0:T(8,128)(2,1)}, bf16[64,32768]{1,0:T(8,128)(2,1)S(1)}, u32[]{:S(2)}) copy-start(bf16[64,32768]{1,0:T(8,128)(2,1)S(1)} %get-tuple-element.13.amp) | copy-start | bytes 12582916
  6.8 4.0 %collective-permute-start.1 = (s32[512]{0:T(512)S(1)}, s32[512]{0:T(512)S(1)}, u32[]{:S(2)}, u32[]{:S(2)}) collective-permute-start(s32[512]{0:T(512)S(1)} %constant_dynamic-update-slice_fusion), channel_id=1, source_target_pairs={{0,8},{4,12},{8,0},{12,4},{16,24},{20,28},{24,16},{28,20},{1,9},{5... | collective-permute-start | bytes 6152 | tf_op jit(solution)/shard_map/ppermute | solution.py:236
  7.3 2.2 %copy-start.1 = (bf16[64,32768]{1,0:T(8,128)(2,1)S(1)}, bf16[64,32768]{1,0:T(8,128)(2,1)}, u32[]{:S(2)}) copy-start(bf16[64,32768]{1,0:T(8,128)(2,1)} %copy-done) | copy-start | bytes 12582916
  9.5 2.2 %copy-start.2 = (bf16[64,32768]{1,0:T(8,128)(2,1)S(1)}, bf16[64,32768]{1,0:T(8,128)(2,1)}, u32[]{:S(2)}) copy-start(bf16[64,32768]{1,0:T(8,128)(2,1)} %copy-done) | copy-start | bytes 12582916
  9.5 6.1 %copy-start.5 = (s32[8]{0:T(128)S(1)}, s32[8]{0:T(128)}, u32[]{:S(2)}) copy-start(s32[8]{0:T(128)} %param.6) | copy-start | bytes 100
  10.2 25.0 %collective-permute-start.7 = (bf16[32,64,128]{2,1,0:T(8,128)(2,1)S(1)}, bf16[32,64,128]{2,1,0:T(8,128)(2,1)S(1)}, u32[]{:S(2)}, u32[]{:S(2)}) collective-permute-start(bf16[32,64,128]{2,1,0:T(8,128)(2,1)S(1)} %pick_tiles.13), channel_id=1, source_target_pairs={{0,16},{4,20},{8,24},{12,28},{16,0},{20,4},{24,8},{28,12},{1,17},{... | collective-permute-start | bytes 1572872 | tf_op jit(solution)/shard_map/ppermute | solution.py:236
  12.4 36.6 %collective-permute-start.4 = (bf16[32,64,128]{2,1,0:T(8,128)(2,1)S(1)}, bf16[32,64,128]{2,1,0:T(8,128)(2,1)S(1)}, u32[]{:S(2)}, u32[]{:S(2)}) collective-permute-start(bf16[32,64,128]{2,1,0:T(8,128)(2,1)S(1)} %pick_tiles.10), channel_id=1, source_target_pairs={{0,8},{4,12},{8,0},{12,4},{16,24},{20,28},{24,16},{28,20},{1,9},{5... | collective-permute-start | bytes 1572872 | tf_op jit(solution)/shard_map/ppermute | solution.py:236
  14.1 4.3 %collective-permute-start.2 = (s32[1024]{0:T(1024)S(1)}, s32[1024]{0:T(1024)S(1)}, u32[]{:S(2)}, u32[]{:S(2)}) collective-permute-start(s32[1024]{0:T(1024)S(1)} %pad_add_fusion.rows), channel_id=1, source_target_pairs={{0,4},{4,0},{8,12},{12,8},{16,20},{20,16},{24,28},{28,24},{1,5},{5... | collective-permute-start | bytes 12296 | tf_op jit(solution)/shard_map/ppermute | solution.py:236
  17.8 43.1 %collective-permute-start.6 = (bf16[32,64,128]{2,1,0:T(8,128)(2,1)}, bf16[32,64,128]{2,1,0:T(8,128)(2,1)}, u32[]{:S(2)}, u32[]{:S(2)}) collective-permute-start(bf16[32,64,128]{2,1,0:T(8,128)(2,1)} %pick_tiles.12), channel_id=1, source_target_pairs={{0,24},{4,28},{8,16},{12,20},{16,8},{20,12},{24,0},{28,4},{1,25},{... | collective-permute-start | bytes 1572872 | tf_op jit(solution)/shard_map/ppermute | solution.py:236
  19.9 43.7 %collective-permute-start.3 = (bf16[32,64,128]{2,1,0:T(8,128)(2,1)}, bf16[32,64,128]{2,1,0:T(8,128)(2,1)S(1)}, u32[]{:S(2)}, u32[]{:S(2)}) collective-permute-start(bf16[32,64,128]{2,1,0:T(8,128)(2,1)} %pick_tiles.9), channel_id=1, source_target_pairs={{0,4},{4,0},{8,12},{12,8},{16,20},{20,16},{24,28},{28,24},{1,5},{5... | collective-permute-start | bytes 1572872 | tf_op jit(solution)/shard_map/ppermute | solution.py:236
  22.3 41.3 %collective-permute-start.5 = (bf16[32,64,128]{2,1,0:T(8,128)(2,1)}, bf16[32,64,128]{2,1,0:T(8,128)(2,1)S(1)}, u32[]{:S(2)}, u32[]{:S(2)}) collective-permute-start(bf16[32,64,128]{2,1,0:T(8,128)(2,1)} %pick_tiles.11), channel_id=1, source_target_pairs={{0,12},{4,8},{8,4},{12,0},{16,28},{20,24},{24,20},{28,16},{1,13},{... | collective-permute-start | bytes 1572872 | tf_op jit(solution)/shard_map/ppermute | solution.py:236
  36.7 13.9 %copy-start.4 = (s32[256]{0:T(256)S(1)}, s32[256]{0:T(256)}, u32[]{:S(2)}) copy-start(s32[256]{0:T(256)} %rows.3) | copy-start | bytes 3076
  36.7 16.8 %copy-start.6 = (s32[256]{0:T(256)S(1)}, s32[256]{0:T(256)}, u32[]{:S(2)}) copy-start(s32[256]{0:T(256)} %param.9) | copy-start | bytes 3076
  36.7 53.2 %collective-permute-start.9 = (bf16[32,64,128]{2,1,0:T(8,128)(2,1)}, bf16[32,64,128]{2,1,0:T(8,128)(2,1)}, u32[]{:S(2)}, u32[]{:S(2)}) collective-permute-start(bf16[32,64,128]{2,1,0:T(8,128)(2,1)} %pick_tiles.15), channel_id=1, source_target_pairs={{0,20},{4,16},{8,28},{12,24},{16,4},{20,0},{24,12},{28,8},{1,21},{... | collective-permute-start | bytes 1572872 | tf_op jit(solution)/shard_map/ppermute | solution.py:236
  50.6 53.3 %collective-permute-start.8 = (bf16[32,64,128]{2,1,0:T(8,128)(2,1)}, bf16[32,64,128]{2,1,0:T(8,128)(2,1)S(1)}, u32[]{:S(2)}, u32[]{:S(2)}) collective-permute-start(bf16[32,64,128]{2,1,0:T(8,128)(2,1)} %pick_tiles.14), channel_id=1, source_target_pairs={{0,28},{4,24},{8,20},{12,16},{16,12},{20,8},{24,4},{28,0},{1,29},{... | collective-permute-start | bytes 1572872 | tf_op jit(solution)/shard_map/ppermute | solution.py:236
  50.6 2.2 %copy-start.3 = (bf16[64,32768]{1,0:T(8,128)(2,1)S(1)}, bf16[64,32768]{1,0:T(8,128)(2,1)}, u32[]{:S(2)}) copy-start(bf16[64,32768]{1,0:T(8,128)(2,1)} %copy-done) | copy-start | bytes 12582916
  105.0 1.6 %collective-permute-start.11 = (f32[8,64,128]{2,1,0:T(8,128)S(1)}, f32[8,64,128]{2,1,0:T(8,128)S(1)}, u32[]{:S(2)}, u32[]{:S(2)}) collective-permute-start(f32[8,64,128]{2,1,0:T(8,128)S(1)} %get-tuple-element.20), channel_id=1, source_target_pairs={{0,1},{1,0},{2,3},{3,2},{4,5},{5,4},{6,7},{7,6},{8,9},{9,8},{10,11... | collective-permute-start | bytes 786440 | tf_op jit(solution)/shard_map/ppermute | solution.py:290
  105.0 3.3 %collective-permute-start.10 = (f32[8,64,128]{2,1,0:T(8,128)S(1)}, f32[8,64,128]{2,1,0:T(8,128)S(1)}, u32[]{:S(2)}, u32[]{:S(2)}) collective-permute-start(f32[8,64,128]{2,1,0:T(8,128)S(1)} %get-tuple-element.18), channel_id=1, source_target_pairs={{0,1},{1,0},{2,3},{3,2},{4,5},{5,4},{6,7},{7,6},{8,9},{9,8},{10,11... | collective-permute-start | bytes 786440 | tf_op jit(solution)/shard_map/ppermute | solution.py:290
  106.8 6.0 %collective-permute-start.12 = (s16[9,64,128]{2,1,0:T(8,128)(2,1)S(1)}, s16[9,64,128]{2,1,0:T(8,128)(2,1)S(1)}, u32[]{:S(2)}, u32[]{:S(2)}) collective-permute-start(s16[9,64,128]{2,1,0:T(8,128)(2,1)S(1)} %encode_sums.1), channel_id=1, source_target_pairs={{0,2},{1,3},{2,0},{3,1},{4,6},{5,7},{6,4},{7,5},{8,10},{9,11},{10,... | collective-permute-start | bytes 442376 | tf_op jit(solution)/shard_map/ppermute | solution.py:290

commit v17 on v15

--- a/solution.py
+++ b/solution.py
@@ -186,9 +186,10 @@
 
 
 def decode_kernel(kept, got, *refs):
-    arrived, out = refs[:-1], refs[-1]
+    *arrived, out, held, sems = refs
     share = kept.shape[0]
     lane = lax.broadcasted_iota(jnp.int32, kept.shape[1:], 1)
+    copies = []
     for j in range(share):
         value = kept[j] + got[j]
         for part in arrived:
@@ -196,7 +197,12 @@
             power = jnp.sum(powers.astype(jnp.float32), axis=1, keepdims=True)
             code = part[j].astype(jnp.int32).astype(jnp.float32)
             value = value + code * (jnp.exp2(power) * (1.0 / CODE_TOP))
-        out[:, j * BLK : (j + 1) * BLK] = value
+        held[j] = value
+        columns = out.at[:, pl.ds(j * BLK, BLK)]
+        copies.append(pltpu.make_async_copy(held.at[j], columns, sems.at[j]))
+        copies[-1].start()
+    for copy in copies:
+        copy.wait()
 
 
 def decode(kept, got, arrived):
@@ -205,7 +211,11 @@
         decode_kernel,
         out_shape=jax.ShapeDtypeStruct((occupied, share * BLK), jnp.float32),
         in_specs=[VMEM_SPEC] * (2 + len(arrived)),
-        out_specs=VMEM_SPEC,
+        out_specs=ANY_SPEC,
+        scratch_shapes=[
+            pltpu.VMEM(kept.shape, jnp.float32),
+            pltpu.SemaphoreType.DMA((share,)),
+        ],
         compiler_params=pltpu.CompilerParams(vmem_limit_bytes=8 * MIB),
         cost_estimate=pl.CostEstimate(
             flops=8 * kept.size, bytes_accessed=14 * kept.size, transcendentals=0
@@ -246,8 +256,8 @@
     far_order = list(range(near, peers, 2)) + list(range(near + 1, peers, 2))
     far = [far_order[j * quarter : (j + 1) * quarter] for j in range(4)]
     arrived = {0: pick(here, tile_rows, 0, amp, per)}
-    for k in far[0] + far[1] + list(range(1, near)) + far[2] + far[3]:
-        after = ()
+    for k in far[0] + far[1] + list(range(2, near, 2)) + list(range(1, near, 2)) + far[2] + far[3]:
+        after = (arrived[far[0][0]],) if k < near else ()
         if k in far[2]:
             after = (arrived[far[0][far[2].index(k)]],)
         if k in far[3]:

time: 111 us -> 115 us (1.036)
  the two profiles are of different devices: /device:TPU:8 before, /device:TPU:0 now
where the time goes in v17:
time: 115 us
  waiting for transfers between devices  60.7 us (53%)
  Pallas kernels  24.9 us (22%)
  starting transfers between devices  20.4 us (18%)
  other arithmetic  4.81 us (4%)
  local copies, waits for them, and re-layouts  3.61 us (3%)
    ppermute x10, waiting for transfers between devices, swap(): return lax.ppermute(x, 'gx', [(i, i ^ k) for i in range(peers)])  55.3 us
    ppermute x10, starting transfers between devices, swap(): return lax.ppermute(x, 'gx', [(i, i ^ k) for i in range(peers)])  18.3 us
    pallas_call x5, Pallas kernels, ladder(): pl.pallas_call(functools.partial(ladder_kernel, peers_at, list(ahead), pe...  12.4 us
    pallas_call x8, Pallas kernels, pick(): pl.pallas_call(functools.partial(pick_kernel, first, per, width // BLK),...  9.2 us
    ppermute x3, waiting for transfers between devices, swap_gy(): return lax.ppermute(x, 'gy', [(i, i ^ k) for i in range(groups)])  5.42 us
    convert_element_type x1, other arithmetic, per_device(): (pair_irrep(row_tile, virt_irreps) == pair_irrep(col_tile, virt_irreps))....  4.77 us
    unnamed x12, local copies, waits for them, and re-layouts  2.92 us
  transfers between devices with their start and end apart: 13, of which 6 were waited for; matrix products, arithmetic and copies ran while one was open for 5% of the time, Pallas kernels for 20%

profile of v17, /device:TPU:0, one launch (start us, length us, event | category | flops | bytes accessed | tf_op | source)
XLA Modules:
  0.0 114.6 jit_solution(13091218100855637903)
XLA Ops:
  0.0 4.0 %collective-permute-start = (s32[256]{0:T(256)}, s32[256]{0:T(256)S(1)}, u32[]{:S(2)}, u32[]{:S(2)}) collective-permute-start(s32[256]{0:T(256)} %rows.1), channel_id=1, source_target_pairs={{0,16},{4,20},{8,24},{12,28},{16,0},{20,4},{24,8},{28,12},{1,17},{... | collective-permute-start | bytes 3080 | tf_op jit(solution)/shard_map/ppermute | solution.py:238
  4.0 0.7 constant_dynamic-update-slice_fusion.2
  4.8 2.2 %stage_amplitudes.1.amp = bf16[64,32768]{1,0:T(8,128)(2,1)S(1)} custom-call(bf16[64,32768]{1,0:T(8,128)(2,1)} %source.1), custom_call_target="tpu_custom_call" | custom-call | bytes 4194304 | tf_op jit(solution)/shard_map/stage_amplitudes/pallas_call | solution.py:36
  7.0 0.0 copy-start
  7.0 0.0 collective-permute-done.rows
  7.0 1.6 %collective-permute-start.1 = (s32[512]{0:T(512)S(1)}, s32[512]{0:T(512)S(1)}, u32[]{:S(2)}, u32[]{:S(2)}) collective-permute-start(s32[512]{0:T(512)S(1)} %pad_add_fusion), channel_id=1, source_target_pairs={{0,8},{4,12},{8,0},{12,4},{16,24},{20,28},{24,16},{28,20},{1,9},{5... | collective-permute-start | bytes 6152 | tf_op jit(solution)/shard_map/ppermute | solution.py:238
  8.7 0.7 pick_tiles.9
  9.4 1.8 %collective-permute-start.3 = (bf16[32,64,128]{2,1,0:T(8,128)(2,1)S(1)}, bf16[32,64,128]{2,1,0:T(8,128)(2,1)S(1)}, u32[]{:S(2)}, u32[]{:S(2)}) collective-permute-start(bf16[32,64,128]{2,1,0:T(8,128)(2,1)S(1)} %pick_tiles.9), channel_id=1, source_target_pairs={{0,16},{4,20},{8,24},{12,28},{16,0},{20,4},{24,8},{28,12},{1,17},{... | collective-permute-start | bytes 1572872 | tf_op jit(solution)/shard_map/ppermute | solution.py:238
  11.2 0.0 collective-permute-done.1
  11.2 0.8 pick_tiles.13
  12.0 2.5 %collective-permute-start.7 = (bf16[32,64,128]{2,1,0:T(8,128)(2,1)S(1)}, bf16[32,64,128]{2,1,0:T(8,128)(2,1)S(1)}, u32[]{:S(2)}, u32[]{:S(2)}) collective-permute-start(bf16[32,64,128]{2,1,0:T(8,128)(2,1)S(1)} %pick_tiles.13), channel_id=1, source_target_pairs={{0,24},{4,28},{8,16},{12,20},{16,8},{20,12},{24,0},{28,4},{1,25},{... | collective-permute-start | bytes 1572872 | tf_op jit(solution)/shard_map/ppermute | solution.py:238
  14.4 1.5 %collective-permute-start.2 = (s32[1024]{0:T(1024)S(1)}, s32[1024]{0:T(1024)S(1)}, u32[]{:S(2)}, u32[]{:S(2)}) collective-permute-start(s32[1024]{0:T(1024)S(1)} %constant_dynamic-update-slice_fusion.rows), channel_id=1, source_target_pairs={{0,4},{4,0},{8,12},{12,8},{16,20},{20,16},{24,28},{28,24},{1,5},{5... | collective-permute-start | bytes 12296 | tf_op jit(solution)/shard_map/ppermute | solution.py:238
  16.0 0.7 fusion.4
  16.6 1.4 %collective-permute-done.2.rows = s32[1024]{0:T(1024)S(1)} collective-permute-done((s32[1024]{0:T(1024)S(1)}, s32[1024]{0:T(1024)S(1)}, u32[]{:S(2)}, u32[]{:S(2)}) %collective-permute-start.2) | collective-permute-done | bytes 4128 | tf_op jit(solution)/shard_map/ppermute | solution.py:238
  18.0 27.9 %collective-permute-done.3.refs_0_ = bf16[32,64,128]{2,1,0:T(8,128)(2,1)S(1)} collective-permute-done((bf16[32,64,128]{2,1,0:T(8,128)(2,1)S(1)}, bf16[32,64,128]{2,1,0:T(8,128)(2,1)S(1)}, u32[]{:S(2)}, u32[]{:S(2)}) %collective-permute-start.3) | collective-permute-done | bytes 524320 | tf_op jit(solution)/shard_map/ppermute | solution.py:238
  45.9 1.6 %pick_tiles.10 = bf16[32,64,128]{2,1,0:T(8,128)(2,1)} custom-call(s32[1]{0:T(128)} %bitcast.9.me, s32[1024]{0:T(1024)S(1)} %collective-permute-done.2.rows, bf16[64,32768]{1,0:T(8,128)(2,1)S(1)} %stage_amplitudes.1.amp, bf16[32,64,128]{2,1,0:T(8,128)(2,1)S(1)} %collective-permute-done.3.refs_0_), custom_call_target="tpu_custom_call" | custom-call | bytes 1048576 | tf_op jit(solution)/shard_map/pick_tiles/pallas_call | solution.py:63
  47.5 1.5 %collective-permute-start.4 = (bf16[32,64,128]{2,1,0:T(8,128)(2,1)}, bf16[32,64,128]{2,1,0:T(8,128)(2,1)S(1)}, u32[]{:S(2)}, u32[]{:S(2)}) collective-permute-start(bf16[32,64,128]{2,1,0:T(8,128)(2,1)} %pick_tiles.10), channel_id=1, source_target_pairs={{0,4},{4,0},{8,12},{12,8},{16,20},{20,16},{24,28},{28,24},{1,5},{5... | collective-permute-start | bytes 1572872 | tf_op jit(solution)/shard_map/ppermute | solution.py:238
  49.0 1.6 %pick_tiles.12 = bf16[32,64,128]{2,1,0:T(8,128)(2,1)} custom-call(s32[1]{0:T(128)} %bitcast.9.me, s32[1024]{0:T(1024)S(1)} %collective-permute-done.2.rows, bf16[64,32768]{1,0:T(8,128)(2,1)S(1)} %stage_amplitudes.1.amp, bf16[32,64,128]{2,1,0:T(8,128)(2,1)S(1)} %collective-permute-done.3.refs_0_), custom_call_target="tpu_custom_call" | custom-call | bytes 1048576 | tf_op jit(solution)/shard_map/pick_tiles/pallas_call | solution.py:63
  50.5 0.0 collective-permute-start.6
  50.5 0.8 pick_tiles.15
  51.3 3.4 %collective-permute-start.9 = (bf16[32,64,128]{2,1,0:T(8,128)(2,1)S(1)}, bf16[32,64,128]{2,1,0:T(8,128)(2,1)S(1)}, u32[]{:S(2)}, u32[]{:S(2)}) collective-permute-start(bf16[32,64,128]{2,1,0:T(8,128)(2,1)S(1)} %pick_tiles.15), channel_id=1, source_target_pairs={{0,20},{4,16},{8,28},{12,24},{16,4},{20,0},{24,12},{28,8},{1,21},{... | collective-permute-start | bytes 1572872 | tf_op jit(solution)/shard_map/ppermute | solution.py:238
  54.8 1.6 %pick_tiles.11 = bf16[32,64,128]{2,1,0:T(8,128)(2,1)} custom-call(s32[1]{0:T(128)} %bitcast.9.me, s32[1024]{0:T(1024)S(1)} %constant_dynamic-update-slice_fusion.rows, bf16[64,32768]{1,0:T(8,128)(2,1)S(1)} %stage_amplitudes.1.amp, bf16[32,64,128]{2,1,0:T(8,128)(2,1)S(1)} %collective-permute-done.3.refs_0_), custom_call_target="tpu_custom_call" | custom-call | bytes 1048576 | tf_op jit(solution)/shard_map/pick_tiles/pallas_call | solution.py:63
  56.3 0.0 collective-permute-start.5
  56.3 0.0 collective-permute-done.7.refs_0_.refs_1_
  56.4 0.0 copy-done
  56.4 1.6 %pick_tiles.14 = bf16[32,64,128]{2,1,0:T(8,128)(2,1)} custom-call(s32[1]{0:T(128)} %bitcast.9.me, s32[1024]{0:T(1024)S(1)} %collective-permute-done.2.rows, bf16[64,32768]{1,0:T(8,128)(2,1)S(1)} %stage_amplitudes.1.amp, bf16[32,64,128]{2,1,0:T(8,128)(2,1)S(1)} %collective-permute-done.3.refs_0_, bf16[32,64,128]{2,1,0:T(8,128)(2,1)S(1)} %collective-permute-done.7.refs_0_.refs_1_), custom_call_target="tpu_custom_call" | custom-call | bytes 1048576 | tf_op jit(solution)/shard_map/pick_tiles/pallas_call | solution.py:63
  57.9 1.9 %collective-permute-start.8 = (bf16[32,64,128]{2,1,0:T(8,128)(2,1)}, bf16[32,64,128]{2,1,0:T(8,128)(2,1)}, u32[]{:S(2)}, u32[]{:S(2)}) collective-permute-start(bf16[32,64,128]{2,1,0:T(8,128)(2,1)} %pick_tiles.14), channel_id=1, source_target_pairs={{0,28},{4,24},{8,20},{12,16},{16,12},{20,8},{24,4},{28,0},{1,29},{... | collective-permute-start | bytes 1572872 | tf_op jit(solution)/shard_map/ppermute | solution.py:238
  59.8 2.2 %copy-done.1 = bf16[64,32768]{1,0:T(8,128)(2,1)S(1)} copy-done((bf16[64,32768]{1,0:T(8,128)(2,1)S(1)}, bf16[64,32768]{1,0:T(8,128)(2,1)}, u32[]{:S(2)}) %copy-start.1) | copy-done | bytes 4194328
  62.0 0.7 pick_tiles.8.refs_0_
  62.8 4.8 %compare_convert_fusion.live = f32[256]{0:T(256)S(1)} fusion(s32[256]{0:T(256)S(1)} %copy-done.4, s32[256]{0:T(256)S(1)} %copy-done.2, s32[]{:T(128)} %bitcast, s32[]{:T(128)} %bitcast.1, s32[]{:T(128)} %bitcast.2, s32[]{:T(128)} %bitcast.3, s32[]{:T(128)} %bitcast.4, s32[]{:T(128)} %bitcast.5, s32[]{:T(128)} %bitcast.6, s32[]{:T(128)} %bitcast.7, ...), kind=kLoop, calls=%fused_computation.36 | loop fusion | flops 44544 | bytes 3112 | tf_op jit(solution)/shard_map/convert_element_type | solution.py:269
  67.6 2.2 %ladder_products.5.refs_1_ = f32[32,64,128]{2,1,0:T(8,128)S(1)} custom-call(s32[8]{0:T(128)S(1)} %iota_xor_fusion.order, s32[256]{0:T(256)S(1)} %fusion.3.cols, f32[256]{0:T(256)S(1)} %compare_convert_fusion.live, bf16[8,32,128,128]{3,2,1,0:T(8,128)(2,1)} %bitcast.10, bf16[32,64,128]{2,1,0:T(8,128)(2,1)S(1)} %collective-permute-done.3.refs_0_), custom_call_target="tpu_custom_call" | custom-call | flops 67108864 | bytes 1048576 | tf_op jit(solution)/shard_map/ladder_products/pallas_call | solution.py:138
  69.8 2.2 %ladder_products.6.refs_4_ = f32[32,64,128]{2,1,0:T(8,128)S(1)} custom-call(s32[8]{0:T(128)S(1)} %iota_xor_fusion.order, s32[256]{0:T(256)S(1)} %fusion.3.cols, f32[256]{0:T(256)S(1)} %compare_convert_fusion.live, bf16[8,32,128,128]{3,2,1,0:T(8,128)(2,1)} %bitcast.11, ...), custom_call_target="tpu_custom_call", output_to_operand_aliasing={{}: (5, {})} | custom-call | flops 67108864 | bytes 1048576 | tf_op jit(solution)/shard_map/ladder_products/pallas_call | solution.py:138
  72.0 11.9 %collective-permute-done.4.refs_1_ = bf16[32,64,128]{2,1,0:T(8,128)(2,1)S(1)} collective-permute-done((bf16[32,64,128]{2,1,0:T(8,128)(2,1)}, bf16[32,64,128]{2,1,0:T(8,128)(2,1)S(1)}, u32[]{:S(2)}, u32[]{:S(2)}) %collective-permute-start.4) | collective-permute-done | bytes 524320 | tf_op jit(solution)/shard_map/ppermute | solution.py:238
  83.9 0.0 collective-permute-done.6.refs_3_
  83.9 14.1 %collective-permute-done.5.refs_2_ = bf16[32,64,128]{2,1,0:T(8,128)(2,1)} collective-permute-done((bf16[32,64,128]{2,1,0:T(8,128)(2,1)}, bf16[32,64,128]{2,1,0:T(8,128)(2,1)}, u32[]{:S(2)}, u32[]{:S(2)}) %collective-permute-start.5) | collective-permute-done | bytes 524320 | tf_op jit(solution)/shard_map/ppermute | solution.py:238
  98.0 4.2 %ladder_products.7 = (f32[32,64,128]{2,1,0:T(8,128)S(1)}, bf16[1,32,128,128]{3,2,1,0:T(8,128)(2,1)S(1)}) custom-call(s32[8]{0:T(128)S(1)} %iota_xor_fusion.order, s32[256]{0:T(256)S(1)} %fusion.3.cols, f32[256]{0:T(256)S(1)} %compare_convert_fusion.live, bf16[8,32,128,128]{3,2,1,0:T(8,128)(2,1)} %bitcast.12, ...), custom_call_target="tpu_custom_call", output_to_operand_aliasing={{0}: (8, {})} | custom-call | flops 268435456 | bytes 5242880 | tf_op jit(solution)/shard_map/ladder_products/pallas_call | solution.py:138
  102.2 0.0 collective-permute-done.9.refs_0_
  102.2 2.2 %ladder_products.8.refs_1_ = f32[32,64,128]{2,1,0:T(8,128)S(1)} custom-call(s32[8]{0:T(128)S(1)} %iota_xor_fusion.order, s32[256]{0:T(256)S(1)} %fusion.3.cols, f32[256]{0:T(256)S(1)} %compare_convert_fusion.live, bf16[8,32,128,128]{3,2,1,0:T(8,128)(2,1)} %bitcast.13, ...), custom_call_target="tpu_custom_call", output_to_operand_aliasing={{}: (5, {})} | custom-call | flops 67108864 | bytes 1048576 | tf_op jit(solution)/shard_map/ladder_products/pallas_call | solution.py:138
  104.4 0.0 collective-permute-done.8.refs_0_
  104.5 1.5 %ladder_products.9 = (f32[8,64,128]{2,1,0:T(8,128)S(1)}, f32[8,64,128]{2,1,0:T(8,128)S(1)}, f32[8,64,128]{2,1,0:T(8,128)S(1)}, f32[8,64,128]{2,1,0:T(8,128)S(1)}) custom-call(s32[8]{0:T(128)S(1)} %iota_xor_fusion.order, s32[256]{0:T(256)S(1)} %fusion.3.cols, f32[256]{0:T(256)S(1)} %compare_convert_fusion.live, ...), custom_call_target="tpu_custom_call" | custom-call | flops 67108864 | bytes 1048576 | tf_op jit(solution)/shard_map/ladder_products/pallas_call | solution.py:138
  106.0 0.1 collective-permute-start.11
  106.1 0.5 collective-permute-start.10
  106.6 1.0 collective-permute-done.11.got
  107.6 0.2 encode_sums.1
  107.8 1.6 %collective-permute-start.12 = (s16[9,64,128]{2,1,0:T(8,128)(2,1)S(1)}, s16[9,64,128]{2,1,0:T(8,128)(2,1)S(1)}, u32[]{:S(2)}, u32[]{:S(2)}) collective-permute-start(s16[9,64,128]{2,1,0:T(8,128)(2,1)S(1)} %encode_sums.1), channel_id=1, source_target_pairs={{0,2},{1,3},{2,0},{3,1},{4,6},{5,7},{6,4},{7,5},{8,10},{9,11},{10,... | collective-permute-start | bytes 442376 | tf_op jit(solution)/shard_map/ppermute | solution.py:292
  109.4 0.0 collective-permute-done.10.got
  109.4 4.4 %collective-permute-done.12.refs_0_ = s16[9,64,128]{2,1,0:T(8,128)(2,1)S(1)} collective-permute-done((s16[9,64,128]{2,1,0:T(8,128)(2,1)S(1)}, s16[9,64,128]{2,1,0:T(8,128)(2,1)S(1)}, u32[]{:S(2)}, u32[]{:S(2)}) %collective-permute-start.12) | collective-permute-done | bytes 147488 | tf_op jit(solution)/shard_map/ppermute | solution.py:292
  113.8 0.9 decode_sums.1
  (13 shorter events, 0.1 us)
Async XLA Ops:
  0.0 7.0 %collective-permute-start = (s32[256]{0:T(256)}, s32[256]{0:T(256)S(1)}, u32[]{:S(2)}, u32[]{:S(2)}) collective-permute-start(s32[256]{0:T(256)} %rows.1), channel_id=1, source_target_pairs={{0,16},{4,20},{8,24},{12,28},{16,0},{20,4},{24,8},{28,12},{1,17},{... | collective-permute-start | bytes 3080 | tf_op jit(solution)/shard_map/ppermute | solution.py:238
  4.8 2.2 %copy-start.2 = (s32[256]{0:T(256)S(1)}, s32[256]{0:T(256)}, u32[]{:S(2)}) copy-start(s32[256]{0:T(256)} %rows.1) | copy-start | bytes 3076
  7.0 49.4 %copy-start = (bf16[64,32768]{1,0:T(8,128)(2,1)}, bf16[64,32768]{1,0:T(8,128)(2,1)S(1)}, u32[]{:S(2)}) copy-start(bf16[64,32768]{1,0:T(8,128)(2,1)S(1)} %stage_amplitudes.1.amp) | copy-start | bytes 12582916
  7.0 4.1 %collective-permute-start.1 = (s32[512]{0:T(512)S(1)}, s32[512]{0:T(512)S(1)}, u32[]{:S(2)}, u32[]{:S(2)}) collective-permute-start(s32[512]{0:T(512)S(1)} %pad_add_fusion), channel_id=1, source_target_pairs={{0,8},{4,12},{8,0},{12,4},{16,24},{20,28},{24,16},{28,20},{1,9},{5... | collective-permute-start | bytes 6152 | tf_op jit(solution)/shard_map/ppermute | solution.py:238
  8.7 7.3 %copy-start.3 = (s32[8]{0:T(128)S(1)}, s32[8]{0:T(128)}, u32[]{:S(2)}) copy-start(s32[8]{0:T(128)} %param.6) | copy-start | bytes 100
  9.4 36.5 %collective-permute-start.3 = (bf16[32,64,128]{2,1,0:T(8,128)(2,1)S(1)}, bf16[32,64,128]{2,1,0:T(8,128)(2,1)S(1)}, u32[]{:S(2)}, u32[]{:S(2)}) collective-permute-start(bf16[32,64,128]{2,1,0:T(8,128)(2,1)S(1)} %pick_tiles.9), channel_id=1, source_target_pairs={{0,16},{4,20},{8,24},{12,28},{16,0},{20,4},{24,8},{28,12},{1,17},{... | collective-permute-start | bytes 1572872 | tf_op jit(solution)/shard_map/ppermute | solution.py:238
  12.0 44.4 %collective-permute-start.7 = (bf16[32,64,128]{2,1,0:T(8,128)(2,1)S(1)}, bf16[32,64,128]{2,1,0:T(8,128)(2,1)S(1)}, u32[]{:S(2)}, u32[]{:S(2)}) collective-permute-start(bf16[32,64,128]{2,1,0:T(8,128)(2,1)S(1)} %pick_tiles.13), channel_id=1, source_target_pairs={{0,24},{4,28},{8,16},{12,20},{16,8},{20,12},{24,0},{28,4},{1,25},{... | collective-permute-start | bytes 1572872 | tf_op jit(solution)/shard_map/ppermute | solution.py:238
  14.4 3.6 %collective-permute-start.2 = (s32[1024]{0:T(1024)S(1)}, s32[1024]{0:T(1024)S(1)}, u32[]{:S(2)}, u32[]{:S(2)}) collective-permute-start(s32[1024]{0:T(1024)S(1)} %constant_dynamic-update-slice_fusion.rows), channel_id=1, source_target_pairs={{0,4},{4,0},{8,12},{12,8},{16,20},{20,16},{24,28},{28,24},{1,5},{5... | collective-permute-start | bytes 12296 | tf_op jit(solution)/shard_map/ppermute | solution.py:238
  47.5 36.4 %collective-permute-start.4 = (bf16[32,64,128]{2,1,0:T(8,128)(2,1)}, bf16[32,64,128]{2,1,0:T(8,128)(2,1)S(1)}, u32[]{:S(2)}, u32[]{:S(2)}) collective-permute-start(bf16[32,64,128]{2,1,0:T(8,128)(2,1)} %pick_tiles.10), channel_id=1, source_target_pairs={{0,4},{4,0},{8,12},{12,8},{16,20},{20,16},{24,28},{28,24},{1,5},{5... | collective-permute-start | bytes 1572872 | tf_op jit(solution)/shard_map/ppermute | solution.py:238
  50.5 33.4 %collective-permute-start.6 = (bf16[32,64,128]{2,1,0:T(8,128)(2,1)}, bf16[32,64,128]{2,1,0:T(8,128)(2,1)}, u32[]{:S(2)}, u32[]{:S(2)}) collective-permute-start(bf16[32,64,128]{2,1,0:T(8,128)(2,1)} %pick_tiles.12), channel_id=1, source_target_pairs={{0,12},{4,8},{8,4},{12,0},{16,28},{20,24},{24,20},{28,16},{1,13},{... | collective-permute-start | bytes 1572872 | tf_op jit(solution)/shard_map/ppermute | solution.py:238
  51.3 50.9 %collective-permute-start.9 = (bf16[32,64,128]{2,1,0:T(8,128)(2,1)S(1)}, bf16[32,64,128]{2,1,0:T(8,128)(2,1)S(1)}, u32[]{:S(2)}, u32[]{:S(2)}) collective-permute-start(bf16[32,64,128]{2,1,0:T(8,128)(2,1)S(1)} %pick_tiles.15), channel_id=1, source_target_pairs={{0,20},{4,16},{8,28},{12,24},{16,4},{20,0},{24,12},{28,8},{1,21},{... | collective-permute-start | bytes 1572872 | tf_op jit(solution)/shard_map/ppermute | solution.py:238
  56.3 6.4 %copy-start.4 = (s32[256]{0:T(256)S(1)}, s32[256]{0:T(256)}, u32[]{:S(2)}) copy-start(s32[256]{0:T(256)} %param.9) | copy-start | bytes 3076
  56.3 41.7 %collective-permute-start.5 = (bf16[32,64,128]{2,1,0:T(8,128)(2,1)}, bf16[32,64,128]{2,1,0:T(8,128)(2,1)}, u32[]{:S(2)}, u32[]{:S(2)}) collective-permute-start(bf16[32,64,128]{2,1,0:T(8,128)(2,1)} %pick_tiles.11), channel_id=1, source_target_pairs={{0,8},{4,12},{8,0},{12,4},{16,24},{20,28},{24,16},{28,20},{1,9},{5... | collective-permute-start | bytes 1572872 | tf_op jit(solution)/shard_map/ppermute | solution.py:238
  57.9 46.5 %collective-permute-start.8 = (bf16[32,64,128]{2,1,0:T(8,128)(2,1)}, bf16[32,64,128]{2,1,0:T(8,128)(2,1)}, u32[]{:S(2)}, u32[]{:S(2)}) collective-permute-start(bf16[32,64,128]{2,1,0:T(8,128)(2,1)} %pick_tiles.14), channel_id=1, source_target_pairs={{0,28},{4,24},{8,20},{12,16},{16,12},{20,8},{24,4},{28,0},{1,29},{... | collective-permute-start | bytes 1572872 | tf_op jit(solution)/shard_map/ppermute | solution.py:238
  59.8 2.2 %copy-start.1 = (bf16[64,32768]{1,0:T(8,128)(2,1)S(1)}, bf16[64,32768]{1,0:T(8,128)(2,1)}, u32[]{:S(2)}) copy-start(bf16[64,32768]{1,0:T(8,128)(2,1)} %copy-done) | copy-start | bytes 12582916
  106.0 1.6 %collective-permute-start.11 = (f32[8,64,128]{2,1,0:T(8,128)S(1)}, f32[8,64,128]{2,1,0:T(8,128)S(1)}, u32[]{:S(2)}, u32[]{:S(2)}) collective-permute-start(f32[8,64,128]{2,1,0:T(8,128)S(1)} %get-tuple-element.16), channel_id=1, source_target_pairs={{0,1},{1,0},{2,3},{3,2},{4,5},{5,4},{6,7},{7,6},{8,9},{9,8},{10,11... | collective-permute-start | bytes 786440 | tf_op jit(solution)/shard_map/ppermute | solution.py:292
  106.1 3.3 %collective-permute-start.10 = (f32[8,64,128]{2,1,0:T(8,128)S(1)}, f32[8,64,128]{2,1,0:T(8,128)S(1)}, u32[]{:S(2)}, u32[]{:S(2)}) collective-permute-start(f32[8,64,128]{2,1,0:T(8,128)S(1)} %get-tuple-element.14), channel_id=1, source_target_pairs={{0,1},{1,0},{2,3},{3,2},{4,5},{5,4},{6,7},{7,6},{8,9},{9,8},{10,11... | collective-permute-start | bytes 786440 | tf_op jit(solution)/shard_map/ppermute | solution.py:292
  107.8 6.0 %collective-permute-start.12 = (s16[9,64,128]{2,1,0:T(8,128)(2,1)S(1)}, s16[9,64,128]{2,1,0:T(8,128)(2,1)S(1)}, u32[]{:S(2)}, u32[]{:S(2)}) collective-permute-start(s16[9,64,128]{2,1,0:T(8,128)(2,1)S(1)} %encode_sums.1), channel_id=1, source_target_pairs={{0,2},{1,3},{2,0},{3,1},{4,6},{5,7},{6,4},{7,5},{8,10},{9,11},{10,... | collective-permute-start | bytes 442376 | tf_op jit(solution)/shard_map/ppermute | solution.py:292

commit v18 on v15

--- a/solution.py
+++ b/solution.py
@@ -58,13 +58,23 @@
     lax.fori_loop(0, per, step, 0, unroll=8)
 
 
-def pick(me, rows, first, amp, per, after=()):
+def passing_pick_kernel(first, per, local_tiles, me, rows, amp, *refs):
+    pick_kernel(first, per, local_tiles, me, rows, amp, refs[-2])
+
+
+def pick(me, rows, first, amp, per, after=(), passed=None):
     occupied, width = amp.shape
-    return pl.pallas_call(
-        functools.partial(pick_kernel, first, per, width // BLK),
-        out_shape=jax.ShapeDtypeStruct((per, occupied, BLK), amp.dtype),
+    shape = jax.ShapeDtypeStruct((per, occupied, BLK), amp.dtype)
+    through = passed is not None
+    if through:
+        after = (passed, *after)
+    kernel = passing_pick_kernel if through else pick_kernel
+    return pl.pallas_call(
+        functools.partial(kernel, first, per, width // BLK),
+        out_shape=[shape, jax.ShapeDtypeStruct(passed.shape, passed.dtype)] if through else shape,
         in_specs=[SMEM_SPEC, SMEM_SPEC, VMEM_SPEC] + [ANY_SPEC] * len(after),
-        out_specs=VMEM_SPEC,
+        out_specs=[VMEM_SPEC, ANY_SPEC] if through else VMEM_SPEC,
+        input_output_aliases={3: 1} if through else {},
         compiler_params=pltpu.CompilerParams(vmem_limit_bytes=8 * MIB),
         cost_estimate=pl.CostEstimate(
             flops=0, bytes_accessed=4 * per * occupied * BLK, transcendentals=0
@@ -230,23 +240,23 @@
     slots = tile_rows.shape[0]
     first_far = swap(tile_rows, near)
     place = {near: (first_far, 0)}
-    known, rows, bit = [0, near], jnp.concatenate([tile_rows, first_far]), 2
+    amp = stage(amplitudes)
+    here = me.reshape(1)
+    picked, own_rows = pick(here, first_far, 0, amp, per, passed=tile_rows)
+    known, rows, bit = [0, near], jnp.concatenate([own_rows, first_far]), 1
     while bit < near:
-        rows = jnp.concatenate([rows, swap(rows, bit)])
+        got = swap(rows, bit)
+        for j, k in enumerate(known):
+            place[k ^ bit] = (got, j * slots)
+        rows = jnp.concatenate([rows, got])
         known = known + [k ^ bit for k in known]
         bit *= 2
-    odd = swap(rows, 1)
-    for j, k in enumerate(known):
-        place.setdefault(k, (rows, j * slots))
-        place[k ^ 1] = (odd, j * slots)
-
-    amp = stage(amplitudes)
-    here = me.reshape(1)
+
     quarter = near // 4
-    far_order = list(range(near, peers, 2)) + list(range(near + 1, peers, 2))
+    far_order = list(range(near, peers))
     far = [far_order[j * quarter : (j + 1) * quarter] for j in range(4)]
-    arrived = {0: pick(here, tile_rows, 0, amp, per)}
-    for k in far[0] + far[1] + list(range(1, near)) + far[2] + far[3]:
+    arrived = {0: pick(here, own_rows, 0, amp, per), near: swap(picked, near)}
+    for k in far[0][1:] + far[1] + list(range(1, near)) + far[2] + far[3]:
         after = ()
         if k in far[2]:
             after = (arrived[far[0][far[2].index(k)]],)

time: 111 us -> 126 us (1.14)
  the two profiles are of different devices: /device:TPU:8 before, /device:TPU:0 now
where the time goes in v18:
time: 126 us; the launch traced here: 125 us
  waiting for transfers between devices  72.5 us (58%)
  Pallas kernels  24.6 us (20%)
  starting transfers between devices  17.7 us (14%)
  other arithmetic  5.76 us (5%)
  local copies, waits for them, and re-layouts  4.5 us (4%)
    ppermute x10, waiting for transfers between devices, swap(): return lax.ppermute(x, 'gx', [(i, i ^ k) for i in range(peers)])  67 us
    ppermute x10, starting transfers between devices, swap(): return lax.ppermute(x, 'gx', [(i, i ^ k) for i in range(peers)])  15.6 us
    pallas_call x5, Pallas kernels, ladder(): pl.pallas_call(functools.partial(ladder_kernel, peers_at, list(ahead), pe...  12.2 us
    pallas_call x8, Pallas kernels, pick(): pl.pallas_call(functools.partial(kernel, first, per, width // BLK), out_s...  9.12 us
    convert_element_type x1, other arithmetic, per_device(): (pair_irrep(row_tile, virt_irreps) == pair_irrep(col_tile, virt_irreps))....  5.72 us
    ppermute x3, waiting for transfers between devices, swap_gy(): return lax.ppermute(x, 'gy', [(i, i ^ k) for i in range(groups)])  5.41 us
    unnamed x7, local copies, waits for them, and re-layouts  2.87 us
  transfers between devices with their start and end apart: 13, of which 8 were waited for; matrix products, arithmetic and copies ran while one was open for 6% of the time, Pallas kernels for 18%

profile of v18, /device:TPU:0, one launch (start us, length us, event | category | flops | bytes accessed | tf_op | source)
XLA Modules:
  0.0 125.3 jit_solution(17793699344688578374)
XLA Ops:
  0.0 0.7 copy.15.refs_0_
  0.7 4.0 %collective-permute-start = (s32[256]{0:T(256)S(1)}, s32[256]{0:T(256)S(1)}, u32[]{:S(2)}, u32[]{:S(2)}) collective-permute-start(s32[256]{0:T(256)S(1)} %copy.15.refs_0_), channel_id=1, source_target_pairs={{0,16},{4,20},{8,24},{12,28},{16,0},{20,4},{24,8},{28,12},{1,17},{... | collective-permute-start | bytes 3080 | tf_op jit(solution)/shard_map/ppermute | solution.py:238
  4.7 1.6 %fusion.4 = (s32[1]{0:T(128)}, s32[1]{0:T(128)}, s32[1]{0:T(128)}, s32[1]{0:T(128)}, s32[1]{0:T(128)}, /*index=5*/s32[1]{0:T(128)}, s32[1]{0:T(128)}, s32[1]{0:T(128)}) fusion(s32[8]{0:T(128)} %param.6), kind=kLoop, calls=%fused_computation.76 | loop fusion | bytes 64 | tf_op jit(solution)/shard_map/gather | solution.py:26
  6.3 5.7 %compare_convert_fusion.live = f32[256]{0:T(256)S(1)} fusion(s32[256]{0:T(256)} %param.9, s32[256]{0:T(256)S(1)} %copy.15.refs_0_, s32[]{:T(128)} %bitcast, s32[]{:T(128)} %bitcast.1, s32[]{:T(128)} %bitcast.2, s32[]{:T(128)} %bitcast.3, s32[]{:T(128)} %bitcast.4, s32[]{:T(128)} %bitcast.5, s32[]{:T(128)} %bitcast.6, s32[]{:T(128)} %bitcast.7, s32[]{:T(128)S(6)} %mul.28, ...), kind=kLoop, calls=%fused_computation.34 | loop fusion | flops 44544 | bytes 3112 | tf_op jit(solution)/shard_map/convert_element_type | solution.py:269
  12.1 2.2 %stage_amplitudes.1.amp = bf16[64,32768]{1,0:T(8,128)(2,1)S(1)} custom-call(bf16[64,32768]{1,0:T(8,128)(2,1)} %source.1), custom_call_target="tpu_custom_call" | custom-call | bytes 4194304 | tf_op jit(solution)/shard_map/stage_amplitudes/pallas_call | solution.py:36
  14.3 0.0 copy-start
  14.3 0.0 collective-permute-done.rows
  14.3 0.7 pick_tiles.8
  15.0 0.1 collective-permute-start.7
  15.1 1.8 %collective-permute-start.1 = (s32[512]{0:T(512)S(1)}, s32[512]{0:T(512)S(1)}, u32[]{:S(2)}, u32[]{:S(2)}) collective-permute-start(s32[512]{0:T(512)S(1)} %pad_add_fusion.1), channel_id=1, source_target_pairs={{0,4},{4,0},{8,12},{12,8},{16,20},{20,16},{24,28},{28,24},{1,5},{5... | collective-permute-start | bytes 6152 | tf_op jit(solution)/shard_map/ppermute | solution.py:238
  16.9 1.8 %collective-permute-done.1.rows = s32[512]{0:T(512)S(1)} collective-permute-done((s32[512]{0:T(512)S(1)}, s32[512]{0:T(512)S(1)}, u32[]{:S(2)}, u32[]{:S(2)}) %collective-permute-start.1) | collective-permute-done | bytes 2080 | tf_op jit(solution)/shard_map/ppermute | solution.py:238
  18.8 0.7 pick_tiles.13
  19.5 3.9 %collective-permute-start.6 = (bf16[32,64,128]{2,1,0:T(8,128)(2,1)S(1)}, bf16[32,64,128]{2,1,0:T(8,128)(2,1)S(1)}, u32[]{:S(2)}, u32[]{:S(2)}) collective-permute-start(bf16[32,64,128]{2,1,0:T(8,128)(2,1)S(1)} %pick_tiles.13), channel_id=1, source_target_pairs={{0,20},{4,16},{8,28},{12,24},{16,4},{20,0},{24,12},{28,8},{1,21},{... | collective-permute-start | bytes 1572872 | tf_op jit(solution)/shard_map/ppermute | solution.py:238
  23.4 1.6 %collective-permute-start.3 = (s32[1024]{0:T(1024)S(1)}, s32[1024]{0:T(1024)S(1)}, u32[]{:S(2)}, u32[]{:S(2)}) collective-permute-start(s32[1024]{0:T(1024)S(1)} %pad_add_fusion), channel_id=1, source_target_pairs={{0,8},{4,12},{8,0},{12,4},{16,24},{20,28},{24,16},{28,20},{1,9},{5... | collective-permute-start | bytes 12296 | tf_op jit(solution)/shard_map/ppermute | solution.py:238
  24.9 0.7 pick_tiles.10
  25.7 0.6 collective-permute-start.2
  26.3 11.4 %collective-permute-done.3.rows = s32[1024]{0:T(1024)S(1)} collective-permute-done((s32[1024]{0:T(1024)S(1)}, s32[1024]{0:T(1024)S(1)}, u32[]{:S(2)}, u32[]{:S(2)}) %collective-permute-start.3) | collective-permute-done | bytes 4128 | tf_op jit(solution)/shard_map/ppermute | solution.py:238
  37.7 1.6 %pick_tiles.11 = bf16[32,64,128]{2,1,0:T(8,128)(2,1)} custom-call(s32[1]{0:T(128)} %bitcast.9.me, s32[1024]{0:T(1024)S(1)} %collective-permute-done.3.rows, bf16[64,32768]{1,0:T(8,128)(2,1)S(1)} %stage_amplitudes.1.amp), custom_call_target="tpu_custom_call" | custom-call | bytes 1048576 | tf_op jit(solution)/shard_map/pick_tiles/pallas_call | solution.py:72
  39.2 2.5 %collective-permute-start.4 = (bf16[32,64,128]{2,1,0:T(8,128)(2,1)}, bf16[32,64,128]{2,1,0:T(8,128)(2,1)S(1)}, u32[]{:S(2)}, u32[]{:S(2)}) collective-permute-start(bf16[32,64,128]{2,1,0:T(8,128)(2,1)} %pick_tiles.11), channel_id=1, source_target_pairs={{0,8},{4,12},{8,0},{12,4},{16,24},{20,28},{24,16},{28,20},{1,9},{5... | collective-permute-start | bytes 1572872 | tf_op jit(solution)/shard_map/ppermute | solution.py:238
  41.7 1.6 %pick_tiles.12 = bf16[32,64,128]{2,1,0:T(8,128)(2,1)} custom-call(s32[1]{0:T(128)} %bitcast.9.me, s32[1024]{0:T(1024)S(1)} %collective-permute-done.3.rows, bf16[64,32768]{1,0:T(8,128)(2,1)S(1)} %stage_amplitudes.1.amp), custom_call_target="tpu_custom_call" | custom-call | bytes 1048576 | tf_op jit(solution)/shard_map/pick_tiles/pallas_call | solution.py:72
  43.3 1.0 collective-permute-start.5
  44.3 8.8 %collective-permute-done.7.refs_0_ = bf16[32,64,128]{2,1,0:T(8,128)(2,1)S(1)} collective-permute-done((bf16[32,64,128]{2,1,0:T(8,128)(2,1)S(1)}, bf16[32,64,128]{2,1,0:T(8,128)(2,1)S(1)}, u32[]{:S(2)}, u32[]{:S(2)}) %collective-permute-start.7) | collective-permute-done | bytes 524320 | tf_op jit(solution)/shard_map/ppermute | solution.py:238
  53.1 1.6 %pick_tiles.15 = bf16[32,64,128]{2,1,0:T(8,128)(2,1)} custom-call(s32[1]{0:T(128)} %bitcast.9.me, s32[1024]{0:T(1024)S(1)} %collective-permute-done.3.rows, bf16[64,32768]{1,0:T(8,128)(2,1)S(1)} %stage_amplitudes.1.amp, bf16[32,64,128]{2,1,0:T(8,128)(2,1)S(1)} %collective-permute-done.7.refs_0_), custom_call_target="tpu_custom_call" | custom-call | bytes 1048576 | tf_op jit(solution)/shard_map/pick_tiles/pallas_call | solution.py:72
  54.7 0.1 collective-permute-start.9
  54.8 10.5 %collective-permute-done.6.refs_0_.refs_1_ = bf16[32,64,128]{2,1,0:T(8,128)(2,1)S(1)} collective-permute-done((bf16[32,64,128]{2,1,0:T(8,128)(2,1)S(1)}, bf16[32,64,128]{2,1,0:T(8,128)(2,1)S(1)}, u32[]{:S(2)}, u32[]{:S(2)}) %collective-permute-start.6) | collective-permute-done | bytes 524320 | tf_op jit(solution)/shard_map/ppermute | solution.py:238
  65.2 1.6 %pick_tiles.14 = bf16[32,64,128]{2,1,0:T(8,128)(2,1)} custom-call(s32[1]{0:T(128)} %bitcast.9.me, s32[1024]{0:T(1024)S(1)} %collective-permute-done.3.rows, bf16[64,32768]{1,0:T(8,128)(2,1)S(1)} %stage_amplitudes.1.amp, bf16[32,64,128]{2,1,0:T(8,128)(2,1)S(1)} %collective-permute-done.7.refs_0_, bf16[32,64,128]{2,1,0:T(8,128)(2,1)S(1)} %collective-permute-done.6.refs_0_.refs_1_), custom_call_target="tpu_custom_call" | custom-call | bytes 1048576 | tf_op jit(solution)/shard_map/pick_tiles/pallas_call | solution.py:72
  66.8 0.1 collective-permute-start.8
  66.9 0.0 copy-done.2
  66.9 2.2 %copy-done.1 = bf16[64,32768]{1,0:T(8,128)(2,1)S(1)} copy-done((bf16[64,32768]{1,0:T(8,128)(2,1)S(1)}, bf16[64,32768]{1,0:T(8,128)(2,1)}, u32[]{:S(2)}) %copy-start.1) | copy-done | bytes 4194328
  69.1 0.7 pick_tiles.9.refs_0_
  69.8 2.2 %ladder_products.5.refs_1_ = f32[32,64,128]{2,1,0:T(8,128)S(1)} custom-call(s32[8]{0:T(128)S(1)} %iota_xor_fusion.order, s32[256]{0:T(256)S(1)} %fusion.3.cols, f32[256]{0:T(256)S(1)} %compare_convert_fusion.live, bf16[8,32,128,128]{3,2,1,0:T(8,128)(2,1)} %bitcast.10, bf16[32,64,128]{2,1,0:T(8,128)(2,1)S(1)} %collective-permute-done.7.refs_0_), custom_call_target="tpu_custom_call" | custom-call | flops 67108864 | bytes 1048576 | tf_op jit(solution)/shard_map/ladder_products/pallas_call | solution.py:148
  72.0 2.2 %ladder_products.6.refs_4_ = f32[32,64,128]{2,1,0:T(8,128)S(1)} custom-call(s32[8]{0:T(128)S(1)} %iota_xor_fusion.order, s32[256]{0:T(256)S(1)} %fusion.3.cols, f32[256]{0:T(256)S(1)} %compare_convert_fusion.live, bf16[8,32,128,128]{3,2,1,0:T(8,128)(2,1)} %bitcast.11, ...), custom_call_target="tpu_custom_call", output_to_operand_aliasing={{}: (5, {})} | custom-call | flops 67108864 | bytes 1048576 | tf_op jit(solution)/shard_map/ladder_products/pallas_call | solution.py:148
  74.3 0.0 collective-permute-done.2.refs_1_
  74.3 22.6 %collective-permute-done.4.refs_2_ = bf16[32,64,128]{2,1,0:T(8,128)(2,1)S(1)} collective-permute-done((bf16[32,64,128]{2,1,0:T(8,128)(2,1)}, bf16[32,64,128]{2,1,0:T(8,128)(2,1)S(1)}, u32[]{:S(2)}, u32[]{:S(2)}) %collective-permute-start.4) | collective-permute-done | bytes 524320 | tf_op jit(solution)/shard_map/ppermute | solution.py:238
  96.9 11.9 %collective-permute-done.5.refs_3_ = bf16[32,64,128]{2,1,0:T(8,128)(2,1)} collective-permute-done((bf16[32,64,128]{2,1,0:T(8,128)(2,1)}, bf16[32,64,128]{2,1,0:T(8,128)(2,1)}, u32[]{:S(2)}, u32[]{:S(2)}) %collective-permute-start.5) | collective-permute-done | bytes 524320 | tf_op jit(solution)/shard_map/ppermute | solution.py:238
  108.8 4.0 %ladder_products.7 = (f32[32,64,128]{2,1,0:T(8,128)S(1)}, bf16[1,32,128,128]{3,2,1,0:T(8,128)(2,1)S(1)}) custom-call(s32[8]{0:T(128)S(1)} %iota_xor_fusion.order, s32[256]{0:T(256)S(1)} %fusion.3.cols, f32[256]{0:T(256)S(1)} %compare_convert_fusion.live, bf16[8,32,128,128]{3,2,1,0:T(8,128)(2,1)} %bitcast.12, ...), custom_call_target="tpu_custom_call", output_to_operand_aliasing={{0}: (8, {})} | custom-call | flops 268435456 | bytes 5242880 | tf_op jit(solution)/shard_map/ladder_products/pallas_call | solution.py:148
  112.8 0.0 collective-permute-done.9.refs_0_
  112.8 2.7 %ladder_products.8.refs_1_ = f32[32,64,128]{2,1,0:T(8,128)S(1)} custom-call(s32[8]{0:T(128)S(1)} %iota_xor_fusion.order, s32[256]{0:T(256)S(1)} %fusion.3.cols, f32[256]{0:T(256)S(1)} %compare_convert_fusion.live, bf16[8,32,128,128]{3,2,1,0:T(8,128)(2,1)} %bitcast.13, ...), custom_call_target="tpu_custom_call", output_to_operand_aliasing={{}: (5, {})} | custom-call | flops 67108864 | bytes 1048576 | tf_op jit(solution)/shard_map/ladder_products/pallas_call | solution.py:148
  115.6 0.0 collective-permute-done.8.refs_0_
  115.6 1.1 ladder_products.9
  116.6 0.1 collective-permute-start.11
  116.7 0.5 collective-permute-start.10
  117.2 1.0 collective-permute-done.11.got
  118.2 0.2 encode_sums.1
  118.4 1.6 %collective-permute-start.12 = (s16[9,64,128]{2,1,0:T(8,128)(2,1)S(1)}, s16[9,64,128]{2,1,0:T(8,128)(2,1)S(1)}, u32[]{:S(2)}, u32[]{:S(2)}) collective-permute-start(s16[9,64,128]{2,1,0:T(8,128)(2,1)S(1)} %encode_sums.1), channel_id=1, source_target_pairs={{0,2},{1,3},{2,0},{3,1},{4,6},{5,7},{6,4},{7,5},{8,10},{9,11},{10,... | collective-permute-start | bytes 442376 | tf_op jit(solution)/shard_map/ppermute | solution.py:292
  120.0 0.0 collective-permute-done.10.got
  120.0 4.4 %collective-permute-done.12.refs_0_ = s16[9,64,128]{2,1,0:T(8,128)(2,1)S(1)} collective-permute-done((s16[9,64,128]{2,1,0:T(8,128)(2,1)S(1)}, s16[9,64,128]{2,1,0:T(8,128)(2,1)S(1)}, u32[]{:S(2)}, u32[]{:S(2)}) %collective-permute-start.12) | collective-permute-done | bytes 147488 | tf_op jit(solution)/shard_map/ppermute | solution.py:292
  124.4 0.9 decode_sums.1
  (7 shorter events, 0.0 us)
Async XLA Ops:
  0.7 13.6 %collective-permute-start = (s32[256]{0:T(256)S(1)}, s32[256]{0:T(256)S(1)}, u32[]{:S(2)}, u32[]{:S(2)}) collective-permute-start(s32[256]{0:T(256)S(1)} %copy.15.refs_0_), channel_id=1, source_target_pairs={{0,16},{4,20},{8,24},{12,28},{16,0},{20,4},{24,8},{28,12},{1,17},{... | collective-permute-start | bytes 3080 | tf_op jit(solution)/shard_map/ppermute | solution.py:238
  14.3 51.0 %copy-start = (bf16[64,32768]{1,0:T(8,128)(2,1)}, bf16[64,32768]{1,0:T(8,128)(2,1)S(1)}, u32[]{:S(2)}) copy-start(bf16[64,32768]{1,0:T(8,128)(2,1)S(1)} %stage_amplitudes.1.amp) | copy-start | bytes 12582916
  15.0 38.1 %collective-permute-start.7 = (bf16[32,64,128]{2,1,0:T(8,128)(2,1)S(1)}, bf16[32,64,128]{2,1,0:T(8,128)(2,1)S(1)}, u32[]{:S(2)}, u32[]{:S(2)}) collective-permute-start(bf16[32,64,128]{2,1,0:T(8,128)(2,1)S(1)} %get-tuple-element.14), channel_id=1, source_target_pairs={{0,16},{4,20},{8,24},{12,28},{16,0},{20,4},{24,8},{28,12},{1,17},{... | collective-permute-start | bytes 1572872 | tf_op jit(solution)/shard_map/ppermute | solution.py:238
  15.1 3.7 %collective-permute-start.1 = (s32[512]{0:T(512)S(1)}, s32[512]{0:T(512)S(1)}, u32[]{:S(2)}, u32[]{:S(2)}) collective-permute-start(s32[512]{0:T(512)S(1)} %pad_add_fusion.1), channel_id=1, source_target_pairs={{0,4},{4,0},{8,12},{12,8},{16,20},{20,16},{24,28},{28,24},{1,5},{5... | collective-permute-start | bytes 6152 | tf_op jit(solution)/shard_map/ppermute | solution.py:238
  19.5 45.7 %collective-permute-start.6 = (bf16[32,64,128]{2,1,0:T(8,128)(2,1)S(1)}, bf16[32,64,128]{2,1,0:T(8,128)(2,1)S(1)}, u32[]{:S(2)}, u32[]{:S(2)}) collective-permute-start(bf16[32,64,128]{2,1,0:T(8,128)(2,1)S(1)} %pick_tiles.13), channel_id=1, source_target_pairs={{0,20},{4,16},{8,28},{12,24},{16,4},{20,0},{24,12},{28,8},{1,21},{... | collective-permute-start | bytes 1572872 | tf_op jit(solution)/shard_map/ppermute | solution.py:238
  23.4 14.3 %collective-permute-start.3 = (s32[1024]{0:T(1024)S(1)}, s32[1024]{0:T(1024)S(1)}, u32[]{:S(2)}, u32[]{:S(2)}) collective-permute-start(s32[1024]{0:T(1024)S(1)} %pad_add_fusion), channel_id=1, source_target_pairs={{0,8},{4,12},{8,0},{12,4},{16,24},{20,28},{24,16},{28,20},{1,9},{5... | collective-permute-start | bytes 12296 | tf_op jit(solution)/shard_map/ppermute | solution.py:238
  25.7 48.6 %collective-permute-start.2 = (bf16[32,64,128]{2,1,0:T(8,128)(2,1)S(1)}, bf16[32,64,128]{2,1,0:T(8,128)(2,1)S(1)}, u32[]{:S(2)}, u32[]{:S(2)}) collective-permute-start(bf16[32,64,128]{2,1,0:T(8,128)(2,1)S(1)} %pick_tiles.10), channel_id=1, source_target_pairs={{0,4},{4,0},{8,12},{12,8},{16,20},{20,16},{24,28},{28,24},{1,5},{5... | collective-permute-start | bytes 1572872 | tf_op jit(solution)/shard_map/ppermute | solution.py:238
  39.2 57.6 %collective-permute-start.4 = (bf16[32,64,128]{2,1,0:T(8,128)(2,1)}, bf16[32,64,128]{2,1,0:T(8,128)(2,1)S(1)}, u32[]{:S(2)}, u32[]{:S(2)}) collective-permute-start(bf16[32,64,128]{2,1,0:T(8,128)(2,1)} %pick_tiles.11), channel_id=1, source_target_pairs={{0,8},{4,12},{8,0},{12,4},{16,24},{20,28},{24,16},{28,20},{1,9},{5... | collective-permute-start | bytes 1572872 | tf_op jit(solution)/shard_map/ppermute | solution.py:238
  43.3 65.5 %collective-permute-start.5 = (bf16[32,64,128]{2,1,0:T(8,128)(2,1)}, bf16[32,64,128]{2,1,0:T(8,128)(2,1)}, u32[]{:S(2)}, u32[]{:S(2)}) collective-permute-start(bf16[32,64,128]{2,1,0:T(8,128)(2,1)} %pick_tiles.12), channel_id=1, source_target_pairs={{0,12},{4,8},{8,4},{12,0},{16,28},{20,24},{24,20},{28,16},{1,13},{... | collective-permute-start | bytes 1572872 | tf_op jit(solution)/shard_map/ppermute | solution.py:238
  54.7 12.2 %copy-start.2 = (s32[256]{0:T(256)S(1)}, s32[256]{0:T(256)}, u32[]{:S(2)}) copy-start(s32[256]{0:T(256)} %param.9) | copy-start | bytes 3076
  54.7 58.2 %collective-permute-start.9 = (bf16[32,64,128]{2,1,0:T(8,128)(2,1)}, bf16[32,64,128]{2,1,0:T(8,128)(2,1)}, u32[]{:S(2)}, u32[]{:S(2)}) collective-permute-start(bf16[32,64,128]{2,1,0:T(8,128)(2,1)} %pick_tiles.15), channel_id=1, source_target_pairs={{0,24},{4,28},{8,16},{12,20},{16,8},{20,12},{24,0},{28,4},{1,25},{... | collective-permute-start | bytes 1572872 | tf_op jit(solution)/shard_map/ppermute | solution.py:238
  66.8 48.7 %collective-permute-start.8 = (bf16[32,64,128]{2,1,0:T(8,128)(2,1)}, bf16[32,64,128]{2,1,0:T(8,128)(2,1)S(1)}, u32[]{:S(2)}, u32[]{:S(2)}) collective-permute-start(bf16[32,64,128]{2,1,0:T(8,128)(2,1)} %pick_tiles.14), channel_id=1, source_target_pairs={{0,28},{4,24},{8,20},{12,16},{16,12},{20,8},{24,4},{28,0},{1,29},{... | collective-permute-start | bytes 1572872 | tf_op jit(solution)/shard_map/ppermute | solution.py:238
  66.9 2.2 %copy-start.1 = (bf16[64,32768]{1,0:T(8,128)(2,1)S(1)}, bf16[64,32768]{1,0:T(8,128)(2,1)}, u32[]{:S(2)}) copy-start(bf16[64,32768]{1,0:T(8,128)(2,1)} %copy-done) | copy-start | bytes 12582916
  116.6 1.6 %collective-permute-start.11 = (f32[8,64,128]{2,1,0:T(8,128)S(1)}, f32[8,64,128]{2,1,0:T(8,128)S(1)}, u32[]{:S(2)}, u32[]{:S(2)}) collective-permute-start(f32[8,64,128]{2,1,0:T(8,128)S(1)} %get-tuple-element.20), channel_id=1, source_target_pairs={{0,1},{1,0},{2,3},{3,2},{4,5},{5,4},{6,7},{7,6},{8,9},{9,8},{10,11... | collective-permute-start | bytes 786440 | tf_op jit(solution)/shard_map/ppermute | solution.py:292
  116.7 3.3 %collective-permute-start.10 = (f32[8,64,128]{2,1,0:T(8,128)S(1)}, f32[8,64,128]{2,1,0:T(8,128)S(1)}, u32[]{:S(2)}, u32[]{:S(2)}) collective-permute-start(f32[8,64,128]{2,1,0:T(8,128)S(1)} %get-tuple-element.18), channel_id=1, source_target_pairs={{0,1},{1,0},{2,3},{3,2},{4,5},{5,4},{6,7},{7,6},{8,9},{9,8},{10,11... | collective-permute-start | bytes 786440 | tf_op jit(solution)/shard_map/ppermute | solution.py:292
  118.4 6.0 %collective-permute-start.12 = (s16[9,64,128]{2,1,0:T(8,128)(2,1)S(1)}, s16[9,64,128]{2,1,0:T(8,128)(2,1)S(1)}, u32[]{:S(2)}, u32[]{:S(2)}) collective-permute-start(s16[9,64,128]{2,1,0:T(8,128)(2,1)S(1)} %encode_sums.1), channel_id=1, source_target_pairs={{0,2},{1,3},{2,0},{3,1},{4,6},{5,7},{6,4},{7,5},{8,10},{9,11},{10,... | collective-permute-start | bytes 442376 | tf_op jit(solution)/shard_map/ppermute | solution.py:292

commit v19 on v15

--- a/solution.py
+++ b/solution.py
@@ -1,4 +1,5 @@
 import functools
+import math
 
 import jax
 import jax.numpy as jnp
@@ -55,26 +56,28 @@
         out[i] = amp[:, pl.ds(lane, BLK)]
         return carry
 
-    lax.fori_loop(0, per, step, 0, unroll=8)
-
-
-def pick(me, rows, first, amp, per, after=()):
+    lax.fori_loop(0, out.shape[0], step, 0, unroll=math.gcd(out.shape[0], 8))
+
+
+def pick(me, rows, first, amp, per, part, after=()):
     occupied, width = amp.shape
-    return pl.pallas_call(
-        functools.partial(pick_kernel, first, per, width // BLK),
-        out_shape=jax.ShapeDtypeStruct((per, occupied, BLK), amp.dtype),
+    low, count = part
+    return pl.pallas_call(
+        functools.partial(pick_kernel, first + low, per, width // BLK),
+        out_shape=jax.ShapeDtypeStruct((count, occupied, BLK), amp.dtype),
         in_specs=[SMEM_SPEC, SMEM_SPEC, VMEM_SPEC] + [ANY_SPEC] * len(after),
         out_specs=VMEM_SPEC,
         compiler_params=pltpu.CompilerParams(vmem_limit_bytes=8 * MIB),
         cost_estimate=pl.CostEstimate(
-            flops=0, bytes_accessed=4 * per * occupied * BLK, transcendentals=0
+            flops=0, bytes_accessed=4 * count * occupied * BLK, transcendentals=0
         ),
         name="pick_tiles",
     )(me, rows, amp, *after)
 
 
-def add_products(per, base, cols, live, piece, weights, total):
-    unroll = min(UNROLL, per)
+def add_products(base, cols, live, piece, weights, total):
+    count = piece.shape[0]
+    unroll = min(UNROLL, count)
 
     def step(i, carry):
         slots = [i * unroll + u for u in range(unroll)]
@@ -85,11 +88,11 @@
             total[cols[base + s]] += product * live[base + s]
         return carry
 
-    lax.fori_loop(0, per // unroll, step, 0)
-
-
-def ladder_kernel(peers_at, ahead, per, first, last, order, cols, live, w, *refs):
-    count = len(peers_at)
+    lax.fori_loop(0, count // unroll, step, 0)
+
+
+def ladder_kernel(parts, ahead, per, first, last, order, cols, live, w, *refs):
+    count = len(parts)
     pieces, refs = refs[:count], refs[count:]
     if not first:
         start, refs = refs[0], refs[1:]
@@ -99,16 +102,17 @@
         *outs, held, sems = refs
         total = outs[0]
     copies = []
-    for j, k in enumerate([] if last else peers_at + ahead):
+    for j, (k, low, size) in enumerate([] if last else parts + ahead):
         target = held.at[j] if j < count else outs[1].at[j - count]
-        copies.append(pltpu.make_async_copy(w.at[order[k]], target, sems.at[j]))
+        source = w.at[order[k], pl.ds(low, size)]
+        copies.append(pltpu.make_async_copy(source, target, sems.at[j]))
         copies[-1].start()
     if first:
         total[...] = jnp.zeros_like(total)
-    for j, k in enumerate(peers_at):
+    for j, (k, low, _) in enumerate(parts):
         if not last:
             copies[j].wait()
-        add_products(per, order[k] * per, cols, live, pieces[j], held.at[j], total)
+        add_products(order[k] * per + low, cols, live, pieces[j], held.at[j], total)
     for copy in copies[count:]:
         copy.wait()
     if last:
@@ -118,10 +122,10 @@
             at += out.shape[0]
 
 
-def ladder(order, cols, live, w, start, arrived, peers_at, ahead=(), last=None):
-    pieces = [arrived[k] for k in peers_at]
+def ladder(order, cols, live, w, start, arrived, per, parts, ahead=(), last=None):
+    pieces = [arrived[part] for part in parts]
     count = len(pieces)
-    per, occupied, _ = pieces[0].shape
+    size, occupied, _ = pieces[0].shape
     first = start is None
     scratch = []
     if last:
@@ -129,14 +133,14 @@
     else:
         out_shape = [pltpu.VMEM((ABT_X, occupied, BLK), jnp.float32)]
         if ahead:
-            out_shape.append(pltpu.VMEM((len(ahead), per, BLK, BLK), w.dtype))
+            out_shape.append(pltpu.VMEM((len(ahead), ahead[0][2], BLK, BLK), w.dtype))
         scratch = [
-            pltpu.VMEM((count, per, BLK, BLK), w.dtype),
+            pltpu.VMEM((count, size, BLK, BLK), w.dtype),
             pltpu.SemaphoreType.DMA((count + len(ahead),)),
         ]
         w = pltpu.with_memory_space_constraint(w, pltpu.HBM)
     return pl.pallas_call(
-        functools.partial(ladder_kernel, peers_at, list(ahead), per, first, bool(last)),
+        functools.partial(ladder_kernel, parts, list(ahead), per, first, bool(last)),
         out_shape=out_shape,
         in_specs=[SMEM_SPEC] * 3
         + [VMEM_SPEC if last else ANY_SPEC]
@@ -146,8 +150,8 @@
         scratch_shapes=scratch,
         compiler_params=pltpu.CompilerParams(vmem_limit_bytes=8 * MIB),
         cost_estimate=pl.CostEstimate(
-            flops=2 * count * per * occupied * BLK * BLK,
-            bytes_accessed=2 * (count + len(ahead)) * per * BLK * BLK,
+            flops=2 * count * size * occupied * BLK * BLK,
+            bytes_accessed=2 * (count + len(ahead)) * size * BLK * BLK,
             transcendentals=0,
         ),
         name="ladder_products",
@@ -245,14 +249,21 @@
     quarter = near // 4
     far_order = list(range(near, peers, 2)) + list(range(near + 1, peers, 2))
     far = [far_order[j * quarter : (j + 1) * quarter] for j in range(4)]
-    arrived = {0: pick(here, tile_rows, 0, amp, per)}
-    for k in far[0] + far[1] + list(range(1, near)) + far[2] + far[3]:
-        after = ()
-        if k in far[2]:
-            after = (arrived[far[0][far[2].index(k)]],)
-        if k in far[3]:
-            after = (arrived[far[0][far[3].index(k)]], arrived[far[1][far[3].index(k)]])
-        arrived[k] = swap(pick(here, *place[k], amp, per, after), k)
+    every = (0, per)
+    late = per // 4
+    cut = [(0, per - late), (per - late, late)]
+    arrived = {(0, *every): pick(here, tile_rows, 0, amp, per, every)}
+
+    def send(k, part, after=()):
+        arrived[k, *part] = swap(pick(here, *place[k], amp, per, part, after), k)
+
+    for k in far[0] + far[1] + list(range(1, near)):
+        send(k, every)
+    for j in range(quarter):
+        first, second, beside = arrived[far[0][j], *every], arrived[far[1][j], *every], arrived[2 + j, *every]
+        send(far[2][j], every, (first,))
+        send(far[3][j], cut[0], (first, second))
+        send(far[3][j], cut[1], (first, second, beside))
 
     row_tile = mine * row_count + tile_rows
     col_tile = me * ABT_X + tile_cols
@@ -269,13 +280,19 @@
 
     w = w_tiles.reshape(peers, per, BLK, BLK)
     args = (order, cols, live, w)
-    (total,) = ladder(*args, None, arrived, far[0])
-    (total,) = ladder(*args, total, arrived, far[1])
-    total, held = ladder(*args, total, arrived, list(range(near)), ahead=far[3])
-    (total,) = ladder(*args, total, arrived, far[2])
+
+    def parts(ks, part=every):
+        return [(k, *part) for k in ks]
+
+    heads, tails = parts(far[3], cut[0]), parts(far[3], cut[1])
+    (total,) = ladder(*args, None, arrived, per, parts(far[0]))
+    (total,) = ladder(*args, total, arrived, per, parts(far[1]))
+    total, held = ladder(*args, total, arrived, per, parts(range(near)), ahead=tails)
+    (total,) = ladder(*args, total, arrived, per, parts(far[2]))
+    (total,) = ladder(*args, total, arrived, per, heads)
     sizes = (share, (xs - 1) * share) * CORES
     keep, keep_rest, give, give_rest = ladder(
-        order, cols, live, held, total, arrived, far[3], last=sizes
+        order, cols, live, held, total, arrived, per, tails, last=sizes
     )
 
     def swap_gy(x, k):

time: 111 us -> 110 us (level)
  starting transfers between devices: 40.4 us -> 21.5 us
  waiting for transfers between devices: 35.6 us -> 48.4 us
  Pallas kernels: 25.5 us -> 28.2 us
  local copies, waits for them, and re-layouts: 3.61 us -> 5.79 us
    ppermute x10 -> x11, starting transfers between devices: 38.3 us -> 19.4 us  [swap(): return lax.ppermute(x, 'gx', [(i, i ^ k) for i in range(peers)])]
    ppermute x10 -> x11, waiting for transfers between devices: 30.2 us -> 43 us  [swap(): return lax.ppermute(x, 'gx', [(i, i ^ k) for i in range(peers)])]
    pallas_call x13 -> x15, Pallas kernels: 22.2 us -> 24.9 us  [the longest x6 13.6 us: ladder(): pl.pallas_call(functools.partial(ladder_kernel, parts, list(ahead), per,...]
    unnamed x12 -> x16, local copies, waits for them, and re-layouts: 2.92 us -> 5.11 us
  transfers between devices with their start and end apart: 13 -> 14, of which waited for: 6 -> 7; matrix products, arithmetic and copies ran while one was open for 6% -> 6% of each run, Pallas kernels for 21% -> 24%
where the time goes in v19:
time: 110 us; the launch traced here: 109 us
  waiting for transfers between devices  48.4 us (44%)
  Pallas kernels  28.2 us (26%)
  starting transfers between devices  21.5 us (20%)
  local copies, waits for them, and re-layouts  5.79 us (5%)
  other arithmetic  5.1 us (5%)
    ppermute x11, waiting for transfers between devices, swap(): return lax.ppermute(x, 'gx', [(i, i ^ k) for i in range(peers)])  43 us
    ppermute x11, starting transfers between devices, swap(): return lax.ppermute(x, 'gx', [(i, i ^ k) for i in range(peers)])  19.4 us
    pallas_call x6, Pallas kernels, ladder(): pl.pallas_call(functools.partial(ladder_kernel, parts, list(ahead), per,...  13.6 us
    pallas_call x9, Pallas kernels, pick(): pl.pallas_call(functools.partial(pick_kernel, first + low, per, width //...  11.3 us
    ppermute x3, waiting for transfers between devices, swap_gy(): return lax.ppermute(x, 'gy', [(i, i ^ k) for i in range(groups)])  5.42 us
    unnamed x16, local copies, waits for them, and re-layouts  5.11 us
    convert_element_type x1, other arithmetic, per_device(): (pair_irrep(row_tile, virt_irreps) == pair_irrep(col_tile, virt_irreps))....  5.06 us
  transfers between devices with their start and end apart: 14, of which 7 were waited for; matrix products, arithmetic and copies ran while one was open for 6% of the time, Pallas kernels for 24%

profile of v19, /device:TPU:8, one launch (start us, length us, event | category | flops | bytes accessed | tf_op | source)
XLA Modules:
  0.0 109.2 jit_solution(9403567931068847304)
XLA Ops:
  0.0 2.6 %collective-permute-start = (s32[256]{0:T(256)}, s32[256]{0:T(256)S(1)}, u32[]{:S(2)}, u32[]{:S(2)}) collective-permute-start(s32[256]{0:T(256)} %rows.1), channel_id=1, source_target_pairs={{0,16},{4,20},{8,24},{12,28},{16,0},{20,4},{24,8},{28,12},{1,17},{... | collective-permute-start | bytes 3080 | tf_op jit(solution)/shard_map/ppermute | solution.py:232
  2.6 0.7 constant_dynamic-update-slice_fusion.2
  3.3 2.2 %stage_amplitudes.1.amp = bf16[64,32768]{1,0:T(8,128)(2,1)S(1)} custom-call(bf16[64,32768]{1,0:T(8,128)(2,1)} %source.1), custom_call_target="tpu_custom_call" | custom-call | bytes 4194304 | tf_op jit(solution)/shard_map/stage_amplitudes/pallas_call | solution.py:37
  5.5 0.0 copy-start.4
  5.5 0.7 pick_tiles.14
  6.3 1.8 %collective-permute-start.7 = (bf16[32,64,128]{2,1,0:T(8,128)(2,1)S(1)}, bf16[32,64,128]{2,1,0:T(8,128)(2,1)S(1)}, u32[]{:S(2)}, u32[]{:S(2)}) collective-permute-start(bf16[32,64,128]{2,1,0:T(8,128)(2,1)S(1)} %pick_tiles.14), channel_id=1, source_target_pairs={{0,16},{4,20},{8,24},{12,28},{16,0},{20,4},{24,8},{28,12},{1,17},{... | collective-permute-start | bytes 1572872 | tf_op jit(solution)/shard_map/ppermute | solution.py:232
  8.1 0.5 collective-permute-start.1
  8.6 10.5 %collective-permute-done.1 = s32[512]{0:T(512)S(1)} collective-permute-done((s32[512]{0:T(512)S(1)}, s32[512]{0:T(512)S(1)}, u32[]{:S(2)}, u32[]{:S(2)}) %collective-permute-start.1) | collective-permute-done | bytes 2080 | tf_op jit(solution)/shard_map/ppermute | solution.py:232
  19.1 1.6 %pick_tiles.13 = bf16[32,64,128]{2,1,0:T(8,128)(2,1)} custom-call(s32[1]{0:T(128)} %bitcast.9.me, s32[1024]{0:T(1024)S(1)} %constant_dynamic-update-slice_fusion.rows, bf16[64,32768]{1,0:T(8,128)(2,1)S(1)} %stage_amplitudes.1.amp), custom_call_target="tpu_custom_call" | custom-call | bytes 1048576 | tf_op jit(solution)/shard_map/pick_tiles/pallas_call | solution.py:65
  20.6 2.2 %collective-permute-start.6 = (bf16[32,64,128]{2,1,0:T(8,128)(2,1)}, bf16[32,64,128]{2,1,0:T(8,128)(2,1)S(1)}, u32[]{:S(2)}, u32[]{:S(2)}) collective-permute-start(bf16[32,64,128]{2,1,0:T(8,128)(2,1)} %pick_tiles.13), channel_id=1, source_target_pairs={{0,24},{4,28},{8,16},{12,20},{16,8},{20,12},{24,0},{28,4},{1,25},{... | collective-permute-start | bytes 1572872 | tf_op jit(solution)/shard_map/ppermute | solution.py:232
  22.8 1.5 %collective-permute-start.2 = (s32[1024]{0:T(1024)S(1)}, s32[1024]{0:T(1024)S(1)}, u32[]{:S(2)}, u32[]{:S(2)}) collective-permute-start(s32[1024]{0:T(1024)S(1)} %constant_dynamic-update-slice_fusion.rows), channel_id=1, source_target_pairs={{0,4},{4,0},{8,12},{12,8},{16,20},{20,16},{24,28},{28,24},{1,5},{5... | collective-permute-start | bytes 12296 | tf_op jit(solution)/shard_map/ppermute | solution.py:232
  24.3 2.2 %copy-done.1 = bf16[64,32768]{1,0:T(8,128)(2,1)S(1)} copy-done((bf16[64,32768]{1,0:T(8,128)(2,1)S(1)}, bf16[64,32768]{1,0:T(8,128)(2,1)}, u32[]{:S(2)}) %copy-start.1) | copy-done | bytes 4194328
  26.5 1.6 %pick_tiles.11 = bf16[32,64,128]{2,1,0:T(8,128)(2,1)} custom-call(s32[1]{0:T(128)} %bitcast.9.me, s32[1024]{0:T(1024)S(1)} %constant_dynamic-update-slice_fusion.rows, bf16[64,32768]{1,0:T(8,128)(2,1)S(1)} %copy-done.1), custom_call_target="tpu_custom_call" | custom-call | bytes 1048576 | tf_op jit(solution)/shard_map/pick_tiles/pallas_call | solution.py:65
  28.1 0.4 collective-permute-start.4
  28.5 0.0 collective-permute-done.2.rows
  28.5 1.6 %pick_tiles.10 = bf16[32,64,128]{2,1,0:T(8,128)(2,1)} custom-call(s32[1]{0:T(128)} %bitcast.9.me, s32[1024]{0:T(1024)S(1)} %collective-permute-done.2.rows, bf16[64,32768]{1,0:T(8,128)(2,1)S(1)} %copy-done.1), custom_call_target="tpu_custom_call" | custom-call | bytes 1048576 | tf_op jit(solution)/shard_map/pick_tiles/pallas_call | solution.py:65
  30.1 0.5 collective-permute-start.3
  30.6 1.5 %pick_tiles.12 = bf16[32,64,128]{2,1,0:T(8,128)(2,1)} custom-call(s32[1]{0:T(128)} %bitcast.9.me, s32[1024]{0:T(1024)S(1)} %collective-permute-done.2.rows, bf16[64,32768]{1,0:T(8,128)(2,1)S(1)} %copy-done.1), custom_call_target="tpu_custom_call" | custom-call | bytes 1048576 | tf_op jit(solution)/shard_map/pick_tiles/pallas_call | solution.py:65
  32.2 2.5 %collective-permute-start.5 = (bf16[32,64,128]{2,1,0:T(8,128)(2,1)}, bf16[32,64,128]{2,1,0:T(8,128)(2,1)S(1)}, u32[]{:S(2)}, u32[]{:S(2)}) collective-permute-start(bf16[32,64,128]{2,1,0:T(8,128)(2,1)} %pick_tiles.12), channel_id=1, source_target_pairs={{0,12},{4,8},{8,4},{12,0},{16,28},{20,24},{24,20},{28,16},{1,13},{... | collective-permute-start | bytes 1572872 | tf_op jit(solution)/shard_map/ppermute | solution.py:232
  34.7 5.9 %collective-permute-done.7.refs_0_ = bf16[32,64,128]{2,1,0:T(8,128)(2,1)S(1)} collective-permute-done((bf16[32,64,128]{2,1,0:T(8,128)(2,1)S(1)}, bf16[32,64,128]{2,1,0:T(8,128)(2,1)S(1)}, u32[]{:S(2)}, u32[]{:S(2)}) %collective-permute-start.7) | collective-permute-done | bytes 524320 | tf_op jit(solution)/shard_map/ppermute | solution.py:232
  40.6 1.6 %pick_tiles.17 = bf16[32,64,128]{2,1,0:T(8,128)(2,1)} custom-call(s32[1]{0:T(128)} %bitcast.9.me, s32[1024]{0:T(1024)S(1)} %collective-permute-done.2.rows, bf16[64,32768]{1,0:T(8,128)(2,1)S(1)} %copy-done.1, bf16[32,64,128]{2,1,0:T(8,128)(2,1)S(1)} %collective-permute-done.7.refs_0_), custom_call_target="tpu_custom_call" | custom-call | bytes 1048576 | tf_op jit(solution)/shard_map/pick_tiles/pallas_call | solution.py:65
  42.1 4.3 %collective-permute-start.10 = (bf16[32,64,128]{2,1,0:T(8,128)(2,1)}, bf16[32,64,128]{2,1,0:T(8,128)(2,1)}, u32[]{:S(2)}, u32[]{:S(2)}) collective-permute-start(bf16[32,64,128]{2,1,0:T(8,128)(2,1)} %pick_tiles.17), channel_id=1, source_target_pairs={{0,20},{4,16},{8,28},{12,24},{16,4},{20,0},{24,12},{28,8},{1,21},{... | collective-permute-start | bytes 1572872 | tf_op jit(solution)/shard_map/ppermute | solution.py:232
  46.5 10.0 %collective-permute-done.6.refs_0_.refs_1_ = bf16[32,64,128]{2,1,0:T(8,128)(2,1)S(1)} collective-permute-done((bf16[32,64,128]{2,1,0:T(8,128)(2,1)}, bf16[32,64,128]{2,1,0:T(8,128)(2,1)S(1)}, u32[]{:S(2)}, u32[]{:S(2)}) %collective-permute-start.6) | collective-permute-done | bytes 524320 | tf_op jit(solution)/shard_map/ppermute | solution.py:232
  56.5 1.5 %pick_tiles.16 = bf16[24,64,128]{2,1,0:T(8,128)(2,1)} custom-call(s32[1]{0:T(128)} %bitcast.9.me, s32[1024]{0:T(1024)S(1)} %collective-permute-done.2.rows, bf16[64,32768]{1,0:T(8,128)(2,1)S(1)} %copy-done.2, bf16[32,64,128]{2,1,0:T(8,128)(2,1)S(1)} %collective-permute-done.7.refs_0_, bf16[32,64,128]{2,1,0:T(8,128)(2,1)S(1)} %collective-permute-done.6.refs_0_.refs_1_), custom_call_target="tpu_custom_call" | custom-call | bytes 786432 | tf_op jit(solution)/shard_map/pick_tiles/pallas_call | solution.py:65
  57.9 0.1 collective-permute-start.9
  58.0 0.7 fusion.4
  58.7 0.7 pick_tiles.9.refs_0_
  59.4 5.1 %compare_convert_fusion.live = f32[256]{0:T(256)S(1)} fusion(s32[256]{0:T(256)S(1)} %copy-done.6, s32[256]{0:T(256)S(1)} %copy-done.4, s32[]{:T(128)} %bitcast, s32[]{:T(128)} %bitcast.1, s32[]{:T(128)} %bitcast.2, s32[]{:T(128)} %bitcast.3, s32[]{:T(128)} %bitcast.4, s32[]{:T(128)} %bitcast.5, s32[]{:T(128)} %bitcast.6, s32[]{:T(128)} %bitcast.7, ...), kind=kLoop, calls=%fused_computation.36 | loop fusion | flops 44544 | bytes 3112 | tf_op jit(solution)/shard_map/convert_element_type | solution.py:270
  64.5 0.0 collective-permute-done.4.refs_2_
  64.5 2.2 %copy-done.3 = bf16[64,32768]{1,0:T(8,128)(2,1)S(1)} copy-done((bf16[64,32768]{1,0:T(8,128)(2,1)S(1)}, bf16[64,32768]{1,0:T(8,128)(2,1)}, u32[]{:S(2)}) %copy-start.3) | copy-done | bytes 4194328
  66.7 0.6 pick_tiles.15
  67.3 2.9 %collective-permute-start.8 = (bf16[8,64,128]{2,1,0:T(8,128)(2,1)S(1)}, bf16[8,64,128]{2,1,0:T(8,128)(2,1)S(1)}, u32[]{:S(2)}, u32[]{:S(2)}) collective-permute-start(bf16[8,64,128]{2,1,0:T(8,128)(2,1)S(1)} %pick_tiles.15), channel_id=1, source_target_pairs={{0,28},{4,24},{8,20},{12,16},{16,12},{20,8},{24,4},{28,0},{1,29},{... | collective-permute-start | bytes 393224 | tf_op jit(solution)/shard_map/ppermute | solution.py:232
  70.3 2.2 %ladder_products.6.refs_1_ = f32[32,64,128]{2,1,0:T(8,128)S(1)} custom-call(s32[8]{0:T(128)S(1)} %iota_xor_fusion.order, s32[256]{0:T(256)S(1)} %fusion.3.cols, f32[256]{0:T(256)S(1)} %compare_convert_fusion.live, bf16[8,32,128,128]{3,2,1,0:T(8,128)(2,1)} %bitcast.10, bf16[32,64,128]{2,1,0:T(8,128)(2,1)S(1)} %collective-permute-done.7.refs_0_), custom_call_target="tpu_custom_call" | custom-call | flops 67108864 | bytes 1048576 | tf_op jit(solution)/shard_map/ladder_products/pallas_call | solution.py:142
  72.5 2.2 %ladder_products.7.refs_4_ = f32[32,64,128]{2,1,0:T(8,128)S(1)} custom-call(s32[8]{0:T(128)S(1)} %iota_xor_fusion.order, s32[256]{0:T(256)S(1)} %fusion.3.cols, f32[256]{0:T(256)S(1)} %compare_convert_fusion.live, bf16[8,32,128,128]{3,2,1,0:T(8,128)(2,1)} %bitcast.11, ...), custom_call_target="tpu_custom_call", output_to_operand_aliasing={{}: (5, {})} | custom-call | flops 67108864 | bytes 1048576 | tf_op jit(solution)/shard_map/ladder_products/pallas_call | solution.py:142
  74.7 0.0 collective-permute-done.3.refs_1_
  74.7 3.5 %ladder_products.8 = (f32[32,64,128]{2,1,0:T(8,128)S(1)}, bf16[1,8,128,128]{3,2,1,0:T(8,128)(2,1)S(1)}) custom-call(s32[8]{0:T(128)S(1)} %iota_xor_fusion.order, s32[256]{0:T(256)S(1)} %fusion.3.cols, f32[256]{0:T(256)S(1)} %compare_convert_fusion.live, bf16[8,32,128,128]{3,2,1,0:T(8,128)(2,1)} %bitcast.12, ...), custom_call_target="tpu_custom_call", output_to_operand_aliasing={{0}: (8, {})} | custom-call | flops 268435456 | bytes 5242880 | tf_op jit(solution)/shard_map/ladder_products/pallas_call | solution.py:142
  78.3 7.4 %collective-permute-done.10.refs_0_ = bf16[32,64,128]{2,1,0:T(8,128)(2,1)} collective-permute-done((bf16[32,64,128]{2,1,0:T(8,128)(2,1)}, bf16[32,64,128]{2,1,0:T(8,128)(2,1)}, u32[]{:S(2)}, u32[]{:S(2)}) %collective-permute-start.10) | collective-permute-done | bytes 524320 | tf_op jit(solution)/shard_map/ppermute | solution.py:232
  85.7 2.7 %ladder_products.9.refs_1_ = f32[32,64,128]{2,1,0:T(8,128)S(1)} custom-call(s32[8]{0:T(128)S(1)} %iota_xor_fusion.order, s32[256]{0:T(256)S(1)} %fusion.3.cols, f32[256]{0:T(256)S(1)} %compare_convert_fusion.live, bf16[8,32,128,128]{3,2,1,0:T(8,128)(2,1)} %bitcast.13, ...), custom_call_target="tpu_custom_call", output_to_operand_aliasing={{}: (5, {})} | custom-call | flops 67108864 | bytes 1048576 | tf_op jit(solution)/shard_map/ladder_products/pallas_call | solution.py:142
  88.4 9.2 %collective-permute-done.9.refs_0_ = bf16[24,64,128]{2,1,0:T(8,128)(2,1)S(1)} collective-permute-done((bf16[24,64,128]{2,1,0:T(8,128)(2,1)}, bf16[24,64,128]{2,1,0:T(8,128)(2,1)S(1)}, u32[]{:S(2)}, u32[]{:S(2)}) %collective-permute-start.9) | collective-permute-done | bytes 393248 | tf_op jit(solution)/shard_map/ppermute | solution.py:232
  97.6 2.1 %ladder_products.10.refs_1_ = f32[32,64,128]{2,1,0:T(8,128)S(1)} custom-call(s32[8]{0:T(128)S(1)} %iota_xor_fusion.order, s32[256]{0:T(256)S(1)} %fusion.3.cols, f32[256]{0:T(256)S(1)} %compare_convert_fusion.live, bf16[8,32,128,128]{3,2,1,0:T(8,128)(2,1)} %bitcast.14, ...), custom_call_target="tpu_custom_call", output_to_operand_aliasing={{}: (5, {})} | custom-call | flops 50331648 | bytes 786432 | tf_op jit(solution)/shard_map/ladder_products/pallas_call | solution.py:142
  99.7 0.8 ladder_products.11
  100.5 0.1 collective-permute-start.12
  100.6 0.5 collective-permute-start.11
  101.1 1.0 collective-permute-done.12.got
  102.1 0.2 encode_sums.1
  102.3 1.6 %collective-permute-start.13 = (s16[9,64,128]{2,1,0:T(8,128)(2,1)S(1)}, s16[9,64,128]{2,1,0:T(8,128)(2,1)S(1)}, u32[]{:S(2)}, u32[]{:S(2)}) collective-permute-start(s16[9,64,128]{2,1,0:T(8,128)(2,1)S(1)} %encode_sums.1), channel_id=1, source_target_pairs={{0,2},{1,3},{2,0},{3,1},{4,6},{5,7},{6,4},{7,5},{8,10},{9,11},{10,... | collective-permute-start | bytes 442376 | tf_op jit(solution)/shard_map/ppermute | solution.py:299
  103.9 4.4 %collective-permute-done.13.refs_0_ = s16[9,64,128]{2,1,0:T(8,128)(2,1)S(1)} collective-permute-done((s16[9,64,128]{2,1,0:T(8,128)(2,1)S(1)}, s16[9,64,128]{2,1,0:T(8,128)(2,1)S(1)}, u32[]{:S(2)}, u32[]{:S(2)}) %collective-permute-start.13) | collective-permute-done | bytes 147488 | tf_op jit(solution)/shard_map/ppermute | solution.py:299
  108.3 0.9 decode_sums.1
  (21 shorter events, 0.1 us)
Async XLA Ops:
  0.0 5.5 %collective-permute-start = (s32[256]{0:T(256)}, s32[256]{0:T(256)S(1)}, u32[]{:S(2)}, u32[]{:S(2)}) collective-permute-start(s32[256]{0:T(256)} %rows.1), channel_id=1, source_target_pairs={{0,16},{4,20},{8,24},{12,28},{16,0},{20,4},{24,8},{28,12},{1,17},{... | collective-permute-start | bytes 3080 | tf_op jit(solution)/shard_map/ppermute | solution.py:232
  5.5 15.1 %copy-start = (bf16[64,32768]{1,0:T(8,128)(2,1)}, bf16[64,32768]{1,0:T(8,128)(2,1)S(1)}, u32[]{:S(2)}) copy-start(bf16[64,32768]{1,0:T(8,128)(2,1)S(1)} %stage_amplitudes.1.amp) | copy-start | bytes 12582916
  5.5 2.5 %copy-start.4 = (s32[256]{0:T(256)S(1)}, s32[256]{0:T(256)}, u32[]{:S(2)}) copy-start(s32[256]{0:T(256)} %rows.1) | copy-start | bytes 3076
  6.3 34.3 %collective-permute-start.7 = (bf16[32,64,128]{2,1,0:T(8,128)(2,1)S(1)}, bf16[32,64,128]{2,1,0:T(8,128)(2,1)S(1)}, u32[]{:S(2)}, u32[]{:S(2)}) collective-permute-start(bf16[32,64,128]{2,1,0:T(8,128)(2,1)S(1)} %pick_tiles.14), channel_id=1, source_target_pairs={{0,16},{4,20},{8,24},{12,28},{16,0},{20,4},{24,8},{28,12},{1,17},{... | collective-permute-start | bytes 1572872 | tf_op jit(solution)/shard_map/ppermute | solution.py:232
  8.1 11.0 %collective-permute-start.1 = (s32[512]{0:T(512)S(1)}, s32[512]{0:T(512)S(1)}, u32[]{:S(2)}, u32[]{:S(2)}) collective-permute-start(s32[512]{0:T(512)S(1)} %pad_add_fusion), channel_id=1, source_target_pairs={{0,8},{4,12},{8,0},{12,4},{16,24},{20,28},{24,16},{28,20},{1,9},{5... | collective-permute-start | bytes 6152 | tf_op jit(solution)/shard_map/ppermute | solution.py:232
  20.6 35.8 %collective-permute-start.6 = (bf16[32,64,128]{2,1,0:T(8,128)(2,1)}, bf16[32,64,128]{2,1,0:T(8,128)(2,1)S(1)}, u32[]{:S(2)}, u32[]{:S(2)}) collective-permute-start(bf16[32,64,128]{2,1,0:T(8,128)(2,1)} %pick_tiles.13), channel_id=1, source_target_pairs={{0,24},{4,28},{8,16},{12,20},{16,8},{20,12},{24,0},{28,4},{1,25},{... | collective-permute-start | bytes 1572872 | tf_op jit(solution)/shard_map/ppermute | solution.py:232
  22.8 5.7 %collective-permute-start.2 = (s32[1024]{0:T(1024)S(1)}, s32[1024]{0:T(1024)S(1)}, u32[]{:S(2)}, u32[]{:S(2)}) collective-permute-start(s32[1024]{0:T(1024)S(1)} %constant_dynamic-update-slice_fusion.rows), channel_id=1, source_target_pairs={{0,4},{4,0},{8,12},{12,8},{16,20},{20,16},{24,28},{28,24},{1,5},{5... | collective-permute-start | bytes 12296 | tf_op jit(solution)/shard_map/ppermute | solution.py:232
  24.3 2.2 %copy-start.1 = (bf16[64,32768]{1,0:T(8,128)(2,1)S(1)}, bf16[64,32768]{1,0:T(8,128)(2,1)}, u32[]{:S(2)}) copy-start(bf16[64,32768]{1,0:T(8,128)(2,1)} %copy-done) | copy-start | bytes 12582916
  28.1 36.4 %collective-permute-start.4 = (bf16[32,64,128]{2,1,0:T(8,128)(2,1)}, bf16[32,64,128]{2,1,0:T(8,128)(2,1)S(1)}, u32[]{:S(2)}, u32[]{:S(2)}) collective-permute-start(bf16[32,64,128]{2,1,0:T(8,128)(2,1)} %pick_tiles.11), channel_id=1, source_target_pairs={{0,8},{4,12},{8,0},{12,4},{16,24},{20,28},{24,16},{28,20},{1,9},{5... | collective-permute-start | bytes 1572872 | tf_op jit(solution)/shard_map/ppermute | solution.py:232
  30.1 16.4 %copy-start.6 = (s32[256]{0:T(256)S(1)}, s32[256]{0:T(256)}, u32[]{:S(2)}) copy-start(s32[256]{0:T(256)} %param.9) | copy-start | bytes 3076
  30.1 26.4 %copy-start.2 = (bf16[64,32768]{1,0:T(8,128)(2,1)S(1)}, bf16[64,32768]{1,0:T(8,128)(2,1)}, u32[]{:S(2)}) copy-start(bf16[64,32768]{1,0:T(8,128)(2,1)} %copy-done) | copy-start | bytes 12582916
  30.1 44.6 %collective-permute-start.3 = (bf16[32,64,128]{2,1,0:T(8,128)(2,1)}, bf16[32,64,128]{2,1,0:T(8,128)(2,1)S(1)}, u32[]{:S(2)}, u32[]{:S(2)}) collective-permute-start(bf16[32,64,128]{2,1,0:T(8,128)(2,1)} %pick_tiles.10), channel_id=1, source_target_pairs={{0,4},{4,0},{8,12},{12,8},{16,20},{20,16},{24,28},{28,24},{1,5},{5... | collective-permute-start | bytes 1572872 | tf_op jit(solution)/shard_map/ppermute | solution.py:232
  32.2 25.9 %copy-start.5 = (s32[8]{0:T(128)S(1)}, s32[8]{0:T(128)}, u32[]{:S(2)}) copy-start(s32[8]{0:T(128)} %param.6) | copy-start | bytes 100
  32.2 42.6 %collective-permute-start.5 = (bf16[32,64,128]{2,1,0:T(8,128)(2,1)}, bf16[32,64,128]{2,1,0:T(8,128)(2,1)S(1)}, u32[]{:S(2)}, u32[]{:S(2)}) collective-permute-start(bf16[32,64,128]{2,1,0:T(8,128)(2,1)} %pick_tiles.12), channel_id=1, source_target_pairs={{0,12},{4,8},{8,4},{12,0},{16,28},{20,24},{24,20},{28,16},{1,13},{... | collective-permute-start | bytes 1572872 | tf_op jit(solution)/shard_map/ppermute | solution.py:232
  42.1 43.5 %collective-permute-start.10 = (bf16[32,64,128]{2,1,0:T(8,128)(2,1)}, bf16[32,64,128]{2,1,0:T(8,128)(2,1)}, u32[]{:S(2)}, u32[]{:S(2)}) collective-permute-start(bf16[32,64,128]{2,1,0:T(8,128)(2,1)} %pick_tiles.17), channel_id=1, source_target_pairs={{0,20},{4,16},{8,28},{12,24},{16,4},{20,0},{24,12},{28,8},{1,21},{... | collective-permute-start | bytes 1572872 | tf_op jit(solution)/shard_map/ppermute | solution.py:232
  57.9 39.7 %collective-permute-start.9 = (bf16[24,64,128]{2,1,0:T(8,128)(2,1)}, bf16[24,64,128]{2,1,0:T(8,128)(2,1)S(1)}, u32[]{:S(2)}, u32[]{:S(2)}) collective-permute-start(bf16[24,64,128]{2,1,0:T(8,128)(2,1)} %pick_tiles.16), channel_id=1, source_target_pairs={{0,28},{4,24},{8,20},{12,16},{16,12},{20,8},{24,4},{28,0},{1,29},{... | collective-permute-start | bytes 1179656 | tf_op jit(solution)/shard_map/ppermute | solution.py:232
  64.5 2.2 %copy-start.3 = (bf16[64,32768]{1,0:T(8,128)(2,1)S(1)}, bf16[64,32768]{1,0:T(8,128)(2,1)}, u32[]{:S(2)}) copy-start(bf16[64,32768]{1,0:T(8,128)(2,1)} %copy-done) | copy-start | bytes 12582916
  67.3 32.3 %collective-permute-start.8 = (bf16[8,64,128]{2,1,0:T(8,128)(2,1)S(1)}, bf16[8,64,128]{2,1,0:T(8,128)(2,1)S(1)}, u32[]{:S(2)}, u32[]{:S(2)}) collective-permute-start(bf16[8,64,128]{2,1,0:T(8,128)(2,1)S(1)} %pick_tiles.15), channel_id=1, source_target_pairs={{0,28},{4,24},{8,20},{12,16},{16,12},{20,8},{24,4},{28,0},{1,29},{... | collective-permute-start | bytes 393224 | tf_op jit(solution)/shard_map/ppermute | solution.py:232
  100.5 1.6 %collective-permute-start.12 = (f32[8,64,128]{2,1,0:T(8,128)S(1)}, f32[8,64,128]{2,1,0:T(8,128)S(1)}, u32[]{:S(2)}, u32[]{:S(2)}) collective-permute-start(f32[8,64,128]{2,1,0:T(8,128)S(1)} %get-tuple-element.16), channel_id=1, source_target_pairs={{0,1},{1,0},{2,3},{3,2},{4,5},{5,4},{6,7},{7,6},{8,9},{9,8},{10,11... | collective-permute-start | bytes 786440 | tf_op jit(solution)/shard_map/ppermute | solution.py:299
  100.6 3.3 %collective-permute-start.11 = (f32[8,64,128]{2,1,0:T(8,128)S(1)}, f32[8,64,128]{2,1,0:T(8,128)S(1)}, u32[]{:S(2)}, u32[]{:S(2)}) collective-permute-start(f32[8,64,128]{2,1,0:T(8,128)S(1)} %get-tuple-element.14), channel_id=1, source_target_pairs={{0,1},{1,0},{2,3},{3,2},{4,5},{5,4},{6,7},{7,6},{8,9},{9,8},{10,11... | collective-permute-start | bytes 786440 | tf_op jit(solution)/shard_map/ppermute | solution.py:299
  102.3 6.0 %collective-permute-start.13 = (s16[9,64,128]{2,1,0:T(8,128)(2,1)S(1)}, s16[9,64,128]{2,1,0:T(8,128)(2,1)S(1)}, u32[]{:S(2)}, u32[]{:S(2)}) collective-permute-start(s16[9,64,128]{2,1,0:T(8,128)(2,1)S(1)} %encode_sums.1), channel_id=1, source_target_pairs={{0,2},{1,3},{2,0},{3,1},{4,6},{5,7},{6,4},{7,5},{8,10},{9,11},{10,... | collective-permute-start | bytes 442376 | tf_op jit(solution)/shard_map/ppermute | solution.py:299

commit v20 on v19

--- a/solution.py
+++ b/solution.py
@@ -250,7 +250,7 @@
     far_order = list(range(near, peers, 2)) + list(range(near + 1, peers, 2))
     far = [far_order[j * quarter : (j + 1) * quarter] for j in range(4)]
     every = (0, per)
-    late = per // 4
+    late = per // 2
     cut = [(0, per - late), (per - late, late)]
     arrived = {(0, *every): pick(here, tile_rows, 0, amp, per, every)}
 

time: 110 us -> 111 us (level)
  waiting for transfers between devices: 48.4 us -> 54 us
  starting transfers between devices: 21.5 us -> 18.2 us
    ppermute x11, waiting for transfers between devices: 43 us -> 48.6 us  [swap(): return lax.ppermute(x, 'gx', [(i, i ^ k) for i in range(peers)])]
    ppermute x11, starting transfers between devices: 19.4 us -> 16.1 us  [swap(): return lax.ppermute(x, 'gx', [(i, i ^ k) for i in range(peers)])]
    unnamed x16 -> x14, local copies, waits for them, and re-layouts: 5.11 us -> 4.4 us
  transfers between devices with their start and end apart: 14 -> 14, of which waited for: 7 -> 9; matrix products, arithmetic and copies ran while one was open for 6% -> 5% of each run, Pallas kernels for 24% -> 23%
where the time goes in v20:
time: 111 us; the launch traced here: 110 us
  waiting for transfers between devices  54 us (49%)
  Pallas kernels  27.4 us (25%)
  starting transfers between devices  18.2 us (16%)
  other arithmetic  5.15 us (5%)
  local copies, waits for them, and re-layouts  5.07 us (5%)
    ppermute x11, waiting for transfers between devices, swap(): return lax.ppermute(x, 'gx', [(i, i ^ k) for i in range(peers)])  48.6 us
    ppermute x11, starting transfers between devices, swap(): return lax.ppermute(x, 'gx', [(i, i ^ k) for i in range(peers)])  16.1 us
    pallas_call x6, Pallas kernels, ladder(): pl.pallas_call(functools.partial(ladder_kernel, parts, list(ahead), per,...  13.5 us
    pallas_call x9, Pallas kernels, pick(): pl.pallas_call(functools.partial(pick_kernel, first + low, per, width //...  10.6 us
    ppermute x3, waiting for transfers between devices, swap_gy(): return lax.ppermute(x, 'gy', [(i, i ^ k) for i in range(groups)])  5.42 us
    convert_element_type x1, other arithmetic, per_device(): (pair_irrep(row_tile, virt_irreps) == pair_irrep(col_tile, virt_irreps))....  5.12 us
    unnamed x14, local copies, waits for them, and re-layouts  4.4 us
  transfers between devices with their start and end apart: 14, of which 9 were waited for; matrix products, arithmetic and copies ran while one was open for 5% of the time, Pallas kernels for 23%

profile of v20, /device:TPU:8, one launch (start us, length us, event | category | flops | bytes accessed | tf_op | source)
XLA Modules:
  0.0 110.1 jit_solution(15149202044064905403)
XLA Ops:
  0.0 2.6 %collective-permute-start = (s32[256]{0:T(256)}, s32[256]{0:T(256)S(1)}, u32[]{:S(2)}, u32[]{:S(2)}) collective-permute-start(s32[256]{0:T(256)} %rows.1), channel_id=1, source_target_pairs={{0,16},{4,20},{8,24},{12,28},{16,0},{20,4},{24,8},{28,12},{1,17},{... | collective-permute-start | bytes 3080 | tf_op jit(solution)/shard_map/ppermute | solution.py:232
  2.6 2.2 %stage_amplitudes.1.amp = bf16[64,32768]{1,0:T(8,128)(2,1)S(1)} custom-call(bf16[64,32768]{1,0:T(8,128)(2,1)} %source.1), custom_call_target="tpu_custom_call" | custom-call | bytes 4194304 | tf_op jit(solution)/shard_map/stage_amplitudes/pallas_call | solution.py:37
  4.8 0.0 copy-start.3
  4.8 0.0 collective-permute-done.rows
  4.8 0.7 pick_tiles.14
  5.5 2.5 %collective-permute-start.7 = (bf16[32,64,128]{2,1,0:T(8,128)(2,1)S(1)}, bf16[32,64,128]{2,1,0:T(8,128)(2,1)S(1)}, u32[]{:S(2)}, u32[]{:S(2)}) collective-permute-start(bf16[32,64,128]{2,1,0:T(8,128)(2,1)S(1)} %pick_tiles.14), channel_id=1, source_target_pairs={{0,16},{4,20},{8,24},{12,28},{16,0},{20,4},{24,8},{28,12},{1,17},{... | collective-permute-start | bytes 1572872 | tf_op jit(solution)/shard_map/ppermute | solution.py:232
  8.1 0.5 collective-permute-start.1
  8.6 10.5 %collective-permute-done.1 = s32[512]{0:T(512)S(1)} collective-permute-done((s32[512]{0:T(512)S(1)}, s32[512]{0:T(512)S(1)}, u32[]{:S(2)}, u32[]{:S(2)}) %collective-permute-start.1) | collective-permute-done | bytes 2080 | tf_op jit(solution)/shard_map/ppermute | solution.py:232
  19.1 1.6 %pick_tiles.13 = bf16[32,64,128]{2,1,0:T(8,128)(2,1)} custom-call(s32[1]{0:T(128)} %bitcast.9.me, s32[1024]{0:T(1024)S(1)} %constant_dynamic-update-slice_fusion.rows, bf16[64,32768]{1,0:T(8,128)(2,1)S(1)} %stage_amplitudes.1.amp), custom_call_target="tpu_custom_call" | custom-call | bytes 1048576 | tf_op jit(solution)/shard_map/pick_tiles/pallas_call | solution.py:65
  20.7 1.6 %pick_tiles.11 = bf16[32,64,128]{2,1,0:T(8,128)(2,1)} custom-call(s32[1]{0:T(128)} %bitcast.9.me, s32[1024]{0:T(1024)S(1)} %constant_dynamic-update-slice_fusion.rows, bf16[64,32768]{1,0:T(8,128)(2,1)S(1)} %stage_amplitudes.1.amp), custom_call_target="tpu_custom_call" | custom-call | bytes 1048576 | tf_op jit(solution)/shard_map/pick_tiles/pallas_call | solution.py:65
  22.2 0.0 collective-permute-start.4
  22.2 1.5 %collective-permute-start.6 = (bf16[32,64,128]{2,1,0:T(8,128)(2,1)}, bf16[32,64,128]{2,1,0:T(8,128)(2,1)S(1)}, u32[]{:S(2)}, u32[]{:S(2)}) collective-permute-start(bf16[32,64,128]{2,1,0:T(8,128)(2,1)} %pick_tiles.13), channel_id=1, source_target_pairs={{0,24},{4,28},{8,16},{12,20},{16,8},{20,12},{24,0},{28,4},{1,25},{... | collective-permute-start | bytes 1572872 | tf_op jit(solution)/shard_map/ppermute | solution.py:232
  23.7 1.5 %collective-permute-start.2 = (s32[1024]{0:T(1024)S(1)}, s32[1024]{0:T(1024)S(1)}, u32[]{:S(2)}, u32[]{:S(2)}) collective-permute-start(s32[1024]{0:T(1024)S(1)} %constant_dynamic-update-slice_fusion.rows), channel_id=1, source_target_pairs={{0,4},{4,0},{8,12},{12,8},{16,20},{20,16},{24,28},{28,24},{1,5},{5... | collective-permute-start | bytes 12296 | tf_op jit(solution)/shard_map/ppermute | solution.py:232
  25.2 0.7 fusion.4
  25.9 1.4 %collective-permute-done.2.rows = s32[1024]{0:T(1024)S(1)} collective-permute-done((s32[1024]{0:T(1024)S(1)}, s32[1024]{0:T(1024)S(1)}, u32[]{:S(2)}, u32[]{:S(2)}) %collective-permute-start.2) | collective-permute-done | bytes 4128 | tf_op jit(solution)/shard_map/ppermute | solution.py:232
  27.3 1.6 %pick_tiles.10 = bf16[32,64,128]{2,1,0:T(8,128)(2,1)} custom-call(s32[1]{0:T(128)} %bitcast.9.me, s32[1024]{0:T(1024)S(1)} %collective-permute-done.2.rows, bf16[64,32768]{1,0:T(8,128)(2,1)S(1)} %stage_amplitudes.1.amp), custom_call_target="tpu_custom_call" | custom-call | bytes 1048576 | tf_op jit(solution)/shard_map/pick_tiles/pallas_call | solution.py:65
  28.8 1.5 %collective-permute-start.3 = (bf16[32,64,128]{2,1,0:T(8,128)(2,1)}, bf16[32,64,128]{2,1,0:T(8,128)(2,1)S(1)}, u32[]{:S(2)}, u32[]{:S(2)}) collective-permute-start(bf16[32,64,128]{2,1,0:T(8,128)(2,1)} %pick_tiles.10), channel_id=1, source_target_pairs={{0,4},{4,0},{8,12},{12,8},{16,20},{20,16},{24,28},{28,24},{1,5},{5... | collective-permute-start | bytes 1572872 | tf_op jit(solution)/shard_map/ppermute | solution.py:232
  30.4 1.6 %pick_tiles.12 = bf16[32,64,128]{2,1,0:T(8,128)(2,1)} custom-call(s32[1]{0:T(128)} %bitcast.9.me, s32[1024]{0:T(1024)S(1)} %collective-permute-done.2.rows, bf16[64,32768]{1,0:T(8,128)(2,1)S(1)} %stage_amplitudes.1.amp), custom_call_target="tpu_custom_call" | custom-call | bytes 1048576 | tf_op jit(solution)/shard_map/pick_tiles/pallas_call | solution.py:65
  31.9 2.9 %collective-permute-start.5 = (bf16[32,64,128]{2,1,0:T(8,128)(2,1)}, bf16[32,64,128]{2,1,0:T(8,128)(2,1)S(1)}, u32[]{:S(2)}, u32[]{:S(2)}) collective-permute-start(bf16[32,64,128]{2,1,0:T(8,128)(2,1)} %pick_tiles.12), channel_id=1, source_target_pairs={{0,12},{4,8},{8,4},{12,0},{16,28},{20,24},{24,20},{28,16},{1,13},{... | collective-permute-start | bytes 1572872 | tf_op jit(solution)/shard_map/ppermute | solution.py:232
  34.8 1.6 %pick_tiles.17 = bf16[32,64,128]{2,1,0:T(8,128)(2,1)} custom-call(s32[1]{0:T(128)} %bitcast.9.me, s32[1024]{0:T(1024)S(1)} %collective-permute-done.2.rows, bf16[64,32768]{1,0:T(8,128)(2,1)S(1)} %stage_amplitudes.1.amp, bf16[32,64,128]{2,1,0:T(8,128)(2,1)S(1)} %collective-permute-done.7.refs_0_), custom_call_target="tpu_custom_call" | custom-call | bytes 1048576 | tf_op jit(solution)/shard_map/pick_tiles/pallas_call | solution.py:65
  36.4 0.1 collective-permute-start.10
  36.4 2.2 %copy-done.1 = bf16[64,32768]{1,0:T(8,128)(2,1)S(1)} copy-done((bf16[64,32768]{1,0:T(8,128)(2,1)S(1)}, bf16[64,32768]{1,0:T(8,128)(2,1)}, u32[]{:S(2)}) %copy-start.1) | copy-done | bytes 4194328
  38.6 0.7 pick_tiles.9.refs_0_
  39.4 5.1 %compare_convert_fusion.live = f32[256]{0:T(256)S(1)} fusion(s32[256]{0:T(256)S(1)} %copy-done.5, s32[256]{0:T(256)S(1)} %copy-done.3, s32[]{:T(128)} %bitcast, s32[]{:T(128)} %bitcast.1, s32[]{:T(128)} %bitcast.2, s32[]{:T(128)} %bitcast.3, s32[]{:T(128)} %bitcast.4, s32[]{:T(128)} %bitcast.5, s32[]{:T(128)} %bitcast.6, s32[]{:T(128)} %bitcast.7, ...), kind=kLoop, calls=%fused_computation.36 | loop fusion | flops 44544 | bytes 3112 | tf_op jit(solution)/shard_map/convert_element_type | solution.py:270
  44.5 8.2 %collective-permute-done.4.refs_2_ = bf16[32,64,128]{2,1,0:T(8,128)(2,1)S(1)} collective-permute-done((bf16[32,64,128]{2,1,0:T(8,128)(2,1)}, bf16[32,64,128]{2,1,0:T(8,128)(2,1)S(1)}, u32[]{:S(2)}, u32[]{:S(2)}) %collective-permute-start.4) | collective-permute-done | bytes 524320 | tf_op jit(solution)/shard_map/ppermute | solution.py:232
  52.7 1.1 %collective-permute-done.6.refs_0_.refs_1_ = bf16[32,64,128]{2,1,0:T(8,128)(2,1)S(1)} collective-permute-done((bf16[32,64,128]{2,1,0:T(8,128)(2,1)}, bf16[32,64,128]{2,1,0:T(8,128)(2,1)S(1)}, u32[]{:S(2)}, u32[]{:S(2)}) %collective-permute-start.6) | collective-permute-done | bytes 524320 | tf_op jit(solution)/shard_map/ppermute | solution.py:232
  53.8 2.2 %copy-done.2 = bf16[64,32768]{1,0:T(8,128)(2,1)S(1)} copy-done((bf16[64,32768]{1,0:T(8,128)(2,1)S(1)}, bf16[64,32768]{1,0:T(8,128)(2,1)}, u32[]{:S(2)}) %copy-start.2) | copy-done | bytes 4194328
  56.0 0.7 pick_tiles.15
  56.7 1.5 %collective-permute-start.8 = (bf16[16,64,128]{2,1,0:T(8,128)(2,1)S(1)}, bf16[16,64,128]{2,1,0:T(8,128)(2,1)S(1)}, u32[]{:S(2)}, u32[]{:S(2)}) collective-permute-start(bf16[16,64,128]{2,1,0:T(8,128)(2,1)S(1)} %pick_tiles.15), channel_id=1, source_target_pairs={{0,28},{4,24},{8,20},{12,16},{16,12},{20,8},{24,4},{28,0},{1,29},{... | collective-permute-start | bytes 786440 | tf_op jit(solution)/shard_map/ppermute | solution.py:232
  58.2 0.7 pick_tiles.16
  58.9 1.5 %collective-permute-start.9 = (bf16[16,64,128]{2,1,0:T(8,128)(2,1)S(1)}, bf16[16,64,128]{2,1,0:T(8,128)(2,1)S(1)}, u32[]{:S(2)}, u32[]{:S(2)}) collective-permute-start(bf16[16,64,128]{2,1,0:T(8,128)(2,1)S(1)} %pick_tiles.16), channel_id=1, source_target_pairs={{0,28},{4,24},{8,20},{12,16},{16,12},{20,8},{24,4},{28,0},{1,29},{... | collective-permute-start | bytes 786440 | tf_op jit(solution)/shard_map/ppermute | solution.py:232
  60.4 2.2 %ladder_products.6.refs_1_ = f32[32,64,128]{2,1,0:T(8,128)S(1)} custom-call(s32[8]{0:T(128)S(1)} %iota_xor_fusion.order, s32[256]{0:T(256)S(1)} %fusion.3.cols, f32[256]{0:T(256)S(1)} %compare_convert_fusion.live, bf16[8,32,128,128]{3,2,1,0:T(8,128)(2,1)} %bitcast.10, bf16[32,64,128]{2,1,0:T(8,128)(2,1)S(1)} %collective-permute-done.7.refs_0_), custom_call_target="tpu_custom_call" | custom-call | flops 67108864 | bytes 1048576 | tf_op jit(solution)/shard_map/ladder_products/pallas_call | solution.py:142
  62.7 2.2 %ladder_products.7.refs_4_ = f32[32,64,128]{2,1,0:T(8,128)S(1)} custom-call(s32[8]{0:T(128)S(1)} %iota_xor_fusion.order, s32[256]{0:T(256)S(1)} %fusion.3.cols, f32[256]{0:T(256)S(1)} %compare_convert_fusion.live, bf16[8,32,128,128]{3,2,1,0:T(8,128)(2,1)} %bitcast.11, ...), custom_call_target="tpu_custom_call", output_to_operand_aliasing={{}: (5, {})} | custom-call | flops 67108864 | bytes 1048576 | tf_op jit(solution)/shard_map/ladder_products/pallas_call | solution.py:142
  64.9 6.2 %collective-permute-done.5.refs_3_ = bf16[32,64,128]{2,1,0:T(8,128)(2,1)S(1)} collective-permute-done((bf16[32,64,128]{2,1,0:T(8,128)(2,1)}, bf16[32,64,128]{2,1,0:T(8,128)(2,1)S(1)}, u32[]{:S(2)}, u32[]{:S(2)}) %collective-permute-start.5) | collective-permute-done | bytes 524320 | tf_op jit(solution)/shard_map/ppermute | solution.py:232
  71.2 3.5 %ladder_products.8 = (f32[32,64,128]{2,1,0:T(8,128)S(1)}, bf16[1,16,128,128]{3,2,1,0:T(8,128)(2,1)S(1)}) custom-call(s32[8]{0:T(128)S(1)} %iota_xor_fusion.order, s32[256]{0:T(256)S(1)} %fusion.3.cols, f32[256]{0:T(256)S(1)} %compare_convert_fusion.live, bf16[8,32,128,128]{3,2,1,0:T(8,128)(2,1)} %bitcast.12, ...), custom_call_target="tpu_custom_call", output_to_operand_aliasing={{0}: (8, {})} | custom-call | flops 268435456 | bytes 5242880 | tf_op jit(solution)/shard_map/ladder_products/pallas_call | solution.py:142
  74.7 10.9 %collective-permute-done.10.refs_0_ = bf16[32,64,128]{2,1,0:T(8,128)(2,1)} collective-permute-done((bf16[32,64,128]{2,1,0:T(8,128)(2,1)}, bf16[32,64,128]{2,1,0:T(8,128)(2,1)}, u32[]{:S(2)}, u32[]{:S(2)}) %collective-permute-start.10) | collective-permute-done | bytes 524320 | tf_op jit(solution)/shard_map/ppermute | solution.py:232
  85.6 2.7 %ladder_products.9.refs_1_ = f32[32,64,128]{2,1,0:T(8,128)S(1)} custom-call(s32[8]{0:T(128)S(1)} %iota_xor_fusion.order, s32[256]{0:T(256)S(1)} %fusion.3.cols, f32[256]{0:T(256)S(1)} %compare_convert_fusion.live, bf16[8,32,128,128]{3,2,1,0:T(8,128)(2,1)} %bitcast.13, ...), custom_call_target="tpu_custom_call", output_to_operand_aliasing={{}: (5, {})} | custom-call | flops 67108864 | bytes 1048576 | tf_op jit(solution)/shard_map/ladder_products/pallas_call | solution.py:142
  88.3 10.2 %collective-permute-done.9.refs_0_ = bf16[16,64,128]{2,1,0:T(8,128)(2,1)S(1)} collective-permute-done((bf16[16,64,128]{2,1,0:T(8,128)(2,1)S(1)}, bf16[16,64,128]{2,1,0:T(8,128)(2,1)S(1)}, u32[]{:S(2)}, u32[]{:S(2)}) %collective-permute-start.9) | collective-permute-done | bytes 262176 | tf_op jit(solution)/shard_map/ppermute | solution.py:232
  98.6 1.9 %ladder_products.10.refs_1_ = f32[32,64,128]{2,1,0:T(8,128)S(1)} custom-call(s32[8]{0:T(128)S(1)} %iota_xor_fusion.order, s32[256]{0:T(256)S(1)} %fusion.3.cols, f32[256]{0:T(256)S(1)} %compare_convert_fusion.live, bf16[8,32,128,128]{3,2,1,0:T(8,128)(2,1)} %bitcast.14, ...), custom_call_target="tpu_custom_call", output_to_operand_aliasing={{}: (5, {})} | custom-call | flops 33554432 | bytes 524288 | tf_op jit(solution)/shard_map/ladder_products/pallas_call | solution.py:142
  100.5 0.9 ladder_products.11
  101.4 0.1 collective-permute-start.12
  101.5 0.5 collective-permute-start.11
  102.0 1.0 collective-permute-done.12.got
  103.0 0.2 encode_sums.1
  103.2 1.6 %collective-permute-start.13 = (s16[9,64,128]{2,1,0:T(8,128)(2,1)S(1)}, s16[9,64,128]{2,1,0:T(8,128)(2,1)S(1)}, u32[]{:S(2)}, u32[]{:S(2)}) collective-permute-start(s16[9,64,128]{2,1,0:T(8,128)(2,1)S(1)} %encode_sums.1), channel_id=1, source_target_pairs={{0,2},{1,3},{2,0},{3,1},{4,6},{5,7},{6,4},{7,5},{8,10},{9,11},{10,... | collective-permute-start | bytes 442376 | tf_op jit(solution)/shard_map/ppermute | solution.py:299
  104.8 0.0 collective-permute-done.11.got
  104.8 4.4 %collective-permute-done.13.refs_0_ = s16[9,64,128]{2,1,0:T(8,128)(2,1)S(1)} collective-permute-done((s16[9,64,128]{2,1,0:T(8,128)(2,1)S(1)}, s16[9,64,128]{2,1,0:T(8,128)(2,1)S(1)}, u32[]{:S(2)}, u32[]{:S(2)}) %collective-permute-start.13) | collective-permute-done | bytes 147488 | tf_op jit(solution)/shard_map/ppermute | solution.py:299
  109.2 0.9 decode_sums.1
  (19 shorter events, 0.1 us)
Async XLA Ops:
  0.0 4.8 %collective-permute-start = (s32[256]{0:T(256)}, s32[256]{0:T(256)S(1)}, u32[]{:S(2)}, u32[]{:S(2)}) collective-permute-start(s32[256]{0:T(256)} %rows.1), channel_id=1, source_target_pairs={{0,16},{4,20},{8,24},{12,28},{16,0},{20,4},{24,8},{28,12},{1,17},{... | collective-permute-start | bytes 3080 | tf_op jit(solution)/shard_map/ppermute | solution.py:232
  4.8 30.0 %copy-start = (bf16[64,32768]{1,0:T(8,128)(2,1)}, bf16[64,32768]{1,0:T(8,128)(2,1)S(1)}, u32[]{:S(2)}) copy-start(bf16[64,32768]{1,0:T(8,128)(2,1)S(1)} %stage_amplitudes.1.amp) | copy-start | bytes 12582916
  4.8 3.3 %copy-start.3 = (s32[256]{0:T(256)S(1)}, s32[256]{0:T(256)}, u32[]{:S(2)}) copy-start(s32[256]{0:T(256)} %rows.1) | copy-start | bytes 3076
  5.5 29.3 %collective-permute-start.7 = (bf16[32,64,128]{2,1,0:T(8,128)(2,1)S(1)}, bf16[32,64,128]{2,1,0:T(8,128)(2,1)S(1)}, u32[]{:S(2)}, u32[]{:S(2)}) collective-permute-start(bf16[32,64,128]{2,1,0:T(8,128)(2,1)S(1)} %pick_tiles.14), channel_id=1, source_target_pairs={{0,16},{4,20},{8,24},{12,28},{16,0},{20,4},{24,8},{28,12},{1,17},{... | collective-permute-start | bytes 1572872 | tf_op jit(solution)/shard_map/ppermute | solution.py:232
  8.1 11.0 %collective-permute-start.1 = (s32[512]{0:T(512)S(1)}, s32[512]{0:T(512)S(1)}, u32[]{:S(2)}, u32[]{:S(2)}) collective-permute-start(s32[512]{0:T(512)S(1)} %pad_add_fusion), channel_id=1, source_target_pairs={{0,8},{4,12},{8,0},{12,4},{16,24},{20,28},{24,16},{28,20},{1,9},{5... | collective-permute-start | bytes 6152 | tf_op jit(solution)/shard_map/ppermute | solution.py:232
  19.1 6.1 %copy-start.4 = (s32[8]{0:T(128)S(1)}, s32[8]{0:T(128)}, u32[]{:S(2)}) copy-start(s32[8]{0:T(128)} %param.6) | copy-start | bytes 100
  22.2 30.4 %collective-permute-start.4 = (bf16[32,64,128]{2,1,0:T(8,128)(2,1)}, bf16[32,64,128]{2,1,0:T(8,128)(2,1)S(1)}, u32[]{:S(2)}, u32[]{:S(2)}) collective-permute-start(bf16[32,64,128]{2,1,0:T(8,128)(2,1)} %pick_tiles.11), channel_id=1, source_target_pairs={{0,8},{4,12},{8,0},{12,4},{16,24},{20,28},{24,16},{28,20},{1,9},{5... | collective-permute-start | bytes 1572872 | tf_op jit(solution)/shard_map/ppermute | solution.py:232
  22.2 31.6 %collective-permute-start.6 = (bf16[32,64,128]{2,1,0:T(8,128)(2,1)}, bf16[32,64,128]{2,1,0:T(8,128)(2,1)S(1)}, u32[]{:S(2)}, u32[]{:S(2)}) collective-permute-start(bf16[32,64,128]{2,1,0:T(8,128)(2,1)} %pick_tiles.13), channel_id=1, source_target_pairs={{0,24},{4,28},{8,16},{12,20},{16,8},{20,12},{24,0},{28,4},{1,25},{... | collective-permute-start | bytes 1572872 | tf_op jit(solution)/shard_map/ppermute | solution.py:232
  23.7 3.6 %collective-permute-start.2 = (s32[1024]{0:T(1024)S(1)}, s32[1024]{0:T(1024)S(1)}, u32[]{:S(2)}, u32[]{:S(2)}) collective-permute-start(s32[1024]{0:T(1024)S(1)} %constant_dynamic-update-slice_fusion.rows), channel_id=1, source_target_pairs={{0,4},{4,0},{8,12},{12,8},{16,20},{20,16},{24,28},{28,24},{1,5},{5... | collective-permute-start | bytes 12296 | tf_op jit(solution)/shard_map/ppermute | solution.py:232
  28.8 36.1 %collective-permute-start.3 = (bf16[32,64,128]{2,1,0:T(8,128)(2,1)}, bf16[32,64,128]{2,1,0:T(8,128)(2,1)S(1)}, u32[]{:S(2)}, u32[]{:S(2)}) collective-permute-start(bf16[32,64,128]{2,1,0:T(8,128)(2,1)} %pick_tiles.10), channel_id=1, source_target_pairs={{0,4},{4,0},{8,12},{12,8},{16,20},{20,16},{24,28},{28,24},{1,5},{5... | collective-permute-start | bytes 1572872 | tf_op jit(solution)/shard_map/ppermute | solution.py:232
  31.9 7.4 %copy-start.5 = (s32[256]{0:T(256)S(1)}, s32[256]{0:T(256)}, u32[]{:S(2)}) copy-start(s32[256]{0:T(256)} %param.9) | copy-start | bytes 3076
  31.9 39.2 %collective-permute-start.5 = (bf16[32,64,128]{2,1,0:T(8,128)(2,1)}, bf16[32,64,128]{2,1,0:T(8,128)(2,1)S(1)}, u32[]{:S(2)}, u32[]{:S(2)}) collective-permute-start(bf16[32,64,128]{2,1,0:T(8,128)(2,1)} %pick_tiles.12), channel_id=1, source_target_pairs={{0,12},{4,8},{8,4},{12,0},{16,28},{20,24},{24,20},{28,16},{1,13},{... | collective-permute-start | bytes 1572872 | tf_op jit(solution)/shard_map/ppermute | solution.py:232
  36.4 49.3 %collective-permute-start.10 = (bf16[32,64,128]{2,1,0:T(8,128)(2,1)}, bf16[32,64,128]{2,1,0:T(8,128)(2,1)}, u32[]{:S(2)}, u32[]{:S(2)}) collective-permute-start(bf16[32,64,128]{2,1,0:T(8,128)(2,1)} %pick_tiles.17), channel_id=1, source_target_pairs={{0,20},{4,16},{8,28},{12,24},{16,4},{20,0},{24,12},{28,8},{1,21},{... | collective-permute-start | bytes 1572872 | tf_op jit(solution)/shard_map/ppermute | solution.py:232
  36.4 2.2 %copy-start.1 = (bf16[64,32768]{1,0:T(8,128)(2,1)S(1)}, bf16[64,32768]{1,0:T(8,128)(2,1)}, u32[]{:S(2)}) copy-start(bf16[64,32768]{1,0:T(8,128)(2,1)} %copy-done) | copy-start | bytes 12582916
  53.8 2.2 %copy-start.2 = (bf16[64,32768]{1,0:T(8,128)(2,1)S(1)}, bf16[64,32768]{1,0:T(8,128)(2,1)}, u32[]{:S(2)}) copy-start(bf16[64,32768]{1,0:T(8,128)(2,1)} %copy-done) | copy-start | bytes 12582916
  56.7 43.8 %collective-permute-start.8 = (bf16[16,64,128]{2,1,0:T(8,128)(2,1)S(1)}, bf16[16,64,128]{2,1,0:T(8,128)(2,1)S(1)}, u32[]{:S(2)}, u32[]{:S(2)}) collective-permute-start(bf16[16,64,128]{2,1,0:T(8,128)(2,1)S(1)} %pick_tiles.15), channel_id=1, source_target_pairs={{0,28},{4,24},{8,20},{12,16},{16,12},{20,8},{24,4},{28,0},{1,29},{... | collective-permute-start | bytes 786440 | tf_op jit(solution)/shard_map/ppermute | solution.py:232
  58.9 39.7 %collective-permute-start.9 = (bf16[16,64,128]{2,1,0:T(8,128)(2,1)S(1)}, bf16[16,64,128]{2,1,0:T(8,128)(2,1)S(1)}, u32[]{:S(2)}, u32[]{:S(2)}) collective-permute-start(bf16[16,64,128]{2,1,0:T(8,128)(2,1)S(1)} %pick_tiles.16), channel_id=1, source_target_pairs={{0,28},{4,24},{8,20},{12,16},{16,12},{20,8},{24,4},{28,0},{1,29},{... | collective-permute-start | bytes 786440 | tf_op jit(solution)/shard_map/ppermute | solution.py:232
  101.4 1.6 %collective-permute-start.12 = (f32[8,64,128]{2,1,0:T(8,128)S(1)}, f32[8,64,128]{2,1,0:T(8,128)S(1)}, u32[]{:S(2)}, u32[]{:S(2)}) collective-permute-start(f32[8,64,128]{2,1,0:T(8,128)S(1)} %get-tuple-element.16), channel_id=1, source_target_pairs={{0,1},{1,0},{2,3},{3,2},{4,5},{5,4},{6,7},{7,6},{8,9},{9,8},{10,11... | collective-permute-start | bytes 786440 | tf_op jit(solution)/shard_map/ppermute | solution.py:299
  101.5 3.3 %collective-permute-start.11 = (f32[8,64,128]{2,1,0:T(8,128)S(1)}, f32[8,64,128]{2,1,0:T(8,128)S(1)}, u32[]{:S(2)}, u32[]{:S(2)}) collective-permute-start(f32[8,64,128]{2,1,0:T(8,128)S(1)} %get-tuple-element.14), channel_id=1, source_target_pairs={{0,1},{1,0},{2,3},{3,2},{4,5},{5,4},{6,7},{7,6},{8,9},{9,8},{10,11... | collective-permute-start | bytes 786440 | tf_op jit(solution)/shard_map/ppermute | solution.py:299
  103.2 6.0 %collective-permute-start.13 = (s16[9,64,128]{2,1,0:T(8,128)(2,1)S(1)}, s16[9,64,128]{2,1,0:T(8,128)(2,1)S(1)}, u32[]{:S(2)}, u32[]{:S(2)}) collective-permute-start(s16[9,64,128]{2,1,0:T(8,128)(2,1)S(1)} %encode_sums.1), channel_id=1, source_target_pairs={{0,2},{1,3},{2,0},{3,1},{4,6},{5,7},{6,4},{7,5},{8,10},{9,11},{10,... | collective-permute-start | bytes 442376 | tf_op jit(solution)/shard_map/ppermute | solution.py:299
